TPU v7x, 32 devices: a whole 2x2x4 slice. The times are simulated.
32 devices in a mesh: segment: 4 (over z), expert: 8 (over y, x, core).
Axes of the slice: x: 2, y: 2, z: 4, core: 2. Of those that a mesh axis runs over, the one named last changes fastest.
Arguments:
- inputs: bfloat16 [4, 2, 1024, 2048], P('segment', None, 'expert'), may hold values from -6 to 6
- entering: bfloat16 [4, 1024, 2048], P('segment', 'expert'), may hold values from -6 to 6
- weight_in: bfloat16 [4, 8, 704, 2048], P('segment', 'expert'), may hold values from -0.125 to 0.125
- weight_out: bfloat16 [4, 8, 704, 2048], P('segment', 'expert'), may hold values from -0.21875 to 0.21875
- gate_probs: bfloat16 [4, 2, 1024, 2], P('segment', None, 'expert'), may hold values from 0.049804688 to 1
- expert_ids: int32 [4, 2, 1024, 2], P('segment', None, 'expert'), may hold values from 0 to 7, as said below
Outputs:
- grad_in: bfloat16 [4, 8, 704, 2048], P('segment', 'expert')
- grad_out: bfloat16 [4, 8, 704, 2048], P('segment', 'expert')
- prob_grads: bfloat16 [4, 2, 1024, 2], P('segment', None, 'expert')
Inputs may be any that keep to these rules, and one draw needn't show every extreme that they name: `expert_ids`: each token names 2 different experts. In each aligned block of 128 tokens of one section and tick no expert is named by more than 48 tokens, and in every section and tick one expert, the same for all blocks of that section and tick, is named by exactly 48 tokens of every block.
All inputs are finite; a program needn't handle non-finite values.
Results may differ from a plain program's by a relative error of at most 0.0085.
Values may be sent and summed in bfloat16 or wider, within the bound.
No kernel may reach another device: no remote copies, remote signals or barrier semaphores. Data moves between devices by JAX's collectives and lax.ppermute only.
A program may use at most 128 MiB of HBM per device.

v0:
```python
import jax
import jax.numpy as jnp
from jax import lax
from jax.sharding import PartitionSpec as P

TICKS = 2


half_root = 0.7071067811865476
density_scale = 0.3989422804014327


def passed_along(block, axis, distance):
    devices = range(lax.axis_size(axis))
    route = [(i - distance, i) for i in devices if i - distance in devices]
    return lax.ppermute(block, axis, route)


def gelu_parts(preact):
    normal_cdf = 0.5 * (1.0 + jax.scipy.special.erf(preact * half_root))
    normal_pdf = density_scale * jnp.exp(-0.5 * preact * preact)
    return (preact * normal_cdf, normal_cdf + preact * normal_pdf)


def slot_places(chosen, experts, capacity):
    flattened = chosen.reshape(-1)
    matches = (flattened[:, None] == jnp.arange(experts, dtype=jnp.int32)[None, :]).astype(
        jnp.int32
    )
    before = jnp.cumsum(matches, axis=0) - matches
    rank_in = jnp.sum(before * matches, axis=1)
    return (flattened * capacity + rank_in).reshape(chosen.shape)


def build_layout(places, slot_count):
    onehot = places[:, :, None] == jnp.arange(slot_count, dtype=jnp.int32)[None, None, :]
    merged = jnp.sum(onehot, axis=1).astype(jnp.bfloat16)
    return (onehot, merged, merged)


def spread_rows(layout, rows):
    return lax.dot_general(
        layout[1], rows, (((0,), (0,)), ((), ())), preferred_element_type=jnp.float32
    ).astype(jnp.bfloat16)


def spread_probs(layout, probs):
    weighted = jnp.where(layout[0], probs.astype(jnp.float32)[:, :, None], 0.0)
    return jnp.sum(weighted, axis=(0, 1)).astype(jnp.bfloat16)


def collect_rows(layout, returned):
    return jnp.dot(layout[1], returned, preferred_element_type=jnp.float32)


def collect_scores(layout, scores):
    picked = jnp.where(layout[0], scores.astype(jnp.float32)[None, None, :], 0.0)
    return jnp.sum(picked, axis=2).astype(jnp.bfloat16)


def expert_pass(rows_x, rows_g, rows_p, w_in, w_out, need_rows):
    contract_feat = (((1,), (1,)), ((), ()))
    contract_rows = (((0,), (0,)), ((), ()))
    preact = lax.dot_general(rows_x, w_in, contract_feat, preferred_element_type=jnp.float32)
    activated, gate_slope = gelu_parts(preact)
    hidden = activated.astype(jnp.bfloat16)
    pulled = lax.dot_general(rows_g, w_out, contract_feat, preferred_element_type=jnp.float32)
    weight_col = rows_p.astype(jnp.float32)[:, None]
    scores = jnp.sum(hidden.astype(jnp.float32) * pulled, axis=1).astype(jnp.bfloat16)
    grad_pre = (weight_col * pulled * gate_slope).astype(jnp.bfloat16)
    grad_y = (weight_col * rows_g.astype(jnp.float32)).astype(jnp.bfloat16)
    part_out = lax.dot_general(hidden, grad_y, contract_rows, preferred_element_type=jnp.float32)
    part_in = lax.dot_general(grad_pre, rows_x, contract_rows, preferred_element_type=jnp.float32)
    returned = None
    if need_rows:
        returned = jnp.dot(grad_pre, w_in, preferred_element_type=jnp.float32).astype(jnp.bfloat16)
    return (returned, scores, part_in, part_out)


def body(inputs, entering, weight_in, weight_out, gate_probs, expert_ids):
    experts = lax.axis_size("expert")
    rows_local = entering.shape[1]
    features = entering.shape[2]
    top_count = expert_ids.shape[3]
    capacity = 3 * rows_local * top_count // (2 * experts)
    slot_count = experts * capacity
    w_in = weight_in[0, 0]
    w_out = weight_out[0, 0]
    layouts = [
        build_layout(slot_places(expert_ids[0, moment], experts, capacity), slot_count)
        for moment in range(TICKS)
    ]
    total_in = jnp.zeros(w_in.shape, jnp.float32)
    total_out = jnp.zeros(w_out.shape, jnp.float32)
    prob_parts = []
    incoming = entering[0]
    for moment in range(TICKS):
        layout = layouts[moment]
        final_tick = moment + 1 == TICKS
        slots_g = spread_rows(layout, incoming).reshape(experts, capacity, features)
        slots_x = spread_rows(layout, inputs[0, moment]).reshape(experts, capacity, features)
        slots_p = spread_probs(layout, gate_probs[0, moment]).reshape(experts, capacity)
        arrived_x, arrived_g, arrived_p = (
            lax.all_to_all(slots_x, "expert", split_axis=0, concat_axis=0, tiled=True),
            lax.all_to_all(slots_g, "expert", split_axis=0, concat_axis=0, tiled=True),
            lax.all_to_all(slots_p, "expert", split_axis=0, concat_axis=0, tiled=True),
        )
        returned, scores, part_in, part_out = expert_pass(
            arrived_x.reshape(slot_count, features),
            arrived_g.reshape(slot_count, features),
            arrived_p.reshape(slot_count),
            w_in,
            w_out,
            not final_tick,
        )
        total_in = total_in + part_in
        total_out = total_out + part_out
        if final_tick:
            back_scores = lax.all_to_all(
                scores.reshape(experts, capacity), "expert", split_axis=0, concat_axis=0, tiled=True
            )
        else:
            back_rows, back_scores = (
                lax.all_to_all(
                    returned.reshape(experts, capacity, features),
                    "expert",
                    split_axis=0,
                    concat_axis=0,
                    tiled=True,
                ),
                lax.all_to_all(
                    scores.reshape(experts, capacity),
                    "expert",
                    split_axis=0,
                    concat_axis=0,
                    tiled=True,
                ),
            )
            summed = collect_rows(layout, back_rows.reshape(slot_count, features))
            leaving = (incoming.astype(jnp.float32) + summed).astype(jnp.bfloat16)
            incoming = passed_along(leaving, "segment", -1)
        prob_parts.append(collect_scores(layout, back_scores.reshape(slot_count)))
    grad_in = total_in.astype(jnp.bfloat16)[None, None]
    grad_out = total_out.astype(jnp.bfloat16)[None, None]
    prob_grads = jnp.stack(prob_parts)[None]
    return (grad_in, grad_out, prob_grads)


def solution(mesh):
    return jax.shard_map(
        body,
        mesh=mesh,
        in_specs=(
            P("segment", None, "expert", None),
            P("segment", "expert", None),
            P("segment", "expert", None, None),
            P("segment", "expert", None, None),
            P("segment", None, "expert", None),
            P("segment", None, "expert", None),
        ),
        out_specs=(
            P("segment", "expert", None, None),
            P("segment", "expert", None, None),
            P("segment", None, "expert", None),
        ),
        check_vma=False,
    )
```

profile of v0, /device:TPU:0, one launch (start us, length us, event | category | flops | bytes accessed | tf_op | source)
XLA Modules:
  0.0 198.0 jit_solution(13708670402742457990)
XLA Ops:
  0.6 0.8 fusion.56
  1.6 0.1 eq.80
  1.8 0.1 eq.76
  1.9 0.6 reduce-window.14
  2.5 0.2 slice_reduce_fusion.1
  2.8 0.1 reduce_sum.95
  3.2 2.8 %convolution_convert_fusion.2 = bf16[384,2048]{1,0:T(8,128)(2,1)} fusion(bf16[1,2,128,2048]{3,2,1,0:T(8,128)(2,1)} %param.6, s32[128,384]{1,0:T(8,128)S(1)} %convert_reduce_fusion.1), kind=kOutput, calls=%fused_computation.19 | convolution fusion | flops 202162176 | bytes 2293760 | tf_op jit(solution)/shard_map/dot_general | solution.py:42
  6.0 5.2 %all-to-all-start.2 = ((bf16[8,48,2048]{2,1,0:T(8,128)(2,1)}), bf16[8,48,2048]{2,1,0:T(8,128)(2,1)}, u32[]{:S(2)}, u32[]{:S(2)}) async-start(bf16[8,48,2048]{2,1,0:T(8,128)(2,1)} %bitcast.95), calls=%async_computation.2 | async-start | bytes 3145728 | tf_op jit(solution)/shard_map/all_to_all | solution.py:104
  11.2 2.8 %convolution_convert_fusion.3 = bf16[384,2048]{1,0:T(8,128)(2,1)} fusion(bf16[1,128,2048]{2,1,0:T(8,128)(2,1)} %param.7, s32[128,384]{1,0:T(8,128)S(1)} %convert_reduce_fusion.1), kind=kOutput, calls=%fused_computation.20 | convolution fusion | flops 202162176 | bytes 2293760 | tf_op jit(solution)/shard_map/dot_general | solution.py:42
  13.9 18.4 %all-to-all-done.2 = bf16[8,48,2048]{2,1,0:T(8,128)(2,1)} async-done(((bf16[8,48,2048]{2,1,0:T(8,128)(2,1)}), bf16[8,48,2048]{2,1,0:T(8,128)(2,1)}, u32[]{:S(2)}, u32[]{:S(2)}) %all-to-all-start.2) | async-done | bytes 1572896 | tf_op jit(solution)/shard_map/all_to_all | solution.py:104
  32.3 4.3 %all-to-all-start.1 = ((bf16[8,48,2048]{2,1,0:T(8,128)(2,1)}), bf16[8,48,2048]{2,1,0:T(8,128)(2,1)}, u32[]{:S(2)}, u32[]{:S(2)}) async-start(bf16[8,48,2048]{2,1,0:T(8,128)(2,1)} %bitcast.94), calls=%async_computation.1 | async-start | bytes 3145728 | tf_op jit(solution)/shard_map/all_to_all | solution.py:105
  36.6 4.1 %fusion.6 = f32[384,704]{0,1:T(8,128)} fusion(bf16[384,2048]{1,0:T(8,128)(2,1)} %bitcast.10, bf16[1,1,704,2048]{3,2,1,0:T(8,128)(2,1)S(1)} %copy-done), kind=kOutput, calls=%fused_computation.10 | convolution fusion | flops 1107296256 | bytes 5537792 | tf_op jit(solution)/shard_map/dot_general | solution.py:64
  40.7 17.0 %all-to-all-done.1 = bf16[8,48,2048]{2,1,0:T(8,128)(2,1)} async-done(((bf16[8,48,2048]{2,1,0:T(8,128)(2,1)}), bf16[8,48,2048]{2,1,0:T(8,128)(2,1)}, u32[]{:S(2)}, u32[]{:S(2)}) %all-to-all-start.1) | async-done | bytes 1572896 | tf_op jit(solution)/shard_map/all_to_all | solution.py:105
  57.6 5.3 %multiply_reduce_fusion.1 = (bf16[384]{0:T(512)(128)(2,1)S(1)}, f32[384,704]{0,1:T(8,128)}) fusion(f32[384,704]{0,1:T(8,128)} %fusion.6, bf16[384,2048]{1,0:T(8,128)(2,1)} %bitcast.6, bf16[1,1,704,2048]{3,2,1,0:T(8,128)(2,1)} %param.9), kind=kOutput, calls=%fused_computation.41 | convolution fusion | flops 1109458560 | bytes 6619904 | tf_op jit(solution)/shard_map/dot_general | solution.py:67
  63.0 0.7 convert_element_type.284
  63.6 3.3 %all-to-all-start.7 = ((bf16[8,1,48]{2,1,0:T(2,128)(2,1)}), bf16[8,1,48]{2,1,0:T(2,128)(2,1)S(1)}, u32[]{:S(2)}, u32[]{:S(2)}) async-start(bf16[8,1,48]{2,1,0:T(2,128)(2,1)} %convert_element_type.284), calls=%async_computation.7 | async-start | bytes 8192 | tf_op jit(solution)/shard_map/all_to_all | solution.py:131
  67.0 4.5 %all-to-all-done.7 = bf16[8,1,48]{2,1,0:T(2,128)(2,1)S(1)} async-done(((bf16[8,1,48]{2,1,0:T(2,128)(2,1)}), bf16[8,1,48]{2,1,0:T(2,128)(2,1)S(1)}, u32[]{:S(2)}, u32[]{:S(2)}) %all-to-all-start.7) | async-done | bytes 800 | tf_op jit(solution)/shard_map/all_to_all | solution.py:131
  71.6 0.2 select_reduce_fusion.1
  71.9 7.0 %all_to_all.49 = bf16[8,1,48]{2,1,0:T(2,128)(2,1)S(1)} all-to-all(bf16[8,1,48]{2,1,0:T(2,128)(2,1)S(1)} %convert_element_type.282), channel_id=1, replica_groups=mesh['segment'=4,'expert'=8] {'expert'}, dimensions={0} | all-to-all | bytes 1536 | tf_op jit(solution)/shard_map/all_to_all | solution.py:106
  79.0 4.3 %fusion.12 = bf16[384,2048]{1,0:T(8,128)(2,1)} fusion(bf16[1,1,704,2048]{3,2,1,0:T(8,128)(2,1)S(1)} %copy-done, f32[384,704]{0,1:T(8,128)} %fusion.6, f32[384,704]{0,1:T(8,128)} %get-tuple-element.12, f32[384]{0:T(512)S(1)} %reshape.233), kind=kOutput, calls=%fused_computation.16 | convolution fusion | flops 1111056384 | bytes 6620672 | tf_op jit(solution)/shard_map/dot_general | solution.py:76
  83.3 4.3 %all-to-all-start.4 = ((bf16[8,48,2048]{2,1,0:T(8,128)(2,1)}), bf16[8,48,2048]{2,1,0:T(8,128)(2,1)}, u32[]{:S(2)}, u32[]{:S(2)}) async-start(bf16[8,48,2048]{2,1,0:T(8,128)(2,1)} %bitcast.96), calls=%async_computation.4 | async-start | bytes 3145728 | tf_op jit(solution)/shard_map/all_to_all | solution.py:124
  87.9 0.1 eq.87
  88.1 0.6 reduce-window.16
  88.7 0.2 slice_reduce_fusion
  89.0 0.1 reduce_sum.99
  89.4 2.8 %convolution_convert_fusion = bf16[384,2048]{1,0:T(8,128)(2,1)} fusion(bf16[1,2,128,2048]{3,2,1,0:T(8,128)(2,1)} %param.6, s32[128,384]{1,0:T(8,128)S(1)} %convert_reduce_fusion), kind=kOutput, calls=%fused_computation.17 | convolution fusion | flops 202162176 | bytes 2293760 | tf_op jit(solution)/shard_map/dot_general | solution.py:42
  92.2 16.5 %all-to-all-done.4 = bf16[8,48,2048]{2,1,0:T(8,128)(2,1)} async-done(((bf16[8,48,2048]{2,1,0:T(8,128)(2,1)}), bf16[8,48,2048]{2,1,0:T(8,128)(2,1)}, u32[]{:S(2)}, u32[]{:S(2)}) %all-to-all-start.4) | async-done | bytes 1572896 | tf_op jit(solution)/shard_map/all_to_all | solution.py:124
  108.7 4.3 %all-to-all-start.6 = ((bf16[8,48,2048]{2,1,0:T(8,128)(2,1)}), bf16[8,48,2048]{2,1,0:T(8,128)(2,1)}, u32[]{:S(2)}, u32[]{:S(2)}) async-start(bf16[8,48,2048]{2,1,0:T(8,128)(2,1)} %bitcast.92), calls=%async_computation.6 | async-start | bytes 3145728 | tf_op jit(solution)/shard_map/all_to_all | solution.py:104
  113.0 2.0 fusion.15
  115.0 1.3 collective-permute-start
  116.3 15.1 %collective-permute-done = bf16[128,2048]{1,0:T(8,128)(2,1)S(1)} collective-permute-done((bf16[128,2048]{1,0:T(8,128)(2,1)S(1)}, bf16[128,2048]{1,0:T(8,128)(2,1)S(1)}, u32[]{:S(2)}, u32[]{:S(2)}) %collective-permute-start) | collective-permute-done | bytes 524320 | tf_op jit(solution)/shard_map/ppermute | solution.py:16
  131.4 1.7 convolution_convert_fusion.1
  133.1 0.9 all-to-all-done.6
  134.0 4.5 %all-to-all-start.5 = ((bf16[8,48,2048]{2,1,0:T(8,128)(2,1)}), bf16[8,48,2048]{2,1,0:T(8,128)(2,1)}, u32[]{:S(2)}, u32[]{:S(2)}) async-start(bf16[8,48,2048]{2,1,0:T(8,128)(2,1)} %bitcast.93), calls=%async_computation.5 | async-start | bytes 3145728 | tf_op jit(solution)/shard_map/all_to_all | solution.py:105
  138.5 4.2 %fusion.2 = f32[384,704]{0,1:T(8,128)} fusion(bf16[384,2048]{1,0:T(8,128)(2,1)} %bitcast.22, bf16[1,1,704,2048]{3,2,1,0:T(8,128)(2,1)S(1)} %copy-done), kind=kOutput, calls=%fused_computation.6 | convolution fusion | flops 1107296256 | bytes 5537792 | tf_op jit(solution)/shard_map/dot_general | solution.py:64
  142.8 5.7 %fusion.54 = f32[704,2048]{1,0:T(8,128)} fusion(bf16[384,2048]{1,0:T(8,128)(2,1)} %bitcast.10, f32[384,704]{0,1:T(8,128)S(1)} %copy-done.1, f32[384,704]{0,1:T(8,128)S(1)} %copy-done.3, f32[384]{0:T(512)S(1)} %reshape.233), kind=kOutput, calls=%fused_computation.94 | convolution fusion | flops 1110269952 | bytes 9504256 | tf_op jit(solution)/shard_map/dot_general | solution.py:73
  148.5 10.9 %all-to-all-done.5 = bf16[8,48,2048]{2,1,0:T(8,128)(2,1)} async-done(((bf16[8,48,2048]{2,1,0:T(8,128)(2,1)}), bf16[8,48,2048]{2,1,0:T(8,128)(2,1)}, u32[]{:S(2)}, u32[]{:S(2)}) %all-to-all-start.5) | async-done | bytes 1572896 | tf_op jit(solution)/shard_map/all_to_all | solution.py:105
  159.4 5.2 %multiply_reduce_fusion = (bf16[384]{0:T(512)(128)(2,1)S(1)}, f32[384,704]{0,1:T(8,128)}) fusion(f32[384,704]{0,1:T(8,128)} %fusion.2, bf16[384,2048]{1,0:T(8,128)(2,1)} %bitcast.19, bf16[1,1,704,2048]{3,2,1,0:T(8,128)(2,1)} %param.9), kind=kOutput, calls=%fused_computation.40 | convolution fusion | flops 1109458560 | bytes 6619904 | tf_op jit(solution)/shard_map/dot_general | solution.py:67
  164.6 0.7 convert_element_type.285
  165.3 3.3 %all-to-all-start.8 = ((bf16[8,1,48]{2,1,0:T(2,128)(2,1)}), bf16[8,1,48]{2,1,0:T(2,128)(2,1)S(1)}, u32[]{:S(2)}, u32[]{:S(2)}) async-start(bf16[8,1,48]{2,1,0:T(2,128)(2,1)} %convert_element_type.285), calls=%async_computation.8 | async-start | bytes 8192 | tf_op jit(solution)/shard_map/all_to_all | solution.py:119
  168.6 6.1 %fusion.16 = f32[704,2048]{1,0:T(8,128)} fusion(bf16[384,2048]{1,0:T(8,128)(2,1)} %bitcast.6, f32[384]{0:T(512)S(1)} %reshape.233, f32[384,704]{0,1:T(8,128)} %fusion.6), kind=kOutput, calls=%fused_computation.25 | convolution fusion | flops 1111007232 | bytes 8422912 | tf_op jit(solution)/shard_map/dot_general | solution.py:72
  174.8 0.2 select_reduce_fusion
  175.0 0.7 convert_element_type.283
  175.7 4.1 %all-to-all-start.3 = ((bf16[8,1,48]{2,1,0:T(2,128)(2,1)}), bf16[8,1,48]{2,1,0:T(2,128)(2,1)S(1)}, u32[]{:S(2)}, u32[]{:S(2)}) async-start(bf16[8,1,48]{2,1,0:T(2,128)(2,1)} %convert_element_type.283), calls=%async_computation.3 | async-start | bytes 8192 | tf_op jit(solution)/shard_map/all_to_all | solution.py:106
  179.8 0.6 maximum_bitcast_fusion
  180.4 4.0 %all-to-all-done.3 = bf16[8,1,48]{2,1,0:T(2,128)(2,1)S(1)} async-done(((bf16[8,1,48]{2,1,0:T(2,128)(2,1)}), bf16[8,1,48]{2,1,0:T(2,128)(2,1)S(1)}, u32[]{:S(2)}, u32[]{:S(2)}) %all-to-all-start.3) | async-done | bytes 800 | tf_op jit(solution)/shard_map/all_to_all | solution.py:106
  184.5 6.9 %fusion.1 = bf16[1,1,704,2048]{3,2,1,0:T(8,128)(2,1)} fusion(f32[704,2048]{1,0:T(8,128)} %fusion.16, bf16[384,2048]{1,0:T(8,128)(2,1)} %bitcast.19, f32[384]{0:T(512)S(1)} %reshape.235, f32[384,704]{0,1:T(8,128)} %fusion.2), kind=kOutput, calls=%fused_computation.5 | convolution fusion | flops 1113890816 | bytes 11306496 | tf_op jit(solution)/shard_map/dot_general | solution.py:72
  191.4 6.5 %fusion = bf16[1,1,704,2048]{3,2,1,0:T(8,128)(2,1)} fusion(f32[704,2048]{1,0:T(8,128)} %fusion.54, bf16[384,2048]{1,0:T(8,128)(2,1)} %bitcast.22, f32[384,704]{0,1:T(8,128)S(1)} %copy-done.2, f32[384,704]{0,1:T(8,128)S(1)} %copy-done.4, f32[384]{0:T(512)S(1)} %reshape.235), kind=kOutput, calls=%fused_computation.4 | convolution fusion | flops 1113153536 | bytes 12387840 | tf_op jit(solution)/shard_map/dot_general | solution.py:73
  (40 shorter events, 1.5 us)
Async XLA Ops:
  0.6 36.0 %copy-start = (bf16[1,1,704,2048]{3,2,1,0:T(8,128)(2,1)S(1)}, bf16[1,1,704,2048]{3,2,1,0:T(8,128)(2,1)}, u32[]{:S(2)}) copy-start(bf16[1,1,704,2048]{3,2,1,0:T(8,128)(2,1)} %param.8) | copy-start | bytes 8650756
  6.0 26.3 %all-to-all-start.2 = ((bf16[8,48,2048]{2,1,0:T(8,128)(2,1)}), bf16[8,48,2048]{2,1,0:T(8,128)(2,1)}, u32[]{:S(2)}, u32[]{:S(2)}) async-start(bf16[8,48,2048]{2,1,0:T(8,128)(2,1)} %bitcast.95), calls=%async_computation.2 | async-start | bytes 3145728 | tf_op jit(solution)/shard_map/all_to_all | solution.py:104
  32.3 25.3 %all-to-all-start.1 = ((bf16[8,48,2048]{2,1,0:T(8,128)(2,1)}), bf16[8,48,2048]{2,1,0:T(8,128)(2,1)}, u32[]{:S(2)}, u32[]{:S(2)}) async-start(bf16[8,48,2048]{2,1,0:T(8,128)(2,1)} %bitcast.94), calls=%async_computation.1 | async-start | bytes 3145728 | tf_op jit(solution)/shard_map/all_to_all | solution.py:105
  57.6 9.3 %copy-start.5 = (bf16[1,2,128,2]{2,3,1,0:T(2,128)(2,1)S(1)}, bf16[1,2,128,2]{2,3,1,0:T(2,128)(2,1)}, u32[]{:S(2)}) copy-start(bf16[1,2,128,2]{2,3,1,0:T(2,128)(2,1)} %param.10) | copy-start | bytes 3076
  63.6 7.8 %all-to-all-start.7 = ((bf16[8,1,48]{2,1,0:T(2,128)(2,1)}), bf16[8,1,48]{2,1,0:T(2,128)(2,1)S(1)}, u32[]{:S(2)}, u32[]{:S(2)}) async-start(bf16[8,1,48]{2,1,0:T(2,128)(2,1)} %convert_element_type.284), calls=%async_computation.7 | async-start | bytes 8192 | tf_op jit(solution)/shard_map/all_to_all | solution.py:131
  83.3 25.3 %all-to-all-start.4 = ((bf16[8,48,2048]{2,1,0:T(8,128)(2,1)}), bf16[8,48,2048]{2,1,0:T(8,128)(2,1)}, u32[]{:S(2)}, u32[]{:S(2)}) async-start(bf16[8,48,2048]{2,1,0:T(8,128)(2,1)} %bitcast.96), calls=%async_computation.4 | async-start | bytes 3145728 | tf_op jit(solution)/shard_map/all_to_all | solution.py:124
  108.7 25.3 %all-to-all-start.6 = ((bf16[8,48,2048]{2,1,0:T(8,128)(2,1)}), bf16[8,48,2048]{2,1,0:T(8,128)(2,1)}, u32[]{:S(2)}, u32[]{:S(2)}) async-start(bf16[8,48,2048]{2,1,0:T(8,128)(2,1)} %bitcast.92), calls=%async_computation.6 | async-start | bytes 3145728 | tf_op jit(solution)/shard_map/all_to_all | solution.py:104
  115.0 16.4 %collective-permute-start = (bf16[128,2048]{1,0:T(8,128)(2,1)S(1)}, bf16[128,2048]{1,0:T(8,128)(2,1)S(1)}, u32[]{:S(2)}, u32[]{:S(2)}) collective-permute-start(bf16[128,2048]{1,0:T(8,128)(2,1)S(1)} %fusion.15), channel_id=1, source_target_pairs={{8,0},{16,8},{24,16},{9,1},{17,9},{25,17},{10,2},{18,10},{26,18},{... | collective-permute-start | bytes 1572872 | tf_op jit(solution)/shard_map/ppermute | solution.py:16
  134.0 25.4 %all-to-all-start.5 = ((bf16[8,48,2048]{2,1,0:T(8,128)(2,1)}), bf16[8,48,2048]{2,1,0:T(8,128)(2,1)}, u32[]{:S(2)}, u32[]{:S(2)}) async-start(bf16[8,48,2048]{2,1,0:T(8,128)(2,1)} %bitcast.93), calls=%async_computation.5 | async-start | bytes 3145728 | tf_op jit(solution)/shard_map/all_to_all | solution.py:105
  138.5 4.2 %copy-start.1 = (f32[384,704]{0,1:T(8,128)S(1)}, f32[384,704]{0,1:T(8,128)}, u32[]{:S(2)}) copy-start(f32[384,704]{0,1:T(8,128)} %fusion.6) | copy-start | bytes 3244036
  138.5 4.2 %copy-start.3 = (f32[384,704]{0,1:T(8,128)S(1)}, f32[384,704]{0,1:T(8,128)}, u32[]{:S(2)}) copy-start(f32[384,704]{0,1:T(8,128)} %get-tuple-element.12) | copy-start | bytes 3244036
  165.3 9.4 %all-to-all-start.8 = ((bf16[8,1,48]{2,1,0:T(2,128)(2,1)}), bf16[8,1,48]{2,1,0:T(2,128)(2,1)S(1)}, u32[]{:S(2)}, u32[]{:S(2)}) async-start(bf16[8,1,48]{2,1,0:T(2,128)(2,1)} %convert_element_type.285), calls=%async_computation.8 | async-start | bytes 8192 | tf_op jit(solution)/shard_map/all_to_all | solution.py:119
  175.7 8.7 %all-to-all-start.3 = ((bf16[8,1,48]{2,1,0:T(2,128)(2,1)}), bf16[8,1,48]{2,1,0:T(2,128)(2,1)S(1)}, u32[]{:S(2)}, u32[]{:S(2)}) async-start(bf16[8,1,48]{2,1,0:T(2,128)(2,1)} %convert_element_type.283), calls=%async_computation.3 | async-start | bytes 8192 | tf_op jit(solution)/shard_map/all_to_all | solution.py:106
  184.5 6.9 %copy-start.2 = (f32[384,704]{0,1:T(8,128)S(1)}, f32[384,704]{0,1:T(8,128)}, u32[]{:S(2)}) copy-start(f32[384,704]{0,1:T(8,128)} %fusion.2) | copy-start | bytes 3244036
  184.5 6.9 %copy-start.4 = (f32[384,704]{0,1:T(8,128)S(1)}, f32[384,704]{0,1:T(8,128)}, u32[]{:S(2)}) copy-start(f32[384,704]{0,1:T(8,128)} %get-tuple-element.14) | copy-start | bytes 3244036
where the time goes:
time: 199 us; the launch traced here: 198 us
  waiting for transfers between devices  87.3 us (44%)
  matrix products  60.5 us (30%)
  starting transfers between devices  34.6 us (17%)
  blocking collectives  7.02 us (4%)
  local copies, waits for them, and re-layouts  4.95 us (2%)
  other arithmetic  2.78 us (1%)
    all_to_all x2, waiting for transfers between devices, body(): lax.all_to_all(slots_g, 'expert', split_axis=0, concat_axis=0, tiled=True)  27.9 us
    all_to_all x2, waiting for transfers between devices, body(): lax.all_to_all(slots_x, 'expert', split_axis=0, concat_axis=0, tiled=True)  19.3 us
    all_to_all x1, waiting for transfers between devices, body(): lax.all_to_all(returned.reshape(experts, capacity, features), 'expert', s...  16.5 us
    ppermute x1, waiting for transfers between devices, passed_along(): return lax.ppermute(block, axis, route)  15.1 us
    dot_general x2, matrix products, expert_pass(): lax.dot_general(hidden, grad_y, contract_rows, preferred_element_type=jnp...  13 us
    dot_general x2, matrix products, expert_pass(): lax.dot_general(grad_pre, rows_x, contract_rows, preferred_element_type=j...  12.2 us
    dot_general x2, matrix products, expert_pass(): lax.dot_general(rows_g, w_out, contract_feat, preferred_element_type=jnp....  10.6 us
    dot_general x4, matrix products, spread_rows(): lax.dot_general(layout[1], rows, (((0,), (0,)), ((), ())), preferred_elem...  10.1 us
  transfers between devices with their start and end apart: 9, of which 8 were waited for; matrix products, arithmetic and copies ran while one was open for 16% of the time, Pallas kernels for 0%

commit v1 on v0

v1 whole, which is shorter than its diff:
```python
import functools

import jax
import jax.numpy as jnp
from jax import lax
from jax.experimental import pallas as pl
from jax.experimental.pallas import tpu as pltpu
from jax.sharding import PartitionSpec as P

half_root = 0.7071067811865476
density_scale = 0.3989422804014327
TAIL = 128
VMEM_LIMIT = 48 * 1024 * 1024
f32 = jnp.float32
bf16 = jnp.bfloat16


def dot(a, b, ca, cb):
    return lax.dot_general(a, b, (((ca,), (cb,)), ((), ())), preferred_element_type=f32)


def call(kernel, out_shape, *args, flops=0, scratch=()):
    size = sum(a.size * a.dtype.itemsize for a in args)
    size += sum(s.size * s.dtype.itemsize for s in out_shape)
    return pl.pallas_call(
        kernel,
        out_shape=out_shape,
        in_specs=[pl.BlockSpec(memory_space=pltpu.VMEM)] * len(args),
        out_specs=[pl.BlockSpec(memory_space=pltpu.VMEM)] * len(out_shape),
        scratch_shapes=scratch,
        compiler_params=pltpu.CompilerParams(vmem_limit_bytes=VMEM_LIMIT),
        cost_estimate=pl.CostEstimate(flops=flops, bytes_accessed=size, transcendentals=0),
    )(*args)


def shaped(shape, dtype):
    return jax.ShapeDtypeStruct(shape, dtype)


def expander(rows, experts, capacity):
    first = lax.broadcasted_iota(jnp.int32, (rows, experts), 1) * capacity
    row = lax.broadcasted_iota(jnp.int32, (rows, experts), 0)
    return ((row >= first) & (row < first + capacity)).astype(f32).astype(bf16)


def slot_masks(ids, experts, capacity):
    tokens = ids.shape[1]
    rows = experts * capacity
    expert = lax.broadcasted_iota(jnp.int32, (experts, tokens), 0)
    named = [(ids[j : j + 1, :] == expert).astype(f32) for j in range(ids.shape[0])]
    count = sum(named)
    earlier = lax.broadcasted_iota(jnp.int32, (tokens, tokens), 0)
    later = lax.broadcasted_iota(jnp.int32, (tokens, tokens), 1)
    before = (earlier < later).astype(f32).astype(bf16)
    rank = dot(count.astype(bf16), before, 1, 0)
    place = jnp.where(count > 0, rank, -1.0).astype(bf16)
    rep = expander(rows, experts, capacity)
    spread = dot(rep, place, 1, 0)
    row = lax.broadcasted_iota(jnp.int32, (rows, tokens), 0)
    owner = ((row.astype(f32) + 0.5) * (1.0 / capacity)).astype(jnp.int32)
    position = (row - owner * capacity).astype(f32)
    return (spread == position).astype(f32), named, rep


def source_kernel(experts, capacity, ids_ref, prob_ref, x_ref, g_ref, xg_ref, hot0_ref, hot1_ref):
    features = x_ref.shape[1]
    rows = experts * capacity
    lane = lax.broadcasted_iota(jnp.int32, (rows, TAIL), 1)
    tail = jnp.zeros((rows, TAIL), f32)
    for k, hot_ref in enumerate((hot0_ref, hot1_ref)):
        hot, named, rep = slot_masks(ids_ref[k], experts, capacity)
        hot_ref[...] = hot.astype(bf16)
        probs = prob_ref[k].astype(f32)
        by_expert = sum(n * probs[j : j + 1, :] for j, n in enumerate(named)).astype(bf16)
        column = jnp.sum(hot * dot(rep, by_expert, 1, 0), axis=1, keepdims=True)
        tail = jnp.where(lane == k, column, tail)
    xg_ref[:, 2 * features :] = tail.astype(bf16)
    hot = hot0_ref[...]
    xg_ref[:, :features] = dot(hot, x_ref[...], 1, 0).astype(bf16)
    xg_ref[:, features : 2 * features] = dot(hot, g_ref[...], 1, 0).astype(bf16)


def spread_kernel(hot_ref, x_ref, out_ref):
    out_ref[...] = dot(hot_ref[...], x_ref[...], 1, 0).astype(bf16)


def combine_kernel(hot_ref, back_ref, g_ref, out_ref):
    summed = dot(hot_ref[...], back_ref[...], 0, 0)
    out_ref[...] = (g_ref[...].astype(f32) + summed).astype(bf16)


def gelu_parts(preact):
    cdf = 0.5 * (1.0 + lax.erf(preact * half_root))
    pdf = density_scale * jnp.exp(-0.5 * preact * preact)
    return preact * cdf, cdf + preact * pdf


def first_kernel(step, xg_ref, win_ref, wout_ref, hid_ref, gp_ref, ret_ref, score_ref):
    units, features = win_ref.shape
    tail = jnp.transpose(xg_ref[:, 2 * features :].astype(f32))
    prob = tail[0:1, :]
    score = jnp.zeros(prob.shape, f32)
    for f in range(0, units, step):
        at = slice(f, f + step)
        preact = dot(win_ref[at, :], xg_ref[:, :features], 1, 1)
        activated, slope = gelu_parts(preact)
        hidden = activated.astype(bf16)
        pulled = dot(wout_ref[at, :], xg_ref[:, features : 2 * features], 1, 1)
        score = score + jnp.sum(hidden.astype(f32) * pulled, axis=0, keepdims=True)
        hid_ref[at, :] = hidden
        gp_ref[at, :] = (prob * pulled * slope).astype(bf16)
    ret_ref[...] = dot(gp_ref[...], win_ref[...], 0, 0).astype(bf16)
    score_ref[...] = score


def preact_kernel(step, x_ref, win_ref, hid_ref, slope_ref):
    units = win_ref.shape[0]
    for f in range(0, units, step):
        at = slice(f, f + step)
        activated, slope = gelu_parts(dot(win_ref[at, :], x_ref[...], 1, 1))
        hid_ref[at, :] = activated.astype(bf16)
        slope_ref[at, :] = slope


def second_kernel(step, g_ref, xg_ref, wout_ref, hid_ref, slope_ref, score0_ref, gp_ref, score_ref):
    units, features = wout_ref.shape
    tail = jnp.transpose(xg_ref[:, 2 * features :].astype(f32))
    prob = tail[1:2, :]
    score = jnp.zeros(prob.shape, f32)
    for f in range(0, units, step):
        at = slice(f, f + step)
        pulled = dot(wout_ref[at, :], g_ref[...], 1, 1)
        score = score + jnp.sum(hid_ref[at, :].astype(f32) * pulled, axis=0, keepdims=True)
        gp_ref[at, :] = (prob * pulled * slope_ref[at, :]).astype(bf16)
    row = lax.broadcasted_iota(jnp.int32, (TAIL, prob.shape[1]), 0)
    both = jnp.where(row == 0, score0_ref[...], jnp.where(row == 1, score, 0.0))
    score_ref[...] = jnp.transpose(both).astype(bf16)


def grads_kernel(xg_ref, x1_ref, g1_ref, hid0_ref, hid1_ref, gp0_ref, gp1_ref, gin_ref, gout_ref, gy0, gy1):
    features = x1_ref.shape[1]

    @pl.when(pl.program_id(0) == 0)
    def _():
        tail = xg_ref[:, 2 * features :].astype(f32)
        gy0[...] = (tail[:, 0:1] * xg_ref[:, features : 2 * features].astype(f32)).astype(bf16)
        gy1[...] = (tail[:, 1:2] * g1_ref[...].astype(f32)).astype(bf16)

    gin = dot(gp0_ref[...], xg_ref[:, :features], 1, 0) + dot(gp1_ref[...], x1_ref[...], 1, 0)
    gin_ref[...] = gin.astype(bf16)
    gout = dot(hid0_ref[...], gy0[...], 1, 0) + dot(hid1_ref[...], gy1[...], 1, 0)
    gout_ref[...] = gout.astype(bf16)


def grads(step, xg, x1, g1, hid0, hid1, gp0, gp1):
    units, rows = hid0.shape
    features = x1.shape[1]
    whole = lambda a: pl.BlockSpec(a.shape, lambda i: (0, 0))
    part = pl.BlockSpec((step, rows), lambda i: (i, 0))
    out = pl.BlockSpec((step, features), lambda i: (i, 0))
    return pl.pallas_call(
        grads_kernel,
        grid=(units // step,),
        out_shape=[shaped((units, features), bf16)] * 2,
        in_specs=[whole(xg), whole(x1), whole(g1)] + [part] * 4,
        out_specs=[out] * 2,
        scratch_shapes=[pltpu.VMEM((rows, features), bf16)] * 2,
        compiler_params=pltpu.CompilerParams(vmem_limit_bytes=VMEM_LIMIT),
        cost_estimate=pl.CostEstimate(
            flops=8 * units * rows * features, bytes_accessed=8 * units * features, transcendentals=0
        ),
    )(xg, x1, g1, hid0, hid1, gp0, gp1)


def collect_kernel(experts, capacity, ids_ref, hot0_ref, hot1_ref, score_ref, out_ref):
    rows = experts * capacity
    tokens = ids_ref.shape[2]
    rep = expander(rows, experts, capacity)
    expert = lax.broadcasted_iota(jnp.int32, (experts, tokens), 0)
    for k, hot_ref in enumerate((hot0_ref, hot1_ref)):
        placed = hot_ref[...].astype(f32) * score_ref[:, k : k + 1].astype(f32)
        by_expert = dot(rep, placed.astype(bf16), 0, 0)
        ids = ids_ref[k]
        for j in range(ids.shape[0]):
            picked = jnp.where(ids[j : j + 1, :] == expert, by_expert, 0.0)
            out_ref[k, j : j + 1, :] = jnp.sum(picked, axis=0, keepdims=True).astype(bf16)


def exchange(rows, experts):
    width = rows.shape[1]
    pieces = rows.reshape(experts, -1, width)
    arrived = lax.all_to_all(pieces, "expert", split_axis=0, concat_axis=0, tiled=True)
    return arrived.reshape(-1, width)


def step_of(units, wanted):
    return next(s for s in range(wanted, 0, -1) if units % s == 0 and (s % 16 == 0 or s == units))


def body(inputs, entering, weight_in, weight_out, gate_probs, expert_ids):
    experts = lax.axis_size("expert")
    segments = lax.axis_size("segment")
    tokens, features = entering.shape[1:]
    topk = expert_ids.shape[3]
    units = weight_in.shape[2]
    capacity = 3 * tokens * topk // (2 * experts)
    rows = experts * capacity
    step = step_of(units, 352)
    matmul = 2 * rows * units * features
    w_in, w_out = weight_in[0, 0], weight_out[0, 0]
    ids = jnp.transpose(expert_ids[0], (0, 2, 1))
    probs = jnp.transpose(gate_probs[0], (0, 2, 1))
    x0, x1, g0 = inputs[0, 0], inputs[0, 1], entering[0]

    spread = 2 * rows * tokens * features
    xg, hot0, hot1 = call(
        functools.partial(source_kernel, experts, capacity),
        [shaped((rows, 2 * features + TAIL), bf16)] + [shaped((rows, tokens), bf16)] * 2,
        ids, probs, x0, g0, flops=2 * spread,
    )
    xg = exchange(xg, experts)
    (x1,) = call(spread_kernel, [shaped((rows, features), bf16)], hot1, x1, flops=spread)

    hid0, gp0, back, score0 = call(
        functools.partial(first_kernel, step),
        [shaped((units, rows), bf16)] * 2 + [shaped((rows, features), bf16), shaped((1, rows), f32)],
        xg, w_in, w_out, flops=3 * matmul,
    )
    back = exchange(back, experts)
    (leaving,) = call(combine_kernel, [shaped((tokens, features), bf16)], hot0, back, g0, flops=spread)
    g1 = lax.ppermute(leaving, "segment", [(i, i - 1) for i in range(1, segments)])
    x1 = exchange(x1, experts)
    hid1, slope1 = call(
        functools.partial(preact_kernel, step),
        [shaped((units, rows), bf16), shaped((units, rows), f32)], x1, w_in, flops=matmul,
    )
    (g1,) = call(spread_kernel, [shaped((rows, features), bf16)], hot1, g1, flops=spread)
    g1 = exchange(g1, experts)
    gp1, scores = call(
        functools.partial(second_kernel, step),
        [shaped((units, rows), bf16), shaped((rows, TAIL), bf16)],
        g1, xg, w_out, hid1, slope1, score0, flops=matmul,
    )
    scores = exchange(scores, experts)
    grad_in, grad_out = grads(step_of(units, 176), xg, x1, g1, hid0, hid1, gp0, gp1)
    (prob_grads,) = call(
        functools.partial(collect_kernel, experts, capacity), [shaped(ids.shape, bf16)], ids, hot0, hot1, scores
    )
    prob_grads = jnp.transpose(prob_grads, (0, 2, 1))
    return grad_in[None, None], grad_out[None, None], prob_grads[None]


def solution(mesh):
    return jax.shard_map(
        body,
        mesh=mesh,
        in_specs=(
            P("segment", None, "expert", None),
            P("segment", "expert", None),
            P("segment", "expert", None, None),
            P("segment", "expert", None, None),
            P("segment", None, "expert", None),
            P("segment", None, "expert", None),
        ),
        out_specs=(
            P("segment", "expert", None, None),
            P("segment", "expert", None, None),
            P("segment", None, "expert", None),
        ),
        check_vma=False,
    )
```

time: 199 us -> 159 us (0.80)
  matrix products: 60.5 us -> 0 us
  blocking collectives: 7.02 us -> 44.2 us
  waiting for transfers between devices: 87.3 us -> 51.2 us
  Pallas kernels: 0 us -> 29.4 us
  starting transfers between devices: 34.6 us -> 15.4 us
  local copies, waits for them, and re-layouts: 4.95 us -> 17.1 us
  other arithmetic: 2.78 us -> 0 us
    dot_general x14 -> x0, matrix products: 60.5 us -> none  [the longest x2 13 us: expert_pass(): lax.dot_general(hidden, grad_y, contract_rows, preferred_element_type=jnp...]
    all_to_all x1, blocking collectives: 7.02 us -> 44.2 us  [exchange(): lax.all_to_all(pieces, 'expert', split_axis=0, concat_axis=0, tiled=True)]
    all_to_all x8 -> x4, waiting for transfers between devices: 72.2 us -> 36.3 us  [exchange(): lax.all_to_all(pieces, 'expert', split_axis=0, concat_axis=0, tiled=True)]
    pallas_call x0 -> x9, Pallas kernels: none -> 29.4 us  [the longest x8 19.2 us: call(): pl.pallas_call(kernel, out_shape=out_shape, in_specs=[pl.BlockSpec(memory...]
    all_to_all x8 -> x4, starting transfers between devices: 33.3 us -> 14.1 us  [exchange(): lax.all_to_all(pieces, 'expert', split_axis=0, concat_axis=0, tiled=True)]
    unnamed x14 -> x38, local copies, waits for them, and re-layouts: 0.26 us -> 15.8 us
    convert_element_type x8 -> x0, local copies, waits for them, and re-layouts: 2.45 us -> none  [the longest x2 1.37 us: expert_pass(): jnp.sum(hidden.astype(jnp.float32) * pulled, axis=1).astype(jnp.bfloat16)]
  transfers between devices with their start and end apart: 9 -> 5, of which waited for: 8 -> 4; matrix products, arithmetic and copies ran while one was open for 16% -> 0% of each run, Pallas kernels for 0% -> 9%
where the time goes in v1:
time: 159 us; the launch traced here: 158 us
  waiting for transfers between devices  51.2 us (32%)
  blocking collectives  44.2 us (28%)
  Pallas kernels  29.4 us (18%)
  local copies, waits for them, and re-layouts  17.1 us (11%)
  starting transfers between devices  15.4 us (10%)
    all_to_all x1, blocking collectives, exchange(): lax.all_to_all(pieces, 'expert', split_axis=0, concat_axis=0, tiled=True)  44.2 us
    all_to_all x4, waiting for transfers between devices, exchange(): lax.all_to_all(pieces, 'expert', split_axis=0, concat_axis=0, tiled=True)  36.3 us
    pallas_call x8, Pallas kernels, call(): pl.pallas_call(kernel, out_shape=out_shape, in_specs=[pl.BlockSpec(memory...  19.2 us
    unnamed x38, local copies, waits for them, and re-layouts  15.8 us
    ppermute x1, waiting for transfers between devices, body(): lax.ppermute(leaving, 'segment', [(i, i - 1) for i in range(1, segments)])  14.9 us
    all_to_all x4, starting transfers between devices, exchange(): lax.all_to_all(pieces, 'expert', split_axis=0, concat_axis=0, tiled=True)  14.1 us
    pallas_call x1, Pallas kernels, grads(): pl.pallas_call(grads_kernel, grid=(units // step,), out_shape=[shaped((un...  10.2 us
  transfers between devices with their start and end apart: 5, of which 4 were waited for; matrix products, arithmetic and copies ran while one was open for 0% of the time, Pallas kernels for 9%

profile of v1, /device:TPU:0, one launch (start us, length us, event | category | flops | bytes accessed | tf_op | source)
XLA Modules:
  0.0 158.1 jit_solution(17590307416170498199)
XLA Ops:
  0.6 0.0 copy-start.11
  0.6 0.0 copy-start.9
  0.7 0.0 copy-start.14
  0.7 1.3 slice_bitcast_fusion
  2.0 0.0 copy-done.11
  2.0 0.0 copy-done.9
  2.0 0.0 copy-done.14
  2.0 1.3 shard_map.85
  3.3 0.0 copy-start.1
  3.4 44.2 %all_to_all.25 = bf16[8,48,4224]{2,1,0:T(8,128)(2,1)} all-to-all(bf16[8,48,4224]{2,1,0:T(8,128)(2,1)S(1)} %bitcast.34), channel_id=1, replica_groups=mesh['segment'=4,'expert'=8] {'expert'}, dimensions={0} | all-to-all | bytes 6488064 | tf_op jit(solution)/shard_map/all_to_all | solution.py:192
  47.6 7.2 %shard_map.87 = (bf16[704,384]{1,0:T(8,128)(2,1)S(1)}, bf16[704,384]{1,0:T(8,128)(2,1)S(1)}, bf16[384,2048]{1,0:T(8,128)(2,1)S(1)}, f32[1,384]{1,0:T(1,128)S(1)}) custom-call(bf16[384,4224]{1,0:T(8,128)(2,1)} %bitcast.44, bf16[704,2048]{1,0:T(8,128)(2,1)S(1)} %bitcast.35, bf16[704,2048]{1,0:T(8,128)(2,1)} %bitcast.47), custom_call_target="tpu_custom_call" | custom-call | flops 3321888768 | bytes 11666944 | tf_op jit(solution)/shard_map/pallas_call | solution.py:25
  54.8 0.0 copy-start.3
  54.8 1.1 copy-done.3
  56.0 0.8 copy-done.15
  56.7 0.8 copy-done.17
  57.6 3.6 %all-to-all-start.2 = ((bf16[8,48,2048]{2,1,0:T(8,128)(2,1)}), bf16[8,48,2048]{2,1,0:T(8,128)(2,1)S(1)}, u32[]{:S(2)}, u32[]{:S(2)}) async-start(bf16[8,48,2048]{2,1,0:T(8,128)(2,1)} %bitcast.37), calls=%async_computation.2 | async-start | bytes 3145728 | tf_op jit(solution)/shard_map/all_to_all | solution.py:192
  61.1 1.7 %shard_map.86 = bf16[384,2048]{1,0:T(8,128)(2,1)} custom-call(bf16[384,128]{1,0:T(8,128)(2,1)S(1)} %get-tuple-element.17.hot_ref.hot1_ref, bf16[128,2048]{1,0:T(8,128)(2,1)S(1)} %get-tuple-element.29.x_ref), custom_call_target="tpu_custom_call" | custom-call | flops 201326592 | bytes 2195456 | tf_op jit(solution)/shard_map/pallas_call | solution.py:25
  62.9 19.3 %all-to-all-done.2 = bf16[8,48,2048]{2,1,0:T(8,128)(2,1)S(1)} async-done(((bf16[8,48,2048]{2,1,0:T(8,128)(2,1)}), bf16[8,48,2048]{2,1,0:T(8,128)(2,1)S(1)}, u32[]{:S(2)}, u32[]{:S(2)}) %all-to-all-start.2) | async-done | bytes 1572896 | tf_op jit(solution)/shard_map/all_to_all | solution.py:192
  82.1 3.6 %all-to-all-start.1 = ((bf16[8,48,2048]{2,1,0:T(8,128)(2,1)}), bf16[8,48,2048]{2,1,0:T(8,128)(2,1)S(1)}, u32[]{:S(2)}, u32[]{:S(2)}) async-start(bf16[8,48,2048]{2,1,0:T(8,128)(2,1)} %bitcast.9), calls=%async_computation.1 | async-start | bytes 3145728 | tf_op jit(solution)/shard_map/all_to_all | solution.py:192
  85.7 0.0 copy-start.10
  85.7 1.0 copy-done.10
  86.7 0.5 shard_map.88
  87.2 1.3 collective-permute-start
  88.5 14.9 %collective-permute-done.x_ref = bf16[128,2048]{1,0:T(8,128)(2,1)S(1)} collective-permute-done((bf16[128,2048]{1,0:T(8,128)(2,1)S(1)}, bf16[128,2048]{1,0:T(8,128)(2,1)S(1)}, u32[]{:S(2)}, u32[]{:S(2)}) %collective-permute-start) | collective-permute-done | bytes 524320 | tf_op jit(solution)/shard_map/ppermute | solution.py:231
  103.4 0.6 shard_map.89
  103.9 0.0 copy-start
  103.9 1.1 copy-done
  105.1 1.6 %all-to-all-done.1 = bf16[8,48,2048]{2,1,0:T(8,128)(2,1)S(1)} async-done(((bf16[8,48,2048]{2,1,0:T(8,128)(2,1)}), bf16[8,48,2048]{2,1,0:T(8,128)(2,1)S(1)}, u32[]{:S(2)}, u32[]{:S(2)}) %all-to-all-start.1) | async-done | bytes 1572896 | tf_op jit(solution)/shard_map/all_to_all | solution.py:192
  106.7 3.6 %all-to-all-start.3 = ((bf16[8,48,2048]{2,1,0:T(8,128)(2,1)}), bf16[8,48,2048]{2,1,0:T(8,128)(2,1)S(1)}, u32[]{:S(2)}, u32[]{:S(2)}) async-start(bf16[8,48,2048]{2,1,0:T(8,128)(2,1)} %bitcast.32), calls=%async_computation.3 | async-start | bytes 3145728 | tf_op jit(solution)/shard_map/all_to_all | solution.py:192
  110.2 0.0 copy-start.2
  110.3 1.8 %copy-done.2 = bf16[1,1,704,2048]{3,2,1,0:T(8,128)(2,1)S(1)} copy-done((bf16[1,1,704,2048]{3,2,1,0:T(8,128)(2,1)S(1)}, bf16[1,1,704,2048]{3,2,1,0:T(8,128)(2,1)}, u32[]{:S(2)}) %copy-start.2) | copy-done | bytes 2883608
  112.1 1.9 %shard_map.90 = (bf16[704,384]{1,0:T(8,128)(2,1)S(1)}, f32[704,384]{1,0:T(8,128)S(1)}) custom-call(bf16[384,2048]{1,0:T(8,128)(2,1)S(1)} %bitcast.28, bf16[704,2048]{1,0:T(8,128)(2,1)S(1)} %bitcast.36), custom_call_target="tpu_custom_call" | custom-call | flops 1107296256 | bytes 6078464 | tf_op jit(solution)/shard_map/pallas_call | solution.py:25
  114.0 0.0 copy-start.4
  114.0 1.0 copy-done.4
  114.9 0.8 copy-done.6
  115.7 15.5 %all-to-all-done.3 = bf16[8,48,2048]{2,1,0:T(8,128)(2,1)S(1)} async-done(((bf16[8,48,2048]{2,1,0:T(8,128)(2,1)}), bf16[8,48,2048]{2,1,0:T(8,128)(2,1)S(1)}, u32[]{:S(2)}, u32[]{:S(2)}) %all-to-all-start.3) | async-done | bytes 1572896 | tf_op jit(solution)/shard_map/all_to_all | solution.py:192
  131.2 1.2 copy-done.5
  132.4 1.0 copy-done.7
  133.5 5.2 %shard_map.91 = (bf16[704,384]{1,0:T(8,128)(2,1)S(1)}, bf16[384,128]{1,0:T(8,128)(2,1)}) custom-call(bf16[384,2048]{1,0:T(8,128)(2,1)S(1)} %bitcast.30, bf16[384,4224]{1,0:T(8,128)(2,1)} %bitcast.45, bf16[704,2048]{1,0:T(8,128)(2,1)} %bitcast.48, bf16[704,384]{1,0:T(8,128)(2,1)S(1)} %copy-done.7, f32[704,384]{1,0:T(8,128)S(1)} %copy-done.5, ...), custom_call_target="tpu_custom_call" | custom-call | flops 1107296256 | bytes 9963008 | tf_op jit(solution)/shard_map/pallas_call | solution.py:25
  138.7 0.8 copy-done.12
  139.5 3.4 %all-to-all-start.4 = ((bf16[8,48,128]{2,1,0:T(8,128)(2,1)}), bf16[8,48,128]{2,1,0:T(8,128)(2,1)S(1)}, u32[]{:S(2)}, u32[]{:S(2)}) async-start(bf16[8,48,128]{2,1,0:T(8,128)(2,1)} %bitcast.20), calls=%async_computation.4 | async-start | bytes 196608 | tf_op jit(solution)/shard_map/all_to_all | solution.py:192
  142.9 1.0 copy-done.8
  143.9 1.0 copy-done.13
  145.0 1.0 copy-done.16
  146.0 1.0 copy-done.18
  147.1 10.2 %shard_map.92 = (bf16[704,2048]{1,0:T(8,128)(2,1)}, bf16[704,2048]{1,0:T(8,128)(2,1)}) custom-call(bf16[384,4224]{1,0:T(8,128)(2,1)} %bitcast.46, bf16[384,2048]{1,0:T(8,128)(2,1)S(1)} %bitcast.29, bf16[384,2048]{1,0:T(8,128)(2,1)S(1)} %bitcast.31, bf16[704,384]{1,0:T(8,128)(2,1)S(1)} %copy-done.16, bf16[704,384]{1,0:T(8,128)(2,1)S(1)} %copy-done.8, ...), custom_call_target="tpu_custom_call" | custom-call | flops 4429185024 | bytes 11534336 | tf_op jit(solution)/shard_map/pallas_call | solution.py:161
  157.2 0.0 all-to-all-done.4
  157.2 0.8 shard_map.93
  (11 shorter events, 0.0 us)
Async XLA Ops:
  0.6 1.4 copy-start.11
  0.6 1.4 copy-start.9
  0.7 1.4 copy-start.14
  3.3 44.2 %copy-start.1 = (bf16[1,1,704,2048]{3,2,1,0:T(8,128)(2,1)S(1)}, bf16[1,1,704,2048]{3,2,1,0:T(8,128)(2,1)}, u32[]{:S(2)}) copy-start(bf16[1,1,704,2048]{3,2,1,0:T(8,128)(2,1)} %param.8) | copy-start | bytes 8650756
  54.8 1.1 copy-start.3
  56.0 0.8 copy-start.15
  56.7 0.8 copy-start.17
  57.6 24.5 %all-to-all-start.2 = ((bf16[8,48,2048]{2,1,0:T(8,128)(2,1)}), bf16[8,48,2048]{2,1,0:T(8,128)(2,1)S(1)}, u32[]{:S(2)}, u32[]{:S(2)}) async-start(bf16[8,48,2048]{2,1,0:T(8,128)(2,1)} %bitcast.37), calls=%async_computation.2 | async-start | bytes 3145728 | tf_op jit(solution)/shard_map/all_to_all | solution.py:192
  82.1 24.5 %all-to-all-start.1 = ((bf16[8,48,2048]{2,1,0:T(8,128)(2,1)}), bf16[8,48,2048]{2,1,0:T(8,128)(2,1)S(1)}, u32[]{:S(2)}, u32[]{:S(2)}) async-start(bf16[8,48,2048]{2,1,0:T(8,128)(2,1)} %bitcast.9), calls=%async_computation.1 | async-start | bytes 3145728 | tf_op jit(solution)/shard_map/all_to_all | solution.py:192
  85.7 1.0 copy-start.10
  87.2 16.2 %collective-permute-start = (bf16[128,2048]{1,0:T(8,128)(2,1)S(1)}, bf16[128,2048]{1,0:T(8,128)(2,1)S(1)}, u32[]{:S(2)}, u32[]{:S(2)}) collective-permute-start(bf16[128,2048]{1,0:T(8,128)(2,1)S(1)} %shard_map.88), channel_id=1, source_target_pairs={{8,0},{16,8},{24,16},{9,1},{17,9},{25,17},{10,2},{18,10},{26,18},{... | collective-permute-start | bytes 1572872 | tf_op jit(solution)/shard_map/ppermute | solution.py:231
  103.9 1.1 copy-start
  106.7 24.5 %all-to-all-start.3 = ((bf16[8,48,2048]{2,1,0:T(8,128)(2,1)}), bf16[8,48,2048]{2,1,0:T(8,128)(2,1)S(1)}, u32[]{:S(2)}, u32[]{:S(2)}) async-start(bf16[8,48,2048]{2,1,0:T(8,128)(2,1)} %bitcast.32), calls=%async_computation.3 | async-start | bytes 3145728 | tf_op jit(solution)/shard_map/all_to_all | solution.py:192
  110.2 1.8 %copy-start.2 = (bf16[1,1,704,2048]{3,2,1,0:T(8,128)(2,1)S(1)}, bf16[1,1,704,2048]{3,2,1,0:T(8,128)(2,1)}, u32[]{:S(2)}) copy-start(bf16[1,1,704,2048]{3,2,1,0:T(8,128)(2,1)} %param.8) | copy-start | bytes 8650756
  114.0 1.0 copy-start.4
  114.9 0.8 copy-start.6
  131.2 1.2 copy-start.5
  132.4 1.0 copy-start.7
  138.7 0.8 copy-start.12
  139.5 17.7 %all-to-all-start.4 = ((bf16[8,48,128]{2,1,0:T(8,128)(2,1)}), bf16[8,48,128]{2,1,0:T(8,128)(2,1)S(1)}, u32[]{:S(2)}, u32[]{:S(2)}) async-start(bf16[8,48,128]{2,1,0:T(8,128)(2,1)} %bitcast.20), calls=%async_computation.4 | async-start | bytes 196608 | tf_op jit(solution)/shard_map/all_to_all | solution.py:192
  142.9 1.0 copy-start.8
  143.9 1.0 copy-start.13
  145.0 1.0 copy-start.16
  146.0 1.0 copy-start.18

commit v2 on v1

v2 whole, which is shorter than its diff:
```python
import functools

import jax
import jax.numpy as jnp
from jax import lax
from jax.experimental import pallas as pl
from jax.experimental.pallas import tpu as pltpu
from jax.sharding import PartitionSpec as P

half_root = 0.7071067811865476
density_scale = 0.3989422804014327
LANES = 128
HALVES = 2
VMEM_LIMIT = 16 * 1024 * 1024
f32 = jnp.float32
bf16 = jnp.bfloat16
VMEM = pl.BlockSpec(memory_space=pltpu.VMEM)


def dot(a, b, ca, cb):
    return lax.dot_general(a, b, (((ca,), (cb,)), ((), ())), preferred_element_type=f32)


def shaped(shape, dtype):
    return jax.ShapeDtypeStruct(shape, dtype)


def cost(args, outs, flops):
    size = sum(a.size * a.dtype.itemsize for a in list(args) + list(outs))
    return pl.CostEstimate(flops=flops, bytes_accessed=size, transcendentals=0)


def call(kernel, outs, *args, flops=0):
    return pl.pallas_call(
        kernel,
        out_shape=outs,
        in_specs=[VMEM] * len(args),
        out_specs=[VMEM] * len(outs),
        compiler_params=pltpu.CompilerParams(vmem_limit_bytes=VMEM_LIMIT),
        cost_estimate=cost(args, outs, flops),
    )(*args)


class Plane:
    def __init__(self, experts):
        chips = experts // 2
        across = next(n for n in range(int(chips**0.5), 0, -1) if chips % n == 0)
        self.size = (chips // across, across, 2)
        self.experts = experts

    def other(self, i, offset):
        _, across, cores = self.size
        coords = (i // (across * cores), (i // cores) % across, i % cores)
        a, b, c = ((p + o) % n for p, o, n in zip(coords, offset, self.size))
        return (a * across + b) * cores + c

    def back(self, *offsets):
        return tuple(-sum(o) % n for o, n in zip(zip(*offsets), self.size))

    def send(self, value, offset):
        if not any(offset):
            return value
        route = [(i, self.other(i, offset)) for i in range(self.experts)]
        return lax.ppermute(value, "expert", route)


def other_of(plane, offset):
    _, across, cores = plane.size
    i = lax.axis_index("expert")
    coords = (lax.div(i, across * cores), lax.rem(lax.div(i, cores), across), lax.rem(i, cores))
    a, b, c = (lax.rem(p + o, n) for p, o, n in zip(coords, offset, plane.size))
    return (a * across + b) * cores + c


def expander(rows, groups, capacity):
    first = lax.broadcasted_iota(jnp.int32, (rows, groups), 1) * capacity
    row = lax.broadcasted_iota(jnp.int32, (rows, groups), 0)
    return ((row >= first) & (row < first + capacity)).astype(f32).astype(bf16)


def slot_masks(named, capacity):
    count = sum(named)
    groups, tokens = count.shape
    rows = groups * capacity
    earlier = lax.broadcasted_iota(jnp.int32, (tokens, tokens), 0)
    later = lax.broadcasted_iota(jnp.int32, (tokens, tokens), 1)
    before = (earlier < later).astype(f32).astype(bf16)
    rank = dot(count.astype(bf16), before, 1, 0)
    place = jnp.where(count > 0, rank, -1.0).astype(bf16)
    rep = expander(rows, groups, capacity)
    spread = dot(rep, place, 1, 0)
    row = lax.broadcasted_iota(jnp.int32, (rows, tokens), 0)
    owner = ((row.astype(f32) + 0.5) * (1.0 / capacity)).astype(jnp.int32)
    position = (row - owner * capacity).astype(f32)
    return (spread == position).astype(f32), rep


def slots_kernel(experts, capacity, topk, meta_ref, hot0_ref, hot1_ref, prob_ref):
    tokens = meta_ref.shape[2]
    me = lax.axis_index("expert")
    expert = lax.broadcasted_iota(jnp.int32, (experts, tokens), 0).astype(f32)
    own = meta_ref[me]
    lane = lax.broadcasted_iota(jnp.int32, prob_ref.shape, 1)
    columns = jnp.zeros(prob_ref.shape, f32)
    ranks = range(topk)
    for k, hot_ref in enumerate((hot0_ref, hot1_ref)):
        at = [k * topk + j for j in ranks]
        hot, _ = slot_masks([(own[i : i + 1, :] == expert).astype(f32) for i in at], capacity)
        hot_ref[...] = hot.astype(bf16)
        mine = me.astype(f32)
        named = [(meta_ref[:, i, :] == mine).astype(f32) for i in at]
        hot, rep = slot_masks(named, capacity)
        probs = sum(n * meta_ref[:, 2 * topk + i, :] for n, i in zip(named, at))
        column = jnp.sum(hot * dot(rep, probs.astype(bf16), 1, 0), axis=1, keepdims=True)
        columns = jnp.where(lane == k, column, columns)
    prob_ref[...] = columns


def select_kernel(plane, capacity, ranks, sources, targets, meta_ref, *refs):
    raw_refs, out_refs = refs[: len(sources)], refs[len(sources) :]
    tokens = raw_refs[0].shape[0]
    row = lax.broadcasted_iota(jnp.int32, (len(targets), tokens), 0)
    expert = jnp.zeros(row.shape, f32)
    for i, target in enumerate(targets):
        expert = jnp.where(row == i, other_of(plane, target).astype(f32), expert)
    for s, source in enumerate(sources):
        ids = meta_ref[other_of(plane, source)]
        hot, _ = slot_masks([(ids[i : i + 1, :] == expert).astype(f32) for i in ranks], capacity)
        picked = dot(hot.astype(bf16), raw_refs[s][...], 1, 0).astype(bf16)
        for i, out_ref in enumerate(out_refs):
            out_ref[s * capacity : (s + 1) * capacity, :] = picked[i * capacity : (i + 1) * capacity]


def two_step(plane, capacity, topk, tick, axis, value, meta):
    tokens, width = value.shape
    unit = lambda n: tuple(n if d == axis else 0 for d in range(3))
    hops = range(plane.size[axis])
    sources = [plane.back(unit(n)) for n in hops]
    raws = [plane.send(value, unit(n)) for n in hops]
    cross = 1 - axis
    targets = [
        tuple(n if d == cross else core if d == 2 else 0 for d in range(3))
        for n in range(plane.size[cross])
        for core in range(plane.size[2])
    ]
    ranks = [tick * topk + j for j in range(topk)]
    outs = [shaped((len(sources) * capacity, width), bf16)] * len(targets)
    flops = 2 * tokens * width * capacity * len(sources) * len(targets)
    picked = call(
        functools.partial(select_kernel, plane, capacity, ranks, sources, targets), outs, meta, *raws, flops=flops
    )
    pieces = [plane.send(p, t) for p, t in zip(picked, targets)]
    layout = [[plane.back(t, unit(n)) for n in hops] for t in targets]
    return pieces, layout


def spread_kernel(hot_ref, x_ref, out_ref):
    out_ref[...] = dot(hot_ref[...], x_ref[...], 1, 0).astype(bf16)


def spread(hot, x):
    outs = [shaped((hot.shape[0], x.shape[1]), bf16)]
    return call(spread_kernel, outs, hot, x, flops=2 * hot.size * x.shape[1])[0]


def exchange(rows, experts):
    width = rows.shape[1]
    pieces = rows.reshape(experts, -1, width)
    arrived = lax.all_to_all(pieces, "expert", split_axis=0, concat_axis=0, tiled=True)
    return arrived.reshape(-1, width)


def combine_kernel(first, hot_ref, back_ref, g_ref, out_ref):
    width = out_ref.shape[1]
    summed = dot(hot_ref[...], back_ref[...], 0, 0)
    out_ref[...] = (g_ref[:, first : first + width].astype(f32) + summed).astype(bf16)


def arrange(plane, capacity, groups, refs, out_ref):
    refs = list(refs)
    for first, layout in groups:
        if layout is None:
            piece = refs.pop(0)
            out_ref[:, first : first + piece.shape[1]] = piece[...]
            continue
        for offsets in layout:
            piece = refs.pop(0)
            lanes = slice(first, first + piece.shape[1])
            for s, offset in enumerate(offsets):
                at = pl.multiple_of(other_of(plane, offset) * capacity, 16)
                out_ref[pl.ds(at, capacity), lanes] = piece[s * capacity : (s + 1) * capacity, :]


def gelu_parts(preact):
    cdf = 0.5 * (1.0 + lax.erf(preact * half_root))
    pdf = density_scale * jnp.exp(-0.5 * preact * preact)
    return preact * cdf, cdf + preact * pdf


def preact_kernel(plane, capacity, groups, win_ref, *refs):
    x_ref, hid_ref, slope_ref = refs[-3:]
    arrange(plane, capacity, groups, refs[:-3], x_ref)
    activated, slope = gelu_parts(dot(x_ref[...], win_ref[...], 1, 1))
    hid_ref[...] = activated.astype(bf16)
    slope_ref[...] = slope


def first_kernel(plane, capacity, groups, win_ref, wout_ref, hid_ref, slope_ref, prob_ref, *refs):
    g_ref, gp_ref, score_ref, *back_refs = refs[-3 - HALVES :]
    arrange(plane, capacity, groups, refs[: -3 - HALVES], g_ref)
    pulled = dot(g_ref[...], wout_ref[...], 1, 1)
    grad_pre = (prob_ref[:, 0:1] * pulled * slope_ref[...]).astype(bf16)
    gp_ref[...] = grad_pre
    width = back_refs[0].shape[1]
    for h, back_ref in enumerate(back_refs):
        back_ref[...] = dot(grad_pre, win_ref[:, h * width : (h + 1) * width], 1, 0).astype(bf16)
    score = jnp.sum(hid_ref[...].astype(f32) * pulled, axis=1, keepdims=True)
    score_ref[...] = jnp.broadcast_to(score, score_ref.shape)


def second_kernel(wout_ref, hid_ref, slope_ref, prob_ref, score0_ref, *refs):
    g_refs, (gp_ref, score_ref) = refs[:-2], refs[-2:]
    width = g_refs[0].shape[1]
    pulled = sum(
        dot(g_ref[...], wout_ref[:, h * width : (h + 1) * width], 1, 1) for h, g_ref in enumerate(g_refs)
    )
    score = jnp.sum(hid_ref[...].astype(f32) * pulled, axis=1, keepdims=True)
    lane = lax.broadcasted_iota(jnp.int32, score_ref.shape, 1)
    both = jnp.where(lane == 0, score0_ref[...], jnp.where(lane == 1, score, 0.0))
    score_ref[...] = both.astype(bf16)
    gp_ref[...] = (prob_ref[:, 1:2] * pulled * slope_ref[...]).astype(bf16)


def grads_kernel(prob_ref, x0_ref, x1_ref, g0_ref, *refs):
    g1_refs = refs[:HALVES]
    hid0_ref, hid1_ref, gp0_ref, gp1_ref, gin_ref, gout_ref, hid, gp = refs[HALVES:]
    i = pl.program_id(0)
    rows = hid0_ref.shape[0]
    width = gin_ref.shape[1]

    @pl.when(i == 0)
    def _():
        hid[:rows, :] = hid0_ref[...]
        hid[rows:, :] = hid1_ref[...]
        gp[:rows, :] = gp0_ref[...]
        gp[rows:, :] = gp1_ref[...]

    lanes = pl.ds(pl.multiple_of(i * width, width), width)
    x = jnp.concatenate([x0_ref[:, lanes], x1_ref[:, lanes]], axis=0)
    gin_ref[...] = dot(gp[...], x, 0, 0).astype(bf16)

    per = g1_refs[0].shape[1] // width
    for h, g1_ref in enumerate(g1_refs):

        @pl.when((i >= h * per) & (i < (h + 1) * per))
        def _():
            y0 = prob_ref[:, 0:1] * g0_ref[:, lanes].astype(f32)
            part = pl.ds(pl.multiple_of((i - h * per) * width, width), width)
            y1 = prob_ref[:, 1:2] * g1_ref[:, part].astype(f32)
            y = jnp.concatenate([y0.astype(bf16), y1.astype(bf16)], axis=0)
            gout_ref[...] = dot(hid[...], y, 0, 0).astype(bf16)


def grads(width, *args):
    features = args[1].shape[1]
    rows, units = args[-1].shape
    outs = [shaped((units, features), bf16)] * 2
    return pl.pallas_call(
        grads_kernel,
        grid=(features // width,),
        out_shape=outs,
        in_specs=[VMEM] * len(args),
        out_specs=[pl.BlockSpec((units, width), lambda i: (0, i))] * 2,
        scratch_shapes=[pltpu.VMEM((2 * rows, units), bf16)] * 2,
        compiler_params=pltpu.CompilerParams(vmem_limit_bytes=VMEM_LIMIT),
        cost_estimate=cost(args, outs, 8 * units * rows * features),
    )(*args)


def collect_kernel(experts, capacity, topk, meta_ref, hot0_ref, hot1_ref, score_ref, out_ref):
    tokens = meta_ref.shape[2]
    rep = expander(experts * capacity, experts, capacity)
    expert = lax.broadcasted_iota(jnp.int32, (experts, tokens), 0).astype(f32)
    own = meta_ref[lax.axis_index("expert")]
    for k, hot_ref in enumerate((hot0_ref, hot1_ref)):
        placed = hot_ref[...].astype(f32) * score_ref[:, k : k + 1].astype(f32)
        by_expert = dot(rep, placed.astype(bf16), 0, 0)
        for j in range(topk):
            i = k * topk + j
            picked = jnp.where(own[i : i + 1, :] == expert, by_expert, 0.0)
            out_ref[i : i + 1, :] = jnp.sum(picked, axis=0, keepdims=True).astype(bf16)


def body(inputs, entering, weight_in, weight_out, gate_probs, expert_ids):
    experts = lax.axis_size("expert")
    segments = lax.axis_size("segment")
    tokens, features = entering.shape[1:]
    ticks, topk = expert_ids.shape[1], expert_ids.shape[3]
    units = weight_in.shape[2]
    capacity = 3 * tokens * topk // (2 * experts)
    rows = experts * capacity
    plane = Plane(experts)
    matmul = 2 * rows * units * features
    half = features // HALVES
    w_in, w_out = weight_in[0, 0], weight_out[0, 0]
    x0, x1, g0 = inputs[0, 0], inputs[0, 1], entering[0]

    ids = jnp.transpose(expert_ids[0], (0, 2, 1)).reshape(ticks * topk, tokens)
    probs = jnp.transpose(gate_probs[0], (0, 2, 1)).reshape(ticks * topk, tokens)
    meta = jnp.concatenate([ids.astype(f32), probs.astype(f32)], axis=0)
    meta = jnp.broadcast_to(meta[None], (experts,) + meta.shape)
    meta = lax.all_to_all(meta, "expert", split_axis=0, concat_axis=0, tiled=True)
    hot0, hot1, prob = call(
        functools.partial(slots_kernel, experts, capacity, topk),
        [shaped((rows, tokens), bf16)] * 2 + [shaped((rows, LANES), f32)],
        meta,
    )

    if capacity % 16 == 0:
        step = functools.partial(two_step, plane, capacity, topk)
        x0, x0_layout = step(0, 1, x0, meta)
        g0_in, g0_layout = step(0, 0, g0, meta)
        left, left_layout = step(1, 1, x1[:, :half], meta)
        right, right_layout = step(1, 0, x1[:, half:], meta)
        x1, x1_groups = left + right, [(0, left_layout), (half, right_layout)]
    else:
        x0, x0_layout = [exchange(spread(hot0, x0), experts)], None
        g0_in, g0_layout = [exchange(spread(hot0, g0), experts)], None
        x1, x1_groups = [exchange(spread(hot1, x1), experts)], [(0, None)]

    acts = [shaped((rows, features), bf16), shaped((rows, units), bf16), shaped((rows, units), f32)]
    x0, hid0, slope0 = call(
        functools.partial(preact_kernel, plane, capacity, [(0, x0_layout)]), acts, w_in, *x0, flops=matmul
    )
    g0_in, gp0, score0, *backs = call(
        functools.partial(first_kernel, plane, capacity, [(0, g0_layout)]),
        [shaped((rows, features), bf16), shaped((rows, units), bf16), shaped((rows, LANES), f32)]
        + [shaped((rows, half), bf16)] * HALVES,
        w_in, w_out, hid0, slope0, prob, *g0_in, flops=2 * matmul,
    )
    x1, hid1, slope1 = call(
        functools.partial(preact_kernel, plane, capacity, x1_groups), acts, w_in, *x1, flops=matmul
    )
    g1 = []
    for h, back in enumerate(backs):
        back = exchange(back, experts)
        (leaving,) = call(
            functools.partial(combine_kernel, h * half), [shaped((tokens, half), bf16)], hot0, back, g0,
            flops=2 * rows * tokens * half,
        )
        arrived = lax.ppermute(leaving, "segment", [(i, i - 1) for i in range(1, segments)])
        g1.append(exchange(spread(hot1, arrived), experts))
    gp1, scores = call(
        second_kernel, [shaped((rows, units), bf16), shaped((rows, LANES), bf16)],
        w_out, hid1, slope1, prob, score0, *g1, flops=matmul,
    )
    scores = exchange(scores, experts)
    grad_in, grad_out = grads(half // 2, prob, x0, x1, g0_in, *g1, hid0, hid1, gp0, gp1)
    (prob_grads,) = call(
        functools.partial(collect_kernel, experts, capacity, topk),
        [shaped((ticks * topk, tokens), bf16)], meta, hot0, hot1, scores,
    )
    prob_grads = jnp.transpose(prob_grads.reshape(ticks, topk, tokens), (0, 2, 1))
    return grad_in[None, None], grad_out[None, None], prob_grads[None]


def solution(mesh):
    return jax.shard_map(
        body,
        mesh=mesh,
        in_specs=(
            P("segment", None, "expert", None),
            P("segment", "expert", None),
            P("segment", "expert", None, None),
            P("segment", "expert", None, None),
            P("segment", None, "expert", None),
            P("segment", None, "expert", None),
        ),
        out_specs=(
            P("segment", "expert", None, None),
            P("segment", "expert", None, None),
            P("segment", None, "expert", None),
        ),
        check_vma=False,
    )
```

time: 159 us -> 173 us (1.088)
  starting transfers between devices: 15.4 us -> 34.6 us
  blocking collectives: 44.2 us -> 27.8 us
  local copies, waits for them, and re-layouts: 17.1 us -> 30.7 us
  waiting for transfers between devices: 51.2 us -> 48.6 us
    all_to_all x4, waiting for transfers between devices: 36.3 us -> 0.01 us  [exchange(): lax.all_to_all(pieces, 'expert', split_axis=0, concat_axis=0, tiled=True)]
    ppermute x0 -> x16, waiting for transfers between devices: none -> 33 us  [send(): return lax.ppermute(value, 'expert', route)]
    all_to_all x1, blocking collectives: 44.2 us -> 15.6 us  [exchange(): lax.all_to_all(pieces, 'expert', split_axis=0, concat_axis=0, tiled=True)]
    ppermute x0 -> x16, starting transfers between devices: none -> 15.8 us  [send(): return lax.ppermute(value, 'expert', route)]
    all_to_all x0 -> x1, blocking collectives: none -> 12.2 us  [body(): lax.all_to_all(meta, 'expert', split_axis=0, concat_axis=0, tiled=True)]
    unnamed x38 -> x78, local copies, waits for them, and re-layouts: 15.8 us -> 27.6 us
    all_to_all x4, starting transfers between devices: 14.1 us -> 16.2 us  [exchange(): lax.all_to_all(pieces, 'expert', split_axis=0, concat_axis=0, tiled=True)]
    ppermute x1 -> x2, waiting for transfers between devices: 14.9 us -> 15.6 us  [body(): lax.ppermute(leaving, 'segment', [(i, i - 1) for i in range(1, segments)])]
  transfers between devices with their start and end apart: 5 -> 22, of which waited for: 4 -> 9; matrix products, arithmetic and copies ran while one was open for 0% -> 1% of each run, Pallas kernels for 9% -> 13%
where the time goes in v2:
time: 173 us; the launch traced here: 172 us
  waiting for transfers between devices  48.6 us (28%)
  starting transfers between devices  34.6 us (20%)
  local copies, waits for them, and re-layouts  30.7 us (18%)
  Pallas kernels  29 us (17%)
  blocking collectives  27.8 us (16%)
    ppermute x16, waiting for transfers between devices, send(): return lax.ppermute(value, 'expert', route)  33 us
    unnamed x78, local copies, waits for them, and re-layouts  27.6 us
    pallas_call x14, Pallas kernels, call(): pl.pallas_call(kernel, out_shape=outs, in_specs=[VMEM] * len(args), out_s...  19.9 us
    all_to_all x4, starting transfers between devices, exchange(): lax.all_to_all(pieces, 'expert', split_axis=0, concat_axis=0, tiled=True)  16.2 us
    ppermute x16, starting transfers between devices, send(): return lax.ppermute(value, 'expert', route)  15.8 us
    all_to_all x1, blocking collectives, exchange(): lax.all_to_all(pieces, 'expert', split_axis=0, concat_axis=0, tiled=True)  15.6 us
    ppermute x2, waiting for transfers between devices, body(): lax.ppermute(leaving, 'segment', [(i, i - 1) for i in range(1, segments)])  15.6 us
    all_to_all x1, blocking collectives, body(): lax.all_to_all(meta, 'expert', split_axis=0, concat_axis=0, tiled=True)  12.2 us
  transfers between devices with their start and end apart: 22, of which 9 were waited for; matrix products, arithmetic and copies ran while one was open for 1% of the time, Pallas kernels for 13%

profile of v2, /device:TPU:0, one launch (start us, length us, event | category | flops | bytes accessed | tf_op | source)
XLA Modules:
  0.0 171.8 jit_solution(4916813516368122172)
XLA Ops:
  0.7 2.3 %slice_bitcast_fusion = (bf16[128,2048]{1,0:T(8,128)(2,1)}, bf16[128,2048]{1,0:T(8,128)(2,1)S(1)}) fusion(bf16[1,2,128,2048]{3,2,1,0:T(8,128)(2,1)} %param.6), kind=kLoop, calls=%fused_computation | loop fusion | bytes 2097152 | tf_op jit(solution)/shard_map/squeeze | solution.py:306
  2.9 2.9 %collective-permute-start = (bf16[128,2048]{1,0:T(8,128)(2,1)S(1)}, bf16[128,2048]{1,0:T(8,128)(2,1)S(1)}, u32[]{:S(2)}, u32[]{:S(2)}) collective-permute-start(bf16[128,2048]{1,0:T(8,128)(2,1)S(1)} %get-tuple-element.72.refs_0_), channel_id=1, source_target_pairs={{0,2},{1,3},{2,0},{3,1},{4,6},{5,7},{6,4},{7,5},{8,10},{9,11},{10,... | collective-permute-start | bytes 1572872 | tf_op jit(solution)/shard_map/ppermute | solution.py:64
  5.9 1.5 collective-permute-start.12
  7.4 12.2 %all_to_all.30.meta_ref = f32[8,8,128]{2,1,0:T(8,128)S(1)} all-to-all(f32[8,8,128]{2,1,0:T(8,128)S(1)} %broadcast_in_dim.15), channel_id=1, replica_groups=mesh['segment'=4,'expert'=8] {'expert'}, dimensions={0} | all-to-all | bytes 65536 | tf_op jit(solution)/shard_map/all_to_all | solution.py:312
  20.8 1.6 collective-permute-start.2
  22.6 1.0 shard_map.91
  24.1 1.2 collective-permute-start.14
  26.9 5.9 %collective-permute-done.2.refs_2_ = bf16[96,2048]{1,0:T(8,128)(2,1)S(1)} collective-permute-done((bf16[96,2048]{1,0:T(8,128)(2,1)S(1)}, bf16[96,2048]{1,0:T(8,128)(2,1)S(1)}, u32[]{:S(2)}, u32[]{:S(2)}) %collective-permute-start.2) | collective-permute-done | bytes 393248 | tf_op jit(solution)/shard_map/ppermute | solution.py:64
  32.7 7.5 %collective-permute-done.3.refs_3_ = bf16[96,2048]{1,0:T(8,128)(2,1)S(1)} collective-permute-done((bf16[96,2048]{1,0:T(8,128)(2,1)S(1)}, bf16[96,2048]{1,0:T(8,128)(2,1)S(1)}, u32[]{:S(2)}, u32[]{:S(2)}) %collective-permute-start.3) | collective-permute-done | bytes 393248 | tf_op jit(solution)/shard_map/ppermute | solution.py:64
  40.3 1.8 %shard_map.87 = (bf16[384,2048]{1,0:T(8,128)(2,1)S(1)}, bf16[384,704]{1,0:T(8,128)(2,1)S(1)}, f32[384,704]{1,0:T(8,128)S(1)}) custom-call(bf16[704,2048]{1,0:T(8,128)(2,1)S(1)} %bitcast.35, bf16[96,2048]{1,0:T(8,128)(2,1)S(1)} %get-tuple-element.38.refs_0_, bf16[96,2048]{1,0:T(8,128)(2,1)S(1)} %collective-permute-done.1.refs_1_, ...), custom_call_target="tpu_custom_call" | custom-call | flops 1107296256 | bytes 7651328 | tf_op jit(solution)/shard_map/pallas_call | solution.py:34
  42.1 1.1 copy-done.26
  43.2 3.1 %shard_map.92 = (bf16[384,2048]{1,0:T(8,128)(2,1)S(1)}, bf16[384,704]{1,0:T(8,128)(2,1)S(1)}, f32[384,128]{1,0:T(8,128)S(1)}, bf16[384,1024]{1,0:T(8,128)(2,1)S(1)}, bf16[384,1024]{1,0:T(8,128)(2,1)S(1)}) custom-call(bf16[704,2048]{1,0:T(8,128)(2,1)S(1)} %bitcast.36, bf16[704,2048]{1,0:T(8,128)(2,1)S(1)} %bitcast.38, ...), custom_call_target="tpu_custom_call" | custom-call | flops 2214592512 | bytes 13041664 | tf_op jit(solution)/shard_map/pallas_call | solution.py:34
  46.4 1.2 copy-done.28
  47.6 15.6 %all_to_all.31 = bf16[8,48,1024]{2,1,0:T(8,128)(2,1)} all-to-all(bf16[8,48,1024]{2,1,0:T(8,128)(2,1)S(1)} %bitcast.48), channel_id=1, replica_groups=mesh['segment'=4,'expert'=8] {'expert'}, dimensions={0} | all-to-all | bytes 1572864 | tf_op jit(solution)/shard_map/all_to_all | solution.py:169
  63.2 4.2 %all-to-all-start.3 = ((bf16[8,48,1024]{2,1,0:T(8,128)(2,1)}), bf16[8,48,1024]{2,1,0:T(8,128)(2,1)}, u32[]{:S(2)}, u32[]{:S(2)}) async-start(bf16[8,48,1024]{2,1,0:T(8,128)(2,1)} %bitcast.47), calls=%async_computation.3 | async-start | bytes 1572864 | tf_op jit(solution)/shard_map/all_to_all | solution.py:169
  67.5 1.1 copy-done.6
  68.9 1.3 collective-permute-start.16
  70.2 9.2 %collective-permute-done.16.x_ref = bf16[128,1024]{1,0:T(8,128)(2,1)S(1)} collective-permute-done((bf16[128,1024]{1,0:T(8,128)(2,1)S(1)}, bf16[128,1024]{1,0:T(8,128)(2,1)S(1)}, u32[]{:S(2)}, u32[]{:S(2)}) %collective-permute-start.16) | collective-permute-done | bytes 262176 | tf_op jit(solution)/shard_map/ppermute | solution.py:351
  80.6 4.2 %all-to-all-start.2 = ((bf16[8,48,1024]{2,1,0:T(8,128)(2,1)}), bf16[8,48,1024]{2,1,0:T(8,128)(2,1)}, u32[]{:S(2)}, u32[]{:S(2)}) async-start(bf16[8,48,1024]{2,1,0:T(8,128)(2,1)} %bitcast.45), calls=%async_computation.2 | async-start | bytes 1572864 | tf_op jit(solution)/shard_map/all_to_all | solution.py:169
  84.9 1.5 shard_map.95
  86.4 1.3 collective-permute-start.17
  88.6 1.9 %collective-permute-start.8 = (bf16[128,1024]{1,0:T(8,128)(2,1)}, bf16[128,1024]{1,0:T(8,128)(2,1)S(1)}, u32[]{:S(2)}, u32[]{:S(2)}) collective-permute-start(bf16[128,1024]{1,0:T(8,128)(2,1)} %get-tuple-element.73.refs_0_), channel_id=1, source_target_pairs={{0,4},{1,5},{2,6},{3,7},{4,0},{5,1},{6,2},{7,3},{8,12},{9,13},{10,... | collective-permute-start | bytes 786440 | tf_op jit(solution)/shard_map/ppermute | solution.py:64
  90.5 6.4 %collective-permute-done.17.x_ref = bf16[128,1024]{1,0:T(8,128)(2,1)S(1)} collective-permute-done((bf16[128,1024]{1,0:T(8,128)(2,1)S(1)}, bf16[128,1024]{1,0:T(8,128)(2,1)S(1)}, u32[]{:S(2)}, u32[]{:S(2)}) %collective-permute-start.17) | collective-permute-done | bytes 262176 | tf_op jit(solution)/shard_map/ppermute | solution.py:351
  98.2 4.4 %all-to-all-start.4 = ((bf16[8,48,1024]{2,1,0:T(8,128)(2,1)}), bf16[8,48,1024]{2,1,0:T(8,128)(2,1)}, u32[]{:S(2)}, u32[]{:S(2)}) async-start(bf16[8,48,1024]{2,1,0:T(8,128)(2,1)} %bitcast.44), calls=%async_computation.4 | async-start | bytes 1572864 | tf_op jit(solution)/shard_map/all_to_all | solution.py:169
  102.6 1.7 %collective-permute-start.4 = (bf16[128,1024]{1,0:T(8,128)(2,1)}, bf16[128,1024]{1,0:T(8,128)(2,1)S(1)}, u32[]{:S(2)}, u32[]{:S(2)}) collective-permute-start(bf16[128,1024]{1,0:T(8,128)(2,1)} %get-tuple-element.74.refs_0_), channel_id=1, source_target_pairs={{0,2},{1,3},{2,0},{3,1},{4,6},{5,7},{6,4},{7,5},{8,10},{9,11},{10,... | collective-permute-start | bytes 786440 | tf_op jit(solution)/shard_map/ppermute | solution.py:64
  105.9 1.8 %shard_map.89 = (bf16[96,1024]{1,0:T(8,128)(2,1)S(1)}, bf16[96,1024]{1,0:T(8,128)(2,1)S(1)}, bf16[96,1024]{1,0:T(8,128)(2,1)S(1)}, bf16[96,1024]{1,0:T(8,128)(2,1)S(1)}) custom-call(f32[8,8,128]{2,1,0:T(8,128)S(1)} %all_to_all.30.meta_ref, bf16[128,1024]{1,0:T(8,128)(2,1)} %get-tuple-element.73.refs_0_, bf16[128,1024]{1,0:T(8,128)(2,1)S(1)} %copy-done.23), custom_call_target="tpu_custom_call" | custom-call | flops 100663296 | bytes 1343488 | tf_op jit(solution)/shard_map/pallas_call | solution.py:34
  108.3 1.4 collective-permute-start.11
  109.7 10.4 %collective-permute-done.4.refs_1_ = bf16[128,1024]{1,0:T(8,128)(2,1)S(1)} collective-permute-done((bf16[128,1024]{1,0:T(8,128)(2,1)}, bf16[128,1024]{1,0:T(8,128)(2,1)S(1)}, u32[]{:S(2)}, u32[]{:S(2)}) %collective-permute-start.4) | collective-permute-done | bytes 262176 | tf_op jit(solution)/shard_map/ppermute | solution.py:64
  120.1 1.8 %shard_map.88 = (bf16[96,1024]{1,0:T(8,128)(2,1)S(1)}, bf16[96,1024]{1,0:T(8,128)(2,1)S(1)}, bf16[96,1024]{1,0:T(8,128)(2,1)S(1)}, bf16[96,1024]{1,0:T(8,128)(2,1)S(1)}) custom-call(f32[8,8,128]{2,1,0:T(8,128)S(1)} %all_to_all.30.meta_ref, bf16[128,1024]{1,0:T(8,128)(2,1)} %get-tuple-element.74.refs_0_, bf16[128,1024]{1,0:T(8,128)(2,1)S(1)} %collective-permute-done.4.refs_1_), custom_call_target="tpu_custom_call" | custom-call | flops 100663296 | bytes 1343488 | tf_op jit(solution)/shard_map/pallas_call | solution.py:34
  121.9 1.6 collective-permute-start.6
  124.3 3.3 %collective-permute-done.11.refs_7_ = bf16[96,1024]{1,0:T(8,128)(2,1)S(1)} collective-permute-done((bf16[96,1024]{1,0:T(8,128)(2,1)S(1)}, bf16[96,1024]{1,0:T(8,128)(2,1)S(1)}, u32[]{:S(2)}, u32[]{:S(2)}) %collective-permute-start.11) | collective-permute-done | bytes 196640 | tf_op jit(solution)/shard_map/ppermute | solution.py:64
  127.5 2.2 %collective-permute-done.6.refs_2_ = bf16[96,1024]{1,0:T(8,128)(2,1)S(1)} collective-permute-done((bf16[96,1024]{1,0:T(8,128)(2,1)S(1)}, bf16[96,1024]{1,0:T(8,128)(2,1)S(1)}, u32[]{:S(2)}, u32[]{:S(2)}) %collective-permute-start.6) | collective-permute-done | bytes 196640 | tf_op jit(solution)/shard_map/ppermute | solution.py:64
  129.7 3.3 %collective-permute-done.7.refs_3_ = bf16[96,1024]{1,0:T(8,128)(2,1)S(1)} collective-permute-done((bf16[96,1024]{1,0:T(8,128)(2,1)S(1)}, bf16[96,1024]{1,0:T(8,128)(2,1)S(1)}, u32[]{:S(2)}, u32[]{:S(2)}) %collective-permute-start.7) | collective-permute-done | bytes 196640 | tf_op jit(solution)/shard_map/ppermute | solution.py:64
  133.0 1.8 %shard_map.90 = (bf16[384,2048]{1,0:T(8,128)(2,1)S(1)}, bf16[384,704]{1,0:T(8,128)(2,1)S(1)}, f32[384,704]{1,0:T(8,128)S(1)}) custom-call(bf16[704,2048]{1,0:T(8,128)(2,1)S(1)} %bitcast.37, bf16[96,1024]{1,0:T(8,128)(2,1)S(1)} %get-tuple-element.43.refs_0_, bf16[96,1024]{1,0:T(8,128)(2,1)S(1)} %collective-permute-done.5.refs_1_, ...), custom_call_target="tpu_custom_call" | custom-call | flops 1107296256 | bytes 7651328 | tf_op jit(solution)/shard_map/pallas_call | solution.py:34
  136.6 1.1 copy-done.30
  137.8 1.8 %copy-done.2 = bf16[1,1,704,2048]{3,2,1,0:T(8,128)(2,1)S(1)} copy-done((bf16[1,1,704,2048]{3,2,1,0:T(8,128)(2,1)S(1)}, bf16[1,1,704,2048]{3,2,1,0:T(8,128)(2,1)}, u32[]{:S(2)}) %copy-start.2) | copy-done | bytes 2883608
  139.6 1.3 copy-done.8
  141.8 1.1 copy-done.20
  143.8 3.5 %shard_map.97 = (bf16[384,704]{1,0:T(8,128)(2,1)S(1)}, bf16[384,128]{1,0:T(8,128)(2,1)}) custom-call(bf16[704,2048]{1,0:T(8,128)(2,1)S(1)} %bitcast.39, bf16[384,704]{1,0:T(8,128)(2,1)S(1)} %copy-done.20, f32[384,704]{1,0:T(8,128)S(1)} %copy-done.8, f32[384,128]{1,0:T(8,128)S(1)} %copy-done.14, f32[384,128]{1,0:T(8,128)S(1)} %copy-done.25, ...), custom_call_target="tpu_custom_call" | custom-call | flops 1107296256 | bytes 7110656 | tf_op jit(solution)/shard_map/pallas_call | solution.py:34
  148.1 3.4 %all-to-all-start.5 = ((bf16[8,48,128]{2,1,0:T(8,128)(2,1)}), bf16[8,48,128]{2,1,0:T(8,128)(2,1)S(1)}, u32[]{:S(2)}, u32[]{:S(2)}) async-start(bf16[8,48,128]{2,1,0:T(8,128)(2,1)} %bitcast.21), calls=%async_computation.5 | async-start | bytes 196608 | tf_op jit(solution)/shard_map/all_to_all | solution.py:169
  152.4 1.1 copy-done.18
  153.5 1.1 copy-done.21
  154.6 1.4 copy-done.27
  156.0 1.4 copy-done.29
  157.4 1.4 copy-done.31
  158.8 1.1 copy-done.33
  159.9 1.1 copy-done.35
  160.9 9.1 %shard_map.98 = (bf16[704,2048]{1,0:T(8,128)(2,1)}, bf16[704,2048]{1,0:T(8,128)(2,1)}) custom-call(f32[384,128]{1,0:T(8,128)S(1)} %copy-done.15, bf16[384,2048]{1,0:T(8,128)(2,1)S(1)} %copy-done.27, bf16[384,2048]{1,0:T(8,128)(2,1)S(1)} %copy-done.31, bf16[384,2048]{1,0:T(8,128)(2,1)S(1)} %copy-done.29, bf16[384,1024]{1,0:T(8,128)(2,1)} %bitcast.14.refs_0_, ...), custom_call_target="tpu_custom_call" | custom-call | flops 4429185024 | bytes 14417920 | tf_op jit(solution)/shard_map/pallas_call | solution.py:268
  (97 shorter events, 17.3 us)
Async XLA Ops:
  0.6 5.3 %copy-start.3 = (bf16[1,128,2048]{2,1,0:T(8,128)(2,1)S(1)}, bf16[1,128,2048]{2,1,0:T(8,128)(2,1)}, u32[]{:S(2)}) copy-start(bf16[1,128,2048]{2,1,0:T(8,128)(2,1)} %param.7) | copy-start | bytes 1572868
  0.6 6.8 %copy-start.37 = (s32[1,2,128,2]{2,3,1,0:T(2,128)S(1)}, s32[1,2,128,2]{2,3,1,0:T(2,128)}, u32[]{:S(2)}) copy-start(s32[1,2,128,2]{2,3,1,0:T(2,128)} %param.11) | copy-start | bytes 6148
  0.7 6.8 %copy-start.38 = (bf16[1,2,128,2]{2,3,1,0:T(2,128)(2,1)S(1)}, bf16[1,2,128,2]{2,3,1,0:T(2,128)(2,1)}, u32[]{:S(2)}) copy-start(bf16[1,2,128,2]{2,3,1,0:T(2,128)(2,1)} %param.10) | copy-start | bytes 3076
  0.7 39.6 %copy-start = (bf16[1,1,704,2048]{3,2,1,0:T(8,128)(2,1)S(1)}, bf16[1,1,704,2048]{3,2,1,0:T(8,128)(2,1)}, u32[]{:S(2)}) copy-start(bf16[1,1,704,2048]{3,2,1,0:T(8,128)(2,1)} %param.8) | copy-start | bytes 8650756
  2.9 16.7 %collective-permute-start = (bf16[128,2048]{1,0:T(8,128)(2,1)S(1)}, bf16[128,2048]{1,0:T(8,128)(2,1)S(1)}, u32[]{:S(2)}, u32[]{:S(2)}) collective-permute-start(bf16[128,2048]{1,0:T(8,128)(2,1)S(1)} %get-tuple-element.72.refs_0_), channel_id=1, source_target_pairs={{0,2},{1,3},{2,0},{3,1},{4,6},{5,7},{6,4},{7,5},{8,10},{9,11},{10,... | collective-permute-start | bytes 1572872 | tf_op jit(solution)/shard_map/ppermute | solution.py:64
  5.9 16.7 %collective-permute-start.12 = (bf16[128,2048]{1,0:T(8,128)(2,1)S(1)}, bf16[128,2048]{1,0:T(8,128)(2,1)S(1)}, u32[]{:S(2)}, u32[]{:S(2)}) collective-permute-start(bf16[128,2048]{1,0:T(8,128)(2,1)S(1)} %bitcast.40), channel_id=1, source_target_pairs={{0,4},{1,5},{2,6},{3,7},{4,0},{5,1},{6,2},{7,3},{8,12},{9,13},{10,... | collective-permute-start | bytes 1572872 | tf_op jit(solution)/shard_map/ppermute | solution.py:64
  20.7 4.6 %collective-permute-start.1 = (bf16[96,2048]{1,0:T(8,128)(2,1)S(1)}, bf16[96,2048]{1,0:T(8,128)(2,1)S(1)}, u32[]{:S(2)}, u32[]{:S(2)}) collective-permute-start(bf16[96,2048]{1,0:T(8,128)(2,1)S(1)} %get-tuple-element.39), channel_id=1, source_target_pairs={{0,1},{1,0},{2,3},{3,2},{4,5},{5,4},{6,7},{7,6},{8,9},{9,8},{10,11... | collective-permute-start | bytes 1179656 | tf_op jit(solution)/shard_map/ppermute | solution.py:64
  20.8 12.0 %collective-permute-start.2 = (bf16[96,2048]{1,0:T(8,128)(2,1)S(1)}, bf16[96,2048]{1,0:T(8,128)(2,1)S(1)}, u32[]{:S(2)}, u32[]{:S(2)}) collective-permute-start(bf16[96,2048]{1,0:T(8,128)(2,1)S(1)} %get-tuple-element.40), channel_id=1, source_target_pairs={{0,4},{1,5},{2,6},{3,7},{4,0},{5,1},{6,2},{7,3},{8,12},{9,13},{10,... | collective-permute-start | bytes 1179656 | tf_op jit(solution)/shard_map/ppermute | solution.py:64
  22.3 17.9 %collective-permute-start.3 = (bf16[96,2048]{1,0:T(8,128)(2,1)S(1)}, bf16[96,2048]{1,0:T(8,128)(2,1)S(1)}, u32[]{:S(2)}, u32[]{:S(2)}) collective-permute-start(bf16[96,2048]{1,0:T(8,128)(2,1)S(1)} %get-tuple-element.41), channel_id=1, source_target_pairs={{0,5},{1,4},{2,7},{3,6},{4,1},{5,0},{6,3},{7,2},{8,13},{9,12},{10,... | collective-permute-start | bytes 1179656 | tf_op jit(solution)/shard_map/ppermute | solution.py:64
  23.7 19.5 %collective-permute-start.13 = (bf16[96,2048]{1,0:T(8,128)(2,1)S(1)}, bf16[96,2048]{1,0:T(8,128)(2,1)S(1)}, u32[]{:S(2)}, u32[]{:S(2)}) collective-permute-start(bf16[96,2048]{1,0:T(8,128)(2,1)S(1)} %get-tuple-element.55), channel_id=1, source_target_pairs={{0,1},{1,0},{2,3},{3,2},{4,5},{5,4},{6,7},{7,6},{8,9},{9,8},{10,11... | collective-permute-start | bytes 1179656 | tf_op jit(solution)/shard_map/ppermute | solution.py:64
  24.1 19.1 %collective-permute-start.14 = (bf16[96,2048]{1,0:T(8,128)(2,1)S(1)}, bf16[96,2048]{1,0:T(8,128)(2,1)S(1)}, u32[]{:S(2)}, u32[]{:S(2)}) collective-permute-start(bf16[96,2048]{1,0:T(8,128)(2,1)S(1)} %get-tuple-element.56), channel_id=1, source_target_pairs={{0,2},{1,3},{2,0},{3,1},{4,6},{5,7},{6,4},{7,5},{8,10},{9,11},{10,... | collective-permute-start | bytes 1179656 | tf_op jit(solution)/shard_map/ppermute | solution.py:64
  25.3 17.9 %collective-permute-start.15 = (bf16[96,2048]{1,0:T(8,128)(2,1)S(1)}, bf16[96,2048]{1,0:T(8,128)(2,1)S(1)}, u32[]{:S(2)}, u32[]{:S(2)}) collective-permute-start(bf16[96,2048]{1,0:T(8,128)(2,1)S(1)} %get-tuple-element.57), channel_id=1, source_target_pairs={{0,3},{1,2},{2,1},{3,0},{4,7},{5,6},{6,5},{7,4},{8,11},{9,10},{10,... | collective-permute-start | bytes 1179656 | tf_op jit(solution)/shard_map/ppermute | solution.py:64
  26.9 16.4 %copy-start.13 = (f32[384,128]{1,0:T(8,128)}, f32[384,128]{1,0:T(8,128)S(1)}, u32[]{:S(2)}) copy-start(f32[384,128]{1,0:T(8,128)S(1)} %get-tuple-element.37.prob_ref) | copy-start | bytes 589828
  40.3 3.0 %copy-start.1 = (bf16[1,1,704,2048]{3,2,1,0:T(8,128)(2,1)S(1)}, bf16[1,1,704,2048]{3,2,1,0:T(8,128)(2,1)}, u32[]{:S(2)}) copy-start(bf16[1,1,704,2048]{3,2,1,0:T(8,128)(2,1)} %param.9) | copy-start | bytes 8650756
  42.0 1.1 copy-start.26
  43.2 3.2 %copy-start.17 = (bf16[384,704]{1,0:T(8,128)(2,1)}, bf16[384,704]{1,0:T(8,128)(2,1)S(1)}, u32[]{:S(2)}) copy-start(bf16[384,704]{1,0:T(8,128)(2,1)S(1)} %get-tuple-element.52.hid_ref.refs_2_) | copy-start | bytes 1622020
  46.4 1.2 copy-start.28
  47.6 15.7 %copy-start.24 = (f32[384,128]{1,0:T(8,128)}, f32[384,128]{1,0:T(8,128)S(1)}, u32[]{:S(2)}) copy-start(f32[384,128]{1,0:T(8,128)S(1)} %get-tuple-element.66.score0_ref) | copy-start | bytes 589828
  47.6 15.7 %copy-start.16 = (bf16[384,1024]{1,0:T(8,128)(2,1)}, bf16[384,1024]{1,0:T(8,128)(2,1)S(1)}, u32[]{:S(2)}) copy-start(bf16[384,1024]{1,0:T(8,128)(2,1)S(1)} %get-tuple-element.62) | copy-start | bytes 2359300
  47.6 15.7 %copy-start.32 = (bf16[384,704]{1,0:T(8,128)(2,1)}, bf16[384,704]{1,0:T(8,128)(2,1)S(1)}, u32[]{:S(2)}) copy-start(bf16[384,704]{1,0:T(8,128)(2,1)S(1)} %get-tuple-element.64.refs_4_) | copy-start | bytes 1622020
  63.2 17.4 %all-to-all-start.3 = ((bf16[8,48,1024]{2,1,0:T(8,128)(2,1)}), bf16[8,48,1024]{2,1,0:T(8,128)(2,1)}, u32[]{:S(2)}, u32[]{:S(2)}) async-start(bf16[8,48,1024]{2,1,0:T(8,128)(2,1)} %bitcast.47), calls=%async_computation.3 | async-start | bytes 1572864 | tf_op jit(solution)/shard_map/all_to_all | solution.py:169
  67.5 1.1 copy-start.6
  68.6 10.8 %copy-start.10 = (bf16[384,128]{1,0:T(8,128)(2,1)S(1)}, bf16[384,128]{1,0:T(8,128)(2,1)}, u32[]{:S(2)}) copy-start(bf16[384,128]{1,0:T(8,128)(2,1)} %copy-done.9) | copy-start | bytes 294916
  68.9 10.5 %collective-permute-start.16 = (bf16[128,1024]{1,0:T(8,128)(2,1)S(1)}, bf16[128,1024]{1,0:T(8,128)(2,1)S(1)}, u32[]{:S(2)}, u32[]{:S(2)}) collective-permute-start(bf16[128,1024]{1,0:T(8,128)(2,1)S(1)} %shard_map.93), channel_id=1, source_target_pairs={{8,0},{16,8},{24,16},{9,1},{17,9},{25,17},{10,2},{18,10},{26,18},{... | collective-permute-start | bytes 786440 | tf_op jit(solution)/shard_map/ppermute | solution.py:351
  80.6 17.5 %all-to-all-start.2 = ((bf16[8,48,1024]{2,1,0:T(8,128)(2,1)}), bf16[8,48,1024]{2,1,0:T(8,128)(2,1)}, u32[]{:S(2)}, u32[]{:S(2)}) async-start(bf16[8,48,1024]{2,1,0:T(8,128)(2,1)} %bitcast.45), calls=%async_computation.2 | async-start | bytes 1572864 | tf_op jit(solution)/shard_map/all_to_all | solution.py:169
  84.9 2.8 %copy-start.36 = (bf16[128,2048]{1,0:T(8,128)(2,1)S(1)}, bf16[128,2048]{1,0:T(8,128)(2,1)}, u32[]{:S(2)}) copy-start(bf16[128,2048]{1,0:T(8,128)(2,1)} %get-tuple-element.71) | copy-start | bytes 1572868
  84.9 12.0 %copy-start.11 = (bf16[384,128]{1,0:T(8,128)(2,1)S(1)}, bf16[384,128]{1,0:T(8,128)(2,1)}, u32[]{:S(2)}) copy-start(bf16[384,128]{1,0:T(8,128)(2,1)} %copy-done.9) | copy-start | bytes 294916
  86.4 10.5 %collective-permute-start.17 = (bf16[128,1024]{1,0:T(8,128)(2,1)S(1)}, bf16[128,1024]{1,0:T(8,128)(2,1)S(1)}, u32[]{:S(2)}, u32[]{:S(2)}) collective-permute-start(bf16[128,1024]{1,0:T(8,128)(2,1)S(1)} %shard_map.95), channel_id=1, source_target_pairs={{8,0},{16,8},{24,16},{9,1},{17,9},{25,17},{10,2},{18,10},{26,18},{... | collective-permute-start | bytes 786440 | tf_op jit(solution)/shard_map/ppermute | solution.py:351
  88.6 15.7 %collective-permute-start.8 = (bf16[128,1024]{1,0:T(8,128)(2,1)}, bf16[128,1024]{1,0:T(8,128)(2,1)S(1)}, u32[]{:S(2)}, u32[]{:S(2)}) collective-permute-start(bf16[128,1024]{1,0:T(8,128)(2,1)} %get-tuple-element.73.refs_0_), channel_id=1, source_target_pairs={{0,4},{1,5},{2,6},{3,7},{4,0},{5,1},{6,2},{7,3},{8,12},{9,13},{10,... | collective-permute-start | bytes 786440 | tf_op jit(solution)/shard_map/ppermute | solution.py:64
  98.2 39.6 %all-to-all-start.4 = ((bf16[8,48,1024]{2,1,0:T(8,128)(2,1)}), bf16[8,48,1024]{2,1,0:T(8,128)(2,1)}, u32[]{:S(2)}, u32[]{:S(2)}) async-start(bf16[8,48,1024]{2,1,0:T(8,128)(2,1)} %bitcast.44), calls=%async_computation.4 | async-start | bytes 1572864 | tf_op jit(solution)/shard_map/all_to_all | solution.py:169
  102.6 17.5 %collective-permute-start.4 = (bf16[128,1024]{1,0:T(8,128)(2,1)}, bf16[128,1024]{1,0:T(8,128)(2,1)S(1)}, u32[]{:S(2)}, u32[]{:S(2)}) collective-permute-start(bf16[128,1024]{1,0:T(8,128)(2,1)} %get-tuple-element.74.refs_0_), channel_id=1, source_target_pairs={{0,2},{1,3},{2,0},{3,1},{4,6},{5,7},{6,4},{7,5},{8,10},{9,11},{10,... | collective-permute-start | bytes 786440 | tf_op jit(solution)/shard_map/ppermute | solution.py:64
  107.7 15.7 %collective-permute-start.9 = (bf16[96,1024]{1,0:T(8,128)(2,1)S(1)}, bf16[96,1024]{1,0:T(8,128)(2,1)S(1)}, u32[]{:S(2)}, u32[]{:S(2)}) collective-permute-start(bf16[96,1024]{1,0:T(8,128)(2,1)S(1)} %get-tuple-element.48), channel_id=1, source_target_pairs={{0,1},{1,0},{2,3},{3,2},{4,5},{5,4},{6,7},{7,6},{8,9},{9,8},{10,11... | collective-permute-start | bytes 589832 | tf_op jit(solution)/shard_map/ppermute | solution.py:64
  107.8 16.4 %collective-permute-start.10 = (bf16[96,1024]{1,0:T(8,128)(2,1)S(1)}, bf16[96,1024]{1,0:T(8,128)(2,1)S(1)}, u32[]{:S(2)}, u32[]{:S(2)}) collective-permute-start(bf16[96,1024]{1,0:T(8,128)(2,1)S(1)} %get-tuple-element.49), channel_id=1, source_target_pairs={{0,2},{1,3},{2,0},{3,1},{4,6},{5,7},{6,4},{7,5},{8,10},{9,11},{10,... | collective-permute-start | bytes 589832 | tf_op jit(solution)/shard_map/ppermute | solution.py:64
  108.3 19.3 %collective-permute-start.11 = (bf16[96,1024]{1,0:T(8,128)(2,1)S(1)}, bf16[96,1024]{1,0:T(8,128)(2,1)S(1)}, u32[]{:S(2)}, u32[]{:S(2)}) collective-permute-start(bf16[96,1024]{1,0:T(8,128)(2,1)S(1)} %get-tuple-element.50), channel_id=1, source_target_pairs={{0,3},{1,2},{2,1},{3,0},{4,7},{5,6},{6,5},{7,4},{8,11},{9,10},{10,... | collective-permute-start | bytes 589832 | tf_op jit(solution)/shard_map/ppermute | solution.py:64
  121.8 5.7 %collective-permute-start.5 = (bf16[96,1024]{1,0:T(8,128)(2,1)S(1)}, bf16[96,1024]{1,0:T(8,128)(2,1)S(1)}, u32[]{:S(2)}, u32[]{:S(2)}) collective-permute-start(bf16[96,1024]{1,0:T(8,128)(2,1)S(1)} %get-tuple-element.44), channel_id=1, source_target_pairs={{0,1},{1,0},{2,3},{3,2},{4,5},{5,4},{6,7},{7,6},{8,9},{9,8},{10,11... | collective-permute-start | bytes 589832 | tf_op jit(solution)/shard_map/ppermute | solution.py:64
  121.9 7.8 %collective-permute-start.6 = (bf16[96,1024]{1,0:T(8,128)(2,1)S(1)}, bf16[96,1024]{1,0:T(8,128)(2,1)S(1)}, u32[]{:S(2)}, u32[]{:S(2)}) collective-permute-start(bf16[96,1024]{1,0:T(8,128)(2,1)S(1)} %get-tuple-element.45), channel_id=1, source_target_pairs={{0,4},{1,5},{2,6},{3,7},{4,0},{5,1},{6,2},{7,3},{8,12},{9,13},{10,... | collective-permute-start | bytes 589832 | tf_op jit(solution)/shard_map/ppermute | solution.py:64
  123.5 9.5 %collective-permute-start.7 = (bf16[96,1024]{1,0:T(8,128)(2,1)S(1)}, bf16[96,1024]{1,0:T(8,128)(2,1)S(1)}, u32[]{:S(2)}, u32[]{:S(2)}) collective-permute-start(bf16[96,1024]{1,0:T(8,128)(2,1)S(1)} %get-tuple-element.46), channel_id=1, source_target_pairs={{0,5},{1,4},{2,7},{3,6},{4,1},{5,0},{6,3},{7,2},{8,13},{9,12},{10,... | collective-permute-start | bytes 589832 | tf_op jit(solution)/shard_map/ppermute | solution.py:64
  136.6 1.1 copy-start.30
  137.8 1.8 %copy-start.2 = (bf16[1,1,704,2048]{3,2,1,0:T(8,128)(2,1)S(1)}, bf16[1,1,704,2048]{3,2,1,0:T(8,128)(2,1)}, u32[]{:S(2)}) copy-start(bf16[1,1,704,2048]{3,2,1,0:T(8,128)(2,1)} %param.9) | copy-start | bytes 8650756
  139.6 1.3 copy-start.8
  141.8 1.1 copy-start.20
  148.1 21.9 %all-to-all-start.5 = ((bf16[8,48,128]{2,1,0:T(8,128)(2,1)}), bf16[8,48,128]{2,1,0:T(8,128)(2,1)S(1)}, u32[]{:S(2)}, u32[]{:S(2)}) async-start(bf16[8,48,128]{2,1,0:T(8,128)(2,1)} %bitcast.21), calls=%async_computation.5 | async-start | bytes 196608 | tf_op jit(solution)/shard_map/all_to_all | solution.py:169
  152.4 1.1 copy-start.18
  153.5 1.1 copy-start.21
  154.6 1.4 copy-start.27
  156.0 1.4 copy-start.29
  157.4 1.4 copy-start.31
  158.8 1.1 copy-start.33
  (13 other events, 11.5 us)

commit v3 on v2

--- a/solution.py
+++ b/solution.py
@@ -10,11 +10,11 @@
 half_root = 0.7071067811865476
 density_scale = 0.3989422804014327
 LANES = 128
-HALVES = 2
-VMEM_LIMIT = 16 * 1024 * 1024
+AXES = (2, 2)
+HALVES = len(AXES)
+VMEM_LIMIT = 20 * 1024 * 1024
 f32 = jnp.float32
 bf16 = jnp.bfloat16
-VMEM = pl.BlockSpec(memory_space=pltpu.VMEM)
 
 
 def dot(a, b, ca, cb):
@@ -30,12 +30,11 @@
     return pl.CostEstimate(flops=flops, bytes_accessed=size, transcendentals=0)
 
 
-def call(kernel, outs, *args, flops=0):
+def call(kernel, outs, *args, flops=0, scratch=()):
     return pl.pallas_call(
         kernel,
         out_shape=outs,
-        in_specs=[VMEM] * len(args),
-        out_specs=[VMEM] * len(outs),
+        scratch_shapes=scratch,
         compiler_params=pltpu.CompilerParams(vmem_limit_bytes=VMEM_LIMIT),
         cost_estimate=cost(args, outs, flops),
     )(*args)
@@ -56,6 +55,13 @@
 
     def back(self, *offsets):
         return tuple(-sum(o) % n for o, n in zip(zip(*offsets), self.size))
+
+    def along(self, axis):
+        return [tuple(n if d == axis else 0 for d in range(3)) for n in range(self.size[axis])]
+
+    def across(self, axis):
+        spans = [range(1 if d == axis else n) for d, n in enumerate(self.size)]
+        return [(a, b, c) for a in spans[0] for b in spans[1] for c in spans[2]]
 
     def send(self, value, offset):
         if not any(offset):
@@ -116,42 +122,92 @@
     prob_ref[...] = columns
 
 
-def select_kernel(plane, capacity, ranks, sources, targets, meta_ref, *refs):
+def block_masks(plane, capacity, ranks, meta_ref, block, experts):
+    tokens = meta_ref.shape[2]
+    row = lax.broadcasted_iota(jnp.int32, (len(experts), tokens), 0)
+    expert = jnp.zeros(row.shape, f32)
+    for i, offset in enumerate(experts):
+        expert = jnp.where(row == i, other_of(plane, offset).astype(f32), expert)
+    ids = meta_ref[other_of(plane, block)]
+    return slot_masks([(ids[i : i + 1, :] == expert).astype(f32) for i in ranks], capacity)[0]
+
+
+def masks_kernel(plane, capacity, plans, meta_ref, *out_refs):
+    for (ranks, blocks, experts), out_ref in zip(plans, out_refs):
+        for s, block in enumerate(blocks):
+            out_ref[s] = block_masks(plane, capacity, ranks, meta_ref, block, experts).astype(bf16)
+
+
+def select_kernel(plane, capacity, plan, meta_ref, *refs):
+    ranks, sources, targets = plan
     raw_refs, out_refs = refs[: len(sources)], refs[len(sources) :]
-    tokens = raw_refs[0].shape[0]
-    row = lax.broadcasted_iota(jnp.int32, (len(targets), tokens), 0)
-    expert = jnp.zeros(row.shape, f32)
-    for i, target in enumerate(targets):
-        expert = jnp.where(row == i, other_of(plane, target).astype(f32), expert)
     for s, source in enumerate(sources):
-        ids = meta_ref[other_of(plane, source)]
-        hot, _ = slot_masks([(ids[i : i + 1, :] == expert).astype(f32) for i in ranks], capacity)
+        hot = block_masks(plane, capacity, ranks, meta_ref, source, targets)
         picked = dot(hot.astype(bf16), raw_refs[s][...], 1, 0).astype(bf16)
         for i, out_ref in enumerate(out_refs):
             out_ref[s * capacity : (s + 1) * capacity, :] = picked[i * capacity : (i + 1) * capacity]
 
 
-def two_step(plane, capacity, topk, tick, axis, value, meta):
+def pick_kernel(capacity, sources, hot_ref, *refs):
+    raw_refs, out_refs = refs[:sources], refs[sources:]
+    for s, raw_ref in enumerate(raw_refs):
+        picked = dot(hot_ref[s], raw_ref[...], 1, 0).astype(bf16)
+        for i, out_ref in enumerate(out_refs):
+            out_ref[s * capacity : (s + 1) * capacity, :] = picked[i * capacity : (i + 1) * capacity]
+
+
+def gather_plan(plane, ranks, axis):
+    return ranks, [plane.back(u) for u in plane.along(axis)], plane.across(axis)
+
+
+def return_plan(plane, ranks, axis):
+    return ranks, plane.along(axis), [plane.back(t) for t in plane.across(axis)]
+
+
+def picked_rows(plane, capacity, ranks, axis, value, meta, hot=None):
     tokens, width = value.shape
-    unit = lambda n: tuple(n if d == axis else 0 for d in range(3))
-    hops = range(plane.size[axis])
-    sources = [plane.back(unit(n)) for n in hops]
-    raws = [plane.send(value, unit(n)) for n in hops]
-    cross = 1 - axis
-    targets = [
-        tuple(n if d == cross else core if d == 2 else 0 for d in range(3))
-        for n in range(plane.size[cross])
-        for core in range(plane.size[2])
-    ]
-    ranks = [tick * topk + j for j in range(topk)]
-    outs = [shaped((len(sources) * capacity, width), bf16)] * len(targets)
-    flops = 2 * tokens * width * capacity * len(sources) * len(targets)
-    picked = call(
-        functools.partial(select_kernel, plane, capacity, ranks, sources, targets), outs, meta, *raws, flops=flops
-    )
+    plan = gather_plan(plane, ranks, axis)
+    raws = [plane.send(value, u) for u in plane.along(axis)]
+    outs = [shaped((len(plan[1]) * capacity, width), bf16)] * len(plan[2])
+    flops = 2 * tokens * width * capacity * len(plan[1]) * len(plan[2])
+    if hot is None:
+        return call(functools.partial(select_kernel, plane, capacity, plan), outs, meta, *raws, flops=flops)
+    return call(functools.partial(pick_kernel, capacity, len(raws)), outs, hot, *raws, flops=flops)
+
+
+def sent_rows(plane, axis, picked):
+    targets = plane.across(axis)
     pieces = [plane.send(p, t) for p, t in zip(picked, targets)]
-    layout = [[plane.back(t, unit(n)) for n in hops] for t in targets]
-    return pieces, layout
+    return pieces, [[plane.back(t, u) for u in plane.along(axis)] for t in targets]
+
+
+def combine_parts_kernel(capacity, blocks, hot_ref, *refs):
+    pieces, out_refs = refs[:-blocks], refs[-blocks:]
+    for s, out_ref in enumerate(out_refs):
+        rows = jnp.concatenate([p[s * capacity : (s + 1) * capacity, :] for p in pieces], axis=0)
+        out_ref[...] = dot(hot_ref[s], rows, 0, 0).astype(out_ref.dtype)
+
+
+def add_kernel(first, g_ref, own_ref, *refs):
+    out_ref = refs[-1]
+    width = out_ref.shape[1]
+    total = g_ref[:, first : first + width].astype(f32) + own_ref[...]
+    for ref in refs[:-1]:
+        total = total + ref[...].astype(f32)
+    out_ref[...] = total.astype(bf16)
+
+
+def returned_rows(plane, capacity, axis, pieces, hot, g, first):
+    width, tokens = pieces[0].shape[1], g.shape[0]
+    pieces = [plane.send(p, t) for p, t in zip(pieces, plane.across(axis))]
+    along = plane.along(axis)
+    outs = [shaped((tokens, width), bf16 if any(u) else f32) for u in along]
+    own, *parts = call(
+        functools.partial(combine_parts_kernel, capacity, len(along)), outs, hot, *pieces,
+        flops=2 * hot.size * width,
+    )
+    parts = [plane.send(p, u) for p, u in zip(parts, along[1:])]
+    return call(functools.partial(add_kernel, first), [shaped((tokens, width), bf16)], g, own, *parts)[0]
 
 
 def spread_kernel(hot_ref, x_ref, out_ref):
@@ -205,25 +261,34 @@
     slope_ref[...] = slope
 
 
-def first_kernel(plane, capacity, groups, win_ref, wout_ref, hid_ref, slope_ref, prob_ref, *refs):
-    g_ref, gp_ref, score_ref, *back_refs = refs[-3 - HALVES :]
-    arrange(plane, capacity, groups, refs[: -3 - HALVES], g_ref)
+def first_kernel(plane, capacity, groups, plans, win_ref, wout_ref, hid_ref, slope_ref, prob_ref, *refs):
+    refs, back = refs[:-1], refs[-1]
+    pieces = sum(1 if plan is None else len(plan) for plan in plans)
+    refs, back_refs = refs[:-pieces], list(refs[-pieces:])
+    g_ref, gp_ref, score_ref = refs[-3:]
+    arrange(plane, capacity, groups, refs[:-3], g_ref)
     pulled = dot(g_ref[...], wout_ref[...], 1, 1)
     grad_pre = (prob_ref[:, 0:1] * pulled * slope_ref[...]).astype(bf16)
     gp_ref[...] = grad_pre
-    width = back_refs[0].shape[1]
-    for h, back_ref in enumerate(back_refs):
-        back_ref[...] = dot(grad_pre, win_ref[:, h * width : (h + 1) * width], 1, 0).astype(bf16)
+    width = back.shape[1]
+    for h, plan in enumerate(plans):
+        back[...] = dot(grad_pre, win_ref[:, h * width : (h + 1) * width], 1, 0).astype(bf16)
+        if plan is None:
+            back_refs.pop(0)[...] = back[...]
+            continue
+        for blocks in plan:
+            out_ref = back_refs.pop(0)
+            for s, block in enumerate(blocks):
+                at = pl.multiple_of(other_of(plane, block) * capacity, 16)
+                out_ref[s * capacity : (s + 1) * capacity, :] = back[pl.ds(at, capacity), :]
     score = jnp.sum(hid_ref[...].astype(f32) * pulled, axis=1, keepdims=True)
     score_ref[...] = jnp.broadcast_to(score, score_ref.shape)
 
 
-def second_kernel(wout_ref, hid_ref, slope_ref, prob_ref, score0_ref, *refs):
-    g_refs, (gp_ref, score_ref) = refs[:-2], refs[-2:]
-    width = g_refs[0].shape[1]
-    pulled = sum(
-        dot(g_ref[...], wout_ref[:, h * width : (h + 1) * width], 1, 1) for h, g_ref in enumerate(g_refs)
-    )
+def second_kernel(plane, capacity, groups, wout_ref, hid_ref, slope_ref, prob_ref, score0_ref, *refs):
+    g_ref, gp_ref, score_ref = refs[-3:]
+    arrange(plane, capacity, groups, refs[:-3], g_ref)
+    pulled = dot(g_ref[...], wout_ref[...], 1, 1)
     score = jnp.sum(hid_ref[...].astype(f32) * pulled, axis=1, keepdims=True)
     lane = lax.broadcasted_iota(jnp.int32, score_ref.shape, 1)
     both = jnp.where(lane == 0, score0_ref[...], jnp.where(lane == 1, score, 0.0))
@@ -231,45 +296,35 @@
     gp_ref[...] = (prob_ref[:, 1:2] * pulled * slope_ref[...]).astype(bf16)
 
 
-def grads_kernel(prob_ref, x0_ref, x1_ref, g0_ref, *refs):
-    g1_refs = refs[:HALVES]
-    hid0_ref, hid1_ref, gp0_ref, gp1_ref, gin_ref, gout_ref, hid, gp = refs[HALVES:]
-    i = pl.program_id(0)
+def grads_kernel(prob_ref, x0_ref, x1_ref, g0_ref, g1_ref, hid0_ref, hid1_ref, gp0_ref, gp1_ref, gin_ref, gout_ref, hid, gp):
     rows = hid0_ref.shape[0]
-    width = gin_ref.shape[1]
-
-    @pl.when(i == 0)
+
+    @pl.when(pl.program_id(0) == 0)
     def _():
         hid[:rows, :] = hid0_ref[...]
         hid[rows:, :] = hid1_ref[...]
         gp[:rows, :] = gp0_ref[...]
         gp[rows:, :] = gp1_ref[...]
 
-    lanes = pl.ds(pl.multiple_of(i * width, width), width)
-    x = jnp.concatenate([x0_ref[:, lanes], x1_ref[:, lanes]], axis=0)
+    x = jnp.concatenate([x0_ref[...], x1_ref[...]], axis=0)
     gin_ref[...] = dot(gp[...], x, 0, 0).astype(bf16)
-
-    per = g1_refs[0].shape[1] // width
-    for h, g1_ref in enumerate(g1_refs):
-
-        @pl.when((i >= h * per) & (i < (h + 1) * per))
-        def _():
-            y0 = prob_ref[:, 0:1] * g0_ref[:, lanes].astype(f32)
-            part = pl.ds(pl.multiple_of((i - h * per) * width, width), width)
-            y1 = prob_ref[:, 1:2] * g1_ref[:, part].astype(f32)
-            y = jnp.concatenate([y0.astype(bf16), y1.astype(bf16)], axis=0)
-            gout_ref[...] = dot(hid[...], y, 0, 0).astype(bf16)
-
-
-def grads(width, *args):
-    features = args[1].shape[1]
-    rows, units = args[-1].shape
+    y0 = (prob_ref[:, 0:1] * g0_ref[...].astype(f32)).astype(bf16)
+    y1 = (prob_ref[:, 1:2] * g1_ref[...].astype(f32)).astype(bf16)
+    gout_ref[...] = dot(hid[...], jnp.concatenate([y0, y1], axis=0), 0, 0).astype(bf16)
+
+
+def grads(width, prob, x0, x1, g0, g1, hid0, hid1, gp0, gp1):
+    args = (prob, x0, x1, g0, g1, hid0, hid1, gp0, gp1)
+    rows, units = hid0.shape
+    features = x0.shape[1]
     outs = [shaped((units, features), bf16)] * 2
+    tile = pl.BlockSpec((rows, width), lambda i: (0, i))
+    whole = lambda a: pl.BlockSpec(a.shape, lambda i: (0, 0))
     return pl.pallas_call(
         grads_kernel,
         grid=(features // width,),
         out_shape=outs,
-        in_specs=[VMEM] * len(args),
+        in_specs=[whole(prob)] + [tile] * 4 + [whole(hid0)] * 4,
         out_specs=[pl.BlockSpec((units, width), lambda i: (0, i))] * 2,
         scratch_shapes=[pltpu.VMEM((2 * rows, units), bf16)] * 2,
         compiler_params=pltpu.CompilerParams(vmem_limit_bytes=VMEM_LIMIT),
@@ -316,46 +371,72 @@
         meta,
     )
 
-    if capacity % 16 == 0:
-        step = functools.partial(two_step, plane, capacity, topk)
-        x0, x0_layout = step(0, 1, x0, meta)
-        g0_in, g0_layout = step(0, 0, g0, meta)
-        left, left_layout = step(1, 1, x1[:, :half], meta)
-        right, right_layout = step(1, 0, x1[:, half:], meta)
-        x1, x1_groups = left + right, [(0, left_layout), (half, right_layout)]
+    acts = [shaped((rows, features), bf16), shaped((rows, units), bf16), shaped((rows, units), f32)]
+    stepped = capacity % 16 == 0
+    ranks = [list(range(k * topk, (k + 1) * topk)) for k in range(ticks)]
+    pick = functools.partial(picked_rows, plane, capacity)
+    if stepped:
+        x0, x0_layout = sent_rows(plane, 1, pick(ranks[0], 1, x0, meta))
+        g0_in, g0_layout = sent_rows(plane, 0, pick(ranks[0], 0, g0, meta))
+        left = pick(ranks[1], 1, x1[:, :half], meta)
+        right = pick(ranks[1], 0, x1[:, half:], meta)
+        g0_in, _ = lax.optimization_barrier((g0_in, (left, right)))
+        plans = [return_plan(plane, ranks[0], axis) for axis in AXES]
+        plans += [gather_plan(plane, ranks[1], axis) for axis in AXES]
+        shapes = [shaped((len(b), len(e) * capacity, tokens), bf16) for _, b, e in plans]
+        masks = call(functools.partial(masks_kernel, plane, capacity, plans), shapes, meta)
+        back_plans = [[[plane.back(plane.back(t, u)) for u in plane.along(axis)] for t in plane.across(axis)] for axis in AXES]
+        shapes = [shaped((len(blocks) * capacity, half), bf16) for plan in back_plans for blocks in plan]
     else:
         x0, x0_layout = [exchange(spread(hot0, x0), experts)], None
         g0_in, g0_layout = [exchange(spread(hot0, g0), experts)], None
-        x1, x1_groups = [exchange(spread(hot1, x1), experts)], [(0, None)]
-
-    acts = [shaped((rows, features), bf16), shaped((rows, units), bf16), shaped((rows, units), f32)]
+        back_plans = [None] * HALVES
+        shapes = [shaped((rows, half), bf16)] * HALVES
+
     x0, hid0, slope0 = call(
         functools.partial(preact_kernel, plane, capacity, [(0, x0_layout)]), acts, w_in, *x0, flops=matmul
     )
     g0_in, gp0, score0, *backs = call(
-        functools.partial(first_kernel, plane, capacity, [(0, g0_layout)]),
-        [shaped((rows, features), bf16), shaped((rows, units), bf16), shaped((rows, LANES), f32)]
-        + [shaped((rows, half), bf16)] * HALVES,
+        functools.partial(first_kernel, plane, capacity, [(0, g0_layout)], back_plans),
+        [shaped((rows, features), bf16), shaped((rows, units), bf16), shaped((rows, LANES), f32)] + shapes,
         w_in, w_out, hid0, slope0, prob, *g0_in, flops=2 * matmul,
-    )
+        scratch=[pltpu.VMEM((rows, half), bf16)],
+    )
+    if stepped:
+        left, left_layout = sent_rows(plane, 1, left)
+        right, right_layout = sent_rows(plane, 0, right)
+        x1, x1_groups = left + right, [(0, left_layout), (half, right_layout)]
+    else:
+        x1, x1_groups = [exchange(spread(hot1, x1), experts)], [(0, None)]
     x1, hid1, slope1 = call(
         functools.partial(preact_kernel, plane, capacity, x1_groups), acts, w_in, *x1, flops=matmul
     )
-    g1 = []
-    for h, back in enumerate(backs):
-        back = exchange(back, experts)
-        (leaving,) = call(
-            functools.partial(combine_kernel, h * half), [shaped((tokens, half), bf16)], hot0, back, g0,
-            flops=2 * rows * tokens * half,
-        )
+
+    g1, g1_groups = [], []
+    for h, axis in enumerate(AXES):
+        if stepped:
+            count = len(plane.across(axis))
+            pieces, backs = backs[:count], backs[count:]
+            leaving = returned_rows(plane, capacity, axis, pieces, masks[h], g0, h * half)
+        else:
+            (leaving,) = call(
+                functools.partial(combine_kernel, h * half), [shaped((tokens, half), bf16)],
+                hot0, exchange(backs[h], experts), g0, flops=2 * rows * tokens * half,
+            )
         arrived = lax.ppermute(leaving, "segment", [(i, i - 1) for i in range(1, segments)])
-        g1.append(exchange(spread(hot1, arrived), experts))
-    gp1, scores = call(
-        second_kernel, [shaped((rows, units), bf16), shaped((rows, LANES), bf16)],
+        if stepped:
+            pieces, layout = sent_rows(plane, axis, pick(ranks[1], axis, arrived, meta, masks[HALVES + h]))
+        else:
+            pieces, layout = [exchange(spread(hot1, arrived), experts)], None
+        g1 += pieces
+        g1_groups.append((h * half, layout))
+    g1, gp1, scores = call(
+        functools.partial(second_kernel, plane, capacity, g1_groups),
+        [shaped((rows, features), bf16), shaped((rows, units), bf16), shaped((rows, LANES), bf16)],
         w_out, hid1, slope1, prob, score0, *g1, flops=matmul,
     )
     scores = exchange(scores, experts)
-    grad_in, grad_out = grads(half // 2, prob, x0, x1, g0_in, *g1, hid0, hid1, gp0, gp1)
+    grad_in, grad_out = grads(half // 2, prob, x0, x1, g0_in, g1, hid0, hid1, gp0, gp1)
     (prob_grads,) = call(
         functools.partial(collect_kernel, experts, capacity, topk),
         [shaped((ticks * topk, tokens), bf16)], meta, hot0, hot1, scores,

time: 173 us -> 143 us (0.83)
  blocking collectives: 27.8 us -> 0 us
  local copies, waits for them, and re-layouts: 30.7 us -> 8.73 us
  waiting for transfers between devices: 48.6 us -> 69.3 us
  Pallas kernels: 29 us -> 23.5 us
  starting transfers between devices: 34.6 us -> 38.9 us
    all_to_all x2 -> x0, blocking collectives: 27.8 us -> none  [the longest x1 15.6 us: exchange(): lax.all_to_all(pieces, 'expert', split_axis=0, concat_axis=0, tiled=True)]
    unnamed x78 -> x22, local copies, waits for them, and re-layouts: 27.6 us -> 6.8 us
    ppermute x16 -> x32, waiting for transfers between devices: 33 us -> 52.2 us  [send(): return lax.ppermute(value, 'expert', route)]
    ppermute x16 -> x32, starting transfers between devices: 15.8 us -> 29.4 us  [send(): return lax.ppermute(value, 'expert', route)]
    all_to_all x4 -> x1, starting transfers between devices: 16.2 us -> 3.37 us  [exchange(): lax.all_to_all(pieces, 'expert', split_axis=0, concat_axis=0, tiled=True)]
    all_to_all x0 -> x1, waiting for transfers between devices: none -> 3.88 us  [body(): lax.all_to_all(meta, 'expert', split_axis=0, concat_axis=0, tiled=True)]
    all_to_all x0 -> x1, starting transfers between devices: none -> 3.34 us  [body(): lax.all_to_all(meta, 'expert', split_axis=0, concat_axis=0, tiled=True)]
    pallas_call x14 -> x17, Pallas kernels: 19.9 us -> 16.6 us  [call(): pl.pallas_call(kernel, out_shape=outs, scratch_shapes=scratch, compiler_p...]
  transfers between devices with their start and end apart: 22 -> 36, of which waited for: 9 -> 19; matrix products, arithmetic and copies ran while one was open for 1% -> 2% of each run, Pallas kernels for 13% -> 11%
where the time goes in v3:
time: 143 us
  waiting for transfers between devices  69.3 us (48%)
  starting transfers between devices  38.9 us (27%)
  Pallas kernels  23.5 us (16%)
  local copies, waits for them, and re-layouts  8.73 us (6%)
    ppermute x32, waiting for transfers between devices, send(): return lax.ppermute(value, 'expert', route)  52.2 us
    ppermute x32, starting transfers between devices, send(): return lax.ppermute(value, 'expert', route)  29.4 us
    pallas_call x17, Pallas kernels, call(): pl.pallas_call(kernel, out_shape=outs, scratch_shapes=scratch, compiler_p...  16.6 us
    ppermute x2, waiting for transfers between devices, body(): lax.ppermute(leaving, 'segment', [(i, i - 1) for i in range(1, segments)])  13.2 us
    pallas_call x1, Pallas kernels, grads(): pl.pallas_call(grads_kernel, grid=(features // width,), out_shape=outs, i...  6.87 us
    unnamed x22, local copies, waits for them, and re-layouts  6.8 us
    all_to_all x1, waiting for transfers between devices, body(): lax.all_to_all(meta, 'expert', split_axis=0, concat_axis=0, tiled=True)  3.88 us
    all_to_all x1, starting transfers between devices, exchange(): lax.all_to_all(pieces, 'expert', split_axis=0, concat_axis=0, tiled=True)  3.37 us
  transfers between devices with their start and end apart: 36, of which 19 were waited for; matrix products, arithmetic and copies ran while one was open for 2% of the time, Pallas kernels for 11%

profile of v3, /device:TPU:0, one launch (start us, length us, event | category | flops | bytes accessed | tf_op | source)
XLA Modules:
  0.0 142.7 jit_solution(6465518312010542884)
XLA Ops:
  0.6 3.0 %collective-permute-start.12 = (bf16[128,2048]{1,0:T(8,128)(2,1)}, bf16[128,2048]{1,0:T(8,128)(2,1)S(1)}, u32[]{:S(2)}, u32[]{:S(2)}) collective-permute-start(bf16[128,2048]{1,0:T(8,128)(2,1)} %bitcast.32), channel_id=1, source_target_pairs={{0,4},{1,5},{2,6},{3,7},{4,0},{5,1},{6,2},{7,3},{8,12},{9,13},{10,... | collective-permute-start | bytes 1572872 | tf_op jit(solution)/shard_map/ppermute | solution.py:70
  5.7 3.3 %all-to-all-start = ((f32[8,8,128]{2,1,0:T(8,128)}), f32[8,8,128]{2,1,0:T(8,128)S(1)}, u32[]{:S(2)}, u32[]{:S(2)}) async-start(f32[8,8,128]{2,1,0:T(8,128)} %broadcast_in_dim.15), calls=%async_computation | async-start | bytes 65536 | tf_op jit(solution)/shard_map/all_to_all | solution.py:367
  9.0 1.3 slice_bitcast_fusion
  10.3 2.0 %collective-permute-start = (bf16[128,2048]{1,0:T(8,128)(2,1)S(1)}, bf16[128,2048]{1,0:T(8,128)(2,1)S(1)}, u32[]{:S(2)}, u32[]{:S(2)}) collective-permute-start(bf16[128,2048]{1,0:T(8,128)(2,1)S(1)} %get-tuple-element.126.refs_0_), channel_id=1, source_target_pairs={{0,2},{1,3},{2,0},{3,1},{4,6},{5,7},{6,4},{7,5},{8,10},{9,11},{10,... | collective-permute-start | bytes 1572872 | tf_op jit(solution)/shard_map/ppermute | solution.py:70
  12.3 3.9 %all-to-all-done.meta_ref = f32[8,8,128]{2,1,0:T(8,128)S(1)} async-done(((f32[8,8,128]{2,1,0:T(8,128)}), f32[8,8,128]{2,1,0:T(8,128)S(1)}, u32[]{:S(2)}, u32[]{:S(2)}) %all-to-all-start) | async-done | bytes 32800 | tf_op jit(solution)/shard_map/all_to_all | solution.py:367
  16.2 1.0 shard_map.91
  17.4 1.8 %collective-permute-start.8 = (bf16[128,1024]{1,0:T(8,128)(2,1)S(1)}, bf16[128,1024]{1,0:T(8,128)(2,1)S(1)}, u32[]{:S(2)}, u32[]{:S(2)}) collective-permute-start(bf16[128,1024]{1,0:T(8,128)(2,1)S(1)} %get-tuple-element.127.refs_0_), channel_id=1, source_target_pairs={{0,4},{1,5},{2,6},{3,7},{4,0},{5,1},{6,2},{7,3},{8,12},{9,13},{10,... | collective-permute-start | bytes 786440 | tf_op jit(solution)/shard_map/ppermute | solution.py:70
  19.2 1.5 %collective-permute-start.4 = (bf16[128,1024]{1,0:T(8,128)(2,1)S(1)}, bf16[128,1024]{1,0:T(8,128)(2,1)S(1)}, u32[]{:S(2)}, u32[]{:S(2)}) collective-permute-start(bf16[128,1024]{1,0:T(8,128)(2,1)S(1)} %get-tuple-element.128.refs_0_), channel_id=1, source_target_pairs={{0,2},{1,3},{2,0},{3,1},{4,6},{5,7},{6,4},{7,5},{8,10},{9,11},{10,... | collective-permute-start | bytes 786440 | tf_op jit(solution)/shard_map/ppermute | solution.py:70
  21.2 3.9 %collective-permute-done.refs_1_ = bf16[128,2048]{1,0:T(8,128)(2,1)S(1)} collective-permute-done((bf16[128,2048]{1,0:T(8,128)(2,1)S(1)}, bf16[128,2048]{1,0:T(8,128)(2,1)S(1)}, u32[]{:S(2)}, u32[]{:S(2)}) %collective-permute-start) | collective-permute-done | bytes 524320 | tf_op jit(solution)/shard_map/ppermute | solution.py:70
  25.2 1.0 shard_map.86
  26.2 2.0 %collective-permute-start.1 = (bf16[96,2048]{1,0:T(8,128)(2,1)S(1)}, bf16[96,2048]{1,0:T(8,128)(2,1)S(1)}, u32[]{:S(2)}, u32[]{:S(2)}) collective-permute-start(bf16[96,2048]{1,0:T(8,128)(2,1)S(1)} %get-tuple-element.66), channel_id=1, source_target_pairs={{0,1},{1,0},{2,3},{3,2},{4,5},{5,4},{6,7},{7,6},{8,9},{9,8},{10,11... | collective-permute-start | bytes 1179656 | tf_op jit(solution)/shard_map/ppermute | solution.py:70
  28.3 2.4 %collective-permute-done.4.refs_1_ = bf16[128,1024]{1,0:T(8,128)(2,1)S(1)} collective-permute-done((bf16[128,1024]{1,0:T(8,128)(2,1)S(1)}, bf16[128,1024]{1,0:T(8,128)(2,1)S(1)}, u32[]{:S(2)}, u32[]{:S(2)}) %collective-permute-start.4) | collective-permute-done | bytes 262176 | tf_op jit(solution)/shard_map/ppermute | solution.py:70
  30.7 2.0 %collective-permute-start.2 = (bf16[96,2048]{1,0:T(8,128)(2,1)S(1)}, bf16[96,2048]{1,0:T(8,128)(2,1)S(1)}, u32[]{:S(2)}, u32[]{:S(2)}) collective-permute-start(bf16[96,2048]{1,0:T(8,128)(2,1)S(1)} %get-tuple-element.67), channel_id=1, source_target_pairs={{0,4},{1,5},{2,6},{3,7},{4,0},{5,1},{6,2},{7,3},{8,12},{9,13},{10,... | collective-permute-start | bytes 1179656 | tf_op jit(solution)/shard_map/ppermute | solution.py:70
  35.0 4.1 %collective-permute-done.14.refs_2_ = bf16[96,2048]{1,0:T(8,128)(2,1)S(1)} collective-permute-done((bf16[96,2048]{1,0:T(8,128)(2,1)S(1)}, bf16[96,2048]{1,0:T(8,128)(2,1)S(1)}, u32[]{:S(2)}, u32[]{:S(2)}) %collective-permute-start.14) | collective-permute-done | bytes 393248 | tf_op jit(solution)/shard_map/ppermute | solution.py:70
  39.1 7.5 %collective-permute-done.15.refs_3_ = bf16[96,2048]{1,0:T(8,128)(2,1)S(1)} collective-permute-done((bf16[96,2048]{1,0:T(8,128)(2,1)S(1)}, bf16[96,2048]{1,0:T(8,128)(2,1)S(1)}, u32[]{:S(2)}, u32[]{:S(2)}) %collective-permute-start.15) | collective-permute-done | bytes 393248 | tf_op jit(solution)/shard_map/ppermute | solution.py:70
  46.6 1.6 %collective-permute-done.3.refs_3_ = bf16[96,2048]{1,0:T(8,128)(2,1)S(1)} collective-permute-done((bf16[96,2048]{1,0:T(8,128)(2,1)S(1)}, bf16[96,2048]{1,0:T(8,128)(2,1)S(1)}, u32[]{:S(2)}, u32[]{:S(2)}) %collective-permute-start.3) | collective-permute-done | bytes 393248 | tf_op jit(solution)/shard_map/ppermute | solution.py:70
  48.2 1.8 %shard_map.87 = (bf16[384,2048]{1,0:T(8,128)(2,1)S(1)}, bf16[384,704]{1,0:T(8,128)(2,1)S(1)}, f32[384,704]{1,0:T(8,128)S(1)}) custom-call(bf16[704,2048]{1,0:T(8,128)(2,1)S(1)} %bitcast.27, bf16[96,2048]{1,0:T(8,128)(2,1)S(1)} %get-tuple-element.65.refs_0_, bf16[96,2048]{1,0:T(8,128)(2,1)S(1)} %collective-permute-done.1.refs_1_, ...), custom_call_target="tpu_custom_call" | custom-call | flops 1107296256 | bytes 7651328 | tf_op jit(solution)/shard_map/pallas_call | solution.py:34
  50.0 3.3 %shard_map.92 = (bf16[384,2048]{1,0:T(8,128)(2,1)S(1)}, bf16[384,704]{1,0:T(8,128)(2,1)S(1)}, f32[384,128]{1,0:T(8,128)S(1)}, bf16[96,1024]{1,0:T(8,128)(2,1)S(1...) custom-call(bf16[704,2048]{1,0:T(8,128)(2,1)S(1)} %bitcast.28, ...), custom_call_target="tpu_custom_call" | custom-call | flops 2214592512 | bytes 13041664 | tf_op jit(solution)/shard_map/pallas_call | solution.py:34
  53.3 1.5 %collective-permute-start.25 = (bf16[96,1024]{1,0:T(8,128)(2,1)S(1)}, bf16[96,1024]{1,0:T(8,128)(2,1)S(1)}, u32[]{:S(2)}, u32[]{:S(2)}) collective-permute-start(bf16[96,1024]{1,0:T(8,128)(2,1)S(1)} %get-tuple-element.108), channel_id=1, source_target_pairs={{0,2},{1,3},{2,0},{3,1},{4,6},{5,7},{6,4},{7,5},{8,10},{9,11},{10,... | collective-permute-start | bytes 589832 | tf_op jit(solution)/shard_map/ppermute | solution.py:70
  55.4 1.5 %collective-permute-start.27 = (bf16[96,1024]{1,0:T(8,128)(2,1)S(1)}, bf16[96,1024]{1,0:T(8,128)(2,1)S(1)}, u32[]{:S(2)}, u32[]{:S(2)}) collective-permute-start(bf16[96,1024]{1,0:T(8,128)(2,1)S(1)} %get-tuple-element.110), channel_id=1, source_target_pairs={{0,6},{1,7},{2,4},{3,5},{4,2},{5,3},{6,0},{7,1},{8,14},{9,15},{10,... | collective-permute-start | bytes 589832 | tf_op jit(solution)/shard_map/ppermute | solution.py:70
  56.8 1.5 %collective-permute-start.16 = (bf16[96,1024]{1,0:T(8,128)(2,1)S(1)}, bf16[96,1024]{1,0:T(8,128)(2,1)S(1)}, u32[]{:S(2)}, u32[]{:S(2)}) collective-permute-start(bf16[96,1024]{1,0:T(8,128)(2,1)S(1)} %get-tuple-element.96), channel_id=1, source_target_pairs={{0,2},{1,3},{2,0},{3,1},{4,6},{5,7},{6,4},{7,5},{8,10},{9,11},{10,... | collective-permute-start | bytes 589832 | tf_op jit(solution)/shard_map/ppermute | solution.py:70
  58.8 2.3 %collective-permute-done.25.refs_1_ = bf16[96,1024]{1,0:T(8,128)(2,1)S(1)} collective-permute-done((bf16[96,1024]{1,0:T(8,128)(2,1)S(1)}, bf16[96,1024]{1,0:T(8,128)(2,1)S(1)}, u32[]{:S(2)}, u32[]{:S(2)}) %collective-permute-start.25) | collective-permute-done | bytes 196640 | tf_op jit(solution)/shard_map/ppermute | solution.py:70
  62.7 4.0 %collective-permute-done.26.refs_2_ = bf16[96,1024]{1,0:T(8,128)(2,1)S(1)} collective-permute-done((bf16[96,1024]{1,0:T(8,128)(2,1)S(1)}, bf16[96,1024]{1,0:T(8,128)(2,1)S(1)}, u32[]{:S(2)}, u32[]{:S(2)}) %collective-permute-start.26) | collective-permute-done | bytes 196640 | tf_op jit(solution)/shard_map/ppermute | solution.py:70
  67.1 2.5 %collective-permute-done.16.refs_1_ = bf16[96,1024]{1,0:T(8,128)(2,1)S(1)} collective-permute-done((bf16[96,1024]{1,0:T(8,128)(2,1)S(1)}, bf16[96,1024]{1,0:T(8,128)(2,1)S(1)}, u32[]{:S(2)}, u32[]{:S(2)}) %collective-permute-start.16) | collective-permute-done | bytes 196640 | tf_op jit(solution)/shard_map/ppermute | solution.py:70
  69.6 5.2 %collective-permute-done.17.refs_2_ = bf16[96,1024]{1,0:T(8,128)(2,1)S(1)} collective-permute-done((bf16[96,1024]{1,0:T(8,128)(2,1)S(1)}, bf16[96,1024]{1,0:T(8,128)(2,1)S(1)}, u32[]{:S(2)}, u32[]{:S(2)}) %collective-permute-start.17) | collective-permute-done | bytes 196640 | tf_op jit(solution)/shard_map/ppermute | solution.py:70
  75.3 1.3 collective-permute-start.29
  76.8 1.5 %collective-permute-start.20 = (bf16[128,1024]{1,0:T(8,128)(2,1)S(1)}, bf16[128,1024]{1,0:T(8,128)(2,1)S(1)}, u32[]{:S(2)}, u32[]{:S(2)}) collective-permute-start(bf16[128,1024]{1,0:T(8,128)(2,1)S(1)} %shard_map.95), channel_id=1, source_target_pairs={{8,0},{16,8},{24,16},{9,1},{17,9},{25,17},{10,2},{18,10},{26,18},{... | collective-permute-start | bytes 786440 | tf_op jit(solution)/shard_map/ppermute | solution.py:426
  78.3 8.0 %collective-permute-done.29.refs_0_ = bf16[128,1024]{1,0:T(8,128)(2,1)S(1)} collective-permute-done((bf16[128,1024]{1,0:T(8,128)(2,1)S(1)}, bf16[128,1024]{1,0:T(8,128)(2,1)S(1)}, u32[]{:S(2)}, u32[]{:S(2)}) %collective-permute-start.29) | collective-permute-done | bytes 262176 | tf_op jit(solution)/shard_map/ppermute | solution.py:426
  86.3 5.2 %collective-permute-done.20.refs_0_ = bf16[128,1024]{1,0:T(8,128)(2,1)S(1)} collective-permute-done((bf16[128,1024]{1,0:T(8,128)(2,1)S(1)}, bf16[128,1024]{1,0:T(8,128)(2,1)S(1)}, u32[]{:S(2)}, u32[]{:S(2)}) %collective-permute-start.20) | collective-permute-done | bytes 262176 | tf_op jit(solution)/shard_map/ppermute | solution.py:426
  95.1 4.7 %collective-permute-done.10.refs_6_ = bf16[96,1024]{1,0:T(8,128)(2,1)S(1)} collective-permute-done((bf16[96,1024]{1,0:T(8,128)(2,1)S(1)}, bf16[96,1024]{1,0:T(8,128)(2,1)S(1)}, u32[]{:S(2)}, u32[]{:S(2)}) %collective-permute-start.10) | collective-permute-done | bytes 196640 | tf_op jit(solution)/shard_map/ppermute | solution.py:70
  100.9 1.2 collective-permute-done.11.refs_7_
  102.7 1.6 %collective-permute-start.33 = (bf16[96,1024]{1,0:T(8,128)(2,1)S(1)}, bf16[96,1024]{1,0:T(8,128)(2,1)S(1)}, u32[]{:S(2)}, u32[]{:S(2)}) collective-permute-start(bf16[96,1024]{1,0:T(8,128)(2,1)S(1)} %get-tuple-element.116), channel_id=1, source_target_pairs={{0,6},{1,7},{2,4},{3,5},{4,2},{5,3},{6,0},{7,1},{8,14},{9,15},{10,... | collective-permute-start | bytes 589832 | tf_op jit(solution)/shard_map/ppermute | solution.py:70
  104.3 1.3 collective-permute-start.22
  105.6 0.9 collective-permute-done.7.refs_3_
  106.5 1.0 collective-permute-start.23
  107.6 1.5 %collective-permute-start.24 = (bf16[96,1024]{1,0:T(8,128)(2,1)S(1)}, bf16[96,1024]{1,0:T(8,128)(2,1)S(1)}, u32[]{:S(2)}, u32[]{:S(2)}) collective-permute-start(bf16[96,1024]{1,0:T(8,128)(2,1)S(1)} %get-tuple-element.104), channel_id=1, source_target_pairs={{0,6},{1,7},{2,4},{3,5},{4,2},{5,3},{6,0},{7,1},{8,14},{9,15},{10,... | collective-permute-start | bytes 589832 | tf_op jit(solution)/shard_map/ppermute | solution.py:70
  109.1 1.8 %shard_map.90 = (bf16[384,2048]{1,0:T(8,128)(2,1)S(1)}, bf16[384,704]{1,0:T(8,128)(2,1)S(1)}, f32[384,704]{1,0:T(8,128)S(1)}) custom-call(bf16[704,2048]{1,0:T(8,128)(2,1)S(1)} %bitcast.29, bf16[96,1024]{1,0:T(8,128)(2,1)S(1)} %get-tuple-element.70.refs_0_, bf16[96,1024]{1,0:T(8,128)(2,1)S(1)} %collective-permute-done.5.refs_1_, ...), custom_call_target="tpu_custom_call" | custom-call | flops 1107296256 | bytes 7651328 | tf_op jit(solution)/shard_map/pallas_call | solution.py:34
  110.9 3.3 %collective-permute-done.32.refs_6_ = bf16[96,1024]{1,0:T(8,128)(2,1)S(1)} collective-permute-done((bf16[96,1024]{1,0:T(8,128)(2,1)S(1)}, bf16[96,1024]{1,0:T(8,128)(2,1)S(1)}, u32[]{:S(2)}, u32[]{:S(2)}) %collective-permute-start.32) | collective-permute-done | bytes 196640 | tf_op jit(solution)/shard_map/ppermute | solution.py:70
  114.2 1.9 %collective-permute-done.22.refs_1_ = bf16[96,1024]{1,0:T(8,128)(2,1)S(1)} collective-permute-done((bf16[96,1024]{1,0:T(8,128)(2,1)S(1)}, bf16[96,1024]{1,0:T(8,128)(2,1)S(1)}, u32[]{:S(2)}, u32[]{:S(2)}) %collective-permute-start.22) | collective-permute-done | bytes 196640 | tf_op jit(solution)/shard_map/ppermute | solution.py:70
  116.1 6.5 %collective-permute-done.23.refs_2_ = bf16[96,1024]{1,0:T(8,128)(2,1)S(1)} collective-permute-done((bf16[96,1024]{1,0:T(8,128)(2,1)S(1)}, bf16[96,1024]{1,0:T(8,128)(2,1)S(1)}, u32[]{:S(2)}, u32[]{:S(2)}) %collective-permute-start.23) | collective-permute-done | bytes 196640 | tf_op jit(solution)/shard_map/ppermute | solution.py:70
  122.6 2.2 %shard_map.100 = (bf16[384,2048]{1,0:T(8,128)(2,1)S(1)}, bf16[384,704]{1,0:T(8,128)(2,1)S(1)}, bf16[384,128]{1,0:T(8,128)(2,1)}) custom-call(bf16[704,2048]{1,0:T(8,128)(2,1)S(1)} %bitcast.31, bf16[384,704]{1,0:T(8,128)(2,1)S(1)} %get-tuple-element.90.hid_ref.hid1_ref, f32[384,704]{1,0:T(8,128)S(1)} %get-tuple-element.91.slope_ref, ...), custom_call_target="tpu_custom_call" | custom-call | flops 1107296256 | bytes 8683520 | tf_op jit(solution)/shard_map/pallas_call | solution.py:34
  124.8 1.1 copy-done.9
  126.0 3.4 %all-to-all-start.1 = ((bf16[8,48,128]{2,1,0:T(8,128)(2,1)}), bf16[8,48,128]{2,1,0:T(8,128)(2,1)S(1)}, u32[]{:S(2)}, u32[]{:S(2)}) async-start(bf16[8,48,128]{2,1,0:T(8,128)(2,1)} %bitcast.13), calls=%async_computation.1 | async-start | bytes 196608 | tf_op jit(solution)/shard_map/all_to_all | solution.py:225
  129.4 1.4 copy-done.4
  130.8 1.4 copy-done.6
  132.2 1.4 copy-done.8
  133.6 1.4 copy-done.10
  135.0 6.9 %shard_map.101 = (bf16[704,2048]{1,0:T(8,128)(2,1)}, bf16[704,2048]{1,0:T(8,128)(2,1)}) custom-call(f32[384,128]{1,0:T(8,128)S(1)} %get-tuple-element.64.prob_ref, bf16[384,2048]{1,0:T(8,128)(2,1)S(1)} %copy-done.4, bf16[384,2048]{1,0:T(8,128)(2,1)S(1)} %copy-done.8, bf16[384,2048]{1,0:T(8,128)(2,1)S(1)} %copy-done.6, bf16[384,2048]{1,0:T(8,128)(2,1)S(1)} %copy-done.10, ...), custom_call_target="tpu_custom_call" | custom-call | flops 4429185024 | bytes 14417920 | tf_op jit(solution)/shard_map/pallas_call | solution.py:323
  (70 shorter events, 14.9 us)
Async XLA Ops:
  0.6 15.5 %copy-start.2 = (bf16[1,128,2048]{2,1,0:T(8,128)(2,1)S(1)}, bf16[1,128,2048]{2,1,0:T(8,128)(2,1)}, u32[]{:S(2)}) copy-start(bf16[1,128,2048]{2,1,0:T(8,128)(2,1)} %param.7) | copy-start | bytes 1572868
  0.6 15.5 %collective-permute-start.12 = (bf16[128,2048]{1,0:T(8,128)(2,1)}, bf16[128,2048]{1,0:T(8,128)(2,1)S(1)}, u32[]{:S(2)}, u32[]{:S(2)}) collective-permute-start(bf16[128,2048]{1,0:T(8,128)(2,1)} %bitcast.32), channel_id=1, source_target_pairs={{0,4},{1,5},{2,6},{3,7},{4,0},{5,1},{6,2},{7,3},{8,12},{9,13},{10,... | collective-permute-start | bytes 1572872 | tf_op jit(solution)/shard_map/ppermute | solution.py:70
  5.7 10.5 %all-to-all-start = ((f32[8,8,128]{2,1,0:T(8,128)}), f32[8,8,128]{2,1,0:T(8,128)S(1)}, u32[]{:S(2)}, u32[]{:S(2)}) async-start(f32[8,8,128]{2,1,0:T(8,128)} %broadcast_in_dim.15), calls=%async_computation | async-start | bytes 65536 | tf_op jit(solution)/shard_map/all_to_all | solution.py:367
  10.3 14.8 %collective-permute-start = (bf16[128,2048]{1,0:T(8,128)(2,1)S(1)}, bf16[128,2048]{1,0:T(8,128)(2,1)S(1)}, u32[]{:S(2)}, u32[]{:S(2)}) collective-permute-start(bf16[128,2048]{1,0:T(8,128)(2,1)S(1)} %get-tuple-element.126.refs_0_), channel_id=1, source_target_pairs={{0,2},{1,3},{2,0},{3,1},{4,6},{5,7},{6,4},{7,5},{8,10},{9,11},{10,... | collective-permute-start | bytes 1572872 | tf_op jit(solution)/shard_map/ppermute | solution.py:70
  17.2 15.5 %collective-permute-start.13 = (bf16[96,2048]{1,0:T(8,128)(2,1)S(1)}, bf16[96,2048]{1,0:T(8,128)(2,1)S(1)}, u32[]{:S(2)}, u32[]{:S(2)}) collective-permute-start(bf16[96,2048]{1,0:T(8,128)(2,1)S(1)} %get-tuple-element.82), channel_id=1, source_target_pairs={{0,1},{1,0},{2,3},{3,2},{4,5},{5,4},{6,7},{7,6},{8,9},{9,8},{10,11... | collective-permute-start | bytes 1179656 | tf_op jit(solution)/shard_map/ppermute | solution.py:70
  17.3 30.8 %copy-start = (bf16[1,1,704,2048]{3,2,1,0:T(8,128)(2,1)S(1)}, bf16[1,1,704,2048]{3,2,1,0:T(8,128)(2,1)}, u32[]{:S(2)}) copy-start(bf16[1,1,704,2048]{3,2,1,0:T(8,128)(2,1)} %param.8) | copy-start | bytes 8650756
  17.4 8.8 %collective-permute-start.8 = (bf16[128,1024]{1,0:T(8,128)(2,1)S(1)}, bf16[128,1024]{1,0:T(8,128)(2,1)S(1)}, u32[]{:S(2)}, u32[]{:S(2)}) collective-permute-start(bf16[128,1024]{1,0:T(8,128)(2,1)S(1)} %get-tuple-element.127.refs_0_), channel_id=1, source_target_pairs={{0,4},{1,5},{2,6},{3,7},{4,0},{5,1},{6,2},{7,3},{8,12},{9,13},{10,... | collective-permute-start | bytes 786440 | tf_op jit(solution)/shard_map/ppermute | solution.py:70
  19.2 11.5 %collective-permute-start.4 = (bf16[128,1024]{1,0:T(8,128)(2,1)S(1)}, bf16[128,1024]{1,0:T(8,128)(2,1)S(1)}, u32[]{:S(2)}, u32[]{:S(2)}) collective-permute-start(bf16[128,1024]{1,0:T(8,128)(2,1)S(1)} %get-tuple-element.128.refs_0_), channel_id=1, source_target_pairs={{0,2},{1,3},{2,0},{3,1},{4,6},{5,7},{6,4},{7,5},{8,10},{9,11},{10,... | collective-permute-start | bytes 786440 | tf_op jit(solution)/shard_map/ppermute | solution.py:70
  20.7 18.4 %collective-permute-start.14 = (bf16[96,2048]{1,0:T(8,128)(2,1)S(1)}, bf16[96,2048]{1,0:T(8,128)(2,1)S(1)}, u32[]{:S(2)}, u32[]{:S(2)}) collective-permute-start(bf16[96,2048]{1,0:T(8,128)(2,1)S(1)} %get-tuple-element.83), channel_id=1, source_target_pairs={{0,2},{1,3},{2,0},{3,1},{4,6},{5,7},{6,4},{7,5},{8,10},{9,11},{10,... | collective-permute-start | bytes 1179656 | tf_op jit(solution)/shard_map/ppermute | solution.py:70
  25.1 21.5 %collective-permute-start.15 = (bf16[96,2048]{1,0:T(8,128)(2,1)S(1)}, bf16[96,2048]{1,0:T(8,128)(2,1)S(1)}, u32[]{:S(2)}, u32[]{:S(2)}) collective-permute-start(bf16[96,2048]{1,0:T(8,128)(2,1)S(1)} %get-tuple-element.84), channel_id=1, source_target_pairs={{0,3},{1,2},{2,1},{3,0},{4,7},{5,6},{6,5},{7,4},{8,11},{9,10},{10,... | collective-permute-start | bytes 1179656 | tf_op jit(solution)/shard_map/ppermute | solution.py:70
  26.2 20.4 %collective-permute-start.1 = (bf16[96,2048]{1,0:T(8,128)(2,1)S(1)}, bf16[96,2048]{1,0:T(8,128)(2,1)S(1)}, u32[]{:S(2)}, u32[]{:S(2)}) collective-permute-start(bf16[96,2048]{1,0:T(8,128)(2,1)S(1)} %get-tuple-element.66), channel_id=1, source_target_pairs={{0,1},{1,0},{2,3},{3,2},{4,5},{5,4},{6,7},{7,6},{8,9},{9,8},{10,11... | collective-permute-start | bytes 1179656 | tf_op jit(solution)/shard_map/ppermute | solution.py:70
  30.7 15.9 %collective-permute-start.2 = (bf16[96,2048]{1,0:T(8,128)(2,1)S(1)}, bf16[96,2048]{1,0:T(8,128)(2,1)S(1)}, u32[]{:S(2)}, u32[]{:S(2)}) collective-permute-start(bf16[96,2048]{1,0:T(8,128)(2,1)S(1)} %get-tuple-element.67), channel_id=1, source_target_pairs={{0,4},{1,5},{2,6},{3,7},{4,0},{5,1},{6,2},{7,3},{8,12},{9,13},{10,... | collective-permute-start | bytes 1179656 | tf_op jit(solution)/shard_map/ppermute | solution.py:70
  32.7 15.5 %collective-permute-start.3 = (bf16[96,2048]{1,0:T(8,128)(2,1)S(1)}, bf16[96,2048]{1,0:T(8,128)(2,1)S(1)}, u32[]{:S(2)}, u32[]{:S(2)}) collective-permute-start(bf16[96,2048]{1,0:T(8,128)(2,1)S(1)} %get-tuple-element.68), channel_id=1, source_target_pairs={{0,5},{1,4},{2,7},{3,6},{4,1},{5,0},{6,3},{7,2},{8,13},{9,12},{10,... | collective-permute-start | bytes 1179656 | tf_op jit(solution)/shard_map/ppermute | solution.py:70
  48.2 1.8 %copy-start.1 = (bf16[1,1,704,2048]{3,2,1,0:T(8,128)(2,1)S(1)}, bf16[1,1,704,2048]{3,2,1,0:T(8,128)(2,1)}, u32[]{:S(2)}) copy-start(bf16[1,1,704,2048]{3,2,1,0:T(8,128)(2,1)} %param.9) | copy-start | bytes 8650756
  50.0 3.3 %copy-start.3 = (bf16[384,2048]{1,0:T(8,128)(2,1)}, bf16[384,2048]{1,0:T(8,128)(2,1)S(1)}, u32[]{:S(2)}) copy-start(bf16[384,2048]{1,0:T(8,128)(2,1)S(1)} %get-tuple-element.69.x0_ref) | copy-start | bytes 4718596
  53.3 22.1 %copy-start.5 = (bf16[384,2048]{1,0:T(8,128)(2,1)}, bf16[384,2048]{1,0:T(8,128)(2,1)S(1)}, u32[]{:S(2)}) copy-start(bf16[384,2048]{1,0:T(8,128)(2,1)S(1)} %get-tuple-element.89.g0_ref) | copy-start | bytes 4718596
  53.3 7.8 %collective-permute-start.25 = (bf16[96,1024]{1,0:T(8,128)(2,1)S(1)}, bf16[96,1024]{1,0:T(8,128)(2,1)S(1)}, u32[]{:S(2)}, u32[]{:S(2)}) collective-permute-start(bf16[96,1024]{1,0:T(8,128)(2,1)S(1)} %get-tuple-element.108), channel_id=1, source_target_pairs={{0,2},{1,3},{2,0},{3,1},{4,6},{5,7},{6,4},{7,5},{8,10},{9,11},{10,... | collective-permute-start | bytes 589832 | tf_op jit(solution)/shard_map/ppermute | solution.py:70
  54.8 11.9 %collective-permute-start.26 = (bf16[96,1024]{1,0:T(8,128)(2,1)S(1)}, bf16[96,1024]{1,0:T(8,128)(2,1)S(1)}, u32[]{:S(2)}, u32[]{:S(2)}) collective-permute-start(bf16[96,1024]{1,0:T(8,128)(2,1)S(1)} %get-tuple-element.109), channel_id=1, source_target_pairs={{0,4},{1,5},{2,6},{3,7},{4,0},{5,1},{6,2},{7,3},{8,12},{9,13},{10,... | collective-permute-start | bytes 589832 | tf_op jit(solution)/shard_map/ppermute | solution.py:70
  55.4 11.4 %collective-permute-start.27 = (bf16[96,1024]{1,0:T(8,128)(2,1)S(1)}, bf16[96,1024]{1,0:T(8,128)(2,1)S(1)}, u32[]{:S(2)}, u32[]{:S(2)}) collective-permute-start(bf16[96,1024]{1,0:T(8,128)(2,1)S(1)} %get-tuple-element.110), channel_id=1, source_target_pairs={{0,6},{1,7},{2,4},{3,5},{4,2},{5,3},{6,0},{7,1},{8,14},{9,15},{10,... | collective-permute-start | bytes 589832 | tf_op jit(solution)/shard_map/ppermute | solution.py:70
  56.8 12.8 %collective-permute-start.16 = (bf16[96,1024]{1,0:T(8,128)(2,1)S(1)}, bf16[96,1024]{1,0:T(8,128)(2,1)S(1)}, u32[]{:S(2)}, u32[]{:S(2)}) collective-permute-start(bf16[96,1024]{1,0:T(8,128)(2,1)S(1)} %get-tuple-element.96), channel_id=1, source_target_pairs={{0,2},{1,3},{2,0},{3,1},{4,6},{5,7},{6,4},{7,5},{8,10},{9,11},{10,... | collective-permute-start | bytes 589832 | tf_op jit(solution)/shard_map/ppermute | solution.py:70
  58.3 16.5 %collective-permute-start.17 = (bf16[96,1024]{1,0:T(8,128)(2,1)S(1)}, bf16[96,1024]{1,0:T(8,128)(2,1)S(1)}, u32[]{:S(2)}, u32[]{:S(2)}) collective-permute-start(bf16[96,1024]{1,0:T(8,128)(2,1)S(1)} %get-tuple-element.97), channel_id=1, source_target_pairs={{0,4},{1,5},{2,6},{3,7},{4,0},{5,1},{6,2},{7,3},{8,12},{9,13},{10,... | collective-permute-start | bytes 589832 | tf_op jit(solution)/shard_map/ppermute | solution.py:70
  61.1 13.7 %collective-permute-start.18 = (bf16[96,1024]{1,0:T(8,128)(2,1)S(1)}, bf16[96,1024]{1,0:T(8,128)(2,1)S(1)}, u32[]{:S(2)}, u32[]{:S(2)}) collective-permute-start(bf16[96,1024]{1,0:T(8,128)(2,1)S(1)} %get-tuple-element.98), channel_id=1, source_target_pairs={{0,6},{1,7},{2,4},{3,5},{4,2},{5,3},{6,0},{7,1},{8,14},{9,15},{10,... | collective-permute-start | bytes 589832 | tf_op jit(solution)/shard_map/ppermute | solution.py:70
  67.0 8.2 %collective-permute-start.28 = (bf16[128,1024]{1,0:T(8,128)(2,1)S(1)}, bf16[128,1024]{1,0:T(8,128)(2,1)S(1)}, u32[]{:S(2)}, u32[]{:S(2)}) collective-permute-start(bf16[128,1024]{1,0:T(8,128)(2,1)S(1)} %get-tuple-element.112), channel_id=1, source_target_pairs={{0,1},{1,0},{2,3},{3,2},{4,5},{5,4},{6,7},{7,6},{8,9},{9,8},{10,11... | collective-permute-start | bytes 786440 | tf_op jit(solution)/shard_map/ppermute | solution.py:70
  75.1 1.6 %collective-permute-start.19 = (bf16[128,1024]{1,0:T(8,128)(2,1)S(1)}, bf16[128,1024]{1,0:T(8,128)(2,1)S(1)}, u32[]{:S(2)}, u32[]{:S(2)}) collective-permute-start(bf16[128,1024]{1,0:T(8,128)(2,1)S(1)} %get-tuple-element.100), channel_id=1, source_target_pairs={{0,1},{1,0},{2,3},{3,2},{4,5},{5,4},{6,7},{7,6},{8,9},{9,8},{10,11... | collective-permute-start | bytes 786440 | tf_op jit(solution)/shard_map/ppermute | solution.py:70
  75.3 11.0 %collective-permute-start.29 = (bf16[128,1024]{1,0:T(8,128)(2,1)S(1)}, bf16[128,1024]{1,0:T(8,128)(2,1)S(1)}, u32[]{:S(2)}, u32[]{:S(2)}) collective-permute-start(bf16[128,1024]{1,0:T(8,128)(2,1)S(1)} %shard_map.98), channel_id=1, source_target_pairs={{8,0},{16,8},{24,16},{9,1},{17,9},{25,17},{10,2},{18,10},{26,18},{... | collective-permute-start | bytes 786440 | tf_op jit(solution)/shard_map/ppermute | solution.py:426
  76.8 14.7 %collective-permute-start.20 = (bf16[128,1024]{1,0:T(8,128)(2,1)S(1)}, bf16[128,1024]{1,0:T(8,128)(2,1)S(1)}, u32[]{:S(2)}, u32[]{:S(2)}) collective-permute-start(bf16[128,1024]{1,0:T(8,128)(2,1)S(1)} %shard_map.95), channel_id=1, source_target_pairs={{8,0},{16,8},{24,16},{9,1},{17,9},{25,17},{10,2},{18,10},{26,18},{... | collective-permute-start | bytes 786440 | tf_op jit(solution)/shard_map/ppermute | solution.py:426
  86.3 7.9 %collective-permute-start.30 = (bf16[128,1024]{1,0:T(8,128)(2,1)S(1)}, bf16[128,1024]{1,0:T(8,128)(2,1)S(1)}, u32[]{:S(2)}, u32[]{:S(2)}) collective-permute-start(bf16[128,1024]{1,0:T(8,128)(2,1)S(1)} %collective-permute-done.29.refs_0_), channel_id=1, source_target_pairs={{0,1},{1,0},{2,3},{3,2},{4,5},{5,4},{6,7},{7,6},{8,9},{9,8},{10,11... | collective-permute-start | bytes 786440 | tf_op jit(solution)/shard_map/ppermute | solution.py:70
  91.5 8.3 %collective-permute-start.21 = (bf16[128,1024]{1,0:T(8,128)(2,1)S(1)}, bf16[128,1024]{1,0:T(8,128)(2,1)S(1)}, u32[]{:S(2)}, u32[]{:S(2)}) collective-permute-start(bf16[128,1024]{1,0:T(8,128)(2,1)S(1)} %collective-permute-done.20.refs_0_), channel_id=1, source_target_pairs={{0,1},{1,0},{2,3},{3,2},{4,5},{5,4},{6,7},{7,6},{8,9},{9,8},{10,11... | collective-permute-start | bytes 786440 | tf_op jit(solution)/shard_map/ppermute | solution.py:70
  91.5 1.9 %collective-permute-start.9 = (bf16[96,1024]{1,0:T(8,128)(2,1)S(1)}, bf16[96,1024]{1,0:T(8,128)(2,1)S(1)}, u32[]{:S(2)}, u32[]{:S(2)}) collective-permute-start(bf16[96,1024]{1,0:T(8,128)(2,1)S(1)} %get-tuple-element.75), channel_id=1, source_target_pairs={{0,1},{1,0},{2,3},{3,2},{4,5},{5,4},{6,7},{7,6},{8,9},{9,8},{10,11... | collective-permute-start | bytes 589832 | tf_op jit(solution)/shard_map/ppermute | solution.py:70
  92.0 7.8 %collective-permute-start.10 = (bf16[96,1024]{1,0:T(8,128)(2,1)S(1)}, bf16[96,1024]{1,0:T(8,128)(2,1)S(1)}, u32[]{:S(2)}, u32[]{:S(2)}) collective-permute-start(bf16[96,1024]{1,0:T(8,128)(2,1)S(1)} %get-tuple-element.76), channel_id=1, source_target_pairs={{0,2},{1,3},{2,0},{3,1},{4,6},{5,7},{6,4},{7,5},{8,10},{9,11},{10,... | collective-permute-start | bytes 589832 | tf_op jit(solution)/shard_map/ppermute | solution.py:70
  92.7 9.4 %collective-permute-start.11 = (bf16[96,1024]{1,0:T(8,128)(2,1)S(1)}, bf16[96,1024]{1,0:T(8,128)(2,1)S(1)}, u32[]{:S(2)}, u32[]{:S(2)}) collective-permute-start(bf16[96,1024]{1,0:T(8,128)(2,1)S(1)} %get-tuple-element.77), channel_id=1, source_target_pairs={{0,3},{1,2},{2,1},{3,0},{4,7},{5,6},{6,5},{7,4},{8,11},{9,10},{10,... | collective-permute-start | bytes 589832 | tf_op jit(solution)/shard_map/ppermute | solution.py:70
  93.4 9.3 %collective-permute-start.5 = (bf16[96,1024]{1,0:T(8,128)(2,1)S(1)}, bf16[96,1024]{1,0:T(8,128)(2,1)S(1)}, u32[]{:S(2)}, u32[]{:S(2)}) collective-permute-start(bf16[96,1024]{1,0:T(8,128)(2,1)S(1)} %get-tuple-element.71), channel_id=1, source_target_pairs={{0,1},{1,0},{2,3},{3,2},{4,5},{5,4},{6,7},{7,6},{8,9},{9,8},{10,11... | collective-permute-start | bytes 589832 | tf_op jit(solution)/shard_map/ppermute | solution.py:70
  94.2 10.1 %collective-permute-start.6 = (bf16[96,1024]{1,0:T(8,128)(2,1)S(1)}, bf16[96,1024]{1,0:T(8,128)(2,1)S(1)}, u32[]{:S(2)}, u32[]{:S(2)}) collective-permute-start(bf16[96,1024]{1,0:T(8,128)(2,1)S(1)} %get-tuple-element.72), channel_id=1, source_target_pairs={{0,4},{1,5},{2,6},{3,7},{4,0},{5,1},{6,2},{7,3},{8,12},{9,13},{10,... | collective-permute-start | bytes 589832 | tf_op jit(solution)/shard_map/ppermute | solution.py:70
  99.8 6.7 %collective-permute-start.7 = (bf16[96,1024]{1,0:T(8,128)(2,1)S(1)}, bf16[96,1024]{1,0:T(8,128)(2,1)S(1)}, u32[]{:S(2)}, u32[]{:S(2)}) collective-permute-start(bf16[96,1024]{1,0:T(8,128)(2,1)S(1)} %get-tuple-element.73), channel_id=1, source_target_pairs={{0,5},{1,4},{2,7},{3,6},{4,1},{5,0},{6,3},{7,2},{8,13},{9,12},{10,... | collective-permute-start | bytes 589832 | tf_op jit(solution)/shard_map/ppermute | solution.py:70
  99.8 7.8 %collective-permute-start.31 = (bf16[96,1024]{1,0:T(8,128)(2,1)S(1)}, bf16[96,1024]{1,0:T(8,128)(2,1)S(1)}, u32[]{:S(2)}, u32[]{:S(2)}) collective-permute-start(bf16[96,1024]{1,0:T(8,128)(2,1)S(1)} %get-tuple-element.114), channel_id=1, source_target_pairs={{0,2},{1,3},{2,0},{3,1},{4,6},{5,7},{6,4},{7,5},{8,10},{9,11},{10,... | collective-permute-start | bytes 589832 | tf_op jit(solution)/shard_map/ppermute | solution.py:70
  102.1 12.1 %collective-permute-start.32 = (bf16[96,1024]{1,0:T(8,128)(2,1)S(1)}, bf16[96,1024]{1,0:T(8,128)(2,1)S(1)}, u32[]{:S(2)}, u32[]{:S(2)}) collective-permute-start(bf16[96,1024]{1,0:T(8,128)(2,1)S(1)} %get-tuple-element.115), channel_id=1, source_target_pairs={{0,4},{1,5},{2,6},{3,7},{4,0},{5,1},{6,2},{7,3},{8,12},{9,13},{10,... | collective-permute-start | bytes 589832 | tf_op jit(solution)/shard_map/ppermute | solution.py:70
  102.7 11.5 %collective-permute-start.33 = (bf16[96,1024]{1,0:T(8,128)(2,1)S(1)}, bf16[96,1024]{1,0:T(8,128)(2,1)S(1)}, u32[]{:S(2)}, u32[]{:S(2)}) collective-permute-start(bf16[96,1024]{1,0:T(8,128)(2,1)S(1)} %get-tuple-element.116), channel_id=1, source_target_pairs={{0,6},{1,7},{2,4},{3,5},{4,2},{5,3},{6,0},{7,1},{8,14},{9,15},{10,... | collective-permute-start | bytes 589832 | tf_op jit(solution)/shard_map/ppermute | solution.py:70
  104.3 11.8 %collective-permute-start.22 = (bf16[96,1024]{1,0:T(8,128)(2,1)S(1)}, bf16[96,1024]{1,0:T(8,128)(2,1)S(1)}, u32[]{:S(2)}, u32[]{:S(2)}) collective-permute-start(bf16[96,1024]{1,0:T(8,128)(2,1)S(1)} %get-tuple-element.102), channel_id=1, source_target_pairs={{0,2},{1,3},{2,0},{3,1},{4,6},{5,7},{6,4},{7,5},{8,10},{9,11},{10,... | collective-permute-start | bytes 589832 | tf_op jit(solution)/shard_map/ppermute | solution.py:70
  106.5 16.1 %collective-permute-start.23 = (bf16[96,1024]{1,0:T(8,128)(2,1)S(1)}, bf16[96,1024]{1,0:T(8,128)(2,1)S(1)}, u32[]{:S(2)}, u32[]{:S(2)}) collective-permute-start(bf16[96,1024]{1,0:T(8,128)(2,1)S(1)} %get-tuple-element.103), channel_id=1, source_target_pairs={{0,4},{1,5},{2,6},{3,7},{4,0},{5,1},{6,2},{7,3},{8,12},{9,13},{10,... | collective-permute-start | bytes 589832 | tf_op jit(solution)/shard_map/ppermute | solution.py:70
  107.6 15.0 %collective-permute-start.24 = (bf16[96,1024]{1,0:T(8,128)(2,1)S(1)}, bf16[96,1024]{1,0:T(8,128)(2,1)S(1)}, u32[]{:S(2)}, u32[]{:S(2)}) collective-permute-start(bf16[96,1024]{1,0:T(8,128)(2,1)S(1)} %get-tuple-element.104), channel_id=1, source_target_pairs={{0,6},{1,7},{2,4},{3,5},{4,2},{5,3},{6,0},{7,1},{8,14},{9,15},{10,... | collective-permute-start | bytes 589832 | tf_op jit(solution)/shard_map/ppermute | solution.py:70
  110.9 14.0 %copy-start.7 = (bf16[384,2048]{1,0:T(8,128)(2,1)}, bf16[384,2048]{1,0:T(8,128)(2,1)S(1)}, u32[]{:S(2)}) copy-start(bf16[384,2048]{1,0:T(8,128)(2,1)S(1)} %get-tuple-element.78.x1_ref) | copy-start | bytes 4718596
  124.8 1.1 copy-start.9
  126.0 15.9 %all-to-all-start.1 = ((bf16[8,48,128]{2,1,0:T(8,128)(2,1)}), bf16[8,48,128]{2,1,0:T(8,128)(2,1)S(1)}, u32[]{:S(2)}, u32[]{:S(2)}) async-start(bf16[8,48,128]{2,1,0:T(8,128)(2,1)} %bitcast.13), calls=%async_computation.1 | async-start | bytes 196608 | tf_op jit(solution)/shard_map/all_to_all | solution.py:225
  129.3 1.4 copy-start.4
  130.8 1.4 copy-start.6
  132.2 1.4 copy-start.8
  133.6 1.4 copy-start.10

commit v4 on v3

--- a/solution.py
+++ b/solution.py
@@ -197,17 +197,22 @@
     out_ref[...] = total.astype(bf16)
 
 
-def returned_rows(plane, capacity, axis, pieces, hot, g, first):
+def returned_rows(plane, capacity, axis, pieces, hot, g, first, after):
     width, tokens = pieces[0].shape[1], g.shape[0]
     pieces = [plane.send(p, t) for p, t in zip(pieces, plane.across(axis))]
+    pieces = behind(pieces, after)
     along = plane.along(axis)
     outs = [shaped((tokens, width), bf16 if any(u) else f32) for u in along]
     own, *parts = call(
         functools.partial(combine_parts_kernel, capacity, len(along)), outs, hot, *pieces,
         flops=2 * hot.size * width,
     )
-    parts = [plane.send(p, u) for p, u in zip(parts, along[1:])]
-    return call(functools.partial(add_kernel, first), [shaped((tokens, width), bf16)], g, own, *parts)[0]
+    sent = [plane.send(p, u) for p, u in zip(parts, along[1:])]
+    return call(functools.partial(add_kernel, first), [shaped((tokens, width), bf16)], g, own, *sent)[0], parts
+
+
+def behind(values, after):
+    return lax.optimization_barrier((values, after))[0] if after else values
 
 
 def spread_kernel(hot_ref, x_ref, out_ref):
@@ -285,10 +290,42 @@
     score_ref[...] = jnp.broadcast_to(score, score_ref.shape)
 
 
-def second_kernel(plane, capacity, groups, wout_ref, hid_ref, slope_ref, prob_ref, score0_ref, *refs):
+def weighted(prob_ref, k, g):
+    return (prob_ref[:, k : k + 1] * g.astype(f32)).astype(bf16)
+
+
+def early_kernel(plane, capacity, groups, wout_ref, hid0_ref, hid1_ref, prob_ref, g0_ref, *refs):
+    g_ref, pulled_ref, gout_ref = refs[-3:]
+    arrange(plane, capacity, groups, refs[:-3], g_ref)
+    pulled_ref[...] = dot(g_ref[...], wout_ref[...], 1, 1)
+    y = jnp.concatenate([weighted(prob_ref, 0, g0_ref[...]), weighted(prob_ref, 1, g_ref[...])], axis=0)
+    hid = jnp.concatenate([hid0_ref[...], hid1_ref[...]], axis=0)
+    gout_ref[...] = dot(hid, y, 0, 0).astype(bf16)
+
+
+def early(plane, capacity, groups, w_out, hid0, hid1, prob, g0, *pieces):
+    rows, units = hid0.shape
+    features = w_out.shape[1]
+    width = features // HALVES
+    args = (w_out, hid0, hid1, prob, g0, *pieces)
+    outs = [shaped((rows, width), bf16), shaped((rows, units), f32), shaped((units, features), bf16)]
+    whole = lambda a: pl.BlockSpec(a.shape, lambda i: (0, 0))
+    first = lambda a: pl.BlockSpec((a.shape[0], width), lambda i: (0, 0))
+    return pl.pallas_call(
+        functools.partial(early_kernel, plane, capacity, groups),
+        grid=(1,),
+        out_shape=outs,
+        in_specs=[first(w_out), whole(hid0), whole(hid1), whole(prob), first(g0)] + [whole(p) for p in pieces],
+        out_specs=[whole(outs[0]), whole(outs[1]), first(outs[2])],
+        compiler_params=pltpu.CompilerParams(vmem_limit_bytes=VMEM_LIMIT),
+        cost_estimate=cost(args, outs, 3 * units * rows * features),
+    )(*args)
+
+
+def second_kernel(plane, capacity, groups, first, wout_ref, hid_ref, slope_ref, prob_ref, score0_ref, pulled_ref, *refs):
     g_ref, gp_ref, score_ref = refs[-3:]
     arrange(plane, capacity, groups, refs[:-3], g_ref)
-    pulled = dot(g_ref[...], wout_ref[...], 1, 1)
+    pulled = pulled_ref[...] + dot(g_ref[...], wout_ref[:, first:], 1, 1)
     score = jnp.sum(hid_ref[...].astype(f32) * pulled, axis=1, keepdims=True)
     lane = lax.broadcasted_iota(jnp.int32, score_ref.shape, 1)
     both = jnp.where(lane == 0, score0_ref[...], jnp.where(lane == 1, score, 0.0))
@@ -296,7 +333,8 @@
     gp_ref[...] = (prob_ref[:, 1:2] * pulled * slope_ref[...]).astype(bf16)
 
 
-def grads_kernel(prob_ref, x0_ref, x1_ref, g0_ref, g1_ref, hid0_ref, hid1_ref, gp0_ref, gp1_ref, gin_ref, gout_ref, hid, gp):
+def late_kernel(done_ref, prob_ref, x0_ref, x1_ref, g0_ref, g1_ref, hid0_ref, hid1_ref, gp0_ref, gp1_ref, *refs):
+    gin_ref, gout_ref, hid, gp = refs
     rows = hid0_ref.shape[0]
 
     @pl.when(pl.program_id(0) == 0)
@@ -306,29 +344,32 @@
         gp[:rows, :] = gp0_ref[...]
         gp[rows:, :] = gp1_ref[...]
 
-    x = jnp.concatenate([x0_ref[...], x1_ref[...]], axis=0)
-    gin_ref[...] = dot(gp[...], x, 0, 0).astype(bf16)
-    y0 = (prob_ref[:, 0:1] * g0_ref[...].astype(f32)).astype(bf16)
-    y1 = (prob_ref[:, 1:2] * g1_ref[...].astype(f32)).astype(bf16)
-    gout_ref[...] = dot(hid[...], jnp.concatenate([y0, y1], axis=0), 0, 0).astype(bf16)
-
-
-def grads(width, prob, x0, x1, g0, g1, hid0, hid1, gp0, gp1):
-    args = (prob, x0, x1, g0, g1, hid0, hid1, gp0, gp1)
+    gin_ref[...] = dot(gp[...], jnp.concatenate([x0_ref[...], x1_ref[...]], axis=0), 0, 0).astype(bf16)
+    y = jnp.concatenate([weighted(prob_ref, 0, g0_ref[...]), weighted(prob_ref, 1, g1_ref[...])], axis=0)
+    gout_ref[...] = dot(hid[...], y, 0, 0).astype(bf16)
+
+
+def late(steps, done, prob, x0, x1, g0, g1, hid0, hid1, gp0, gp1):
+    args = (done, prob, x0, x1, g0, g1, hid0, hid1, gp0, gp1)
     rows, units = hid0.shape
-    features = x0.shape[1]
+    features, part = x0.shape[1], g1.shape[1]
     outs = [shaped((units, features), bf16)] * 2
-    tile = pl.BlockSpec((rows, width), lambda i: (0, i))
+    skip = (features - part) // (part // steps)
+    tile = lambda n, width, at: pl.BlockSpec((n, width // steps), lambda i: (0, at + i))
     whole = lambda a: pl.BlockSpec(a.shape, lambda i: (0, 0))
     return pl.pallas_call(
-        grads_kernel,
-        grid=(features // width,),
+        late_kernel,
+        grid=(steps,),
         out_shape=outs,
-        in_specs=[whole(prob)] + [tile] * 4 + [whole(hid0)] * 4,
-        out_specs=[pl.BlockSpec((units, width), lambda i: (0, i))] * 2,
+        in_specs=[pl.BlockSpec(memory_space=pl.ANY), whole(prob)]
+        + [tile(rows, features, 0)] * 2
+        + [tile(rows, part, skip), tile(rows, part, 0)]
+        + [whole(hid0)] * 4,
+        out_specs=[tile(units, features, 0), tile(units, part, skip)],
         scratch_shapes=[pltpu.VMEM((2 * rows, units), bf16)] * 2,
+        input_output_aliases={0: 1},
         compiler_params=pltpu.CompilerParams(vmem_limit_bytes=VMEM_LIMIT),
-        cost_estimate=cost(args, outs, 8 * units * rows * features),
+        cost_estimate=cost(args, outs, 6 * units * rows * features),
     )(*args)
 
 
@@ -358,8 +399,10 @@
     matmul = 2 * rows * units * features
     half = features // HALVES
     w_in, w_out = weight_in[0, 0], weight_out[0, 0]
-    x0, x1, g0 = inputs[0, 0], inputs[0, 1], entering[0]
-
+    g0 = entering[0]
+
+    x0 = inputs[0, 0]
+    expert_ids, gate_probs = behind((expert_ids, gate_probs), [x0])
     ids = jnp.transpose(expert_ids[0], (0, 2, 1)).reshape(ticks * topk, tokens)
     probs = jnp.transpose(gate_probs[0], (0, 2, 1)).reshape(ticks * topk, tokens)
     meta = jnp.concatenate([ids.astype(f32), probs.astype(f32)], axis=0)
@@ -378,9 +421,8 @@
     if stepped:
         x0, x0_layout = sent_rows(plane, 1, pick(ranks[0], 1, x0, meta))
         g0_in, g0_layout = sent_rows(plane, 0, pick(ranks[0], 0, g0, meta))
-        left = pick(ranks[1], 1, x1[:, :half], meta)
-        right = pick(ranks[1], 0, x1[:, half:], meta)
-        g0_in, _ = lax.optimization_barrier((g0_in, (left, right)))
+        x1 = behind(inputs, [x0[1], g0_in[1]])[0, 1]
+        x1 = pick(ranks[1], 2, x1, meta)
         plans = [return_plan(plane, ranks[0], axis) for axis in AXES]
         plans += [gather_plan(plane, ranks[1], axis) for axis in AXES]
         shapes = [shaped((len(b), len(e) * capacity, tokens), bf16) for _, b, e in plans]
@@ -402,41 +444,49 @@
         w_in, w_out, hid0, slope0, prob, *g0_in, flops=2 * matmul,
         scratch=[pltpu.VMEM((rows, half), bf16)],
     )
-    if stepped:
-        left, left_layout = sent_rows(plane, 1, left)
-        right, right_layout = sent_rows(plane, 0, right)
-        x1, x1_groups = left + right, [(0, left_layout), (half, right_layout)]
-    else:
-        x1, x1_groups = [exchange(spread(hot1, x1), experts)], [(0, None)]
-    x1, hid1, slope1 = call(
-        functools.partial(preact_kernel, plane, capacity, x1_groups), acts, w_in, *x1, flops=matmul
-    )
-
-    g1, g1_groups = [], []
+    leaving, after = [], []
     for h, axis in enumerate(AXES):
         if stepped:
             count = len(plane.across(axis))
             pieces, backs = backs[:count], backs[count:]
-            leaving = returned_rows(plane, capacity, axis, pieces, masks[h], g0, h * half)
+            out, parts = returned_rows(plane, capacity, axis, pieces, masks[h], g0, h * half, after)
         else:
-            (leaving,) = call(
+            (out,) = call(
                 functools.partial(combine_kernel, h * half), [shaped((tokens, half), bf16)],
                 hot0, exchange(backs[h], experts), g0, flops=2 * rows * tokens * half,
             )
-        arrived = lax.ppermute(leaving, "segment", [(i, i - 1) for i in range(1, segments)])
+        leaving.append(out)
+        after = [out]
+
+    if stepped:
+        x1, x1_layout = sent_rows(plane, 2, behind(x1, leaving))
+        x1_groups = [(0, x1_layout)]
+    else:
+        x1, x1_groups = [exchange(spread(hot1, inputs[0, 1]), experts)], [(0, None)]
+    parts, after = [], []
+    for h, axis in enumerate(AXES):
+        arrived = lax.ppermute(leaving[h], "segment", [(i, i - 1) for i in range(1, segments)])
+        arrived = behind(arrived, after)
         if stepped:
-            pieces, layout = sent_rows(plane, axis, pick(ranks[1], axis, arrived, meta, masks[HALVES + h]))
+            picked = pick(ranks[1], axis, arrived, meta, masks[HALVES + h])
+            pieces, layout = sent_rows(plane, axis, picked)
+            after = picked
         else:
             pieces, layout = [exchange(spread(hot1, arrived), experts)], None
-        g1 += pieces
-        g1_groups.append((h * half, layout))
+        parts.append((pieces, [(0, layout)]))
+    x1 = behind(x1, after)
+    x1, hid1, slope1 = call(
+        functools.partial(preact_kernel, plane, capacity, x1_groups), acts, w_in, *x1, flops=matmul
+    )
+    part, pulled, gout = early(plane, capacity, parts[0][1], w_out, hid0, hid1, prob, g0_in, *parts[0][0])
+    pieces = behind(parts[1][0], [pulled])
     g1, gp1, scores = call(
-        functools.partial(second_kernel, plane, capacity, g1_groups),
-        [shaped((rows, features), bf16), shaped((rows, units), bf16), shaped((rows, LANES), bf16)],
-        w_out, hid1, slope1, prob, score0, *g1, flops=matmul,
+        functools.partial(second_kernel, plane, capacity, parts[1][1], half),
+        [shaped((rows, half), bf16), shaped((rows, units), bf16), shaped((rows, LANES), bf16)],
+        w_out, hid1, slope1, prob, score0, pulled, *pieces, flops=matmul // 2,
     )
     scores = exchange(scores, experts)
-    grad_in, grad_out = grads(half // 2, prob, x0, x1, g0_in, g1, hid0, hid1, gp0, gp1)
+    grad_in, grad_out = late(4, gout, prob, x0, x1, g0_in, g1, hid0, hid1, gp0, gp1)
     (prob_grads,) = call(
         functools.partial(collect_kernel, experts, capacity, topk),
         [shaped((ticks * topk, tokens), bf16)], meta, hot0, hot1, scores,

time: 143 us -> 132 us (0.923)
  waiting for transfers between devices: 69.3 us -> 49 us
  blocking collectives: 0 us -> 11 us
  starting transfers between devices: 38.9 us -> 33.6 us
  local copies, waits for them, and re-layouts: 8.73 us -> 11.2 us
    ppermute x32 -> x28, waiting for transfers between devices: 52.2 us -> 41.1 us  [send(): return lax.ppermute(value, 'expert', route)]
    all_to_all x0 -> x1, blocking collectives: none -> 11 us  [body(): lax.all_to_all(meta, 'expert', split_axis=0, concat_axis=0, tiled=True)]
    ppermute x2, waiting for transfers between devices: 13.2 us -> 7.89 us  [body(): lax.ppermute(leaving[h], 'segment', [(i, i - 1) for i in range(1, segment...]
    all_to_all x1 -> x0, waiting for transfers between devices: 3.88 us -> none  [body(): lax.all_to_all(meta, 'expert', split_axis=0, concat_axis=0, tiled=True)]
    all_to_all x1 -> x0, starting transfers between devices: 3.34 us -> none  [body(): lax.all_to_all(meta, 'expert', split_axis=0, concat_axis=0, tiled=True)]
    unnamed x22 -> x30, local copies, waits for them, and re-layouts: 6.8 us -> 9.96 us
    pallas_call x1 -> x2, Pallas kernels: 6.87 us -> 9.16 us  [the longest x1 6.11 us: late(): pl.pallas_call(late_kernel, grid=(steps,), out_shape=outs, in_specs=[pl.B...]
    ppermute x32 -> x28, starting transfers between devices: 29.4 us -> 27.4 us  [send(): return lax.ppermute(value, 'expert', route)]
  transfers between devices with their start and end apart: 36 -> 31, of which waited for: 19 -> 18; matrix products, arithmetic and copies ran while one was open for 2% -> 1% of each run, Pallas kernels for 11% -> 14%
where the time goes in v4:
time: 132 us
  waiting for transfers between devices  49 us (37%)
  starting transfers between devices  33.6 us (25%)
  Pallas kernels  24.5 us (19%)
  local copies, waits for them, and re-layouts  11.2 us (8%)
  blocking collectives  11 us (8%)
  other arithmetic  1.37 us (1%)
    ppermute x28, waiting for transfers between devices, send(): return lax.ppermute(value, 'expert', route)  41.1 us
    ppermute x28, starting transfers between devices, send(): return lax.ppermute(value, 'expert', route)  27.4 us
    pallas_call x16, Pallas kernels, call(): pl.pallas_call(kernel, out_shape=outs, scratch_shapes=scratch, compiler_p...  15.4 us
    all_to_all x1, blocking collectives, body(): lax.all_to_all(meta, 'expert', split_axis=0, concat_axis=0, tiled=True)  11 us
    unnamed x30, local copies, waits for them, and re-layouts  9.96 us
    ppermute x2, waiting for transfers between devices, body(): lax.ppermute(leaving[h], 'segment', [(i, i - 1) for i in range(1, segment...  7.89 us
    pallas_call x1, Pallas kernels, late(): pl.pallas_call(late_kernel, grid=(steps,), out_shape=outs, in_specs=[pl.B...  6.11 us
    all_to_all x1, starting transfers between devices, exchange(): lax.all_to_all(pieces, 'expert', split_axis=0, concat_axis=0, tiled=True)  3.36 us
  transfers between devices with their start and end apart: 31, of which 18 were waited for; matrix products, arithmetic and copies ran while one was open for 1% of the time, Pallas kernels for 14%

profile of v4, /device:TPU:0, one launch (start us, length us, event | category | flops | bytes accessed | tf_op | source)
XLA Modules:
  0.0 131.7 jit_solution(12023432412771389296)
XLA Ops:
  0.6 1.2 slice_bitcast_fusion.1.refs_0_
  1.9 3.0 %collective-permute-start = (bf16[128,2048]{1,0:T(8,128)(2,1)S(1)}, bf16[128,2048]{1,0:T(8,128)(2,1)S(1)}, u32[]{:S(2)}, u32[]{:S(2)}) collective-permute-start(bf16[128,2048]{1,0:T(8,128)(2,1)S(1)} %slice_bitcast_fusion.1.refs_0_), channel_id=1, source_target_pairs={{0,2},{1,3},{2,0},{3,1},{4,6},{5,7},{6,4},{7,5},{8,10},{9,11},{10,... | collective-permute-start | bytes 1572872 | tf_op jit(solution)/shard_map/ppermute | solution.py:70
  4.9 1.5 %collective-permute-start.4 = (bf16[128,2048]{1,0:T(8,128)(2,1)}, bf16[128,2048]{1,0:T(8,128)(2,1)S(1)}, u32[]{:S(2)}, u32[]{:S(2)}) collective-permute-start(bf16[128,2048]{1,0:T(8,128)(2,1)} %bitcast.33), channel_id=1, source_target_pairs={{0,4},{1,5},{2,6},{3,7},{4,0},{5,1},{6,2},{7,3},{8,12},{9,13},{10,... | collective-permute-start | bytes 1572872 | tf_op jit(solution)/shard_map/ppermute | solution.py:70
  7.8 11.0 %all_to_all.10.meta_ref = f32[8,8,128]{2,1,0:T(8,128)S(1)} all-to-all(f32[8,8,128]{2,1,0:T(8,128)S(1)} %broadcast_in_dim.15), channel_id=1, replica_groups=mesh['segment'=4,'expert'=8] {'expert'}, dimensions={0} | all-to-all | bytes 65536 | tf_op jit(solution)/shard_map/all_to_all | solution.py:410
  18.8 1.0 shard_map.85
  20.0 1.6 %collective-permute-start.2 = (bf16[96,2048]{1,0:T(8,128)(2,1)S(1)}, bf16[96,2048]{1,0:T(8,128)(2,1)S(1)}, u32[]{:S(2)}, u32[]{:S(2)}) collective-permute-start(bf16[96,2048]{1,0:T(8,128)(2,1)S(1)} %get-tuple-element.82), channel_id=1, source_target_pairs={{0,4},{1,5},{2,6},{3,7},{4,0},{5,1},{6,2},{7,3},{8,12},{9,13},{10,... | collective-permute-start | bytes 1179656 | tf_op jit(solution)/shard_map/ppermute | solution.py:70
  21.8 1.0 copy-done.2
  22.9 1.0 shard_map.87
  26.5 5.5 %collective-permute-done.2.refs_2_ = bf16[96,2048]{1,0:T(8,128)(2,1)S(1)} collective-permute-done((bf16[96,2048]{1,0:T(8,128)(2,1)S(1)}, bf16[96,2048]{1,0:T(8,128)(2,1)S(1)}, u32[]{:S(2)}, u32[]{:S(2)}) %collective-permute-start.2) | collective-permute-done | bytes 393248 | tf_op jit(solution)/shard_map/ppermute | solution.py:70
  31.9 7.5 %collective-permute-done.3.refs_3_ = bf16[96,2048]{1,0:T(8,128)(2,1)S(1)} collective-permute-done((bf16[96,2048]{1,0:T(8,128)(2,1)S(1)}, bf16[96,2048]{1,0:T(8,128)(2,1)S(1)}, u32[]{:S(2)}, u32[]{:S(2)}) %collective-permute-start.3) | collective-permute-done | bytes 393248 | tf_op jit(solution)/shard_map/ppermute | solution.py:70
  39.5 1.8 %shard_map.86 = (bf16[384,2048]{1,0:T(8,128)(2,1)S(1)}, bf16[384,704]{1,0:T(8,128)(2,1)S(1)}, f32[384,704]{1,0:T(8,128)S(1)}) custom-call(bf16[704,2048]{1,0:T(8,128)(2,1)S(1)} %bitcast.27, bf16[96,2048]{1,0:T(8,128)(2,1)S(1)} %get-tuple-element.80.refs_0_, bf16[96,2048]{1,0:T(8,128)(2,1)S(1)} %collective-permute-done.1.refs_1_, ...), custom_call_target="tpu_custom_call" | custom-call | flops 1107296256 | bytes 7651328 | tf_op jit(solution)/shard_map/pallas_call | solution.py:34
  41.3 1.1 copy-done.4
  43.2 3.2 %shard_map.91 = (bf16[384,2048]{1,0:T(8,128)(2,1)S(1)}, bf16[384,704]{1,0:T(8,128)(2,1)S(1)}, f32[384,128]{1,0:T(8,128)S(1)}, bf16[96,1024]{1,0:T(8,128)(2,1)S(1...) custom-call(bf16[704,2048]{1,0:T(8,128)(2,1)S(1)} %bitcast.28, ...), custom_call_target="tpu_custom_call" | custom-call | flops 2214592512 | bytes 13041664 | tf_op jit(solution)/shard_map/pallas_call | solution.py:34
  46.4 1.1 collective-permute-start.9
  47.5 1.1 collective-permute-start.10
  48.6 1.4 %collective-permute-start.11 = (bf16[96,1024]{1,0:T(8,128)(2,1)S(1)}, bf16[96,1024]{1,0:T(8,128)(2,1)S(1)}, u32[]{:S(2)}, u32[]{:S(2)}) collective-permute-start(bf16[96,1024]{1,0:T(8,128)(2,1)S(1)} %get-tuple-element.100), channel_id=1, source_target_pairs={{0,6},{1,7},{2,4},{3,5},{4,2},{5,3},{6,0},{7,1},{8,14},{9,15},{10,... | collective-permute-start | bytes 589832 | tf_op jit(solution)/shard_map/ppermute | solution.py:70
  50.9 1.1 collective-permute-start.13
  51.9 1.1 collective-permute-start.14
  53.0 1.2 collective-permute-done.9.refs_1_
  54.2 1.5 %collective-permute-start.15 = (bf16[96,1024]{1,0:T(8,128)(2,1)S(1)}, bf16[96,1024]{1,0:T(8,128)(2,1)S(1)}, u32[]{:S(2)}, u32[]{:S(2)}) collective-permute-start(bf16[96,1024]{1,0:T(8,128)(2,1)S(1)} %get-tuple-element.107), channel_id=1, source_target_pairs={{0,6},{1,7},{2,4},{3,5},{4,2},{5,3},{6,0},{7,1},{8,14},{9,15},{10,... | collective-permute-start | bytes 589832 | tf_op jit(solution)/shard_map/ppermute | solution.py:70
  55.7 3.7 %collective-permute-done.10.refs_2_ = bf16[96,1024]{1,0:T(8,128)(2,1)S(1)} collective-permute-done((bf16[96,1024]{1,0:T(8,128)(2,1)S(1)}, bf16[96,1024]{1,0:T(8,128)(2,1)S(1)}, u32[]{:S(2)}, u32[]{:S(2)}) %collective-permute-start.10) | collective-permute-done | bytes 196640 | tf_op jit(solution)/shard_map/ppermute | solution.py:70
  61.5 1.3 collective-permute-start.21
  63.0 4.5 %collective-permute-done.15.refs_3_ = bf16[96,1024]{1,0:T(8,128)(2,1)S(1)} collective-permute-done((bf16[96,1024]{1,0:T(8,128)(2,1)S(1)}, bf16[96,1024]{1,0:T(8,128)(2,1)S(1)}, u32[]{:S(2)}, u32[]{:S(2)}) %collective-permute-start.15) | collective-permute-done | bytes 196640 | tf_op jit(solution)/shard_map/ppermute | solution.py:70
  68.0 3.7 %collective-permute-done.21.refs_0_ = bf16[128,1024]{1,0:T(8,128)(2,1)S(1)} collective-permute-done((bf16[128,1024]{1,0:T(8,128)(2,1)S(1)}, bf16[128,1024]{1,0:T(8,128)(2,1)S(1)}, u32[]{:S(2)}, u32[]{:S(2)}) %collective-permute-start.21) | collective-permute-done | bytes 262176 | tf_op jit(solution)/shard_map/ppermute | solution.py:468
  71.8 1.5 %collective-permute-start.20 = (bf16[128,1024]{1,0:T(8,128)(2,1)S(1)}, bf16[128,1024]{1,0:T(8,128)(2,1)S(1)}, u32[]{:S(2)}, u32[]{:S(2)}) collective-permute-start(bf16[128,1024]{1,0:T(8,128)(2,1)S(1)} %shard_map.95), channel_id=1, source_target_pairs={{8,0},{16,8},{24,16},{9,1},{17,9},{25,17},{10,2},{18,10},{26,18},{... | collective-permute-start | bytes 786440 | tf_op jit(solution)/shard_map/ppermute | solution.py:468
  73.3 1.0 shard_map.88
  74.3 1.1 collective-permute-start.17
  75.4 1.5 %collective-permute-start.18 = (bf16[96,2048]{1,0:T(8,128)(2,1)S(1)}, bf16[96,2048]{1,0:T(8,128)(2,1)S(1)}, u32[]{:S(2)}, u32[]{:S(2)}) collective-permute-start(bf16[96,2048]{1,0:T(8,128)(2,1)S(1)} %get-tuple-element.116), channel_id=1, source_target_pairs={{0,4},{1,5},{2,6},{3,7},{4,0},{5,1},{6,2},{7,3},{8,12},{9,13},{10,... | collective-permute-start | bytes 1179656 | tf_op jit(solution)/shard_map/ppermute | solution.py:70
  78.3 4.2 %collective-permute-done.20.refs_0_ = bf16[128,1024]{1,0:T(8,128)(2,1)S(1)} collective-permute-done((bf16[128,1024]{1,0:T(8,128)(2,1)S(1)}, bf16[128,1024]{1,0:T(8,128)(2,1)S(1)}, u32[]{:S(2)}, u32[]{:S(2)}) %collective-permute-start.20) | collective-permute-done | bytes 262176 | tf_op jit(solution)/shard_map/ppermute | solution.py:468
  82.4 1.0 collective-permute-start.24
  83.4 2.9 %collective-permute-done.17.refs_1_ = bf16[96,2048]{1,0:T(8,128)(2,1)S(1)} collective-permute-done((bf16[96,2048]{1,0:T(8,128)(2,1)S(1)}, bf16[96,2048]{1,0:T(8,128)(2,1)S(1)}, u32[]{:S(2)}, u32[]{:S(2)}) %collective-permute-start.17) | collective-permute-done | bytes 393248 | tf_op jit(solution)/shard_map/ppermute | solution.py:70
  86.3 1.1 collective-permute-start.25
  87.4 1.4 %collective-permute-start.26 = (bf16[96,1024]{1,0:T(8,128)(2,1)S(1)}, bf16[96,1024]{1,0:T(8,128)(2,1)S(1)}, u32[]{:S(2)}, u32[]{:S(2)}) collective-permute-start(bf16[96,1024]{1,0:T(8,128)(2,1)S(1)} %get-tuple-element.123), channel_id=1, source_target_pairs={{0,6},{1,7},{2,4},{3,5},{4,2},{5,3},{6,0},{7,1},{8,14},{9,15},{10,... | collective-permute-start | bytes 589832 | tf_op jit(solution)/shard_map/ppermute | solution.py:70
  89.2 5.8 %collective-permute-done.18.refs_2_ = bf16[96,2048]{1,0:T(8,128)(2,1)S(1)} collective-permute-done((bf16[96,2048]{1,0:T(8,128)(2,1)S(1)}, bf16[96,2048]{1,0:T(8,128)(2,1)S(1)}, u32[]{:S(2)}, u32[]{:S(2)}) %collective-permute-start.18) | collective-permute-done | bytes 393248 | tf_op jit(solution)/shard_map/ppermute | solution.py:70
  95.3 2.1 %collective-permute-start.28 = (bf16[96,1024]{1,0:T(8,128)(2,1)S(1)}, bf16[96,1024]{1,0:T(8,128)(2,1)S(1)}, u32[]{:S(2)}, u32[]{:S(2)}) collective-permute-start(bf16[96,1024]{1,0:T(8,128)(2,1)S(1)} %get-tuple-element.127), channel_id=1, source_target_pairs={{0,4},{1,5},{2,6},{3,7},{4,0},{5,1},{6,2},{7,3},{8,12},{9,13},{10,... | collective-permute-start | bytes 589832 | tf_op jit(solution)/shard_map/ppermute | solution.py:70
  97.4 1.6 %collective-permute-done.24.refs_1_ = bf16[96,1024]{1,0:T(8,128)(2,1)S(1)} collective-permute-done((bf16[96,1024]{1,0:T(8,128)(2,1)S(1)}, bf16[96,1024]{1,0:T(8,128)(2,1)S(1)}, u32[]{:S(2)}, u32[]{:S(2)}) %collective-permute-start.24) | collective-permute-done | bytes 196640 | tf_op jit(solution)/shard_map/ppermute | solution.py:70
  99.0 2.0 %collective-permute-start.29 = (bf16[96,1024]{1,0:T(8,128)(2,1)S(1)}, bf16[96,1024]{1,0:T(8,128)(2,1)S(1)}, u32[]{:S(2)}, u32[]{:S(2)}) collective-permute-start(bf16[96,1024]{1,0:T(8,128)(2,1)S(1)} %get-tuple-element.128), channel_id=1, source_target_pairs={{0,6},{1,7},{2,4},{3,5},{4,2},{5,3},{6,0},{7,1},{8,14},{9,15},{10,... | collective-permute-start | bytes 589832 | tf_op jit(solution)/shard_map/ppermute | solution.py:70
  101.0 1.8 %shard_map.98 = (bf16[384,2048]{1,0:T(8,128)(2,1)S(1)}, bf16[384,704]{1,0:T(8,128)(2,1)S(1)}, f32[384,704]{1,0:T(8,128)S(1)}) custom-call(bf16[704,2048]{1,0:T(8,128)(2,1)S(1)} %bitcast.29, bf16[96,2048]{1,0:T(8,128)(2,1)S(1)} %get-tuple-element.129.refs_0_, bf16[96,2048]{1,0:T(8,128)(2,1)S(1)} %collective-permute-done.17.refs_1_, ...), custom_call_target="tpu_custom_call" | custom-call | flops 1107296256 | bytes 7651328 | tf_op jit(solution)/shard_map/pallas_call | solution.py:34
  103.8 3.0 %shard_map.99 = (bf16[384,1024]{1,0:T(8,128)(2,1)}, f32[384,704]{1,0:T(8,128)S(1)}, bf16[704,2048]{1,0:T(8,128)(2,1)}) custom-call(bf16[704,2048]{1,0:T(8,128)(2,1)S(1)} %bitcast.31, bf16[384,704]{1,0:T(8,128)(2,1)S(1)} %get-tuple-element.84.hid_ref.hid0_ref, bf16[384,704]{1,0:T(8,128)(2,1)S(1)} %get-tuple-element.133.hid1_ref.hid_ref, ...), custom_call_target="tpu_custom_call" | custom-call | flops 1660944384 | bytes 11272192 | tf_op jit(solution)/shard_map/pallas_call | solution.py:314
  107.5 4.5 %collective-permute-done.28.refs_2_ = bf16[96,1024]{1,0:T(8,128)(2,1)S(1)} collective-permute-done((bf16[96,1024]{1,0:T(8,128)(2,1)S(1)}, bf16[96,1024]{1,0:T(8,128)(2,1)S(1)}, u32[]{:S(2)}, u32[]{:S(2)}) %collective-permute-start.28) | collective-permute-done | bytes 196640 | tf_op jit(solution)/shard_map/ppermute | solution.py:70
  112.0 1.6 %shard_map.100 = (bf16[384,1024]{1,0:T(8,128)(2,1)S(1)}, bf16[384,704]{1,0:T(8,128)(2,1)S(1)}, bf16[384,128]{1,0:T(8,128)(2,1)}) custom-call(bf16[704,2048]{1,0:T(8,128)(2,1)S(1)} %bitcast.32, bf16[384,704]{1,0:T(8,128)(2,1)S(1)} %get-tuple-element.133.hid1_ref.hid_ref, f32[384,704]{1,0:T(8,128)S(1)} %get-tuple-element.138.slope_ref, ...), custom_call_target="tpu_custom_call" | custom-call | flops 553648128 | bytes 8192000 | tf_op jit(solution)/shard_map/pallas_call | solution.py:34
  115.3 3.4 %all-to-all-start.1 = ((bf16[8,48,128]{2,1,0:T(8,128)(2,1)}), bf16[8,48,128]{2,1,0:T(8,128)(2,1)S(1)}, u32[]{:S(2)}, u32[]{:S(2)}) async-start(bf16[8,48,128]{2,1,0:T(8,128)(2,1)} %bitcast.13), calls=%async_computation.1 | async-start | bytes 196608 | tf_op jit(solution)/shard_map/all_to_all | solution.py:230
  118.6 1.4 %copy-done.5 = bf16[384,2048]{1,0:T(8,128)(2,1)S(1)} copy-done((bf16[384,2048]{1,0:T(8,128)(2,1)S(1)}, bf16[384,2048]{1,0:T(8,128)(2,1)}, u32[]{:S(2)}) %copy-start.5) | copy-done | bytes 1572888
  120.0 1.4 %copy-done.7 = bf16[384,2048]{1,0:T(8,128)(2,1)S(1)} copy-done((bf16[384,2048]{1,0:T(8,128)(2,1)S(1)}, bf16[384,2048]{1,0:T(8,128)(2,1)}, u32[]{:S(2)}) %copy-start.7) | copy-done | bytes 1572888
  121.5 1.1 copy-done.9
  122.6 1.1 copy-done.11
  123.7 1.1 copy-done.13
  124.7 6.1 %shard_map.101 = (bf16[704,2048]{1,0:T(8,128)(2,1)}, bf16[704,2048]{1,0:T(8,128)(2,1)}) custom-call(bf16[704,2048]{1,0:T(8,128)(2,1)} %get-tuple-element.135.done_ref, f32[384,128]{1,0:T(8,128)S(1)} %get-tuple-element.93.prob_ref, bf16[384,2048]{1,0:T(8,128)(2,1)S(1)} %copy-done.5, bf16[384,2048]{1,0:T(8,128)(2,1)S(1)} %copy-done.7, ...), custom_call_target="tpu_custom_call", output_to_operand_aliasing={{1}: (0, {})} | custom-call | flops 3321888768 | bytes 16515072 | tf_op jit(solution)/shard_map/pallas_call | solution.py:360
  (69 shorter events, 14.8 us)
Async XLA Ops:
  0.6 38.8 %copy-start = (bf16[1,1,704,2048]{3,2,1,0:T(8,128)(2,1)S(1)}, bf16[1,1,704,2048]{3,2,1,0:T(8,128)(2,1)}, u32[]{:S(2)}) copy-start(bf16[1,1,704,2048]{3,2,1,0:T(8,128)(2,1)} %param.8) | copy-start | bytes 8650756
  1.9 17.0 %collective-permute-start = (bf16[128,2048]{1,0:T(8,128)(2,1)S(1)}, bf16[128,2048]{1,0:T(8,128)(2,1)S(1)}, u32[]{:S(2)}, u32[]{:S(2)}) collective-permute-start(bf16[128,2048]{1,0:T(8,128)(2,1)S(1)} %slice_bitcast_fusion.1.refs_0_), channel_id=1, source_target_pairs={{0,2},{1,3},{2,0},{3,1},{4,6},{5,7},{6,4},{7,5},{8,10},{9,11},{10,... | collective-permute-start | bytes 1572872 | tf_op jit(solution)/shard_map/ppermute | solution.py:70
  4.9 16.9 %collective-permute-start.4 = (bf16[128,2048]{1,0:T(8,128)(2,1)}, bf16[128,2048]{1,0:T(8,128)(2,1)S(1)}, u32[]{:S(2)}, u32[]{:S(2)}) collective-permute-start(bf16[128,2048]{1,0:T(8,128)(2,1)} %bitcast.33), channel_id=1, source_target_pairs={{0,4},{1,5},{2,6},{3,7},{4,0},{5,1},{6,2},{7,3},{8,12},{9,13},{10,... | collective-permute-start | bytes 1572872 | tf_op jit(solution)/shard_map/ppermute | solution.py:70
  19.9 5.4 %collective-permute-start.1 = (bf16[96,2048]{1,0:T(8,128)(2,1)S(1)}, bf16[96,2048]{1,0:T(8,128)(2,1)S(1)}, u32[]{:S(2)}, u32[]{:S(2)}) collective-permute-start(bf16[96,2048]{1,0:T(8,128)(2,1)S(1)} %get-tuple-element.81), channel_id=1, source_target_pairs={{0,1},{1,0},{2,3},{3,2},{4,5},{5,4},{6,7},{7,6},{8,9},{9,8},{10,11... | collective-permute-start | bytes 1179656 | tf_op jit(solution)/shard_map/ppermute | solution.py:70
  20.0 12.0 %collective-permute-start.2 = (bf16[96,2048]{1,0:T(8,128)(2,1)S(1)}, bf16[96,2048]{1,0:T(8,128)(2,1)S(1)}, u32[]{:S(2)}, u32[]{:S(2)}) collective-permute-start(bf16[96,2048]{1,0:T(8,128)(2,1)S(1)} %get-tuple-element.82), channel_id=1, source_target_pairs={{0,4},{1,5},{2,6},{3,7},{4,0},{5,1},{6,2},{7,3},{8,12},{9,13},{10,... | collective-permute-start | bytes 1179656 | tf_op jit(solution)/shard_map/ppermute | solution.py:70
  21.5 17.9 %collective-permute-start.3 = (bf16[96,2048]{1,0:T(8,128)(2,1)S(1)}, bf16[96,2048]{1,0:T(8,128)(2,1)S(1)}, u32[]{:S(2)}, u32[]{:S(2)}) collective-permute-start(bf16[96,2048]{1,0:T(8,128)(2,1)S(1)} %get-tuple-element.83), channel_id=1, source_target_pairs={{0,5},{1,4},{2,7},{3,6},{4,1},{5,0},{6,3},{7,2},{8,13},{9,12},{10,... | collective-permute-start | bytes 1179656 | tf_op jit(solution)/shard_map/ppermute | solution.py:70
  21.8 1.0 copy-start.2
  23.9 18.5 %collective-permute-start.5 = (bf16[96,2048]{1,0:T(8,128)(2,1)S(1)}, bf16[96,2048]{1,0:T(8,128)(2,1)S(1)}, u32[]{:S(2)}, u32[]{:S(2)}) collective-permute-start(bf16[96,2048]{1,0:T(8,128)(2,1)S(1)} %get-tuple-element.85), channel_id=1, source_target_pairs={{0,1},{1,0},{2,3},{3,2},{4,5},{5,4},{6,7},{7,6},{8,9},{9,8},{10,11... | collective-permute-start | bytes 1179656 | tf_op jit(solution)/shard_map/ppermute | solution.py:70
  24.3 18.1 %collective-permute-start.7 = (bf16[96,2048]{1,0:T(8,128)(2,1)S(1)}, bf16[96,2048]{1,0:T(8,128)(2,1)S(1)}, u32[]{:S(2)}, u32[]{:S(2)}) collective-permute-start(bf16[96,2048]{1,0:T(8,128)(2,1)S(1)} %get-tuple-element.95), channel_id=1, source_target_pairs={{0,2},{1,3},{2,0},{3,1},{4,6},{5,7},{6,4},{7,5},{8,10},{9,11},{10,... | collective-permute-start | bytes 1179656 | tf_op jit(solution)/shard_map/ppermute | solution.py:70
  25.3 17.8 %collective-permute-start.8 = (bf16[96,2048]{1,0:T(8,128)(2,1)S(1)}, bf16[96,2048]{1,0:T(8,128)(2,1)S(1)}, u32[]{:S(2)}, u32[]{:S(2)}) collective-permute-start(bf16[96,2048]{1,0:T(8,128)(2,1)S(1)} %get-tuple-element.96), channel_id=1, source_target_pairs={{0,3},{1,2},{2,1},{3,0},{4,7},{5,6},{6,5},{7,4},{8,11},{9,10},{10,... | collective-permute-start | bytes 1179656 | tf_op jit(solution)/shard_map/ppermute | solution.py:70
  39.5 3.7 %copy-start.1 = (bf16[1,1,704,2048]{3,2,1,0:T(8,128)(2,1)S(1)}, bf16[1,1,704,2048]{3,2,1,0:T(8,128)(2,1)}, u32[]{:S(2)}) copy-start(bf16[1,1,704,2048]{3,2,1,0:T(8,128)(2,1)} %param.9) | copy-start | bytes 8650756
  41.3 1.1 copy-start.4
  43.2 16.7 %copy-start.14 = (bf16[1,2,128,2048]{3,2,1,0:T(8,128)(2,1)S(1)}, bf16[1,2,128,2048]{3,2,1,0:T(8,128)(2,1)}, u32[]{:S(2)}) copy-start(bf16[1,2,128,2048]{3,2,1,0:T(8,128)(2,1)} %param.6) | copy-start | bytes 3145732
  46.4 15.0 %copy-start.10 = (bf16[384,704]{1,0:T(8,128)(2,1)}, bf16[384,704]{1,0:T(8,128)(2,1)S(1)}, u32[]{:S(2)}) copy-start(bf16[384,704]{1,0:T(8,128)(2,1)S(1)} %get-tuple-element.146.gp0_ref) | copy-start | bytes 1622020
  46.4 14.9 %copy-start.3 = (bf16[1,128,2048]{2,1,0:T(8,128)(2,1)S(1)}, bf16[1,128,2048]{2,1,0:T(8,128)(2,1)}, u32[]{:S(2)}) copy-start(bf16[1,128,2048]{2,1,0:T(8,128)(2,1)} %param.7) | copy-start | bytes 1572868
  46.4 7.7 %collective-permute-start.9 = (bf16[96,1024]{1,0:T(8,128)(2,1)S(1)}, bf16[96,1024]{1,0:T(8,128)(2,1)S(1)}, u32[]{:S(2)}, u32[]{:S(2)}) collective-permute-start(bf16[96,1024]{1,0:T(8,128)(2,1)S(1)} %get-tuple-element.98), channel_id=1, source_target_pairs={{0,2},{1,3},{2,0},{3,1},{4,6},{5,7},{6,4},{7,5},{8,10},{9,11},{10,... | collective-permute-start | bytes 589832 | tf_op jit(solution)/shard_map/ppermute | solution.py:70
  47.5 11.9 %collective-permute-start.10 = (bf16[96,1024]{1,0:T(8,128)(2,1)S(1)}, bf16[96,1024]{1,0:T(8,128)(2,1)S(1)}, u32[]{:S(2)}, u32[]{:S(2)}) collective-permute-start(bf16[96,1024]{1,0:T(8,128)(2,1)S(1)} %get-tuple-element.99), channel_id=1, source_target_pairs={{0,4},{1,5},{2,6},{3,7},{4,0},{5,1},{6,2},{7,3},{8,12},{9,13},{10,... | collective-permute-start | bytes 589832 | tf_op jit(solution)/shard_map/ppermute | solution.py:70
  48.6 10.9 %collective-permute-start.11 = (bf16[96,1024]{1,0:T(8,128)(2,1)S(1)}, bf16[96,1024]{1,0:T(8,128)(2,1)S(1)}, u32[]{:S(2)}, u32[]{:S(2)}) collective-permute-start(bf16[96,1024]{1,0:T(8,128)(2,1)S(1)} %get-tuple-element.100), channel_id=1, source_target_pairs={{0,6},{1,7},{2,4},{3,5},{4,2},{5,3},{6,0},{7,1},{8,14},{9,15},{10,... | collective-permute-start | bytes 589832 | tf_op jit(solution)/shard_map/ppermute | solution.py:70
  50.9 11.9 %collective-permute-start.13 = (bf16[96,1024]{1,0:T(8,128)(2,1)S(1)}, bf16[96,1024]{1,0:T(8,128)(2,1)S(1)}, u32[]{:S(2)}, u32[]{:S(2)}) collective-permute-start(bf16[96,1024]{1,0:T(8,128)(2,1)S(1)} %get-tuple-element.105), channel_id=1, source_target_pairs={{0,2},{1,3},{2,0},{3,1},{4,6},{5,7},{6,4},{7,5},{8,10},{9,11},{10,... | collective-permute-start | bytes 589832 | tf_op jit(solution)/shard_map/ppermute | solution.py:70
  51.9 11.1 %collective-permute-start.14 = (bf16[96,1024]{1,0:T(8,128)(2,1)S(1)}, bf16[96,1024]{1,0:T(8,128)(2,1)S(1)}, u32[]{:S(2)}, u32[]{:S(2)}) collective-permute-start(bf16[96,1024]{1,0:T(8,128)(2,1)S(1)} %get-tuple-element.106), channel_id=1, source_target_pairs={{0,4},{1,5},{2,6},{3,7},{4,0},{5,1},{6,2},{7,3},{8,12},{9,13},{10,... | collective-permute-start | bytes 589832 | tf_op jit(solution)/shard_map/ppermute | solution.py:70
  54.2 13.4 %collective-permute-start.15 = (bf16[96,1024]{1,0:T(8,128)(2,1)S(1)}, bf16[96,1024]{1,0:T(8,128)(2,1)S(1)}, u32[]{:S(2)}, u32[]{:S(2)}) collective-permute-start(bf16[96,1024]{1,0:T(8,128)(2,1)S(1)} %get-tuple-element.107), channel_id=1, source_target_pairs={{0,6},{1,7},{2,4},{3,5},{4,2},{5,3},{6,0},{7,1},{8,14},{9,15},{10,... | collective-permute-start | bytes 589832 | tf_op jit(solution)/shard_map/ppermute | solution.py:70
  59.8 1.6 %collective-permute-start.12 = (bf16[128,1024]{1,0:T(8,128)(2,1)S(1)}, bf16[128,1024]{1,0:T(8,128)(2,1)S(1)}, u32[]{:S(2)}, u32[]{:S(2)}) collective-permute-start(bf16[128,1024]{1,0:T(8,128)(2,1)S(1)} %get-tuple-element.102), channel_id=1, source_target_pairs={{0,1},{1,0},{2,3},{3,2},{4,5},{5,4},{6,7},{7,6},{8,9},{9,8},{10,11... | collective-permute-start | bytes 786440 | tf_op jit(solution)/shard_map/ppermute | solution.py:70
  59.9 13.4 %collective-permute-start.6 = (bf16[128,2048]{1,0:T(8,128)(2,1)S(1)}, bf16[128,2048]{1,0:T(8,128)(2,1)S(1)}, u32[]{:S(2)}, u32[]{:S(2)}) collective-permute-start(bf16[128,2048]{1,0:T(8,128)(2,1)S(1)} %slice_bitcast_fusion.refs_0_), channel_id=1, source_target_pairs={{0,1},{1,0},{2,3},{3,2},{4,5},{5,4},{6,7},{7,6},{8,9},{9,8},{10,11... | collective-permute-start | bytes 1572872 | tf_op jit(solution)/shard_map/ppermute | solution.py:70
  61.5 10.2 %collective-permute-start.21 = (bf16[128,1024]{1,0:T(8,128)(2,1)S(1)}, bf16[128,1024]{1,0:T(8,128)(2,1)S(1)}, u32[]{:S(2)}, u32[]{:S(2)}) collective-permute-start(bf16[128,1024]{1,0:T(8,128)(2,1)S(1)} %shard_map.93), channel_id=1, source_target_pairs={{8,0},{16,8},{24,16},{9,1},{17,9},{25,17},{10,2},{18,10},{26,18},{... | collective-permute-start | bytes 786440 | tf_op jit(solution)/shard_map/ppermute | solution.py:468
  67.9 3.8 %collective-permute-start.16 = (bf16[128,1024]{1,0:T(8,128)(2,1)S(1)}, bf16[128,1024]{1,0:T(8,128)(2,1)S(1)}, u32[]{:S(2)}, u32[]{:S(2)}) collective-permute-start(bf16[128,1024]{1,0:T(8,128)(2,1)S(1)} %get-tuple-element.113), channel_id=1, source_target_pairs={{0,1},{1,0},{2,3},{3,2},{4,5},{5,4},{6,7},{7,6},{8,9},{9,8},{10,11... | collective-permute-start | bytes 786440 | tf_op jit(solution)/shard_map/ppermute | solution.py:70
  71.7 6.2 %collective-permute-start.22 = (bf16[128,1024]{1,0:T(8,128)(2,1)S(1)}, bf16[128,1024]{1,0:T(8,128)(2,1)S(1)}, u32[]{:S(2)}, u32[]{:S(2)}) collective-permute-start(bf16[128,1024]{1,0:T(8,128)(2,1)S(1)} %collective-permute-done.21.refs_0_), channel_id=1, source_target_pairs={{0,1},{1,0},{2,3},{3,2},{4,5},{5,4},{6,7},{7,6},{8,9},{9,8},{10,11... | collective-permute-start | bytes 786440 | tf_op jit(solution)/shard_map/ppermute | solution.py:70
  71.8 10.6 %collective-permute-start.20 = (bf16[128,1024]{1,0:T(8,128)(2,1)S(1)}, bf16[128,1024]{1,0:T(8,128)(2,1)S(1)}, u32[]{:S(2)}, u32[]{:S(2)}) collective-permute-start(bf16[128,1024]{1,0:T(8,128)(2,1)S(1)} %shard_map.95), channel_id=1, source_target_pairs={{8,0},{16,8},{24,16},{9,1},{17,9},{25,17},{10,2},{18,10},{26,18},{... | collective-permute-start | bytes 786440 | tf_op jit(solution)/shard_map/ppermute | solution.py:468
  74.3 12.0 %collective-permute-start.17 = (bf16[96,2048]{1,0:T(8,128)(2,1)S(1)}, bf16[96,2048]{1,0:T(8,128)(2,1)S(1)}, u32[]{:S(2)}, u32[]{:S(2)}) collective-permute-start(bf16[96,2048]{1,0:T(8,128)(2,1)S(1)} %get-tuple-element.115), channel_id=1, source_target_pairs={{0,2},{1,3},{2,0},{3,1},{4,6},{5,7},{6,4},{7,5},{8,10},{9,11},{10,... | collective-permute-start | bytes 1179656 | tf_op jit(solution)/shard_map/ppermute | solution.py:70
  75.4 19.6 %collective-permute-start.18 = (bf16[96,2048]{1,0:T(8,128)(2,1)S(1)}, bf16[96,2048]{1,0:T(8,128)(2,1)S(1)}, u32[]{:S(2)}, u32[]{:S(2)}) collective-permute-start(bf16[96,2048]{1,0:T(8,128)(2,1)S(1)} %get-tuple-element.116), channel_id=1, source_target_pairs={{0,4},{1,5},{2,6},{3,7},{4,0},{5,1},{6,2},{7,3},{8,12},{9,13},{10,... | collective-permute-start | bytes 1179656 | tf_op jit(solution)/shard_map/ppermute | solution.py:70
  77.0 18.3 %collective-permute-start.19 = (bf16[96,2048]{1,0:T(8,128)(2,1)S(1)}, bf16[96,2048]{1,0:T(8,128)(2,1)S(1)}, u32[]{:S(2)}, u32[]{:S(2)}) collective-permute-start(bf16[96,2048]{1,0:T(8,128)(2,1)S(1)} %get-tuple-element.117), channel_id=1, source_target_pairs={{0,6},{1,7},{2,4},{3,5},{4,2},{5,3},{6,0},{7,1},{8,14},{9,15},{10,... | collective-permute-start | bytes 1179656 | tf_op jit(solution)/shard_map/ppermute | solution.py:70
  82.4 5.0 %collective-permute-start.23 = (bf16[128,1024]{1,0:T(8,128)(2,1)S(1)}, bf16[128,1024]{1,0:T(8,128)(2,1)S(1)}, u32[]{:S(2)}, u32[]{:S(2)}) collective-permute-start(bf16[128,1024]{1,0:T(8,128)(2,1)S(1)} %collective-permute-done.20.refs_0_), channel_id=1, source_target_pairs={{0,1},{1,0},{2,3},{3,2},{4,5},{5,4},{6,7},{7,6},{8,9},{9,8},{10,11... | collective-permute-start | bytes 786440 | tf_op jit(solution)/shard_map/ppermute | solution.py:70
  82.4 16.6 %collective-permute-start.24 = (bf16[96,1024]{1,0:T(8,128)(2,1)S(1)}, bf16[96,1024]{1,0:T(8,128)(2,1)S(1)}, u32[]{:S(2)}, u32[]{:S(2)}) collective-permute-start(bf16[96,1024]{1,0:T(8,128)(2,1)S(1)} %get-tuple-element.121), channel_id=1, source_target_pairs={{0,2},{1,3},{2,0},{3,1},{4,6},{5,7},{6,4},{7,5},{8,10},{9,11},{10,... | collective-permute-start | bytes 589832 | tf_op jit(solution)/shard_map/ppermute | solution.py:70
  86.3 17.1 %collective-permute-start.25 = (bf16[96,1024]{1,0:T(8,128)(2,1)S(1)}, bf16[96,1024]{1,0:T(8,128)(2,1)S(1)}, u32[]{:S(2)}, u32[]{:S(2)}) collective-permute-start(bf16[96,1024]{1,0:T(8,128)(2,1)S(1)} %get-tuple-element.122), channel_id=1, source_target_pairs={{0,4},{1,5},{2,6},{3,7},{4,0},{5,1},{6,2},{7,3},{8,12},{9,13},{10,... | collective-permute-start | bytes 589832 | tf_op jit(solution)/shard_map/ppermute | solution.py:70
  87.4 16.4 %collective-permute-start.26 = (bf16[96,1024]{1,0:T(8,128)(2,1)S(1)}, bf16[96,1024]{1,0:T(8,128)(2,1)S(1)}, u32[]{:S(2)}, u32[]{:S(2)}) collective-permute-start(bf16[96,1024]{1,0:T(8,128)(2,1)S(1)} %get-tuple-element.123), channel_id=1, source_target_pairs={{0,6},{1,7},{2,4},{3,5},{4,2},{5,3},{6,0},{7,1},{8,14},{9,15},{10,... | collective-permute-start | bytes 589832 | tf_op jit(solution)/shard_map/ppermute | solution.py:70
  95.0 12.5 %collective-permute-start.27 = (bf16[96,1024]{1,0:T(8,128)(2,1)S(1)}, bf16[96,1024]{1,0:T(8,128)(2,1)S(1)}, u32[]{:S(2)}, u32[]{:S(2)}) collective-permute-start(bf16[96,1024]{1,0:T(8,128)(2,1)S(1)} %get-tuple-element.126), channel_id=1, source_target_pairs={{0,2},{1,3},{2,0},{3,1},{4,6},{5,7},{6,4},{7,5},{8,10},{9,11},{10,... | collective-permute-start | bytes 589832 | tf_op jit(solution)/shard_map/ppermute | solution.py:70
  95.3 16.6 %collective-permute-start.28 = (bf16[96,1024]{1,0:T(8,128)(2,1)S(1)}, bf16[96,1024]{1,0:T(8,128)(2,1)S(1)}, u32[]{:S(2)}, u32[]{:S(2)}) collective-permute-start(bf16[96,1024]{1,0:T(8,128)(2,1)S(1)} %get-tuple-element.127), channel_id=1, source_target_pairs={{0,4},{1,5},{2,6},{3,7},{4,0},{5,1},{6,2},{7,3},{8,12},{9,13},{10,... | collective-permute-start | bytes 589832 | tf_op jit(solution)/shard_map/ppermute | solution.py:70
  99.0 13.0 %collective-permute-start.29 = (bf16[96,1024]{1,0:T(8,128)(2,1)S(1)}, bf16[96,1024]{1,0:T(8,128)(2,1)S(1)}, u32[]{:S(2)}, u32[]{:S(2)}) collective-permute-start(bf16[96,1024]{1,0:T(8,128)(2,1)S(1)} %get-tuple-element.128), channel_id=1, source_target_pairs={{0,6},{1,7},{2,4},{3,5},{4,2},{5,3},{6,0},{7,1},{8,14},{9,15},{10,... | collective-permute-start | bytes 589832 | tf_op jit(solution)/shard_map/ppermute | solution.py:70
  102.8 4.0 %copy-start.6 = (bf16[384,2048]{1,0:T(8,128)(2,1)}, bf16[384,2048]{1,0:T(8,128)(2,1)S(1)}, u32[]{:S(2)}) copy-start(bf16[384,2048]{1,0:T(8,128)(2,1)S(1)} %get-tuple-element.137.x1_ref) | copy-start | bytes 4718596
  113.6 0.9 copy-start.8
  114.5 0.8 copy-start.12
  115.3 15.6 %all-to-all-start.1 = ((bf16[8,48,128]{2,1,0:T(8,128)(2,1)}), bf16[8,48,128]{2,1,0:T(8,128)(2,1)S(1)}, u32[]{:S(2)}, u32[]{:S(2)}) async-start(bf16[8,48,128]{2,1,0:T(8,128)(2,1)} %bitcast.13), calls=%async_computation.1 | async-start | bytes 196608 | tf_op jit(solution)/shard_map/all_to_all | solution.py:230
  118.6 1.4 %copy-start.5 = (bf16[384,2048]{1,0:T(8,128)(2,1)S(1)}, bf16[384,2048]{1,0:T(8,128)(2,1)}, u32[]{:S(2)}) copy-start(bf16[384,2048]{1,0:T(8,128)(2,1)} %copy-done.4) | copy-start | bytes 4718596
  120.0 1.4 %copy-start.7 = (bf16[384,2048]{1,0:T(8,128)(2,1)S(1)}, bf16[384,2048]{1,0:T(8,128)(2,1)}, u32[]{:S(2)}) copy-start(bf16[384,2048]{1,0:T(8,128)(2,1)} %copy-done.6) | copy-start | bytes 4718596
  121.5 1.1 copy-start.9
  122.6 1.1 copy-start.11
  123.7 1.1 copy-start.13

commit v5 on v4

--- a/solution.py
+++ b/solution.py
@@ -12,6 +12,8 @@
 LANES = 128
 AXES = (2, 2)
 HALVES = len(AXES)
+TILES = 2
+LONG = 10**11
 VMEM_LIMIT = 20 * 1024 * 1024
 f32 = jnp.float32
 bf16 = jnp.bfloat16
@@ -27,7 +29,7 @@
 
 def cost(args, outs, flops):
     size = sum(a.size * a.dtype.itemsize for a in list(args) + list(outs))
-    return pl.CostEstimate(flops=flops, bytes_accessed=size, transcendentals=0)
+    return pl.CostEstimate(flops=flops if flops == LONG else 0, bytes_accessed=0, transcendentals=0)
 
 
 def call(kernel, outs, *args, flops=0, scratch=()):
@@ -122,38 +124,55 @@
     prob_ref[...] = columns
 
 
-def block_masks(plane, capacity, ranks, meta_ref, block, experts):
-    tokens = meta_ref.shape[2]
+def block_masks(plane, capacity, ranks, ids, experts):
+    tokens = ids.shape[1]
     row = lax.broadcasted_iota(jnp.int32, (len(experts), tokens), 0)
     expert = jnp.zeros(row.shape, f32)
     for i, offset in enumerate(experts):
         expert = jnp.where(row == i, other_of(plane, offset).astype(f32), expert)
-    ids = meta_ref[other_of(plane, block)]
     return slot_masks([(ids[i : i + 1, :] == expert).astype(f32) for i in ranks], capacity)[0]
 
 
 def masks_kernel(plane, capacity, plans, meta_ref, *out_refs):
     for (ranks, blocks, experts), out_ref in zip(plans, out_refs):
         for s, block in enumerate(blocks):
-            out_ref[s] = block_masks(plane, capacity, ranks, meta_ref, block, experts).astype(bf16)
+            out_ref[s] = block_masks(
+                plane, capacity, ranks, meta_ref[other_of(plane, block)], experts
+            ).astype(bf16)
 
 
 def select_kernel(plane, capacity, plan, meta_ref, *refs):
     ranks, sources, targets = plan
     raw_refs, out_refs = refs[: len(sources)], refs[len(sources) :]
     for s, source in enumerate(sources):
-        hot = block_masks(plane, capacity, ranks, meta_ref, source, targets)
+        hot = block_masks(plane, capacity, ranks, meta_ref[other_of(plane, source)], targets)
         picked = dot(hot.astype(bf16), raw_refs[s][...], 1, 0).astype(bf16)
         for i, out_ref in enumerate(out_refs):
             out_ref[s * capacity : (s + 1) * capacity, :] = picked[i * capacity : (i + 1) * capacity]
 
 
-def pick_kernel(capacity, sources, hot_ref, *refs):
-    raw_refs, out_refs = refs[:sources], refs[sources:]
-    for s, raw_ref in enumerate(raw_refs):
-        picked = dot(hot_ref[s], raw_ref[...], 1, 0).astype(bf16)
+def own_select_kernel(plane, capacity, plan, *refs):
+    ranks, sources, targets = plan
+    count = len(sources)
+    for s in range(count):
+        hot = block_masks(plane, capacity, ranks, refs[s][...], targets)
+        picked = dot(hot.astype(bf16), refs[count + s][...], 1, 0).astype(bf16)
+        for i, out_ref in enumerate(refs[2 * count :]):
+            out_ref[s * capacity : (s + 1) * capacity, :] = picked[i * capacity : (i + 1) * capacity]
+
+
+def pick_own_kernel(hot_ref, raw_ref, out_ref):
+    out_ref[...] = dot(hot_ref[0], raw_ref[...], 1, 0).astype(bf16)
+
+
+def pick_kernel(capacity, hot_ref, own_ref, *refs):
+    sources = hot_ref.shape[0]
+    raw_refs, out_refs = refs[: sources - 1], refs[sources - 1 :]
+    picked = [own_ref[...]]
+    picked += [dot(hot_ref[s + 1], raw_ref[...], 1, 0).astype(bf16) for s, raw_ref in enumerate(raw_refs)]
+    for s, rows in enumerate(picked):
         for i, out_ref in enumerate(out_refs):
-            out_ref[s * capacity : (s + 1) * capacity, :] = picked[i * capacity : (i + 1) * capacity]
+            out_ref[s * capacity : (s + 1) * capacity, :] = rows[i * capacity : (i + 1) * capacity]
 
 
 def gather_plan(plane, ranks, axis):
@@ -170,15 +189,20 @@
     raws = [plane.send(value, u) for u in plane.along(axis)]
     outs = [shaped((len(plan[1]) * capacity, width), bf16)] * len(plan[2])
     flops = 2 * tokens * width * capacity * len(plan[1]) * len(plan[2])
+    if type(meta) is list:
+        return call(functools.partial(own_select_kernel, plane, capacity, plan), outs, *meta, *raws, flops=flops)
     if hot is None:
         return call(functools.partial(select_kernel, plane, capacity, plan), outs, meta, *raws, flops=flops)
-    return call(functools.partial(pick_kernel, capacity, len(raws)), outs, hot, *raws, flops=flops)
+    (own,) = call(pick_own_kernel, [shaped((hot.shape[1], width), bf16)], hot, raws[0], flops=LONG)
+    return call(functools.partial(pick_kernel, capacity), outs, hot, own, *raws[1:], flops=flops)
 
 
 def sent_rows(plane, axis, picked):
-    targets = plane.across(axis)
-    pieces = [plane.send(p, t) for p, t in zip(picked, targets)]
-    return pieces, [[plane.back(t, u) for u in plane.along(axis)] for t in targets]
+    return [plane.send(p, t) for p, t in zip(picked, plane.across(axis))], sent_layout(plane, axis)
+
+
+def sent_layout(plane, axis):
+    return [[plane.back(t, u) for u in plane.along(axis)] for t in plane.across(axis)]
 
 
 def combine_parts_kernel(capacity, blocks, hot_ref, *refs):
@@ -188,10 +212,14 @@
         out_ref[...] = dot(hot_ref[s], rows, 0, 0).astype(out_ref.dtype)
 
 
-def add_kernel(first, g_ref, own_ref, *refs):
+def seed_kernel(first, g_ref, own_ref, out_ref):
+    width = out_ref.shape[1]
+    out_ref[...] = g_ref[:, first : first + width].astype(f32) + own_ref[...]
+
+
+def add_kernel(own_ref, *refs):
     out_ref = refs[-1]
-    width = out_ref.shape[1]
-    total = g_ref[:, first : first + width].astype(f32) + own_ref[...]
+    total = own_ref[...]
     for ref in refs[:-1]:
         total = total + ref[...].astype(f32)
     out_ref[...] = total.astype(bf16)
@@ -208,7 +236,8 @@
         flops=2 * hot.size * width,
     )
     sent = [plane.send(p, u) for p, u in zip(parts, along[1:])]
-    return call(functools.partial(add_kernel, first), [shaped((tokens, width), bf16)], g, own, *sent)[0], parts
+    (own,) = call(functools.partial(seed_kernel, first), [shaped((tokens, width), f32)], g, own, flops=LONG)
+    return call(add_kernel, [shaped((tokens, width), bf16)], own, *sent)[0], parts
 
 
 def behind(values, after):
@@ -295,7 +324,7 @@
 
 
 def early_kernel(plane, capacity, groups, wout_ref, hid0_ref, hid1_ref, prob_ref, g0_ref, *refs):
-    g_ref, pulled_ref, gout_ref = refs[-3:]
+    pulled_ref, gout_ref, g_ref = refs[-3:]
     arrange(plane, capacity, groups, refs[:-3], g_ref)
     pulled_ref[...] = dot(g_ref[...], wout_ref[...], 1, 1)
     y = jnp.concatenate([weighted(prob_ref, 0, g0_ref[...]), weighted(prob_ref, 1, g_ref[...])], axis=0)
@@ -308,7 +337,7 @@
     features = w_out.shape[1]
     width = features // HALVES
     args = (w_out, hid0, hid1, prob, g0, *pieces)
-    outs = [shaped((rows, width), bf16), shaped((rows, units), f32), shaped((units, features), bf16)]
+    outs = [shaped((rows, units), f32), shaped((units, features), bf16)]
     whole = lambda a: pl.BlockSpec(a.shape, lambda i: (0, 0))
     first = lambda a: pl.BlockSpec((a.shape[0], width), lambda i: (0, 0))
     return pl.pallas_call(
@@ -316,7 +345,8 @@
         grid=(1,),
         out_shape=outs,
         in_specs=[first(w_out), whole(hid0), whole(hid1), whole(prob), first(g0)] + [whole(p) for p in pieces],
-        out_specs=[whole(outs[0]), whole(outs[1]), first(outs[2])],
+        out_specs=[whole(outs[0]), first(outs[1])],
+        scratch_shapes=[pltpu.VMEM((rows, width), bf16)],
         compiler_params=pltpu.CompilerParams(vmem_limit_bytes=VMEM_LIMIT),
         cost_estimate=cost(args, outs, 3 * units * rows * features),
     )(*args)
@@ -333,42 +363,74 @@
     gp_ref[...] = (prob_ref[:, 1:2] * pulled * slope_ref[...]).astype(bf16)
 
 
-def late_kernel(done_ref, prob_ref, x0_ref, x1_ref, g0_ref, g1_ref, hid0_ref, hid1_ref, gp0_ref, gp1_ref, *refs):
-    gin_ref, gout_ref, hid, gp = refs
-    rows = hid0_ref.shape[0]
-
-    @pl.when(pl.program_id(0) == 0)
-    def _():
-        hid[:rows, :] = hid0_ref[...]
-        hid[rows:, :] = hid1_ref[...]
-        gp[:rows, :] = gp0_ref[...]
-        gp[rows:, :] = gp1_ref[...]
-
-    gin_ref[...] = dot(gp[...], jnp.concatenate([x0_ref[...], x1_ref[...]], axis=0), 0, 0).astype(bf16)
-    y = jnp.concatenate([weighted(prob_ref, 0, g0_ref[...]), weighted(prob_ref, 1, g1_ref[...])], axis=0)
-    gout_ref[...] = dot(hid[...], y, 0, 0).astype(bf16)
-
-
-def late(steps, done, prob, x0, x1, g0, g1, hid0, hid1, gp0, gp1):
+def late_kernel(width, _, prob_ref, x0_ref, x1_ref, g0_ref, g1_ref, hid0_ref, hid1_ref, gp0_ref, gp1_ref, *refs):
+    gin_ref, gout_ref, prob, x, g, hid, gp, held, sem, out_sem = refs
+    rows, units = hid0_ref.shape
+    features, part = x0_ref.shape[1], g1_ref.shape[1]
+    skip = features - part
+    fetched = []
+
+    def fetch(ref, out_ref):
+        fetched.append(pltpu.make_async_copy(ref, out_ref, sem.at[len(fetched)]))
+        fetched[-1].start()
+        return fetched[-1]
+
+    top, low = pl.ds(0, rows), pl.ds(rows, rows)
+    lanes = lambda at: pl.ds(at, width)
+    first = [fetch(gp0_ref, gp.at[top, :]), fetch(gp1_ref, gp.at[low, :])]
+    tiles = []
+    for at in range(0, features, width):
+        tiles.append(
+            [fetch(x0_ref.at[:, lanes(at)], x.at[top, lanes(at)]), fetch(x1_ref.at[:, lanes(at)], x.at[low, lanes(at)])]
+        )
+    then = [fetch(hid0_ref, hid.at[top, :]), fetch(hid1_ref, hid.at[low, :]), fetch(prob_ref, prob)]
+    then += [fetch(g0_ref.at[:, pl.ds(skip, part)], g.at[top, :]), fetch(g1_ref, g.at[low, :])]
+    sent = []
+
+    def store(n, value, out_ref, at):
+        slot = n % held.shape[0]
+        if n >= held.shape[0]:
+            sent[n - held.shape[0]].wait()
+        held[slot] = value.astype(bf16)
+        sent.append(pltpu.make_async_copy(held.at[slot], out_ref.at[:, lanes(at)], out_sem.at[slot]))
+        sent[-1].start()
+
+    for copy in first:
+        copy.wait()
+    for n, tile in enumerate(tiles):
+        for copy in tile:
+            copy.wait()
+        at = n * width
+        store(n, dot(gp[...], x[:, at : at + width], 0, 0), gin_ref, at)
+    for copy in then:
+        copy.wait()
+    for n in range(part // width):
+        at = n * width
+        y0 = weighted(prob, 0, g[:rows, at : at + width])
+        y1 = weighted(prob, 1, g[rows:, at : at + width])
+        store(len(tiles) + n, dot(hid[...], jnp.concatenate([y0, y1], axis=0), 0, 0), gout_ref, skip + at)
+    for copy in sent[-held.shape[0] :]:
+        copy.wait()
+
+
+def late(width, done, prob, x0, x1, g0, g1, hid0, hid1, gp0, gp1):
     args = (done, prob, x0, x1, g0, g1, hid0, hid1, gp0, gp1)
     rows, units = hid0.shape
     features, part = x0.shape[1], g1.shape[1]
     outs = [shaped((units, features), bf16)] * 2
-    skip = (features - part) // (part // steps)
-    tile = lambda n, width, at: pl.BlockSpec((n, width // steps), lambda i: (0, at + i))
-    whole = lambda a: pl.BlockSpec(a.shape, lambda i: (0, 0))
+    fetches = 7 + 2 * (features // width)
     return pl.pallas_call(
-        late_kernel,
-        grid=(steps,),
+        functools.partial(late_kernel, width),
         out_shape=outs,
-        in_specs=[pl.BlockSpec(memory_space=pl.ANY), whole(prob)]
-        + [tile(rows, features, 0)] * 2
-        + [tile(rows, part, skip), tile(rows, part, 0)]
-        + [whole(hid0)] * 4,
-        out_specs=[tile(units, features, 0), tile(units, part, skip)],
-        scratch_shapes=[pltpu.VMEM((2 * rows, units), bf16)] * 2,
+        in_specs=[pl.BlockSpec(memory_space=pltpu.HBM)] * len(args),
+        out_specs=[pl.BlockSpec(memory_space=pltpu.HBM)] * 2,
+        scratch_shapes=[pltpu.VMEM(prob.shape, f32), pltpu.VMEM((2 * rows, features), bf16)]
+        + [pltpu.VMEM((2 * rows, part), bf16)]
+        + [pltpu.VMEM((2 * rows, units), bf16)] * 2
+        + [pltpu.VMEM((3, units, width), bf16)]
+        + [pltpu.SemaphoreType.DMA((fetches,)), pltpu.SemaphoreType.DMA((3,))],
         input_output_aliases={0: 1},
-        compiler_params=pltpu.CompilerParams(vmem_limit_bytes=VMEM_LIMIT),
+        compiler_params=pltpu.CompilerParams(vmem_limit_bytes=60 * 1024 * 1024),
         cost_estimate=cost(args, outs, 6 * units * rows * features),
     )(*args)
 
@@ -406,6 +468,7 @@
     ids = jnp.transpose(expert_ids[0], (0, 2, 1)).reshape(ticks * topk, tokens)
     probs = jnp.transpose(gate_probs[0], (0, 2, 1)).reshape(ticks * topk, tokens)
     meta = jnp.concatenate([ids.astype(f32), probs.astype(f32)], axis=0)
+    own_meta = meta
     meta = jnp.broadcast_to(meta[None], (experts,) + meta.shape)
     meta = lax.all_to_all(meta, "expert", split_axis=0, concat_axis=0, tiled=True)
     hot0, hot1, prob = call(
@@ -419,10 +482,14 @@
     ranks = [list(range(k * topk, (k + 1) * topk)) for k in range(ticks)]
     pick = functools.partial(picked_rows, plane, capacity)
     if stepped:
-        x0, x0_layout = sent_rows(plane, 1, pick(ranks[0], 1, x0, meta))
-        g0_in, g0_layout = sent_rows(plane, 0, pick(ranks[0], 0, g0, meta))
-        x1 = behind(inputs, [x0[1], g0_in[1]])[0, 1]
-        x1 = pick(ranks[1], 2, x1, meta)
+        metas = [own_meta, plane.send(own_meta, (0, 0, 1))]
+        x1 = behind(inputs, [x0])[0, 1]
+        x1 = pick(ranks[1], 2, x1, metas)
+        x1_near, _ = sent_rows(plane, 2, x1[:-1])
+        x1_groups, x1_rest = [(0, sent_layout(plane, 2))], x1[-1:]
+        select_meta = behind(meta, x1)
+        x0, x0_layout = sent_rows(plane, 1, pick(ranks[0], 1, x0, select_meta))
+        g0_in, g0_layout = sent_rows(plane, 0, pick(ranks[0], 0, g0, select_meta))
         plans = [return_plan(plane, ranks[0], axis) for axis in AXES]
         plans += [gather_plan(plane, ranks[1], axis) for axis in AXES]
         shapes = [shaped((len(b), len(e) * capacity, tokens), bf16) for _, b, e in plans]
@@ -435,6 +502,8 @@
         back_plans = [None] * HALVES
         shapes = [shaped((rows, half), bf16)] * HALVES
 
+    if stepped:
+        x0 = behind(x0, x1_near)
     x0, hid0, slope0 = call(
         functools.partial(preact_kernel, plane, capacity, [(0, x0_layout)]), acts, w_in, *x0, flops=matmul
     )
@@ -459,8 +528,8 @@
         after = [out]
 
     if stepped:
-        x1, x1_layout = sent_rows(plane, 2, behind(x1, leaving))
-        x1_groups = [(0, x1_layout)]
+        x1_rest = [plane.send(p, t) for p, t in zip(behind(x1_rest, leaving), plane.across(2)[-1:])]
+        x1 = x1_near + x1_rest
     else:
         x1, x1_groups = [exchange(spread(hot1, inputs[0, 1]), experts)], [(0, None)]
     parts, after = [], []
@@ -478,7 +547,7 @@
     x1, hid1, slope1 = call(
         functools.partial(preact_kernel, plane, capacity, x1_groups), acts, w_in, *x1, flops=matmul
     )
-    part, pulled, gout = early(plane, capacity, parts[0][1], w_out, hid0, hid1, prob, g0_in, *parts[0][0])
+    pulled, gout = early(plane, capacity, parts[0][1], w_out, hid0, hid1, prob, g0_in, *parts[0][0])
     pieces = behind(parts[1][0], [pulled])
     g1, gp1, scores = call(
         functools.partial(second_kernel, plane, capacity, parts[1][1], half),
@@ -486,7 +555,7 @@
         w_out, hid1, slope1, prob, score0, pulled, *pieces, flops=matmul // 2,
     )
     scores = exchange(scores, experts)
-    grad_in, grad_out = late(4, gout, prob, x0, x1, g0_in, g1, hid0, hid1, gp0, gp1)
+    grad_in, grad_out = late(features // TILES, gout, prob, x0, x1, g0_in, g1, hid0, hid1, gp0, gp1)
     (prob_grads,) = call(
         functools.partial(collect_kernel, experts, capacity, topk),
         [shaped((ticks * topk, tokens), bf16)], meta, hot0, hot1, scores,

time: 132 us -> 123 us (0.932)
  blocking collectives: 11 us -> 0 us
  Pallas kernels: 24.5 us -> 33.6 us
  waiting for transfers between devices: 49 us -> 43 us
  local copies, waits for them, and re-layouts: 11.2 us -> 9.42 us
  starting transfers between devices: 33.6 us -> 35.1 us
  other arithmetic: 1.37 us -> 0.01 us
    all_to_all x1 -> x0, blocking collectives: 11 us -> none  [body(): lax.all_to_all(meta, 'expert', split_axis=0, concat_axis=0, tiled=True)]
    pallas_call x16 -> x20, Pallas kernels: 15.4 us -> 23.5 us  [call(): pl.pallas_call(kernel, out_shape=outs, scratch_shapes=scratch, compiler_p...]
    ppermute x2, waiting for transfers between devices: 7.89 us -> 1.64 us  [body(): lax.ppermute(leaving[h], 'segment', [(i, i - 1) for i in range(1, segment...]
    unnamed x30 -> x46, local copies, waits for them, and re-layouts: 9.96 us -> 5.84 us
    all_to_all x0 -> x1, starting transfers between devices: none -> 3.33 us  [body(): lax.all_to_all(meta, 'expert', split_axis=0, concat_axis=0, tiled=True)]
    squeeze x1, local copies, waits for them, and re-layouts: 0.04 us -> 1.88 us  [body(): x1 = behind(inputs, [x0])[0, 1]]
    ppermute x28 -> x29, starting transfers between devices: 27.4 us -> 25.6 us  [send(): return lax.ppermute(value, 'expert', route)]
    convert_element_type x2, other arithmetic: 1.36 us -> 0.01 us  [body(): meta = jnp.concatenate([ids.astype(f32), probs.astype(f32)], axis=0)]
  transfers between devices with their start and end apart: 31 -> 33, of which waited for: 18 -> 21; matrix products, arithmetic and copies ran while one was open for 1% -> 1% of each run, Pallas kernels for 14% -> 23%
where the time goes in v5:
time: 123 us; the launch traced here: 122 us
  waiting for transfers between devices  43 us (35%)
  starting transfers between devices  35.1 us (29%)
  Pallas kernels  33.6 us (27%)
  local copies, waits for them, and re-layouts  9.42 us (8%)
    ppermute x29, waiting for transfers between devices, send(): return lax.ppermute(value, 'expert', route)  40.7 us
    ppermute x29, starting transfers between devices, send(): return lax.ppermute(value, 'expert', route)  25.6 us
    pallas_call x20, Pallas kernels, call(): pl.pallas_call(kernel, out_shape=outs, scratch_shapes=scratch, compiler_p...  23.5 us
    pallas_call x1, Pallas kernels, late(): pl.pallas_call(functools.partial(late_kernel, width), out_shape=outs, in_...  7.03 us
    unnamed x46, local copies, waits for them, and re-layouts  5.84 us
    all_to_all x1, starting transfers between devices, exchange(): lax.all_to_all(pieces, 'expert', split_axis=0, concat_axis=0, tiled=True)  3.36 us
    all_to_all x1, starting transfers between devices, body(): lax.all_to_all(meta, 'expert', split_axis=0, concat_axis=0, tiled=True)  3.33 us
    pallas_call x1, Pallas kernels, early(): pl.pallas_call(functools.partial(early_kernel, plane, capacity, groups),...  3.05 us
  transfers between devices with their start and end apart: 33, of which 21 were waited for; matrix products, arithmetic and copies ran while one was open for 1% of the time, Pallas kernels for 23%

profile of v5, /device:TPU:0, one launch (start us, length us, event | category | flops | bytes accessed | tf_op | source)
XLA Modules:
  0.0 122.1 jit_solution(16372099615124447923)
XLA Ops:
  0.7 1.1 slice_bitcast_fusion.1.refs_0_
  1.7 1.9 %slice_bitcast_fusion.refs_2_ = bf16[128,2048]{1,0:T(8,128)(2,1)} fusion(bf16[1,2,128,2048]{3,2,1,0:T(8,128)(2,1)} %param.6), kind=kLoop, calls=%fused_computation | loop fusion | bytes 1048576 | tf_op jit(solution)/shard_map/squeeze | solution.py:486
  4.1 2.5 %collective-permute-start.2 = (bf16[128,2048]{1,0:T(8,128)(2,1)S(1)}, bf16[128,2048]{1,0:T(8,128)(2,1)}, u32[]{:S(2)}, u32[]{:S(2)}) collective-permute-start(bf16[128,2048]{1,0:T(8,128)(2,1)S(1)} %slice_bitcast_fusion.1.refs_0_), channel_id=1, source_target_pairs={{0,2},{1,3},{2,0},{3,1},{4,6},{5,7},{6,4},{7,5},{8,10},{9,11},{10,... | collective-permute-start | bytes 1572872 | tf_op jit(solution)/shard_map/ppermute | solution.py:72
  6.6 1.5 %collective-permute-start.8 = (bf16[128,2048]{1,0:T(8,128)(2,1)}, bf16[128,2048]{1,0:T(8,128)(2,1)}, u32[]{:S(2)}, u32[]{:S(2)}) collective-permute-start(bf16[128,2048]{1,0:T(8,128)(2,1)} %bitcast.10.refs_0_.g_ref), channel_id=1, source_target_pairs={{0,4},{1,5},{2,6},{3,7},{4,0},{5,1},{6,2},{7,3},{8,12},{9,13},{10,... | collective-permute-start | bytes 1572872 | tf_op jit(solution)/shard_map/ppermute | solution.py:72
  8.7 3.3 %all-to-all-start = ((f32[8,8,128]{2,1,0:T(8,128)}), f32[8,8,128]{2,1,0:T(8,128)S(1)}, u32[]{:S(2)}, u32[]{:S(2)}) async-start(f32[8,8,128]{2,1,0:T(8,128)} %broadcast_in_dim.15), calls=%async_computation | async-start | bytes 65536 | tf_op jit(solution)/shard_map/all_to_all | solution.py:473
  13.3 3.2 %shard_map.85 = (bf16[96,2048]{1,0:T(8,128)(2,1)S(1)}, bf16[96,2048]{1,0:T(8,128)(2,1)}, bf16[96,2048]{1,0:T(8,128)(2,1)}, bf16[96,2048]{1,0:T(8,128)(2,1)}) custom-call(f32[8,128]{1,0:T(8,128)S(1)} %pad_maximum_fusion.refs_0_, f32[8,128]{1,0:T(8,128)S(1)} %collective-permute-done.refs_1_, bf16[128,2048]{1,0:T(8,128)(2,1)} %slice_bitcast_fusion.refs_2_, ...), custom_call_target="tpu_custom_call" | custom-call | tf_op jit(solution)/shard_map/pallas_call | solution.py:36
  17.3 1.9 %collective-permute-start.6 = (bf16[96,2048]{1,0:T(8,128)(2,1)}, bf16[96,2048]{1,0:T(8,128)(2,1)}, u32[]{:S(2)}, u32[]{:S(2)}) collective-permute-start(bf16[96,2048]{1,0:T(8,128)(2,1)} %get-tuple-element.84), channel_id=1, source_target_pairs={{0,2},{1,3},{2,0},{3,1},{4,6},{5,7},{6,4},{7,5},{8,10},{9,11},{10,... | collective-permute-start | bytes 1179656 | tf_op jit(solution)/shard_map/ppermute | solution.py:72
  19.1 1.5 %collective-permute-start.7 = (bf16[96,2048]{1,0:T(8,128)(2,1)}, bf16[96,2048]{1,0:T(8,128)(2,1)}, u32[]{:S(2)}, u32[]{:S(2)}) collective-permute-start(bf16[96,2048]{1,0:T(8,128)(2,1)} %get-tuple-element.85), channel_id=1, source_target_pairs={{0,4},{1,5},{2,6},{3,7},{4,0},{5,1},{6,2},{7,3},{8,12},{9,13},{10,... | collective-permute-start | bytes 1179656 | tf_op jit(solution)/shard_map/ppermute | solution.py:72
  21.2 2.1 %shard_map.86 = (bf16[96,2048]{1,0:T(8,128)(2,1)S(1)}, bf16[96,2048]{1,0:T(8,128)(2,1)S(1)}, bf16[96,2048]{1,0:T(8,128)(2,1)S(1)}, bf16[96,2048]{1,0:T(8,128)(2,1)S(1)}) custom-call(f32[8,8,128]{2,1,0:T(8,128)S(1)} %all-to-all-done.meta_ref, bf16[128,2048]{1,0:T(8,128)(2,1)S(1)} %slice_bitcast_fusion.1.refs_0_, bf16[128,2048]{1,0:T(8,128)(2,1)} %collective-permute-done.2.refs_1_), custom_call_target="tpu_custom_call" | custom-call | tf_op jit(solution)/shard_map/pallas_call | solution.py:36
  23.5 1.5 %collective-permute-start.4 = (bf16[96,2048]{1,0:T(8,128)(2,1)S(1)}, bf16[96,2048]{1,0:T(8,128)(2,1)S(1)}, u32[]{:S(2)}, u32[]{:S(2)}) collective-permute-start(bf16[96,2048]{1,0:T(8,128)(2,1)S(1)} %get-tuple-element.90), channel_id=1, source_target_pairs={{0,4},{1,5},{2,6},{3,7},{4,0},{5,1},{6,2},{7,3},{8,12},{9,13},{10,... | collective-permute-start | bytes 1179656 | tf_op jit(solution)/shard_map/ppermute | solution.py:72
  25.2 2.2 %shard_map.90 = (bf16[96,2048]{1,0:T(8,128)(2,1)S(1)}, bf16[96,2048]{1,0:T(8,128)(2,1)S(1)}, bf16[96,2048]{1,0:T(8,128)(2,1)S(1)}, bf16[96,2048]{1,0:T(8,128)(2,1)S(1)}) custom-call(f32[8,8,128]{2,1,0:T(8,128)S(1)} %all-to-all-done.meta_ref, bf16[128,2048]{1,0:T(8,128)(2,1)} %bitcast.10.refs_0_.g_ref, bf16[128,2048]{1,0:T(8,128)(2,1)} %collective-permute-done.8.refs_1_), custom_call_target="tpu_custom_call" | custom-call | tf_op jit(solution)/shard_map/pallas_call | solution.py:36
  27.5 1.4 %collective-permute-done.6.refs_1_ = bf16[96,2048]{1,0:T(8,128)(2,1)} collective-permute-done((bf16[96,2048]{1,0:T(8,128)(2,1)}, bf16[96,2048]{1,0:T(8,128)(2,1)}, u32[]{:S(2)}, u32[]{:S(2)}) %collective-permute-start.6) | collective-permute-done | bytes 393248 | tf_op jit(solution)/shard_map/ppermute | solution.py:72
  28.9 2.5 %collective-permute-done.7.refs_2_ = bf16[96,2048]{1,0:T(8,128)(2,1)} collective-permute-done((bf16[96,2048]{1,0:T(8,128)(2,1)}, bf16[96,2048]{1,0:T(8,128)(2,1)}, u32[]{:S(2)}, u32[]{:S(2)}) %collective-permute-start.7) | collective-permute-done | bytes 393248 | tf_op jit(solution)/shard_map/ppermute | solution.py:72
  32.3 7.5 %collective-permute-done.4.refs_2_ = bf16[96,2048]{1,0:T(8,128)(2,1)S(1)} collective-permute-done((bf16[96,2048]{1,0:T(8,128)(2,1)S(1)}, bf16[96,2048]{1,0:T(8,128)(2,1)S(1)}, u32[]{:S(2)}, u32[]{:S(2)}) %collective-permute-start.4) | collective-permute-done | bytes 393248 | tf_op jit(solution)/shard_map/ppermute | solution.py:72
  39.8 6.3 %collective-permute-done.5.refs_3_ = bf16[96,2048]{1,0:T(8,128)(2,1)S(1)} collective-permute-done((bf16[96,2048]{1,0:T(8,128)(2,1)S(1)}, bf16[96,2048]{1,0:T(8,128)(2,1)S(1)}, u32[]{:S(2)}, u32[]{:S(2)}) %collective-permute-start.5) | collective-permute-done | bytes 393248 | tf_op jit(solution)/shard_map/ppermute | solution.py:72
  46.1 1.8 %shard_map.87 = (bf16[384,2048]{1,0:T(8,128)(2,1)S(1)}, bf16[384,704]{1,0:T(8,128)(2,1)S(1)}, f32[384,704]{1,0:T(8,128)S(1)}) custom-call(bf16[704,2048]{1,0:T(8,128)(2,1)S(1)} %bitcast.27, bf16[96,2048]{1,0:T(8,128)(2,1)S(1)} %get-tuple-element.92.refs_0_, bf16[96,2048]{1,0:T(8,128)(2,1)S(1)} %collective-permute-done.3.refs_1_, ...), custom_call_target="tpu_custom_call" | custom-call | tf_op jit(solution)/shard_map/pallas_call | solution.py:36
  47.9 1.2 copy-done.8
  49.1 3.3 %shard_map.91 = (bf16[384,2048]{1,0:T(8,128)(2,1)S(1)}, bf16[384,704]{1,0:T(8,128)(2,1)S(1)}, f32[384,128]{1,0:T(8,128)S(1)}, bf16[96,1024]{1,0:T(8,128)(2,1)S(1...) custom-call(bf16[704,2048]{1,0:T(8,128)(2,1)S(1)} %bitcast.28, ...), custom_call_target="tpu_custom_call" | custom-call | tf_op jit(solution)/shard_map/pallas_call | solution.py:36
  53.1 1.4 %collective-permute-start.13 = (bf16[96,1024]{1,0:T(8,128)(2,1)S(1)}, bf16[96,1024]{1,0:T(8,128)(2,1)S(1)}, u32[]{:S(2)}, u32[]{:S(2)}) collective-permute-start(bf16[96,1024]{1,0:T(8,128)(2,1)S(1)} %get-tuple-element.106), channel_id=1, source_target_pairs={{0,4},{1,5},{2,6},{3,7},{4,0},{5,1},{6,2},{7,3},{8,12},{9,13},{10,... | collective-permute-start | bytes 589832 | tf_op jit(solution)/shard_map/ppermute | solution.py:72
  54.4 1.5 %collective-permute-start.14 = (bf16[96,1024]{1,0:T(8,128)(2,1)S(1)}, bf16[96,1024]{1,0:T(8,128)(2,1)S(1)}, u32[]{:S(2)}, u32[]{:S(2)}) collective-permute-start(bf16[96,1024]{1,0:T(8,128)(2,1)S(1)} %get-tuple-element.107), channel_id=1, source_target_pairs={{0,6},{1,7},{2,4},{3,5},{4,2},{5,3},{6,0},{7,1},{8,14},{9,15},{10,... | collective-permute-start | bytes 589832 | tf_op jit(solution)/shard_map/ppermute | solution.py:72
  57.5 1.4 %collective-permute-start.17 = (bf16[96,1024]{1,0:T(8,128)(2,1)S(1)}, bf16[96,1024]{1,0:T(8,128)(2,1)S(1)}, u32[]{:S(2)}, u32[]{:S(2)}) collective-permute-start(bf16[96,1024]{1,0:T(8,128)(2,1)S(1)} %get-tuple-element.113), channel_id=1, source_target_pairs={{0,4},{1,5},{2,6},{3,7},{4,0},{5,1},{6,2},{7,3},{8,12},{9,13},{10,... | collective-permute-start | bytes 589832 | tf_op jit(solution)/shard_map/ppermute | solution.py:72
  58.9 1.4 %collective-permute-done.12.refs_1_ = bf16[96,1024]{1,0:T(8,128)(2,1)S(1)} collective-permute-done((bf16[96,1024]{1,0:T(8,128)(2,1)S(1)}, bf16[96,1024]{1,0:T(8,128)(2,1)S(1)}, u32[]{:S(2)}, u32[]{:S(2)}) %collective-permute-start.12) | collective-permute-done | bytes 196640 | tf_op jit(solution)/shard_map/ppermute | solution.py:72
  60.3 1.1 collective-permute-start.18
  61.4 2.5 %collective-permute-done.13.refs_2_ = bf16[96,1024]{1,0:T(8,128)(2,1)S(1)} collective-permute-done((bf16[96,1024]{1,0:T(8,128)(2,1)S(1)}, bf16[96,1024]{1,0:T(8,128)(2,1)S(1)}, u32[]{:S(2)}, u32[]{:S(2)}) %collective-permute-start.13) | collective-permute-done | bytes 196640 | tf_op jit(solution)/shard_map/ppermute | solution.py:72
  63.9 1.4 %collective-permute-done.14.refs_3_ = bf16[96,1024]{1,0:T(8,128)(2,1)S(1)} collective-permute-done((bf16[96,1024]{1,0:T(8,128)(2,1)S(1)}, bf16[96,1024]{1,0:T(8,128)(2,1)S(1)}, u32[]{:S(2)}, u32[]{:S(2)}) %collective-permute-start.14) | collective-permute-done | bytes 196640 | tf_op jit(solution)/shard_map/ppermute | solution.py:72
  65.8 1.1 shard_map.93.own_ref
  67.4 1.3 %collective-permute-start.22 = (bf16[128,1024]{1,0:T(8,128)(2,1)S(1)}, bf16[128,1024]{1,0:T(8,128)(2,1)S(1)}, u32[]{:S(2)}, u32[]{:S(2)}) collective-permute-start(bf16[128,1024]{1,0:T(8,128)(2,1)S(1)} %shard_map.94), channel_id=1, source_target_pairs={{8,0},{16,8},{24,16},{9,1},{17,9},{25,17},{10,2},{18,10},{26,18},{... | collective-permute-start | bytes 786440 | tf_op jit(solution)/shard_map/ppermute | solution.py:537
  68.7 3.6 %collective-permute-done.17.refs_2_ = bf16[96,1024]{1,0:T(8,128)(2,1)S(1)} collective-permute-done((bf16[96,1024]{1,0:T(8,128)(2,1)S(1)}, bf16[96,1024]{1,0:T(8,128)(2,1)S(1)}, u32[]{:S(2)}, u32[]{:S(2)}) %collective-permute-start.17) | collective-permute-done | bytes 196640 | tf_op jit(solution)/shard_map/ppermute | solution.py:72
  72.4 1.4 %collective-permute-done.18.refs_3_ = bf16[96,1024]{1,0:T(8,128)(2,1)S(1)} collective-permute-done((bf16[96,1024]{1,0:T(8,128)(2,1)S(1)}, bf16[96,1024]{1,0:T(8,128)(2,1)S(1)}, u32[]{:S(2)}, u32[]{:S(2)}) %collective-permute-start.18) | collective-permute-done | bytes 196640 | tf_op jit(solution)/shard_map/ppermute | solution.py:72
  74.2 1.1 shard_map.96.own_ref
  75.7 1.5 %collective-permute-start.21 = (bf16[128,1024]{1,0:T(8,128)(2,1)S(1)}, bf16[128,1024]{1,0:T(8,128)(2,1)S(1)}, u32[]{:S(2)}, u32[]{:S(2)}) collective-permute-start(bf16[128,1024]{1,0:T(8,128)(2,1)S(1)} %shard_map.97), channel_id=1, source_target_pairs={{8,0},{16,8},{24,16},{9,1},{17,9},{25,17},{10,2},{18,10},{26,18},{... | collective-permute-start | bytes 786440 | tf_op jit(solution)/shard_map/ppermute | solution.py:537
  77.2 1.8 %collective-permute-start.20 = (bf16[96,2048]{1,0:T(8,128)(2,1)}, bf16[96,2048]{1,0:T(8,128)(2,1)}, u32[]{:S(2)}, u32[]{:S(2)}) collective-permute-start(bf16[96,2048]{1,0:T(8,128)(2,1)} %get-tuple-element.121), channel_id=1, source_target_pairs={{0,6},{1,7},{2,4},{3,5},{4,2},{5,3},{6,0},{7,1},{8,14},{9,15},{10,... | collective-permute-start | bytes 1179656 | tf_op jit(solution)/shard_map/ppermute | solution.py:72
  79.2 1.3 %collective-permute-done.23.refs_0_ = bf16[128,1024]{1,0:T(8,128)(2,1)S(1)} collective-permute-done((bf16[128,1024]{1,0:T(8,128)(2,1)S(1)}, bf16[128,1024]{1,0:T(8,128)(2,1)S(1)}, u32[]{:S(2)}, u32[]{:S(2)}) %collective-permute-start.23) | collective-permute-done | bytes 262176 | tf_op jit(solution)/shard_map/ppermute | solution.py:72
  81.7 0.9 collective-permute-start.26
  82.6 1.7 %collective-permute-start.27 = (bf16[96,1024]{1,0:T(8,128)(2,1)S(1)}, bf16[96,1024]{1,0:T(8,128)(2,1)S(1)}, u32[]{:S(2)}, u32[]{:S(2)}) collective-permute-start(bf16[96,1024]{1,0:T(8,128)(2,1)S(1)} %get-tuple-element.127), channel_id=1, source_target_pairs={{0,6},{1,7},{2,4},{3,5},{4,2},{5,3},{6,0},{7,1},{8,14},{9,15},{10,... | collective-permute-start | bytes 589832 | tf_op jit(solution)/shard_map/ppermute | solution.py:72
  84.3 1.6 %collective-permute-done.21.raw_ref = bf16[128,1024]{1,0:T(8,128)(2,1)S(1)} collective-permute-done((bf16[128,1024]{1,0:T(8,128)(2,1)S(1)}, bf16[128,1024]{1,0:T(8,128)(2,1)S(1)}, u32[]{:S(2)}, u32[]{:S(2)}) %collective-permute-start.21) | collective-permute-done | bytes 262176 | tf_op jit(solution)/shard_map/ppermute | solution.py:537
  86.2 1.3 %collective-permute-done.24.refs_0_ = bf16[128,1024]{1,0:T(8,128)(2,1)S(1)} collective-permute-done((bf16[128,1024]{1,0:T(8,128)(2,1)S(1)}, bf16[128,1024]{1,0:T(8,128)(2,1)S(1)}, u32[]{:S(2)}, u32[]{:S(2)}) %collective-permute-start.24) | collective-permute-done | bytes 262176 | tf_op jit(solution)/shard_map/ppermute | solution.py:72
  88.6 1.9 %collective-permute-done.20.refs_3_ = bf16[96,2048]{1,0:T(8,128)(2,1)} collective-permute-done((bf16[96,2048]{1,0:T(8,128)(2,1)}, bf16[96,2048]{1,0:T(8,128)(2,1)}, u32[]{:S(2)}, u32[]{:S(2)}) %collective-permute-start.20) | collective-permute-done | bytes 393248 | tf_op jit(solution)/shard_map/ppermute | solution.py:72
  90.5 1.1 collective-permute-start.29
  91.6 2.6 %collective-permute-done.25.refs_1_ = bf16[96,1024]{1,0:T(8,128)(2,1)S(1)} collective-permute-done((bf16[96,1024]{1,0:T(8,128)(2,1)S(1)}, bf16[96,1024]{1,0:T(8,128)(2,1)S(1)}, u32[]{:S(2)}, u32[]{:S(2)}) %collective-permute-start.25) | collective-permute-done | bytes 196640 | tf_op jit(solution)/shard_map/ppermute | solution.py:72
  94.2 1.1 collective-permute-start.30
  95.4 3.1 %shard_map.102 = (bf16[384,2048]{1,0:T(8,128)(2,1)S(1)}, bf16[384,704]{1,0:T(8,128)(2,1)S(1)}, f32[384,704]{1,0:T(8,128)S(1)}) custom-call(bf16[704,2048]{1,0:T(8,128)(2,1)S(1)} %bitcast.29, bf16[96,2048]{1,0:T(8,128)(2,1)S(1)} %copy-done.16, bf16[96,2048]{1,0:T(8,128)(2,1)} %collective-permute-done.6.refs_1_, ...), custom_call_target="tpu_custom_call" | custom-call | tf_op jit(solution)/shard_map/pallas_call | solution.py:36
  98.5 1.2 copy-done.9
  99.7 3.1 %shard_map.103 = (f32[384,704]{1,0:T(8,128)S(1)}, bf16[704,2048]{1,0:T(8,128)(2,1)}) custom-call(bf16[704,2048]{1,0:T(8,128)(2,1)S(1)} %bitcast.31, bf16[384,704]{1,0:T(8,128)(2,1)S(1)} %copy-done.4, bf16[384,704]{1,0:T(8,128)(2,1)S(1)} %get-tuple-element.137.hid1_ref.hid_ref, f32[384,128]{1,0:T(8,128)S(1)} %get-tuple-element.99.prob_ref, ...), custom_call_target="tpu_custom_call" | custom-call | tf_op jit(solution)/shard_map/pallas_call | solution.py:343
  102.9 3.6 %collective-permute-done.30.refs_3_ = bf16[96,1024]{1,0:T(8,128)(2,1)S(1)} collective-permute-done((bf16[96,1024]{1,0:T(8,128)(2,1)S(1)}, bf16[96,1024]{1,0:T(8,128)(2,1)S(1)}, u32[]{:S(2)}, u32[]{:S(2)}) %collective-permute-start.30) | collective-permute-done | bytes 196640 | tf_op jit(solution)/shard_map/ppermute | solution.py:72
  107.4 1.6 %shard_map.104 = (bf16[384,1024]{1,0:T(8,128)(2,1)S(1)}, bf16[384,704]{1,0:T(8,128)(2,1)S(1)}, bf16[384,128]{1,0:T(8,128)(2,1)}) custom-call(bf16[704,2048]{1,0:T(8,128)(2,1)S(1)} %bitcast.32, bf16[384,704]{1,0:T(8,128)(2,1)S(1)} %get-tuple-element.137.hid1_ref.hid_ref, f32[384,704]{1,0:T(8,128)S(1)} %get-tuple-element.142.slope_ref, ...), custom_call_target="tpu_custom_call" | custom-call | tf_op jit(solution)/shard_map/pallas_call | solution.py:36
  110.8 3.4 %all-to-all-start.1 = ((bf16[8,48,128]{2,1,0:T(8,128)(2,1)}), bf16[8,48,128]{2,1,0:T(8,128)(2,1)S(1)}, u32[]{:S(2)}, u32[]{:S(2)}) async-start(bf16[8,48,128]{2,1,0:T(8,128)(2,1)} %bitcast.13), calls=%async_computation.1 | async-start | bytes 196608 | tf_op jit(solution)/shard_map/all_to_all | solution.py:259
  114.2 7.0 %shard_map.105 = (bf16[704,2048]{1,0:T(8,128)(2,1)}, bf16[704,2048]{1,0:T(8,128)(2,1)}) custom-call(bf16[704,2048]{1,0:T(8,128)(2,1)} %get-tuple-element.139._, f32[384,128]{1,0:T(8,128)} %copy-done.6, bf16[384,2048]{1,0:T(8,128)(2,1)} %copy-done.8, bf16[384,2048]{1,0:T(8,128)(2,1)} %copy-done.9, ...), custom_call_target="tpu_custom_call", output_to_operand_aliasing={{1}: (0, {})} | custom-call | tf_op jit(solution)/shard_map/pallas_call | solution.py:422
  (92 shorter events, 15.4 us)
Async XLA Ops:
  0.6 7.5 %copy-start.21 = (s32[1,2,128,2]{2,3,1,0:T(2,128)S(1)}, s32[1,2,128,2]{2,3,1,0:T(2,128)}, u32[]{:S(2)}) copy-start(s32[1,2,128,2]{2,3,1,0:T(2,128)} %param.11) | copy-start | bytes 6148
  0.6 7.5 %copy-start.22 = (bf16[1,2,128,2]{2,3,1,0:T(2,128)(2,1)S(1)}, bf16[1,2,128,2]{2,3,1,0:T(2,128)(2,1)}, u32[]{:S(2)}) copy-start(bf16[1,2,128,2]{2,3,1,0:T(2,128)(2,1)} %param.10) | copy-start | bytes 3076
  3.6 9.7 %collective-permute-start.1 = (bf16[128,2048]{1,0:T(8,128)(2,1)}, bf16[128,2048]{1,0:T(8,128)(2,1)}, u32[]{:S(2)}, u32[]{:S(2)}) collective-permute-start(bf16[128,2048]{1,0:T(8,128)(2,1)} %slice_bitcast_fusion.refs_2_), channel_id=1, source_target_pairs={{0,1},{1,0},{2,3},{3,2},{4,5},{5,4},{6,7},{7,6},{8,9},{9,8},{10,11... | collective-permute-start | bytes 1572872 | tf_op jit(solution)/shard_map/ppermute | solution.py:72
  4.1 17.1 %collective-permute-start.2 = (bf16[128,2048]{1,0:T(8,128)(2,1)S(1)}, bf16[128,2048]{1,0:T(8,128)(2,1)}, u32[]{:S(2)}, u32[]{:S(2)}) collective-permute-start(bf16[128,2048]{1,0:T(8,128)(2,1)S(1)} %slice_bitcast_fusion.1.refs_0_), channel_id=1, source_target_pairs={{0,2},{1,3},{2,0},{3,1},{4,6},{5,7},{6,4},{7,5},{8,10},{9,11},{10,... | collective-permute-start | bytes 1572872 | tf_op jit(solution)/shard_map/ppermute | solution.py:72
  6.6 18.4 %collective-permute-start.8 = (bf16[128,2048]{1,0:T(8,128)(2,1)}, bf16[128,2048]{1,0:T(8,128)(2,1)}, u32[]{:S(2)}, u32[]{:S(2)}) collective-permute-start(bf16[128,2048]{1,0:T(8,128)(2,1)} %bitcast.10.refs_0_.g_ref), channel_id=1, source_target_pairs={{0,4},{1,5},{2,6},{3,7},{4,0},{5,1},{6,2},{7,3},{8,12},{9,13},{10,... | collective-permute-start | bytes 1572872 | tf_op jit(solution)/shard_map/ppermute | solution.py:72
  8.7 12.5 %all-to-all-start = ((f32[8,8,128]{2,1,0:T(8,128)}), f32[8,8,128]{2,1,0:T(8,128)S(1)}, u32[]{:S(2)}, u32[]{:S(2)}) async-start(f32[8,8,128]{2,1,0:T(8,128)} %broadcast_in_dim.15), calls=%async_computation | async-start | bytes 65536 | tf_op jit(solution)/shard_map/all_to_all | solution.py:473
  12.1 34.1 %copy-start = (bf16[1,1,704,2048]{3,2,1,0:T(8,128)(2,1)S(1)}, bf16[1,1,704,2048]{3,2,1,0:T(8,128)(2,1)}, u32[]{:S(2)}) copy-start(bf16[1,1,704,2048]{3,2,1,0:T(8,128)(2,1)} %param.8) | copy-start | bytes 8650756
  12.1 1.2 %collective-permute-start = (f32[8,128]{1,0:T(8,128)S(1)}, f32[8,128]{1,0:T(8,128)S(1)}, u32[]{:S(2)}, u32[]{:S(2)}) collective-permute-start(f32[8,128]{1,0:T(8,128)S(1)} %pad_maximum_fusion.refs_0_), channel_id=1, source_target_pairs={{0,1},{1,0},{2,3},{3,2},{4,5},{5,4},{6,7},{7,6},{8,9},{9,8},{10,11... | collective-permute-start | bytes 12296 | tf_op jit(solution)/shard_map/ppermute | solution.py:72
  17.3 11.7 %collective-permute-start.6 = (bf16[96,2048]{1,0:T(8,128)(2,1)}, bf16[96,2048]{1,0:T(8,128)(2,1)}, u32[]{:S(2)}, u32[]{:S(2)}) collective-permute-start(bf16[96,2048]{1,0:T(8,128)(2,1)} %get-tuple-element.84), channel_id=1, source_target_pairs={{0,2},{1,3},{2,0},{3,1},{4,6},{5,7},{6,4},{7,5},{8,10},{9,11},{10,... | collective-permute-start | bytes 1179656 | tf_op jit(solution)/shard_map/ppermute | solution.py:72
  19.1 12.3 %collective-permute-start.7 = (bf16[96,2048]{1,0:T(8,128)(2,1)}, bf16[96,2048]{1,0:T(8,128)(2,1)}, u32[]{:S(2)}, u32[]{:S(2)}) collective-permute-start(bf16[96,2048]{1,0:T(8,128)(2,1)} %get-tuple-element.85), channel_id=1, source_target_pairs={{0,4},{1,5},{2,6},{3,7},{4,0},{5,1},{6,2},{7,3},{8,12},{9,13},{10,... | collective-permute-start | bytes 1179656 | tf_op jit(solution)/shard_map/ppermute | solution.py:72
  21.2 34.8 %copy-start.10 = (f32[8,8,128]{2,1,0:T(8,128)}, f32[8,8,128]{2,1,0:T(8,128)S(1)}, u32[]{:S(2)}) copy-start(f32[8,8,128]{2,1,0:T(8,128)S(1)} %all-to-all-done.meta_ref) | copy-start | bytes 98308
  23.3 8.3 %collective-permute-start.3 = (bf16[96,2048]{1,0:T(8,128)(2,1)S(1)}, bf16[96,2048]{1,0:T(8,128)(2,1)S(1)}, u32[]{:S(2)}, u32[]{:S(2)}) collective-permute-start(bf16[96,2048]{1,0:T(8,128)(2,1)S(1)} %get-tuple-element.89), channel_id=1, source_target_pairs={{0,1},{1,0},{2,3},{3,2},{4,5},{5,4},{6,7},{7,6},{8,9},{9,8},{10,11... | collective-permute-start | bytes 1179656 | tf_op jit(solution)/shard_map/ppermute | solution.py:72
  23.5 16.2 %collective-permute-start.4 = (bf16[96,2048]{1,0:T(8,128)(2,1)S(1)}, bf16[96,2048]{1,0:T(8,128)(2,1)S(1)}, u32[]{:S(2)}, u32[]{:S(2)}) collective-permute-start(bf16[96,2048]{1,0:T(8,128)(2,1)S(1)} %get-tuple-element.90), channel_id=1, source_target_pairs={{0,4},{1,5},{2,6},{3,7},{4,0},{5,1},{6,2},{7,3},{8,12},{9,13},{10,... | collective-permute-start | bytes 1179656 | tf_op jit(solution)/shard_map/ppermute | solution.py:72
  25.0 21.1 %collective-permute-start.5 = (bf16[96,2048]{1,0:T(8,128)(2,1)S(1)}, bf16[96,2048]{1,0:T(8,128)(2,1)S(1)}, u32[]{:S(2)}, u32[]{:S(2)}) collective-permute-start(bf16[96,2048]{1,0:T(8,128)(2,1)S(1)} %get-tuple-element.91), channel_id=1, source_target_pairs={{0,5},{1,4},{2,7},{3,6},{4,1},{5,0},{6,3},{7,2},{8,13},{9,12},{10,... | collective-permute-start | bytes 1179656 | tf_op jit(solution)/shard_map/ppermute | solution.py:72
  28.9 20.2 %collective-permute-start.9 = (bf16[96,2048]{1,0:T(8,128)(2,1)S(1)}, bf16[96,2048]{1,0:T(8,128)(2,1)S(1)}, u32[]{:S(2)}, u32[]{:S(2)}) collective-permute-start(bf16[96,2048]{1,0:T(8,128)(2,1)S(1)} %get-tuple-element.101), channel_id=1, source_target_pairs={{0,1},{1,0},{2,3},{3,2},{4,5},{5,4},{6,7},{7,6},{8,9},{9,8},{10,11... | collective-permute-start | bytes 1179656 | tf_op jit(solution)/shard_map/ppermute | solution.py:72
  31.5 17.7 %collective-permute-start.10 = (bf16[96,2048]{1,0:T(8,128)(2,1)S(1)}, bf16[96,2048]{1,0:T(8,128)(2,1)S(1)}, u32[]{:S(2)}, u32[]{:S(2)}) collective-permute-start(bf16[96,2048]{1,0:T(8,128)(2,1)S(1)} %get-tuple-element.102), channel_id=1, source_target_pairs={{0,2},{1,3},{2,0},{3,1},{4,6},{5,7},{6,4},{7,5},{8,10},{9,11},{10,... | collective-permute-start | bytes 1179656 | tf_op jit(solution)/shard_map/ppermute | solution.py:72
  31.6 17.5 %collective-permute-start.11 = (bf16[96,2048]{1,0:T(8,128)(2,1)S(1)}, bf16[96,2048]{1,0:T(8,128)(2,1)S(1)}, u32[]{:S(2)}, u32[]{:S(2)}) collective-permute-start(bf16[96,2048]{1,0:T(8,128)(2,1)S(1)} %get-tuple-element.103), channel_id=1, source_target_pairs={{0,3},{1,2},{2,1},{3,0},{4,7},{5,6},{6,5},{7,4},{8,11},{9,10},{10,... | collective-permute-start | bytes 1179656 | tf_op jit(solution)/shard_map/ppermute | solution.py:72
  32.2 15.7 %copy-start.17 = (bf16[384,128]{1,0:T(8,128)(2,1)}, bf16[384,128]{1,0:T(8,128)(2,1)S(1)}, u32[]{:S(2)}) copy-start(bf16[384,128]{1,0:T(8,128)(2,1)S(1)} %get-tuple-element.154.hot0_ref) | copy-start | bytes 294916
  32.3 15.7 %copy-start.19 = (bf16[384,128]{1,0:T(8,128)(2,1)}, bf16[384,128]{1,0:T(8,128)(2,1)S(1)}, u32[]{:S(2)}) copy-start(bf16[384,128]{1,0:T(8,128)(2,1)S(1)} %get-tuple-element.155.hot1_ref) | copy-start | bytes 294916
  32.3 67.4 %copy-start.6 = (f32[384,128]{1,0:T(8,128)}, f32[384,128]{1,0:T(8,128)S(1)}, u32[]{:S(2)}) copy-start(f32[384,128]{1,0:T(8,128)S(1)} %get-tuple-element.99.prob_ref) | copy-start | bytes 589828
  52.4 14.5 %copy-start.13 = (bf16[384,704]{1,0:T(8,128)(2,1)}, bf16[384,704]{1,0:T(8,128)(2,1)S(1)}, u32[]{:S(2)}) copy-start(bf16[384,704]{1,0:T(8,128)(2,1)S(1)} %get-tuple-element.150.gp0_ref) | copy-start | bytes 1622020
  52.4 47.2 %copy-start.2 = (bf16[384,2048]{1,0:T(8,128)(2,1)}, bf16[384,2048]{1,0:T(8,128)(2,1)S(1)}, u32[]{:S(2)}) copy-start(bf16[384,2048]{1,0:T(8,128)(2,1)S(1)} %get-tuple-element.138.g0_ref) | copy-start | bytes 4718596
  52.4 7.8 %collective-permute-start.12 = (bf16[96,1024]{1,0:T(8,128)(2,1)S(1)}, bf16[96,1024]{1,0:T(8,128)(2,1)S(1)}, u32[]{:S(2)}, u32[]{:S(2)}) collective-permute-start(bf16[96,1024]{1,0:T(8,128)(2,1)S(1)} %get-tuple-element.105), channel_id=1, source_target_pairs={{0,2},{1,3},{2,0},{3,1},{4,6},{5,7},{6,4},{7,5},{8,10},{9,11},{10,... | collective-permute-start | bytes 589832 | tf_op jit(solution)/shard_map/ppermute | solution.py:72
  53.1 10.9 %collective-permute-start.13 = (bf16[96,1024]{1,0:T(8,128)(2,1)S(1)}, bf16[96,1024]{1,0:T(8,128)(2,1)S(1)}, u32[]{:S(2)}, u32[]{:S(2)}) collective-permute-start(bf16[96,1024]{1,0:T(8,128)(2,1)S(1)} %get-tuple-element.106), channel_id=1, source_target_pairs={{0,4},{1,5},{2,6},{3,7},{4,0},{5,1},{6,2},{7,3},{8,12},{9,13},{10,... | collective-permute-start | bytes 589832 | tf_op jit(solution)/shard_map/ppermute | solution.py:72
  54.4 10.9 %collective-permute-start.14 = (bf16[96,1024]{1,0:T(8,128)(2,1)S(1)}, bf16[96,1024]{1,0:T(8,128)(2,1)S(1)}, u32[]{:S(2)}, u32[]{:S(2)}) collective-permute-start(bf16[96,1024]{1,0:T(8,128)(2,1)S(1)} %get-tuple-element.107), channel_id=1, source_target_pairs={{0,6},{1,7},{2,4},{3,5},{4,2},{5,3},{6,0},{7,1},{8,14},{9,15},{10,... | collective-permute-start | bytes 589832 | tf_op jit(solution)/shard_map/ppermute | solution.py:72
  56.9 11.9 %collective-permute-start.16 = (bf16[96,1024]{1,0:T(8,128)(2,1)S(1)}, bf16[96,1024]{1,0:T(8,128)(2,1)S(1)}, u32[]{:S(2)}, u32[]{:S(2)}) collective-permute-start(bf16[96,1024]{1,0:T(8,128)(2,1)S(1)} %get-tuple-element.112), channel_id=1, source_target_pairs={{0,2},{1,3},{2,0},{3,1},{4,6},{5,7},{6,4},{7,5},{8,10},{9,11},{10,... | collective-permute-start | bytes 589832 | tf_op jit(solution)/shard_map/ppermute | solution.py:72
  57.5 14.9 %collective-permute-start.17 = (bf16[96,1024]{1,0:T(8,128)(2,1)S(1)}, bf16[96,1024]{1,0:T(8,128)(2,1)S(1)}, u32[]{:S(2)}, u32[]{:S(2)}) collective-permute-start(bf16[96,1024]{1,0:T(8,128)(2,1)S(1)} %get-tuple-element.113), channel_id=1, source_target_pairs={{0,4},{1,5},{2,6},{3,7},{4,0},{5,1},{6,2},{7,3},{8,12},{9,13},{10,... | collective-permute-start | bytes 589832 | tf_op jit(solution)/shard_map/ppermute | solution.py:72
  60.3 13.5 %collective-permute-start.18 = (bf16[96,1024]{1,0:T(8,128)(2,1)S(1)}, bf16[96,1024]{1,0:T(8,128)(2,1)S(1)}, u32[]{:S(2)}, u32[]{:S(2)}) collective-permute-start(bf16[96,1024]{1,0:T(8,128)(2,1)S(1)} %get-tuple-element.114), channel_id=1, source_target_pairs={{0,6},{1,7},{2,4},{3,5},{4,2},{5,3},{6,0},{7,1},{8,14},{9,15},{10,... | collective-permute-start | bytes 589832 | tf_op jit(solution)/shard_map/ppermute | solution.py:72
  65.7 1.6 %collective-permute-start.15 = (bf16[128,1024]{1,0:T(8,128)(2,1)S(1)}, bf16[128,1024]{1,0:T(8,128)(2,1)S(1)}, u32[]{:S(2)}, u32[]{:S(2)}) collective-permute-start(bf16[128,1024]{1,0:T(8,128)(2,1)S(1)} %get-tuple-element.109), channel_id=1, source_target_pairs={{0,1},{1,0},{2,3},{3,2},{4,5},{5,4},{6,7},{7,6},{8,9},{9,8},{10,11... | collective-permute-start | bytes 786440 | tf_op jit(solution)/shard_map/ppermute | solution.py:72
  67.4 11.6 %collective-permute-start.22 = (bf16[128,1024]{1,0:T(8,128)(2,1)S(1)}, bf16[128,1024]{1,0:T(8,128)(2,1)S(1)}, u32[]{:S(2)}, u32[]{:S(2)}) collective-permute-start(bf16[128,1024]{1,0:T(8,128)(2,1)S(1)} %shard_map.94), channel_id=1, source_target_pairs={{8,0},{16,8},{24,16},{9,1},{17,9},{25,17},{10,2},{18,10},{26,18},{... | collective-permute-start | bytes 786440 | tf_op jit(solution)/shard_map/ppermute | solution.py:537
  74.1 1.6 %collective-permute-start.19 = (bf16[128,1024]{1,0:T(8,128)(2,1)S(1)}, bf16[128,1024]{1,0:T(8,128)(2,1)S(1)}, u32[]{:S(2)}, u32[]{:S(2)}) collective-permute-start(bf16[128,1024]{1,0:T(8,128)(2,1)S(1)} %get-tuple-element.120), channel_id=1, source_target_pairs={{0,1},{1,0},{2,3},{3,2},{4,5},{5,4},{6,7},{7,6},{8,9},{9,8},{10,11... | collective-permute-start | bytes 786440 | tf_op jit(solution)/shard_map/ppermute | solution.py:72
  75.7 10.2 %collective-permute-start.21 = (bf16[128,1024]{1,0:T(8,128)(2,1)S(1)}, bf16[128,1024]{1,0:T(8,128)(2,1)S(1)}, u32[]{:S(2)}, u32[]{:S(2)}) collective-permute-start(bf16[128,1024]{1,0:T(8,128)(2,1)S(1)} %shard_map.97), channel_id=1, source_target_pairs={{8,0},{16,8},{24,16},{9,1},{17,9},{25,17},{10,2},{18,10},{26,18},{... | collective-permute-start | bytes 786440 | tf_op jit(solution)/shard_map/ppermute | solution.py:537
  77.2 13.3 %collective-permute-start.20 = (bf16[96,2048]{1,0:T(8,128)(2,1)}, bf16[96,2048]{1,0:T(8,128)(2,1)}, u32[]{:S(2)}, u32[]{:S(2)}) collective-permute-start(bf16[96,2048]{1,0:T(8,128)(2,1)} %get-tuple-element.121), channel_id=1, source_target_pairs={{0,6},{1,7},{2,4},{3,5},{4,2},{5,3},{6,0},{7,1},{8,14},{9,15},{10,... | collective-permute-start | bytes 1179656 | tf_op jit(solution)/shard_map/ppermute | solution.py:72
  79.0 1.5 %collective-permute-start.23 = (bf16[128,1024]{1,0:T(8,128)(2,1)S(1)}, bf16[128,1024]{1,0:T(8,128)(2,1)S(1)}, u32[]{:S(2)}, u32[]{:S(2)}) collective-permute-start(bf16[128,1024]{1,0:T(8,128)(2,1)S(1)} %collective-permute-done.22.raw_ref), channel_id=1, source_target_pairs={{0,1},{1,0},{2,3},{3,2},{4,5},{5,4},{6,7},{7,6},{8,9},{9,8},{10,11... | collective-permute-start | bytes 786440 | tf_op jit(solution)/shard_map/ppermute | solution.py:72
  80.8 13.5 %collective-permute-start.25 = (bf16[96,1024]{1,0:T(8,128)(2,1)S(1)}, bf16[96,1024]{1,0:T(8,128)(2,1)S(1)}, u32[]{:S(2)}, u32[]{:S(2)}) collective-permute-start(bf16[96,1024]{1,0:T(8,128)(2,1)S(1)} %get-tuple-element.125), channel_id=1, source_target_pairs={{0,2},{1,3},{2,0},{3,1},{4,6},{5,7},{6,4},{7,5},{8,10},{9,11},{10,... | collective-permute-start | bytes 589832 | tf_op jit(solution)/shard_map/ppermute | solution.py:72
  81.7 17.9 %collective-permute-start.26 = (bf16[96,1024]{1,0:T(8,128)(2,1)S(1)}, bf16[96,1024]{1,0:T(8,128)(2,1)S(1)}, u32[]{:S(2)}, u32[]{:S(2)}) collective-permute-start(bf16[96,1024]{1,0:T(8,128)(2,1)S(1)} %get-tuple-element.126), channel_id=1, source_target_pairs={{0,4},{1,5},{2,6},{3,7},{4,0},{5,1},{6,2},{7,3},{8,12},{9,13},{10,... | collective-permute-start | bytes 589832 | tf_op jit(solution)/shard_map/ppermute | solution.py:72
  82.6 17.0 %collective-permute-start.27 = (bf16[96,1024]{1,0:T(8,128)(2,1)S(1)}, bf16[96,1024]{1,0:T(8,128)(2,1)S(1)}, u32[]{:S(2)}, u32[]{:S(2)}) collective-permute-start(bf16[96,1024]{1,0:T(8,128)(2,1)S(1)} %get-tuple-element.127), channel_id=1, source_target_pairs={{0,6},{1,7},{2,4},{3,5},{4,2},{5,3},{6,0},{7,1},{8,14},{9,15},{10,... | collective-permute-start | bytes 589832 | tf_op jit(solution)/shard_map/ppermute | solution.py:72
  86.0 1.5 %collective-permute-start.24 = (bf16[128,1024]{1,0:T(8,128)(2,1)S(1)}, bf16[128,1024]{1,0:T(8,128)(2,1)S(1)}, u32[]{:S(2)}, u32[]{:S(2)}) collective-permute-start(bf16[128,1024]{1,0:T(8,128)(2,1)S(1)} %collective-permute-done.21.raw_ref), channel_id=1, source_target_pairs={{0,1},{1,0},{2,3},{3,2},{4,5},{5,4},{6,7},{7,6},{8,9},{9,8},{10,11... | collective-permute-start | bytes 786440 | tf_op jit(solution)/shard_map/ppermute | solution.py:72
  86.0 9.4 %copy-start.16 = (bf16[96,2048]{1,0:T(8,128)(2,1)S(1)}, bf16[96,2048]{1,0:T(8,128)(2,1)}, u32[]{:S(2)}) copy-start(bf16[96,2048]{1,0:T(8,128)(2,1)} %copy-done.15) | copy-start | bytes 1179652
  87.7 15.0 %collective-permute-start.28 = (bf16[96,1024]{1,0:T(8,128)(2,1)S(1)}, bf16[96,1024]{1,0:T(8,128)(2,1)S(1)}, u32[]{:S(2)}, u32[]{:S(2)}) collective-permute-start(bf16[96,1024]{1,0:T(8,128)(2,1)S(1)} %get-tuple-element.130), channel_id=1, source_target_pairs={{0,2},{1,3},{2,0},{3,1},{4,6},{5,7},{6,4},{7,5},{8,10},{9,11},{10,... | collective-permute-start | bytes 589832 | tf_op jit(solution)/shard_map/ppermute | solution.py:72
  90.5 12.4 %collective-permute-start.29 = (bf16[96,1024]{1,0:T(8,128)(2,1)S(1)}, bf16[96,1024]{1,0:T(8,128)(2,1)S(1)}, u32[]{:S(2)}, u32[]{:S(2)}) collective-permute-start(bf16[96,1024]{1,0:T(8,128)(2,1)S(1)} %get-tuple-element.131), channel_id=1, source_target_pairs={{0,4},{1,5},{2,6},{3,7},{4,0},{5,1},{6,2},{7,3},{8,12},{9,13},{10,... | collective-permute-start | bytes 589832 | tf_op jit(solution)/shard_map/ppermute | solution.py:72
  94.2 12.2 %collective-permute-start.30 = (bf16[96,1024]{1,0:T(8,128)(2,1)S(1)}, bf16[96,1024]{1,0:T(8,128)(2,1)S(1)}, u32[]{:S(2)}, u32[]{:S(2)}) collective-permute-start(bf16[96,1024]{1,0:T(8,128)(2,1)S(1)} %get-tuple-element.132), channel_id=1, source_target_pairs={{0,6},{1,7},{2,4},{3,5},{4,2},{5,3},{6,0},{7,1},{8,14},{9,15},{10,... | collective-permute-start | bytes 589832 | tf_op jit(solution)/shard_map/ppermute | solution.py:72
  95.4 4.3 %copy-start.4 = (bf16[384,704]{1,0:T(8,128)(2,1)S(1)}, bf16[384,704]{1,0:T(8,128)(2,1)}, u32[]{:S(2)}) copy-start(bf16[384,704]{1,0:T(8,128)(2,1)} %copy-done.3) | copy-start | bytes 1622020
  99.6 6.9 %copy-start.5 = (bf16[384,704]{1,0:T(8,128)(2,1)}, bf16[384,704]{1,0:T(8,128)(2,1)S(1)}, u32[]{:S(2)}) copy-start(bf16[384,704]{1,0:T(8,128)(2,1)S(1)} %get-tuple-element.137.hid1_ref.hid_ref) | copy-start | bytes 1622020
  110.8 10.4 %all-to-all-start.1 = ((bf16[8,48,128]{2,1,0:T(8,128)(2,1)}), bf16[8,48,128]{2,1,0:T(8,128)(2,1)S(1)}, u32[]{:S(2)}, u32[]{:S(2)}) async-start(bf16[8,48,128]{2,1,0:T(8,128)(2,1)} %bitcast.13), calls=%async_computation.1 | async-start | bytes 196608 | tf_op jit(solution)/shard_map/all_to_all | solution.py:259
  114.2 7.1 %copy-start.11 = (f32[8,8,128]{2,1,0:T(8,128)S(1)}, f32[8,8,128]{2,1,0:T(8,128)}, u32[]{:S(2)}) copy-start(f32[8,8,128]{2,1,0:T(8,128)} %copy-done.10) | copy-start | bytes 98308
  114.2 7.1 %copy-start.18 = (bf16[384,128]{1,0:T(8,128)(2,1)S(1)}, bf16[384,128]{1,0:T(8,128)(2,1)}, u32[]{:S(2)}) copy-start(bf16[384,128]{1,0:T(8,128)(2,1)} %copy-done.17) | copy-start | bytes 294916
  114.2 7.1 %copy-start.20 = (bf16[384,128]{1,0:T(8,128)(2,1)S(1)}, bf16[384,128]{1,0:T(8,128)(2,1)}, u32[]{:S(2)}) copy-start(bf16[384,128]{1,0:T(8,128)(2,1)} %copy-done.19) | copy-start | bytes 294916
  (8 other events, 12.1 us)

commit v6 on v5

--- a/solution.py
+++ b/solution.py
@@ -14,6 +14,9 @@
 HALVES = len(AXES)
 TILES = 2
 LONG = 10**11
+LATE_LIMIT = 32 * 1024 * 1024
+X0, G0, X1, G1, HID0, HID1, GP0, GP1, COLS = range(9)
+PAD_BYTES = 66 * 1024 * 1024
 VMEM_LIMIT = 20 * 1024 * 1024
 f32 = jnp.float32
 bf16 = jnp.bfloat16
@@ -29,13 +32,21 @@
 
 def cost(args, outs, flops):
     size = sum(a.size * a.dtype.itemsize for a in list(args) + list(outs))
-    return pl.CostEstimate(flops=flops if flops == LONG else 0, bytes_accessed=0, transcendentals=0)
-
-
-def call(kernel, outs, *args, flops=0, scratch=()):
+    return pl.CostEstimate(flops=flops if flops == LONG else 0, bytes_accessed=size * 64, transcendentals=0)
+
+
+def in_hbm(ref):
+    return pl.BlockSpec(memory_space=pltpu.HBM)
+
+
+def call(kernel, outs, *args, flops=0, scratch=(), pad=None, pad_out=False):
+    specs = [pl.BlockSpec() if n != pad else in_hbm(a) for n, a in enumerate(args)]
     return pl.pallas_call(
         kernel,
         out_shape=outs,
+        in_specs=specs,
+        out_specs=[in_hbm(o) if pad_out and n == 0 else pl.BlockSpec() for n, o in enumerate(outs)],
+        input_output_aliases={pad: 0} if pad is not None and pad_out else {},
         scratch_shapes=scratch,
         compiler_params=pltpu.CompilerParams(vmem_limit_bytes=VMEM_LIMIT),
         cost_estimate=cost(args, outs, flops),
@@ -121,7 +132,7 @@
         probs = sum(n * meta_ref[:, 2 * topk + i, :] for n, i in zip(named, at))
         column = jnp.sum(hot * dot(rep, probs.astype(bf16), 1, 0), axis=1, keepdims=True)
         columns = jnp.where(lane == k, column, columns)
-    prob_ref[...] = columns
+    prob_ref[...] = columns.astype(bf16)
 
 
 def block_masks(plane, capacity, ranks, ids, experts):
@@ -157,7 +168,7 @@
     for s in range(count):
         hot = block_masks(plane, capacity, ranks, refs[s][...], targets)
         picked = dot(hot.astype(bf16), refs[count + s][...], 1, 0).astype(bf16)
-        for i, out_ref in enumerate(refs[2 * count :]):
+        for i, out_ref in enumerate(refs[2 * count + 1 :]):
             out_ref[s * capacity : (s + 1) * capacity, :] = picked[i * capacity : (i + 1) * capacity]
 
 
@@ -183,14 +194,15 @@
     return ranks, plane.along(axis), [plane.back(t) for t in plane.across(axis)]
 
 
-def picked_rows(plane, capacity, ranks, axis, value, meta, hot=None):
+def picked_rows(plane, capacity, ranks, axis, value, meta, hot=None, pad=None):
     tokens, width = value.shape
     plan = gather_plan(plane, ranks, axis)
     raws = [plane.send(value, u) for u in plane.along(axis)]
     outs = [shaped((len(plan[1]) * capacity, width), bf16)] * len(plan[2])
     flops = 2 * tokens * width * capacity * len(plan[1]) * len(plan[2])
-    if type(meta) is list:
-        return call(functools.partial(own_select_kernel, plane, capacity, plan), outs, *meta, *raws, flops=flops)
+    if pad is not None:
+        kernel = functools.partial(own_select_kernel, plane, capacity, plan)
+        return call(kernel, [pad] + outs, *meta, *raws, pad_out=True)
     if hot is None:
         return call(functools.partial(select_kernel, plane, capacity, plan), outs, meta, *raws, flops=flops)
     (own,) = call(pick_own_kernel, [shaped((hot.shape[1], width), bf16)], hot, raws[0], flops=LONG)
@@ -287,11 +299,58 @@
     return preact * cdf, cdf + preact * pdf
 
 
-def preact_kernel(plane, capacity, groups, win_ref, *refs):
+class Copies:
+    def __init__(self, sem):
+        self.sem, self.started = sem, []
+
+    def start(self, source, target):
+        self.started.append(pltpu.make_async_copy(source, target, self.sem.at[len(self.started)]))
+        self.started[-1].start()
+        return self.started[-1]
+
+    def wait(self):
+        for copy in self.started:
+            copy.wait()
+
+
+def lanes_of(units):
+    return -(-units // LANES) * LANES
+
+
+def plate(pad_ref, n, lanes):
+    return pad_ref.at[n, :, pl.ds(0, lanes)]
+
+
+def preact_kernel(plane, capacity, groups, places, win_ref, _, *refs):
+    pad_ref, hid_ref, slope_ref, x, hid, sem = refs[-6:]
+    units, copies = win_ref.shape[0], Copies(sem)
+    arrange(plane, capacity, groups, refs[:-6], x)
+    copies.start(x, pad_ref.at[places[0]])
+    activated, slope = gelu_parts(dot(x[...], win_ref[...], 1, 1))
+    hidden = activated.astype(bf16)
+    hid[:, :units] = hidden
+    copies.start(hid, plate(pad_ref, places[1], hid.shape[1]))
+    hid_ref[...] = hidden
+    slope_ref[...] = slope
+    copies.wait()
+
+
+def preact(plane, capacity, groups, places, w_in, pad, *pieces):
+    units = w_in.shape[0]
+    rows, features = pad.shape[1:]
+    return call(
+        functools.partial(preact_kernel, plane, capacity, groups, places),
+        [shaped(pad.shape, bf16), shaped((rows, units), bf16), shaped((rows, units), f32)],
+        w_in, pad, *pieces, pad=1, pad_out=True,
+        scratch=[pltpu.VMEM((rows, n), bf16) for n in (features, lanes_of(units))] + [pltpu.SemaphoreType.DMA((2,))],
+    )
+
+
+def first_preact_kernel(plane, capacity, groups, win_ref, *refs):
     x_ref, hid_ref, slope_ref = refs[-3:]
     arrange(plane, capacity, groups, refs[:-3], x_ref)
     activated, slope = gelu_parts(dot(x_ref[...], win_ref[...], 1, 1))
-    hid_ref[...] = activated.astype(bf16)
+    hid_ref[:, : slope.shape[1]] = activated.astype(bf16)
     slope_ref[...] = slope
 
 
@@ -299,11 +358,15 @@
     refs, back = refs[:-1], refs[-1]
     pieces = sum(1 if plan is None else len(plan) for plan in plans)
     refs, back_refs = refs[:-pieces], list(refs[-pieces:])
-    g_ref, gp_ref, score_ref = refs[-3:]
+    g_ref, gp_ref, cols_ref = refs[-3:]
+    units = win_ref.shape[0]
     arrange(plane, capacity, groups, refs[:-3], g_ref)
     pulled = dot(g_ref[...], wout_ref[...], 1, 1)
-    grad_pre = (prob_ref[:, 0:1] * pulled * slope_ref[...]).astype(bf16)
-    gp_ref[...] = grad_pre
+    grad_pre = (prob_ref[:, 0:1].astype(f32) * pulled * slope_ref[...]).astype(bf16)
+    gp_ref[:, :units] = grad_pre
+    score = jnp.sum(hid_ref[:, :units].astype(f32) * pulled, axis=1, keepdims=True)
+    cols_ref[:, :LANES] = prob_ref[...]
+    cols_ref[:, LANES:] = jnp.broadcast_to(score, (score.shape[0], LANES)).astype(bf16)
     width = back.shape[1]
     for h, plan in enumerate(plans):
         back[...] = dot(grad_pre, win_ref[:, h * width : (h + 1) * width], 1, 0).astype(bf16)
@@ -315,28 +378,52 @@
             for s, block in enumerate(blocks):
                 at = pl.multiple_of(other_of(plane, block) * capacity, 16)
                 out_ref[s * capacity : (s + 1) * capacity, :] = back[pl.ds(at, capacity), :]
-    score = jnp.sum(hid_ref[...].astype(f32) * pulled, axis=1, keepdims=True)
-    score_ref[...] = jnp.broadcast_to(score, score_ref.shape)
+
+
+def stash_kernel(places, *refs):
+    pad_ref, sem = refs[-2:]
+    copies = Copies(sem)
+    for n, ref in zip(places, refs):
+        copies.start(ref, plate(pad_ref, n, ref.shape[1]))
+    copies.wait()
+
+
+def stash(pad, places, *arrays):
+    return pl.pallas_call(
+        functools.partial(stash_kernel, places),
+        out_shape=shaped(pad.shape, bf16),
+        in_specs=[pl.BlockSpec()] * len(arrays) + [in_hbm(pad)],
+        out_specs=in_hbm(pad),
+        compiler_params=pltpu.CompilerParams(vmem_limit_bytes=VMEM_LIMIT),
+        scratch_shapes=[pltpu.SemaphoreType.DMA((len(arrays),))],
+        input_output_aliases={len(arrays): 0},
+        cost_estimate=pl.CostEstimate(flops=0, bytes_accessed=0, transcendentals=0),
+    )(*arrays, pad)
 
 
 def weighted(prob_ref, k, g):
-    return (prob_ref[:, k : k + 1] * g.astype(f32)).astype(bf16)
-
-
-def early_kernel(plane, capacity, groups, wout_ref, hid0_ref, hid1_ref, prob_ref, g0_ref, *refs):
-    pulled_ref, gout_ref, g_ref = refs[-3:]
-    arrange(plane, capacity, groups, refs[:-3], g_ref)
-    pulled_ref[...] = dot(g_ref[...], wout_ref[...], 1, 1)
-    y = jnp.concatenate([weighted(prob_ref, 0, g0_ref[...]), weighted(prob_ref, 1, g_ref[...])], axis=0)
-    hid = jnp.concatenate([hid0_ref[...], hid1_ref[...]], axis=0)
+    return (prob_ref[:, k : k + 1].astype(f32) * g.astype(f32)).astype(bf16)
+
+
+def early_kernel(plane, capacity, groups, wout_ref, hid1_ref, pad_ref, *refs):
+    pulled_ref, gout_ref, g, g0, hid0, cols, sem = refs[-7:]
+    units, copies = wout_ref.shape[0], Copies(sem)
+    copies.start(plate(pad_ref, G0, g0.shape[1]), g0)
+    copies.start(plate(pad_ref, HID0, hid0.shape[1]), hid0)
+    copies.start(plate(pad_ref, COLS, cols.shape[1]), cols)
+    arrange(plane, capacity, groups, refs[:-7], g)
+    pulled_ref[...] = dot(g[...], wout_ref[...], 1, 1)
+    copies.wait()
+    y = jnp.concatenate([weighted(cols, 0, g0[...]), weighted(cols, 1, g[...])], axis=0)
+    hid = jnp.concatenate([hid0[:, :units], hid1_ref[...]], axis=0)
     gout_ref[...] = dot(hid, y, 0, 0).astype(bf16)
 
 
-def early(plane, capacity, groups, w_out, hid0, hid1, prob, g0, *pieces):
-    rows, units = hid0.shape
+def early(plane, capacity, groups, w_out, hid1, pad, *pieces):
+    rows, units = hid1.shape
     features = w_out.shape[1]
     width = features // HALVES
-    args = (w_out, hid0, hid1, prob, g0, *pieces)
+    args = (w_out, hid1, *pieces)
     outs = [shaped((rows, units), f32), shaped((units, features), bf16)]
     whole = lambda a: pl.BlockSpec(a.shape, lambda i: (0, 0))
     first = lambda a: pl.BlockSpec((a.shape[0], width), lambda i: (0, 0))
@@ -344,47 +431,45 @@
         functools.partial(early_kernel, plane, capacity, groups),
         grid=(1,),
         out_shape=outs,
-        in_specs=[first(w_out), whole(hid0), whole(hid1), whole(prob), first(g0)] + [whole(p) for p in pieces],
+        in_specs=[first(w_out), whole(hid1), in_hbm(pad)] + [whole(p) for p in pieces],
         out_specs=[whole(outs[0]), first(outs[1])],
-        scratch_shapes=[pltpu.VMEM((rows, width), bf16)],
+        scratch_shapes=[pltpu.VMEM((rows, n), bf16) for n in (width, width, lanes_of(units), 2 * LANES)]
+        + [pltpu.SemaphoreType.DMA((3,))],
         compiler_params=pltpu.CompilerParams(vmem_limit_bytes=VMEM_LIMIT),
         cost_estimate=cost(args, outs, 3 * units * rows * features),
-    )(*args)
-
-
-def second_kernel(plane, capacity, groups, first, wout_ref, hid_ref, slope_ref, prob_ref, score0_ref, pulled_ref, *refs):
-    g_ref, gp_ref, score_ref = refs[-3:]
-    arrange(plane, capacity, groups, refs[:-3], g_ref)
+    )(w_out, hid1, pad, *pieces)
+
+
+def second_kernel(plane, capacity, groups, first, wout_ref, hid_ref, slope_ref, pulled_ref, pad_ref, *refs):
+    g_ref, gp_ref, score_ref, cols, sem = refs[-5:]
+    units, copies = wout_ref.shape[0], Copies(sem)
+    copies.start(plate(pad_ref, COLS, cols.shape[1]), cols)
+    arrange(plane, capacity, groups, refs[:-5], g_ref)
     pulled = pulled_ref[...] + dot(g_ref[...], wout_ref[:, first:], 1, 1)
+    copies.wait()
+    gp_ref[:, :units] = (cols[:, 1:2].astype(f32) * pulled * slope_ref[...]).astype(bf16)
     score = jnp.sum(hid_ref[...].astype(f32) * pulled, axis=1, keepdims=True)
     lane = lax.broadcasted_iota(jnp.int32, score_ref.shape, 1)
-    both = jnp.where(lane == 0, score0_ref[...], jnp.where(lane == 1, score, 0.0))
+    both = jnp.where(lane == 0, cols[:, LANES:].astype(f32), jnp.where(lane == 1, score, 0.0))
     score_ref[...] = both.astype(bf16)
-    gp_ref[...] = (prob_ref[:, 1:2] * pulled * slope_ref[...]).astype(bf16)
-
-
-def late_kernel(width, _, prob_ref, x0_ref, x1_ref, g0_ref, g1_ref, hid0_ref, hid1_ref, gp0_ref, gp1_ref, *refs):
-    gin_ref, gout_ref, prob, x, g, hid, gp, held, sem, out_sem = refs
-    rows, units = hid0_ref.shape
-    features, part = x0_ref.shape[1], g1_ref.shape[1]
+
+
+def late_kernel(width, part, units, _, pad_ref, g1_ref, gp1_ref, *refs):
+    gin_ref, gout_ref, cols, x, g, hid, gp, held, sem, out_sem = refs
+    rows, features = pad_ref.shape[1:]
     skip = features - part
-    fetched = []
-
-    def fetch(ref, out_ref):
-        fetched.append(pltpu.make_async_copy(ref, out_ref, sem.at[len(fetched)]))
-        fetched[-1].start()
-        return fetched[-1]
-
+    copies = Copies(sem)
     top, low = pl.ds(0, rows), pl.ds(rows, rows)
     lanes = lambda at: pl.ds(at, width)
-    first = [fetch(gp0_ref, gp.at[top, :]), fetch(gp1_ref, gp.at[low, :])]
+    first = [copies.start(plate(pad_ref, GP0, gp.shape[1]), gp.at[top, :])]
     tiles = []
     for at in range(0, features, width):
         tiles.append(
-            [fetch(x0_ref.at[:, lanes(at)], x.at[top, lanes(at)]), fetch(x1_ref.at[:, lanes(at)], x.at[low, lanes(at)])]
+            [copies.start(pad_ref.at[n, :, lanes(at)], x.at[to, lanes(at)]) for n, to in ((X0, top), (X1, low))]
         )
-    then = [fetch(hid0_ref, hid.at[top, :]), fetch(hid1_ref, hid.at[low, :]), fetch(prob_ref, prob)]
-    then += [fetch(g0_ref.at[:, pl.ds(skip, part)], g.at[top, :]), fetch(g1_ref, g.at[low, :])]
+    then = [copies.start(plate(pad_ref, n, hid.shape[1]), hid.at[at, :]) for n, at in ((HID0, top), (HID1, low))]
+    then.append(copies.start(plate(pad_ref, COLS, cols.shape[1]), cols))
+    then.append(copies.start(pad_ref.at[G0, :, pl.ds(skip, part)], g))
     sent = []
 
     def store(n, value, out_ref, at):
@@ -395,44 +480,43 @@
         sent.append(pltpu.make_async_copy(held.at[slot], out_ref.at[:, lanes(at)], out_sem.at[slot]))
         sent[-1].start()
 
+    gp[rows:, :] = gp1_ref[...]
     for copy in first:
         copy.wait()
     for n, tile in enumerate(tiles):
         for copy in tile:
             copy.wait()
         at = n * width
-        store(n, dot(gp[...], x[:, at : at + width], 0, 0), gin_ref, at)
+        store(n, dot(gp[:, :units], x[:, at : at + width], 0, 0), gin_ref, at)
     for copy in then:
         copy.wait()
     for n in range(part // width):
         at = n * width
-        y0 = weighted(prob, 0, g[:rows, at : at + width])
-        y1 = weighted(prob, 1, g[rows:, at : at + width])
-        store(len(tiles) + n, dot(hid[...], jnp.concatenate([y0, y1], axis=0), 0, 0), gout_ref, skip + at)
+        y0 = weighted(cols, 0, g[:, at : at + width])
+        y1 = weighted(cols, 1, g1_ref[:, at : at + width])
+        store(len(tiles) + n, dot(hid[:, :units], jnp.concatenate([y0, y1], axis=0), 0, 0), gout_ref, skip + at)
     for copy in sent[-held.shape[0] :]:
         copy.wait()
 
 
-def late(width, done, prob, x0, x1, g0, g1, hid0, hid1, gp0, gp1):
-    args = (done, prob, x0, x1, g0, g1, hid0, hid1, gp0, gp1)
-    rows, units = hid0.shape
-    features, part = x0.shape[1], g1.shape[1]
+def late(width, done, pad, g1, gp1):
+    units, features = done.shape
+    rows, part = g1.shape
     outs = [shaped((units, features), bf16)] * 2
-    fetches = 7 + 2 * (features // width)
     return pl.pallas_call(
-        functools.partial(late_kernel, width),
+        functools.partial(late_kernel, width, part, units),
         out_shape=outs,
-        in_specs=[pl.BlockSpec(memory_space=pltpu.HBM)] * len(args),
-        out_specs=[pl.BlockSpec(memory_space=pltpu.HBM)] * 2,
-        scratch_shapes=[pltpu.VMEM(prob.shape, f32), pltpu.VMEM((2 * rows, features), bf16)]
-        + [pltpu.VMEM((2 * rows, part), bf16)]
-        + [pltpu.VMEM((2 * rows, units), bf16)] * 2
+        in_specs=[in_hbm(done), in_hbm(pad), pl.BlockSpec(), pl.BlockSpec()],
+        out_specs=[in_hbm(o) for o in outs],
+        scratch_shapes=[pltpu.VMEM((rows, 2 * LANES), bf16), pltpu.VMEM((2 * rows, features), bf16)]
+        + [pltpu.VMEM((rows, part), bf16)]
+        + [pltpu.VMEM((2 * rows, lanes_of(units)), bf16)] * 2
         + [pltpu.VMEM((3, units, width), bf16)]
-        + [pltpu.SemaphoreType.DMA((fetches,)), pltpu.SemaphoreType.DMA((3,))],
+        + [pltpu.SemaphoreType.DMA((7 + 2 * (features // width),)), pltpu.SemaphoreType.DMA((3,))],
         input_output_aliases={0: 1},
-        compiler_params=pltpu.CompilerParams(vmem_limit_bytes=60 * 1024 * 1024),
-        cost_estimate=cost(args, outs, 6 * units * rows * features),
-    )(*args)
+        compiler_params=pltpu.CompilerParams(vmem_limit_bytes=LATE_LIMIT),
+        cost_estimate=cost((), outs, 6 * units * rows * features),
+    )(done, pad, g1, gp1)
 
 
 def collect_kernel(experts, capacity, topk, meta_ref, hot0_ref, hot1_ref, score_ref, out_ref):
@@ -473,23 +557,25 @@
     meta = lax.all_to_all(meta, "expert", split_axis=0, concat_axis=0, tiled=True)
     hot0, hot1, prob = call(
         functools.partial(slots_kernel, experts, capacity, topk),
-        [shaped((rows, tokens), bf16)] * 2 + [shaped((rows, LANES), f32)],
+        [shaped((rows, tokens), bf16)] * 2 + [shaped((rows, LANES), bf16)],
         meta,
     )
-
-    acts = [shaped((rows, features), bf16), shaped((rows, units), bf16), shaped((rows, units), f32)]
+    plate_bytes = rows * features * 2
+    pad = shaped((max(9, -(-PAD_BYTES // plate_bytes)), rows, features), bf16)
+
     stepped = capacity % 16 == 0
     ranks = [list(range(k * topk, (k + 1) * topk)) for k in range(ticks)]
     pick = functools.partial(picked_rows, plane, capacity)
     if stepped:
         metas = [own_meta, plane.send(own_meta, (0, 0, 1))]
-        x1 = behind(inputs, [x0])[0, 1]
-        x1 = pick(ranks[1], 2, x1, metas)
+        x1 = inputs[0, 1]
+        pad, *x1 = pick(ranks[1], 2, x1, metas, pad=pad)
         x1_near, _ = sent_rows(plane, 2, x1[:-1])
         x1_groups, x1_rest = [(0, sent_layout(plane, 2))], x1[-1:]
         select_meta = behind(meta, x1)
         x0, x0_layout = sent_rows(plane, 1, pick(ranks[0], 1, x0, select_meta))
-        g0_in, g0_layout = sent_rows(plane, 0, pick(ranks[0], 0, g0, select_meta))
+        *g0_first, g0_last = pick(ranks[0], 0, g0, select_meta)
+        g0_in, g0_layout = sent_rows(plane, 0, [*g0_first, behind(g0_last, [*x1_near, prob])])
         plans = [return_plan(plane, ranks[0], axis) for axis in AXES]
         plans += [gather_plan(plane, ranks[1], axis) for axis in AXES]
         shapes = [shaped((len(b), len(e) * capacity, tokens), bf16) for _, b, e in plans]
@@ -497,23 +583,31 @@
         back_plans = [[[plane.back(plane.back(t, u)) for u in plane.along(axis)] for t in plane.across(axis)] for axis in AXES]
         shapes = [shaped((len(blocks) * capacity, half), bf16) for plan in back_plans for blocks in plan]
     else:
+        (pad,) = call(lambda meta_ref, _: None, [pad], meta, pad_out=True)
         x0, x0_layout = [exchange(spread(hot0, x0), experts)], None
         g0_in, g0_layout = [exchange(spread(hot0, g0), experts)], None
         back_plans = [None] * HALVES
         shapes = [shaped((rows, half), bf16)] * HALVES
 
     if stepped:
+        arrived = [*x0, *g0_in]
         x0 = behind(x0, x1_near)
+    wide = lanes_of(units)
+    vmem = lambda n: pltpu.VMEM((rows, n), bf16)
     x0, hid0, slope0 = call(
-        functools.partial(preact_kernel, plane, capacity, [(0, x0_layout)]), acts, w_in, *x0, flops=matmul
-    )
-    g0_in, gp0, score0, *backs = call(
+        functools.partial(first_preact_kernel, plane, capacity, [(0, x0_layout)]),
+        [shaped((rows, features), bf16), shaped((rows, wide), bf16), shaped((rows, units), f32)], w_in, *x0,
+    )
+    g0_in, gp0, cols, *backs = call(
         functools.partial(first_kernel, plane, capacity, [(0, g0_layout)], back_plans),
-        [shaped((rows, features), bf16), shaped((rows, units), bf16), shaped((rows, LANES), f32)] + shapes,
-        w_in, w_out, hid0, slope0, prob, *g0_in, flops=2 * matmul,
-        scratch=[pltpu.VMEM((rows, half), bf16)],
-    )
+        [shaped((rows, n), bf16) for n in (features, wide, 2 * LANES)] + shapes,
+        w_in, w_out, hid0, slope0, prob, *g0_in, scratch=[vmem(half)],
+    )
+    pad = stash(pad, (X0, G0, HID0, GP0, COLS), x0, g0_in, hid0, gp0, cols)
     leaving, after = [], []
+    if stepped:
+        x1_rest = [plane.send(p, t) for p, t in zip(behind(x1_rest, [hid0, *arrived]), plane.across(2)[-1:])]
+        after = [pad, *x1_rest]
     for h, axis in enumerate(AXES):
         if stepped:
             count = len(plane.across(axis))
@@ -528,7 +622,6 @@
         after = [out]
 
     if stepped:
-        x1_rest = [plane.send(p, t) for p, t in zip(behind(x1_rest, leaving), plane.across(2)[-1:])]
         x1 = x1_near + x1_rest
     else:
         x1, x1_groups = [exchange(spread(hot1, inputs[0, 1]), experts)], [(0, None)]
@@ -544,18 +637,17 @@
             pieces, layout = [exchange(spread(hot1, arrived), experts)], None
         parts.append((pieces, [(0, layout)]))
     x1 = behind(x1, after)
-    x1, hid1, slope1 = call(
-        functools.partial(preact_kernel, plane, capacity, x1_groups), acts, w_in, *x1, flops=matmul
-    )
-    pulled, gout = early(plane, capacity, parts[0][1], w_out, hid0, hid1, prob, g0_in, *parts[0][0])
+    pad, hid1, slope1 = preact(plane, capacity, x1_groups, (X1, HID1), w_in, pad, *x1)
+    pulled, gout = early(plane, capacity, parts[0][1], w_out, hid1, pad, *parts[0][0])
     pieces = behind(parts[1][0], [pulled])
     g1, gp1, scores = call(
         functools.partial(second_kernel, plane, capacity, parts[1][1], half),
-        [shaped((rows, half), bf16), shaped((rows, units), bf16), shaped((rows, LANES), bf16)],
-        w_out, hid1, slope1, prob, score0, pulled, *pieces, flops=matmul // 2,
+        [shaped((rows, half), bf16), shaped((rows, wide), bf16), shaped((rows, LANES), bf16)],
+        w_out, hid1, slope1, pulled, pad, *pieces, flops=matmul // 2, pad=4,
+        scratch=[vmem(2 * LANES), pltpu.SemaphoreType.DMA((1,))],
     )
     scores = exchange(scores, experts)
-    grad_in, grad_out = late(features // TILES, gout, prob, x0, x1, g0_in, g1, hid0, hid1, gp0, gp1)
+    grad_in, grad_out = late(features // TILES, gout, pad, g1, gp1)
     (prob_grads,) = call(
         functools.partial(collect_kernel, experts, capacity, topk),
         [shaped((ticks * topk, tokens), bf16)], meta, hot0, hot1, scores,

time: 123 us -> 119 us (0.967)
  waiting for transfers between devices: 43 us -> 37.6 us
  local copies, waits for them, and re-layouts: 9.42 us -> 5.41 us
  Pallas kernels: 33.6 us -> 36.1 us
  starting transfers between devices: 35.1 us -> 37.3 us
  other arithmetic: 0.01 us -> 1.37 us
    ppermute x29, waiting for transfers between devices: 40.7 us -> 34.2 us  [send(): return lax.ppermute(value, 'expert', route)]
    unnamed x46 -> x18, local copies, waits for them, and re-layouts: 5.84 us -> 2.57 us
    ppermute x29, starting transfers between devices: 25.6 us -> 27.8 us  [send(): return lax.ppermute(value, 'expert', route)]
    ppermute x2, waiting for transfers between devices: 1.64 us -> 3.42 us  [body(): lax.ppermute(leaving[h], 'segment', [(i, i - 1) for i in range(1, segment...]
    pallas_call x1, Pallas kernels: 3.05 us -> 4.44 us  [early(): pl.pallas_call(functools.partial(early_kernel, plane, capacity, groups),...]
    convert_element_type x2, other arithmetic: 0.01 us -> 1.36 us  [body(): meta = jnp.concatenate([ids.astype(f32), probs.astype(f32)], axis=0)]
    pallas_call x21 -> x22, Pallas kernels: 30.6 us -> 31.6 us  [the longest x20 22.7 us: call(): pl.pallas_call(kernel, out_shape=outs, in_specs=specs, out_specs=[in_hbm(...]
    squeeze x2 -> x1, local copies, waits for them, and re-layouts: 2.97 us -> 2.23 us  [body(): x1 = inputs[0, 1]]
  transfers between devices with their start and end apart: 33 -> 33, of which waited for: 21 -> 17; matrix products, arithmetic and copies ran while one was open for 1% -> 2% of each run, Pallas kernels for 23% -> 28%
where the time goes in v6:
time: 119 us
  waiting for transfers between devices  37.6 us (32%)
  starting transfers between devices  37.3 us (31%)
  Pallas kernels  36.1 us (30%)
  local copies, waits for them, and re-layouts  5.41 us (5%)
  other arithmetic  1.37 us (1%)
    ppermute x29, waiting for transfers between devices, send(): return lax.ppermute(value, 'expert', route)  34.2 us
    ppermute x29, starting transfers between devices, send(): return lax.ppermute(value, 'expert', route)  27.8 us
    pallas_call x20, Pallas kernels, call(): pl.pallas_call(kernel, out_shape=outs, in_specs=specs, out_specs=[in_hbm(...  22.7 us
    pallas_call x1, Pallas kernels, late(): pl.pallas_call(functools.partial(late_kernel, width, part, units), out_sh...  6.84 us
    pallas_call x1, Pallas kernels, early(): pl.pallas_call(functools.partial(early_kernel, plane, capacity, groups),...  4.44 us
    ppermute x2, waiting for transfers between devices, body(): lax.ppermute(leaving[h], 'segment', [(i, i - 1) for i in range(1, segment...  3.42 us
    all_to_all x1, starting transfers between devices, exchange(): lax.all_to_all(pieces, 'expert', split_axis=0, concat_axis=0, tiled=True)  3.37 us
    all_to_all x1, starting transfers between devices, body(): lax.all_to_all(meta, 'expert', split_axis=0, concat_axis=0, tiled=True)  3.33 us
  transfers between devices with their start and end apart: 33, of which 17 were waited for; matrix products, arithmetic and copies ran while one was open for 2% of the time, Pallas kernels for 28%

profile of v6, /device:TPU:0, one launch (start us, length us, event | category | flops | bytes accessed | tf_op | source)
XLA Modules:
  0.0 118.7 jit_solution(16460013353218999621)
XLA Ops:
  0.6 2.2 %slice_bitcast_fusion = (bf16[128,2048]{1,0:T(8,128)(2,1)}, bf16[128,2048]{1,0:T(8,128)(2,1)S(1)}) fusion(bf16[1,2,128,2048]{3,2,1,0:T(8,128)(2,1)} %param.6), kind=kLoop, calls=%fused_computation | loop fusion | bytes 2097152 | tf_op jit(solution)/shard_map/squeeze | solution.py:571
  3.3 2.5 %collective-permute-start.2 = (bf16[128,2048]{1,0:T(8,128)(2,1)S(1)}, bf16[128,2048]{1,0:T(8,128)(2,1)}, u32[]{:S(2)}, u32[]{:S(2)}) collective-permute-start(bf16[128,2048]{1,0:T(8,128)(2,1)S(1)} %get-tuple-element.168.refs_0_), channel_id=1, source_target_pairs={{0,2},{1,3},{2,0},{3,1},{4,6},{5,7},{6,4},{7,5},{8,10},{9,11},{10,... | collective-permute-start | bytes 1572872 | tf_op jit(solution)/shard_map/ppermute | solution.py:83
  5.8 1.5 %collective-permute-start.8 = (bf16[128,2048]{1,0:T(8,128)(2,1)}, bf16[128,2048]{1,0:T(8,128)(2,1)}, u32[]{:S(2)}, u32[]{:S(2)}) collective-permute-start(bf16[128,2048]{1,0:T(8,128)(2,1)} %bitcast.33), channel_id=1, source_target_pairs={{0,4},{1,5},{2,6},{3,7},{4,0},{5,1},{6,2},{7,3},{8,12},{9,13},{10,... | collective-permute-start | bytes 1572872 | tf_op jit(solution)/shard_map/ppermute | solution.py:83
  9.3 3.3 %all-to-all-start = ((f32[8,8,128]{2,1,0:T(8,128)}), f32[8,8,128]{2,1,0:T(8,128)S(1)}, u32[]{:S(2)}, u32[]{:S(2)}) async-start(f32[8,8,128]{2,1,0:T(8,128)} %broadcast_in_dim.15), calls=%async_computation | async-start | bytes 65536 | tf_op jit(solution)/shard_map/all_to_all | solution.py:557
  13.1 0.8 collective-permute-done.refs_1_
  13.9 3.1 %shard_map.85 = (bf16[44,384,2048]{2,1,0:T(8,128)(2,1)}, bf16[96,2048]{1,0:T(8,128)(2,1)S(1)}, bf16[96,2048]{1,0:T(8,128)(2,1)}, bf16[96,2048]{1,0:T(8,128)(2,1)}, bf16[96,2048]{1,0:T(8,128)(2,1)S(1)}) custom-call(f32[8,128]{1,0:T(8,128)S(1)} %pad_maximum_fusion.refs_0_, f32[8,128]{1,0:T(8,128)S(1)} %collective-permute-done.refs_1_, ...), custom_call_target="tpu_custom_call" | custom-call | bytes 4597481472 | tf_op jit(solution)/shard_map/pallas_call | solution.py:44
  17.0 0.7 copy-done.3
  17.7 0.8 copy-done.7
  18.5 1.9 %collective-permute-start.6 = (bf16[96,2048]{1,0:T(8,128)(2,1)}, bf16[96,2048]{1,0:T(8,128)(2,1)}, u32[]{:S(2)}, u32[]{:S(2)}) collective-permute-start(bf16[96,2048]{1,0:T(8,128)(2,1)} %get-tuple-element.88), channel_id=1, source_target_pairs={{0,2},{1,3},{2,0},{3,1},{4,6},{5,7},{6,4},{7,5},{8,10},{9,11},{10,... | collective-permute-start | bytes 1179656 | tf_op jit(solution)/shard_map/ppermute | solution.py:83
  20.3 1.5 %collective-permute-start.7 = (bf16[96,2048]{1,0:T(8,128)(2,1)}, bf16[96,2048]{1,0:T(8,128)(2,1)}, u32[]{:S(2)}, u32[]{:S(2)}) collective-permute-start(bf16[96,2048]{1,0:T(8,128)(2,1)} %get-tuple-element.89), channel_id=1, source_target_pairs={{0,4},{1,5},{2,6},{3,7},{4,0},{5,1},{6,2},{7,3},{8,12},{9,13},{10,... | collective-permute-start | bytes 1179656 | tf_op jit(solution)/shard_map/ppermute | solution.py:83
  21.8 2.1 %shard_map.86 = (bf16[96,2048]{1,0:T(8,128)(2,1)S(1)}, bf16[96,2048]{1,0:T(8,128)(2,1)S(1)}, bf16[96,2048]{1,0:T(8,128)(2,1)S(1)}, bf16[96,2048]{1,0:T(8,128)(2,1)S(1)}) custom-call(f32[8,8,128]{2,1,0:T(8,128)S(1)} %all-to-all-done.meta_ref, bf16[128,2048]{1,0:T(8,128)(2,1)S(1)} %get-tuple-element.168.refs_0_, bf16[128,2048]{1,0:T(8,128)(2,1)} %collective-permute-done.2.refs_1_), custom_call_target="tpu_custom_call" | custom-call | bytes 169869312 | tf_op jit(solution)/shard_map/pallas_call | solution.py:44
  25.3 1.3 %collective-permute-start.5 = (bf16[96,2048]{1,0:T(8,128)(2,1)S(1)}, bf16[96,2048]{1,0:T(8,128)(2,1)S(1)}, u32[]{:S(2)}, u32[]{:S(2)}) collective-permute-start(bf16[96,2048]{1,0:T(8,128)(2,1)S(1)} %get-tuple-element.95), channel_id=1, source_target_pairs={{0,5},{1,4},{2,7},{3,6},{4,1},{5,0},{6,3},{7,2},{8,13},{9,12},{10,... | collective-permute-start | bytes 1179656 | tf_op jit(solution)/shard_map/ppermute | solution.py:83
  26.6 1.0 copy-done.2
  27.7 2.1 %shard_map.89 = (bf16[96,2048]{1,0:T(8,128)(2,1)S(1)}, bf16[96,2048]{1,0:T(8,128)(2,1)S(1)}, bf16[96,2048]{1,0:T(8,128)(2,1)S(1)}, bf16[96,2048]{1,0:T(8,128)(2,1)S(1)}) custom-call(f32[8,8,128]{2,1,0:T(8,128)S(1)} %all-to-all-done.meta_ref, bf16[128,2048]{1,0:T(8,128)(2,1)S(1)} %bitcast.34, bf16[128,2048]{1,0:T(8,128)(2,1)} %collective-permute-done.8.refs_1_), custom_call_target="tpu_custom_call" | custom-call | bytes 169869312 | tf_op jit(solution)/shard_map/pallas_call | solution.py:44
  30.2 1.7 %collective-permute-start.10 = (bf16[96,2048]{1,0:T(8,128)(2,1)S(1)}, bf16[96,2048]{1,0:T(8,128)(2,1)S(1)}, u32[]{:S(2)}, u32[]{:S(2)}) collective-permute-start(bf16[96,2048]{1,0:T(8,128)(2,1)S(1)} %get-tuple-element.106), channel_id=1, source_target_pairs={{0,2},{1,3},{2,0},{3,1},{4,6},{5,7},{6,4},{7,5},{8,10},{9,11},{10,... | collective-permute-start | bytes 1179656 | tf_op jit(solution)/shard_map/ppermute | solution.py:83
  31.8 0.8 collective-permute-done.7.refs_2_
  32.9 8.1 %collective-permute-done.4.refs_2_ = bf16[96,2048]{1,0:T(8,128)(2,1)S(1)} collective-permute-done((bf16[96,2048]{1,0:T(8,128)(2,1)S(1)}, bf16[96,2048]{1,0:T(8,128)(2,1)S(1)}, u32[]{:S(2)}, u32[]{:S(2)}) %collective-permute-start.4) | collective-permute-done | bytes 393248 | tf_op jit(solution)/shard_map/ppermute | solution.py:83
  41.0 6.3 %collective-permute-done.5.refs_3_ = bf16[96,2048]{1,0:T(8,128)(2,1)S(1)} collective-permute-done((bf16[96,2048]{1,0:T(8,128)(2,1)S(1)}, bf16[96,2048]{1,0:T(8,128)(2,1)S(1)}, u32[]{:S(2)}, u32[]{:S(2)}) %collective-permute-start.5) | collective-permute-done | bytes 393248 | tf_op jit(solution)/shard_map/ppermute | solution.py:83
  47.3 1.8 %shard_map.87 = (bf16[384,2048]{1,0:T(8,128)(2,1)S(1)}, bf16[384,768]{1,0:T(8,128)(2,1)S(1)}, f32[384,704]{1,0:T(8,128)S(1)}) custom-call(bf16[704,2048]{1,0:T(8,128)(2,1)S(1)} %bitcast.27, bf16[96,2048]{1,0:T(8,128)(2,1)S(1)} %get-tuple-element.96.refs_0_, bf16[96,2048]{1,0:T(8,128)(2,1)S(1)} %collective-permute-done.3.refs_1_, ...), custom_call_target="tpu_custom_call" | custom-call | bytes 492830720 | tf_op jit(solution)/shard_map/pallas_call | solution.py:44
  49.2 1.4 %collective-permute-start.12 = (bf16[96,2048]{1,0:T(8,128)(2,1)S(1)}, bf16[96,2048]{1,0:T(8,128)(2,1)S(1)}, u32[]{:S(2)}, u32[]{:S(2)}) collective-permute-start(bf16[96,2048]{1,0:T(8,128)(2,1)S(1)} %copy-done.8), channel_id=1, source_target_pairs={{0,6},{1,7},{2,4},{3,5},{4,2},{5,3},{6,0},{7,1},{8,14},{9,15},{10,... | collective-permute-start | bytes 1179656 | tf_op jit(solution)/shard_map/ppermute | solution.py:83
  50.6 3.2 %shard_map.90 = (bf16[384,2048]{1,0:T(8,128)(2,1)S(1)}, bf16[384,768]{1,0:T(8,128)(2,1)S(1)}, bf16[384,256]{1,0:T(8,128)(2,1)S(1)}, bf16[96,1024]{1,0:T(8,128)(2...) custom-call(bf16[704,2048]{1,0:T(8,128)(2,1)S(1)} %bitcast.28, ...), custom_call_target="tpu_custom_call" | custom-call | bytes 834666496 | tf_op jit(solution)/shard_map/pallas_call | solution.py:44
  53.8 1.6 %collective-permute-start.16 = (bf16[96,1024]{1,0:T(8,128)(2,1)S(1)}, bf16[96,1024]{1,0:T(8,128)(2,1)S(1)}, u32[]{:S(2)}, u32[]{:S(2)}) collective-permute-start(bf16[96,1024]{1,0:T(8,128)(2,1)S(1)} %get-tuple-element.122), channel_id=1, source_target_pairs={{0,2},{1,3},{2,0},{3,1},{4,6},{5,7},{6,4},{7,5},{8,10},{9,11},{10,... | collective-permute-start | bytes 589832 | tf_op jit(solution)/shard_map/ppermute | solution.py:83
  56.0 1.4 %collective-permute-start.18 = (bf16[96,1024]{1,0:T(8,128)(2,1)S(1)}, bf16[96,1024]{1,0:T(8,128)(2,1)S(1)}, u32[]{:S(2)}, u32[]{:S(2)}) collective-permute-start(bf16[96,1024]{1,0:T(8,128)(2,1)S(1)} %get-tuple-element.124), channel_id=1, source_target_pairs={{0,6},{1,7},{2,4},{3,5},{4,2},{5,3},{6,0},{7,1},{8,14},{9,15},{10,... | collective-permute-start | bytes 589832 | tf_op jit(solution)/shard_map/ppermute | solution.py:83
  57.4 0.9 shard_map.92
  58.3 1.5 %collective-permute-start.13 = (bf16[96,1024]{1,0:T(8,128)(2,1)S(1)}, bf16[96,1024]{1,0:T(8,128)(2,1)S(1)}, u32[]{:S(2)}, u32[]{:S(2)}) collective-permute-start(bf16[96,1024]{1,0:T(8,128)(2,1)S(1)} %get-tuple-element.117), channel_id=1, source_target_pairs={{0,2},{1,3},{2,0},{3,1},{4,6},{5,7},{6,4},{7,5},{8,10},{9,11},{10,... | collective-permute-start | bytes 589832 | tf_op jit(solution)/shard_map/ppermute | solution.py:83
  59.8 2.1 %shard_map.91._ = bf16[44,384,2048]{2,1,0:T(8,128)(2,1)} custom-call(bf16[384,2048]{1,0:T(8,128)(2,1)S(1)} %get-tuple-element.100.refs_0_, bf16[384,2048]{1,0:T(8,128)(2,1)S(1)} %get-tuple-element.109.refs_1_, bf16[384,768]{1,0:T(8,128)(2,1)S(1)} %get-tuple-element.101.hid_ref.refs_2_, ...), custom_call_target="tpu_custom_call", output_to_operand_aliasing={{}: (5, {})} | custom-call | tf_op jit(solution)/shard_map/pallas_call | solution.py:392
  61.9 4.3 %collective-permute-done.16.refs_1_ = bf16[96,1024]{1,0:T(8,128)(2,1)S(1)} collective-permute-done((bf16[96,1024]{1,0:T(8,128)(2,1)S(1)}, bf16[96,1024]{1,0:T(8,128)(2,1)S(1)}, u32[]{:S(2)}, u32[]{:S(2)}) %collective-permute-start.16) | collective-permute-done | bytes 196640 | tf_op jit(solution)/shard_map/ppermute | solution.py:83
  66.8 1.2 %collective-permute-start.15 = (bf16[96,1024]{1,0:T(8,128)(2,1)S(1)}, bf16[96,1024]{1,0:T(8,128)(2,1)S(1)}, u32[]{:S(2)}, u32[]{:S(2)}) collective-permute-start(bf16[96,1024]{1,0:T(8,128)(2,1)S(1)} %get-tuple-element.119), channel_id=1, source_target_pairs={{0,6},{1,7},{2,4},{3,5},{4,2},{5,3},{6,0},{7,1},{8,14},{9,15},{10,... | collective-permute-start | bytes 589832 | tf_op jit(solution)/shard_map/ppermute | solution.py:83
  68.1 2.5 %collective-permute-done.18.refs_3_ = bf16[96,1024]{1,0:T(8,128)(2,1)S(1)} collective-permute-done((bf16[96,1024]{1,0:T(8,128)(2,1)S(1)}, bf16[96,1024]{1,0:T(8,128)(2,1)S(1)}, u32[]{:S(2)}, u32[]{:S(2)}) %collective-permute-start.18) | collective-permute-done | bytes 196640 | tf_op jit(solution)/shard_map/ppermute | solution.py:83
  71.0 1.5 %collective-permute-done.19.refs_0_ = bf16[128,1024]{1,0:T(8,128)(2,1)S(1)} collective-permute-done((bf16[128,1024]{1,0:T(8,128)(2,1)S(1)}, bf16[128,1024]{1,0:T(8,128)(2,1)S(1)}, u32[]{:S(2)}, u32[]{:S(2)}) %collective-permute-start.19) | collective-permute-done | bytes 262176 | tf_op jit(solution)/shard_map/ppermute | solution.py:83
  72.5 1.3 %collective-permute-start.22 = (bf16[128,1024]{1,0:T(8,128)(2,1)S(1)}, bf16[128,1024]{1,0:T(8,128)(2,1)S(1)}, u32[]{:S(2)}, u32[]{:S(2)}) collective-permute-start(bf16[128,1024]{1,0:T(8,128)(2,1)S(1)} %shard_map.95), channel_id=1, source_target_pairs={{8,0},{16,8},{24,16},{9,1},{17,9},{25,17},{10,2},{18,10},{26,18},{... | collective-permute-start | bytes 786440 | tf_op jit(solution)/shard_map/ppermute | solution.py:630
  73.8 0.9 collective-permute-done.13.refs_1_
  74.9 4.0 %collective-permute-done.15.refs_3_ = bf16[96,1024]{1,0:T(8,128)(2,1)S(1)} collective-permute-done((bf16[96,1024]{1,0:T(8,128)(2,1)S(1)}, bf16[96,1024]{1,0:T(8,128)(2,1)S(1)}, u32[]{:S(2)}, u32[]{:S(2)}) %collective-permute-start.15) | collective-permute-done | bytes 196640 | tf_op jit(solution)/shard_map/ppermute | solution.py:83
  79.4 1.4 %collective-permute-done.20.refs_0_ = bf16[128,1024]{1,0:T(8,128)(2,1)S(1)} collective-permute-done((bf16[128,1024]{1,0:T(8,128)(2,1)S(1)}, bf16[128,1024]{1,0:T(8,128)(2,1)S(1)}, u32[]{:S(2)}, u32[]{:S(2)}) %collective-permute-start.20) | collective-permute-done | bytes 262176 | tf_op jit(solution)/shard_map/ppermute | solution.py:83
  80.9 1.5 %collective-permute-start.21 = (bf16[128,1024]{1,0:T(8,128)(2,1)S(1)}, bf16[128,1024]{1,0:T(8,128)(2,1)S(1)}, u32[]{:S(2)}, u32[]{:S(2)}) collective-permute-start(bf16[128,1024]{1,0:T(8,128)(2,1)S(1)} %shard_map.98), channel_id=1, source_target_pairs={{8,0},{16,8},{24,16},{9,1},{17,9},{25,17},{10,2},{18,10},{26,18},{... | collective-permute-start | bytes 786440 | tf_op jit(solution)/shard_map/ppermute | solution.py:630
  83.0 1.3 %collective-permute-done.23.refs_0_ = bf16[128,1024]{1,0:T(8,128)(2,1)S(1)} collective-permute-done((bf16[128,1024]{1,0:T(8,128)(2,1)S(1)}, bf16[128,1024]{1,0:T(8,128)(2,1)S(1)}, u32[]{:S(2)}, u32[]{:S(2)}) %collective-permute-start.23) | collective-permute-done | bytes 262176 | tf_op jit(solution)/shard_map/ppermute | solution.py:83
  85.2 1.3 %collective-permute-start.26 = (bf16[96,1024]{1,0:T(8,128)(2,1)S(1)}, bf16[96,1024]{1,0:T(8,128)(2,1)S(1)}, u32[]{:S(2)}, u32[]{:S(2)}) collective-permute-start(bf16[96,1024]{1,0:T(8,128)(2,1)S(1)} %get-tuple-element.140), channel_id=1, source_target_pairs={{0,4},{1,5},{2,6},{3,7},{4,0},{5,1},{6,2},{7,3},{8,12},{9,13},{10,... | collective-permute-start | bytes 589832 | tf_op jit(solution)/shard_map/ppermute | solution.py:83
  86.6 1.6 %collective-permute-start.27 = (bf16[96,1024]{1,0:T(8,128)(2,1)S(1)}, bf16[96,1024]{1,0:T(8,128)(2,1)S(1)}, u32[]{:S(2)}, u32[]{:S(2)}) collective-permute-start(bf16[96,1024]{1,0:T(8,128)(2,1)S(1)} %get-tuple-element.141), channel_id=1, source_target_pairs={{0,6},{1,7},{2,4},{3,5},{4,2},{5,3},{6,0},{7,1},{8,14},{9,15},{10,... | collective-permute-start | bytes 589832 | tf_op jit(solution)/shard_map/ppermute | solution.py:83
  88.1 3.0 %collective-permute-done.21.raw_ref = bf16[128,1024]{1,0:T(8,128)(2,1)S(1)} collective-permute-done((bf16[128,1024]{1,0:T(8,128)(2,1)S(1)}, bf16[128,1024]{1,0:T(8,128)(2,1)S(1)}, u32[]{:S(2)}, u32[]{:S(2)}) %collective-permute-start.21) | collective-permute-done | bytes 262176 | tf_op jit(solution)/shard_map/ppermute | solution.py:630
  91.4 1.3 %collective-permute-done.24.refs_0_ = bf16[128,1024]{1,0:T(8,128)(2,1)S(1)} collective-permute-done((bf16[128,1024]{1,0:T(8,128)(2,1)S(1)}, bf16[128,1024]{1,0:T(8,128)(2,1)S(1)}, u32[]{:S(2)}, u32[]{:S(2)}) %collective-permute-start.24) | collective-permute-done | bytes 262176 | tf_op jit(solution)/shard_map/ppermute | solution.py:83
  93.6 1.2 %collective-permute-start.29 = (bf16[96,1024]{1,0:T(8,128)(2,1)S(1)}, bf16[96,1024]{1,0:T(8,128)(2,1)S(1)}, u32[]{:S(2)}, u32[]{:S(2)}) collective-permute-start(bf16[96,1024]{1,0:T(8,128)(2,1)S(1)} %get-tuple-element.145), channel_id=1, source_target_pairs={{0,4},{1,5},{2,6},{3,7},{4,0},{5,1},{6,2},{7,3},{8,12},{9,13},{10,... | collective-permute-start | bytes 589832 | tf_op jit(solution)/shard_map/ppermute | solution.py:83
  94.8 1.6 %collective-permute-start.30 = (bf16[96,1024]{1,0:T(8,128)(2,1)S(1)}, bf16[96,1024]{1,0:T(8,128)(2,1)S(1)}, u32[]{:S(2)}, u32[]{:S(2)}) collective-permute-start(bf16[96,1024]{1,0:T(8,128)(2,1)S(1)} %get-tuple-element.146), channel_id=1, source_target_pairs={{0,6},{1,7},{2,4},{3,5},{4,2},{5,3},{6,0},{7,1},{8,14},{9,15},{10,... | collective-permute-start | bytes 589832 | tf_op jit(solution)/shard_map/ppermute | solution.py:83
  96.5 3.8 %shard_map.103 = (bf16[44,384,2048]{2,1,0:T(8,128)(2,1)}, bf16[384,704]{1,0:T(8,128)(2,1)S(1)}, f32[384,704]{1,0:T(8,128)S(1)}) custom-call(bf16[704,2048]{1,0:T(8,128)(2,1)S(1)} %bitcast.29, bf16[44,384,2048]{2,1,0:T(8,128)(2,1)} %shard_map.91._, bf16[96,2048]{1,0:T(8,128)(2,1)S(1)} %copy-done.4, ...), custom_call_target="tpu_custom_call", output_to_operand_aliasing={{0}: (1, {})} | custom-call | bytes 9247391744 | tf_op jit(solution)/shard_map/pallas_call | solution.py:44
  100.3 4.4 %shard_map.104 = (f32[384,704]{1,0:T(8,128)S(1)}, bf16[704,2048]{1,0:T(8,128)(2,1)}) custom-call(bf16[704,2048]{1,0:T(8,128)(2,1)S(1)} %bitcast.31, bf16[384,704]{1,0:T(8,128)(2,1)S(1)} %get-tuple-element.151.hid1_ref.hid_ref, bf16[44,384,2048]{2,1,0:T(8,128)(2,1)} %get-tuple-element.152.pad_ref, bf16[96,1024]{1,0:T(8,128)(2,1)S(1)} %get-tuple-element.138.refs_0_, ...), custom_call_target="tpu_custom_call" | custom-call | bytes 523239424 | tf_op jit(solution)/shard_map/pallas_call | solution.py:430
  105.1 2.4 %shard_map.105 = (bf16[384,1024]{1,0:T(8,128)(2,1)S(1)}, bf16[384,768]{1,0:T(8,128)(2,1)S(1)}, bf16[384,128]{1,0:T(8,128)(2,1)}) custom-call(bf16[704,2048]{1,0:T(8,128)(2,1)S(1)} %bitcast.32, bf16[384,704]{1,0:T(8,128)(2,1)S(1)} %get-tuple-element.151.hid1_ref.hid_ref, f32[384,704]{1,0:T(8,128)S(1)} %get-tuple-element.154.slope_ref, ...), custom_call_target="tpu_custom_call" | custom-call | bytes 4931452928 | tf_op jit(solution)/shard_map/pallas_call | solution.py:44
  107.6 3.4 %all-to-all-start.1 = ((bf16[8,48,128]{2,1,0:T(8,128)(2,1)}), bf16[8,48,128]{2,1,0:T(8,128)(2,1)S(1)}, u32[]{:S(2)}, u32[]{:S(2)}) async-start(bf16[8,48,128]{2,1,0:T(8,128)(2,1)} %bitcast.13), calls=%async_computation.1 | async-start | bytes 196608 | tf_op jit(solution)/shard_map/all_to_all | solution.py:271
  110.9 6.8 %shard_map.106 = (bf16[704,2048]{1,0:T(8,128)(2,1)}, bf16[704,2048]{1,0:T(8,128)(2,1)}) custom-call(bf16[704,2048]{1,0:T(8,128)(2,1)} %get-tuple-element.153._, bf16[44,384,2048]{2,1,0:T(8,128)(2,1)} %get-tuple-element.152.pad_ref, bf16[384,1024]{1,0:T(8,128)(2,1)S(1)} %get-tuple-element.160.g1_ref, ...), custom_call_target="tpu_custom_call", output_to_operand_aliasing={{1}: (0, {})} | custom-call | bytes 369098752 | tf_op jit(solution)/shard_map/pallas_call | solution.py:506
  117.8 0.9 shard_map.107
  (64 shorter events, 10.4 us)
Async XLA Ops:
  0.6 46.7 %copy-start = (bf16[1,1,704,2048]{3,2,1,0:T(8,128)(2,1)S(1)}, bf16[1,1,704,2048]{3,2,1,0:T(8,128)(2,1)}, u32[]{:S(2)}) copy-start(bf16[1,1,704,2048]{3,2,1,0:T(8,128)(2,1)} %param.8) | copy-start | bytes 8650756
  2.9 11.0 %collective-permute-start.1 = (bf16[128,2048]{1,0:T(8,128)(2,1)}, bf16[128,2048]{1,0:T(8,128)(2,1)}, u32[]{:S(2)}, u32[]{:S(2)}) collective-permute-start(bf16[128,2048]{1,0:T(8,128)(2,1)} %get-tuple-element.167.refs_2_), channel_id=1, source_target_pairs={{0,1},{1,0},{2,3},{3,2},{4,5},{5,4},{6,7},{7,6},{8,9},{9,8},{10,11... | collective-permute-start | bytes 1572872 | tf_op jit(solution)/shard_map/ppermute | solution.py:83
  3.3 18.5 %collective-permute-start.2 = (bf16[128,2048]{1,0:T(8,128)(2,1)S(1)}, bf16[128,2048]{1,0:T(8,128)(2,1)}, u32[]{:S(2)}, u32[]{:S(2)}) collective-permute-start(bf16[128,2048]{1,0:T(8,128)(2,1)S(1)} %get-tuple-element.168.refs_0_), channel_id=1, source_target_pairs={{0,2},{1,3},{2,0},{3,1},{4,6},{5,7},{6,4},{7,5},{8,10},{9,11},{10,... | collective-permute-start | bytes 1572872 | tf_op jit(solution)/shard_map/ppermute | solution.py:83
  5.8 19.5 %collective-permute-start.8 = (bf16[128,2048]{1,0:T(8,128)(2,1)}, bf16[128,2048]{1,0:T(8,128)(2,1)}, u32[]{:S(2)}, u32[]{:S(2)}) collective-permute-start(bf16[128,2048]{1,0:T(8,128)(2,1)} %bitcast.33), channel_id=1, source_target_pairs={{0,4},{1,5},{2,6},{3,7},{4,0},{5,1},{6,2},{7,3},{8,12},{9,13},{10,... | collective-permute-start | bytes 1572872 | tf_op jit(solution)/shard_map/ppermute | solution.py:83
  9.3 12.5 %all-to-all-start = ((f32[8,8,128]{2,1,0:T(8,128)}), f32[8,8,128]{2,1,0:T(8,128)S(1)}, u32[]{:S(2)}, u32[]{:S(2)}) async-start(f32[8,8,128]{2,1,0:T(8,128)} %broadcast_in_dim.15), calls=%async_computation | async-start | bytes 65536 | tf_op jit(solution)/shard_map/all_to_all | solution.py:557
  12.7 1.2 %collective-permute-start = (f32[8,128]{1,0:T(8,128)S(1)}, f32[8,128]{1,0:T(8,128)S(1)}, u32[]{:S(2)}, u32[]{:S(2)}) collective-permute-start(f32[8,128]{1,0:T(8,128)S(1)} %pad_maximum_fusion.refs_0_), channel_id=1, source_target_pairs={{0,1},{1,0},{2,3},{3,2},{4,5},{5,4},{6,7},{7,6},{8,9},{9,8},{10,11... | collective-permute-start | bytes 12296 | tf_op jit(solution)/shard_map/ppermute | solution.py:83
  17.0 0.7 copy-start.3
  17.7 0.8 copy-start.7
  18.5 11.7 %collective-permute-start.6 = (bf16[96,2048]{1,0:T(8,128)(2,1)}, bf16[96,2048]{1,0:T(8,128)(2,1)}, u32[]{:S(2)}, u32[]{:S(2)}) collective-permute-start(bf16[96,2048]{1,0:T(8,128)(2,1)} %get-tuple-element.88), channel_id=1, source_target_pairs={{0,2},{1,3},{2,0},{3,1},{4,6},{5,7},{6,4},{7,5},{8,10},{9,11},{10,... | collective-permute-start | bytes 1179656 | tf_op jit(solution)/shard_map/ppermute | solution.py:83
  20.3 12.3 %collective-permute-start.7 = (bf16[96,2048]{1,0:T(8,128)(2,1)}, bf16[96,2048]{1,0:T(8,128)(2,1)}, u32[]{:S(2)}, u32[]{:S(2)}) collective-permute-start(bf16[96,2048]{1,0:T(8,128)(2,1)} %get-tuple-element.89), channel_id=1, source_target_pairs={{0,4},{1,5},{2,6},{3,7},{4,0},{5,1},{6,2},{7,3},{8,12},{9,13},{10,... | collective-permute-start | bytes 1179656 | tf_op jit(solution)/shard_map/ppermute | solution.py:83
  21.8 27.3 %copy-start.8 = (bf16[96,2048]{1,0:T(8,128)(2,1)S(1)}, bf16[96,2048]{1,0:T(8,128)(2,1)}, u32[]{:S(2)}) copy-start(bf16[96,2048]{1,0:T(8,128)(2,1)} %copy-done.7) | copy-start | bytes 1179652
  24.0 26.6 %copy-start.1 = (bf16[1,1,704,2048]{3,2,1,0:T(8,128)(2,1)S(1)}, bf16[1,1,704,2048]{3,2,1,0:T(8,128)(2,1)}, u32[]{:S(2)}) copy-start(bf16[1,1,704,2048]{3,2,1,0:T(8,128)(2,1)} %param.9) | copy-start | bytes 8650756
  24.0 8.7 %collective-permute-start.3 = (bf16[96,2048]{1,0:T(8,128)(2,1)S(1)}, bf16[96,2048]{1,0:T(8,128)(2,1)S(1)}, u32[]{:S(2)}, u32[]{:S(2)}) collective-permute-start(bf16[96,2048]{1,0:T(8,128)(2,1)S(1)} %get-tuple-element.93), channel_id=1, source_target_pairs={{0,1},{1,0},{2,3},{3,2},{4,5},{5,4},{6,7},{7,6},{8,9},{9,8},{10,11... | collective-permute-start | bytes 1179656 | tf_op jit(solution)/shard_map/ppermute | solution.py:83
  24.7 5.5 %copy-start.5 = (bf16[384,128]{1,0:T(8,128)(2,1)}, bf16[384,128]{1,0:T(8,128)(2,1)S(1)}, u32[]{:S(2)}) copy-start(bf16[384,128]{1,0:T(8,128)(2,1)S(1)} %get-tuple-element.165.hot1_ref) | copy-start | bytes 294916
  24.7 16.3 %collective-permute-start.4 = (bf16[96,2048]{1,0:T(8,128)(2,1)S(1)}, bf16[96,2048]{1,0:T(8,128)(2,1)S(1)}, u32[]{:S(2)}, u32[]{:S(2)}) collective-permute-start(bf16[96,2048]{1,0:T(8,128)(2,1)S(1)} %get-tuple-element.94), channel_id=1, source_target_pairs={{0,4},{1,5},{2,6},{3,7},{4,0},{5,1},{6,2},{7,3},{8,12},{9,13},{10,... | collective-permute-start | bytes 1179656 | tf_op jit(solution)/shard_map/ppermute | solution.py:83
  25.3 22.0 %collective-permute-start.5 = (bf16[96,2048]{1,0:T(8,128)(2,1)S(1)}, bf16[96,2048]{1,0:T(8,128)(2,1)S(1)}, u32[]{:S(2)}, u32[]{:S(2)}) collective-permute-start(bf16[96,2048]{1,0:T(8,128)(2,1)S(1)} %get-tuple-element.95), channel_id=1, source_target_pairs={{0,5},{1,4},{2,7},{3,6},{4,1},{5,0},{6,3},{7,2},{8,13},{9,12},{10,... | collective-permute-start | bytes 1179656 | tf_op jit(solution)/shard_map/ppermute | solution.py:83
  26.6 1.0 copy-start.2
  30.2 19.0 %collective-permute-start.10 = (bf16[96,2048]{1,0:T(8,128)(2,1)S(1)}, bf16[96,2048]{1,0:T(8,128)(2,1)S(1)}, u32[]{:S(2)}, u32[]{:S(2)}) collective-permute-start(bf16[96,2048]{1,0:T(8,128)(2,1)S(1)} %get-tuple-element.106), channel_id=1, source_target_pairs={{0,2},{1,3},{2,0},{3,1},{4,6},{5,7},{6,4},{7,5},{8,10},{9,11},{10,... | collective-permute-start | bytes 1179656 | tf_op jit(solution)/shard_map/ppermute | solution.py:83
  32.7 16.5 %collective-permute-start.9 = (bf16[96,2048]{1,0:T(8,128)(2,1)S(1)}, bf16[96,2048]{1,0:T(8,128)(2,1)S(1)}, u32[]{:S(2)}, u32[]{:S(2)}) collective-permute-start(bf16[96,2048]{1,0:T(8,128)(2,1)S(1)} %get-tuple-element.105), channel_id=1, source_target_pairs={{0,1},{1,0},{2,3},{3,2},{4,5},{5,4},{6,7},{7,6},{8,9},{9,8},{10,11... | collective-permute-start | bytes 1179656 | tf_op jit(solution)/shard_map/ppermute | solution.py:83
  32.7 16.5 %collective-permute-start.11 = (bf16[96,2048]{1,0:T(8,128)(2,1)S(1)}, bf16[96,2048]{1,0:T(8,128)(2,1)S(1)}, u32[]{:S(2)}, u32[]{:S(2)}) collective-permute-start(bf16[96,2048]{1,0:T(8,128)(2,1)S(1)} %get-tuple-element.108), channel_id=1, source_target_pairs={{0,3},{1,2},{2,1},{3,0},{4,7},{5,6},{6,5},{7,4},{8,11},{9,10},{10,... | collective-permute-start | bytes 1179656 | tf_op jit(solution)/shard_map/ppermute | solution.py:83
  49.2 21.4 %collective-permute-start.12 = (bf16[96,2048]{1,0:T(8,128)(2,1)S(1)}, bf16[96,2048]{1,0:T(8,128)(2,1)S(1)}, u32[]{:S(2)}, u32[]{:S(2)}) collective-permute-start(bf16[96,2048]{1,0:T(8,128)(2,1)S(1)} %copy-done.8), channel_id=1, source_target_pairs={{0,6},{1,7},{2,4},{3,5},{4,2},{5,3},{6,0},{7,1},{8,14},{9,15},{10,... | collective-permute-start | bytes 1179656 | tf_op jit(solution)/shard_map/ppermute | solution.py:83
  53.8 12.4 %collective-permute-start.16 = (bf16[96,1024]{1,0:T(8,128)(2,1)S(1)}, bf16[96,1024]{1,0:T(8,128)(2,1)S(1)}, u32[]{:S(2)}, u32[]{:S(2)}) collective-permute-start(bf16[96,1024]{1,0:T(8,128)(2,1)S(1)} %get-tuple-element.122), channel_id=1, source_target_pairs={{0,2},{1,3},{2,0},{3,1},{4,6},{5,7},{6,4},{7,5},{8,10},{9,11},{10,... | collective-permute-start | bytes 589832 | tf_op jit(solution)/shard_map/ppermute | solution.py:83
  55.4 11.4 %collective-permute-start.17 = (bf16[96,1024]{1,0:T(8,128)(2,1)S(1)}, bf16[96,1024]{1,0:T(8,128)(2,1)S(1)}, u32[]{:S(2)}, u32[]{:S(2)}) collective-permute-start(bf16[96,1024]{1,0:T(8,128)(2,1)S(1)} %get-tuple-element.123), channel_id=1, source_target_pairs={{0,4},{1,5},{2,6},{3,7},{4,0},{5,1},{6,2},{7,3},{8,12},{9,13},{10,... | collective-permute-start | bytes 589832 | tf_op jit(solution)/shard_map/ppermute | solution.py:83
  56.0 14.5 %collective-permute-start.18 = (bf16[96,1024]{1,0:T(8,128)(2,1)S(1)}, bf16[96,1024]{1,0:T(8,128)(2,1)S(1)}, u32[]{:S(2)}, u32[]{:S(2)}) collective-permute-start(bf16[96,1024]{1,0:T(8,128)(2,1)S(1)} %get-tuple-element.124), channel_id=1, source_target_pairs={{0,6},{1,7},{2,4},{3,5},{4,2},{5,3},{6,0},{7,1},{8,14},{9,15},{10,... | collective-permute-start | bytes 589832 | tf_op jit(solution)/shard_map/ppermute | solution.py:83
  58.3 16.5 %collective-permute-start.13 = (bf16[96,1024]{1,0:T(8,128)(2,1)S(1)}, bf16[96,1024]{1,0:T(8,128)(2,1)S(1)}, u32[]{:S(2)}, u32[]{:S(2)}) collective-permute-start(bf16[96,1024]{1,0:T(8,128)(2,1)S(1)} %get-tuple-element.117), channel_id=1, source_target_pairs={{0,2},{1,3},{2,0},{3,1},{4,6},{5,7},{6,4},{7,5},{8,10},{9,11},{10,... | collective-permute-start | bytes 589832 | tf_op jit(solution)/shard_map/ppermute | solution.py:83
  66.3 8.6 %collective-permute-start.14 = (bf16[96,1024]{1,0:T(8,128)(2,1)S(1)}, bf16[96,1024]{1,0:T(8,128)(2,1)S(1)}, u32[]{:S(2)}, u32[]{:S(2)}) collective-permute-start(bf16[96,1024]{1,0:T(8,128)(2,1)S(1)} %get-tuple-element.118), channel_id=1, source_target_pairs={{0,4},{1,5},{2,6},{3,7},{4,0},{5,1},{6,2},{7,3},{8,12},{9,13},{10,... | collective-permute-start | bytes 589832 | tf_op jit(solution)/shard_map/ppermute | solution.py:83
  66.8 12.1 %collective-permute-start.15 = (bf16[96,1024]{1,0:T(8,128)(2,1)S(1)}, bf16[96,1024]{1,0:T(8,128)(2,1)S(1)}, u32[]{:S(2)}, u32[]{:S(2)}) collective-permute-start(bf16[96,1024]{1,0:T(8,128)(2,1)S(1)} %get-tuple-element.119), channel_id=1, source_target_pairs={{0,6},{1,7},{2,4},{3,5},{4,2},{5,3},{6,0},{7,1},{8,14},{9,15},{10,... | collective-permute-start | bytes 589832 | tf_op jit(solution)/shard_map/ppermute | solution.py:83
  70.9 1.6 %collective-permute-start.19 = (bf16[128,1024]{1,0:T(8,128)(2,1)S(1)}, bf16[128,1024]{1,0:T(8,128)(2,1)S(1)}, u32[]{:S(2)}, u32[]{:S(2)}) collective-permute-start(bf16[128,1024]{1,0:T(8,128)(2,1)S(1)} %get-tuple-element.130), channel_id=1, source_target_pairs={{0,1},{1,0},{2,3},{3,2},{4,5},{5,4},{6,7},{7,6},{8,9},{9,8},{10,11... | collective-permute-start | bytes 786440 | tf_op jit(solution)/shard_map/ppermute | solution.py:83
  72.5 10.2 %collective-permute-start.22 = (bf16[128,1024]{1,0:T(8,128)(2,1)S(1)}, bf16[128,1024]{1,0:T(8,128)(2,1)S(1)}, u32[]{:S(2)}, u32[]{:S(2)}) collective-permute-start(bf16[128,1024]{1,0:T(8,128)(2,1)S(1)} %shard_map.95), channel_id=1, source_target_pairs={{8,0},{16,8},{24,16},{9,1},{17,9},{25,17},{10,2},{18,10},{26,18},{... | collective-permute-start | bytes 786440 | tf_op jit(solution)/shard_map/ppermute | solution.py:630
  79.2 1.6 %collective-permute-start.20 = (bf16[128,1024]{1,0:T(8,128)(2,1)S(1)}, bf16[128,1024]{1,0:T(8,128)(2,1)S(1)}, u32[]{:S(2)}, u32[]{:S(2)}) collective-permute-start(bf16[128,1024]{1,0:T(8,128)(2,1)S(1)} %get-tuple-element.136), channel_id=1, source_target_pairs={{0,1},{1,0},{2,3},{3,2},{4,5},{5,4},{6,7},{7,6},{8,9},{9,8},{10,11... | collective-permute-start | bytes 786440 | tf_op jit(solution)/shard_map/ppermute | solution.py:83
  80.9 10.2 %collective-permute-start.21 = (bf16[128,1024]{1,0:T(8,128)(2,1)S(1)}, bf16[128,1024]{1,0:T(8,128)(2,1)S(1)}, u32[]{:S(2)}, u32[]{:S(2)}) collective-permute-start(bf16[128,1024]{1,0:T(8,128)(2,1)S(1)} %shard_map.98), channel_id=1, source_target_pairs={{8,0},{16,8},{24,16},{9,1},{17,9},{25,17},{10,2},{18,10},{26,18},{... | collective-permute-start | bytes 786440 | tf_op jit(solution)/shard_map/ppermute | solution.py:630
  82.8 1.5 %collective-permute-start.23 = (bf16[128,1024]{1,0:T(8,128)(2,1)S(1)}, bf16[128,1024]{1,0:T(8,128)(2,1)S(1)}, u32[]{:S(2)}, u32[]{:S(2)}) collective-permute-start(bf16[128,1024]{1,0:T(8,128)(2,1)S(1)} %collective-permute-done.22.raw_ref), channel_id=1, source_target_pairs={{0,1},{1,0},{2,3},{3,2},{4,5},{5,4},{6,7},{7,6},{8,9},{9,8},{10,11... | collective-permute-start | bytes 786440 | tf_op jit(solution)/shard_map/ppermute | solution.py:83
  84.6 10.2 %collective-permute-start.25 = (bf16[96,1024]{1,0:T(8,128)(2,1)S(1)}, bf16[96,1024]{1,0:T(8,128)(2,1)S(1)}, u32[]{:S(2)}, u32[]{:S(2)}) collective-permute-start(bf16[96,1024]{1,0:T(8,128)(2,1)S(1)} %get-tuple-element.139), channel_id=1, source_target_pairs={{0,2},{1,3},{2,0},{3,1},{4,6},{5,7},{6,4},{7,5},{8,10},{9,11},{10,... | collective-permute-start | bytes 589832 | tf_op jit(solution)/shard_map/ppermute | solution.py:83
  85.2 15.0 %collective-permute-start.26 = (bf16[96,1024]{1,0:T(8,128)(2,1)S(1)}, bf16[96,1024]{1,0:T(8,128)(2,1)S(1)}, u32[]{:S(2)}, u32[]{:S(2)}) collective-permute-start(bf16[96,1024]{1,0:T(8,128)(2,1)S(1)} %get-tuple-element.140), channel_id=1, source_target_pairs={{0,4},{1,5},{2,6},{3,7},{4,0},{5,1},{6,2},{7,3},{8,12},{9,13},{10,... | collective-permute-start | bytes 589832 | tf_op jit(solution)/shard_map/ppermute | solution.py:83
  86.6 13.7 %collective-permute-start.27 = (bf16[96,1024]{1,0:T(8,128)(2,1)S(1)}, bf16[96,1024]{1,0:T(8,128)(2,1)S(1)}, u32[]{:S(2)}, u32[]{:S(2)}) collective-permute-start(bf16[96,1024]{1,0:T(8,128)(2,1)S(1)} %get-tuple-element.141), channel_id=1, source_target_pairs={{0,6},{1,7},{2,4},{3,5},{4,2},{5,3},{6,0},{7,1},{8,14},{9,15},{10,... | collective-permute-start | bytes 589832 | tf_op jit(solution)/shard_map/ppermute | solution.py:83
  91.1 1.5 %collective-permute-start.24 = (bf16[128,1024]{1,0:T(8,128)(2,1)S(1)}, bf16[128,1024]{1,0:T(8,128)(2,1)S(1)}, u32[]{:S(2)}, u32[]{:S(2)}) collective-permute-start(bf16[128,1024]{1,0:T(8,128)(2,1)S(1)} %collective-permute-done.21.raw_ref), channel_id=1, source_target_pairs={{0,1},{1,0},{2,3},{3,2},{4,5},{5,4},{6,7},{7,6},{8,9},{9,8},{10,11... | collective-permute-start | bytes 786440 | tf_op jit(solution)/shard_map/ppermute | solution.py:83
  91.1 5.3 %copy-start.4 = (bf16[96,2048]{1,0:T(8,128)(2,1)S(1)}, bf16[96,2048]{1,0:T(8,128)(2,1)}, u32[]{:S(2)}) copy-start(bf16[96,2048]{1,0:T(8,128)(2,1)} %copy-done.3) | copy-start | bytes 1179652
  92.9 11.8 %collective-permute-start.28 = (bf16[96,1024]{1,0:T(8,128)(2,1)S(1)}, bf16[96,1024]{1,0:T(8,128)(2,1)S(1)}, u32[]{:S(2)}, u32[]{:S(2)}) collective-permute-start(bf16[96,1024]{1,0:T(8,128)(2,1)S(1)} %get-tuple-element.144), channel_id=1, source_target_pairs={{0,2},{1,3},{2,0},{3,1},{4,6},{5,7},{6,4},{7,5},{8,10},{9,11},{10,... | collective-permute-start | bytes 589832 | tf_op jit(solution)/shard_map/ppermute | solution.py:83
  93.6 11.2 %collective-permute-start.29 = (bf16[96,1024]{1,0:T(8,128)(2,1)S(1)}, bf16[96,1024]{1,0:T(8,128)(2,1)S(1)}, u32[]{:S(2)}, u32[]{:S(2)}) collective-permute-start(bf16[96,1024]{1,0:T(8,128)(2,1)S(1)} %get-tuple-element.145), channel_id=1, source_target_pairs={{0,4},{1,5},{2,6},{3,7},{4,0},{5,1},{6,2},{7,3},{8,12},{9,13},{10,... | collective-permute-start | bytes 589832 | tf_op jit(solution)/shard_map/ppermute | solution.py:83
  94.8 10.3 %collective-permute-start.30 = (bf16[96,1024]{1,0:T(8,128)(2,1)S(1)}, bf16[96,1024]{1,0:T(8,128)(2,1)S(1)}, u32[]{:S(2)}, u32[]{:S(2)}) collective-permute-start(bf16[96,1024]{1,0:T(8,128)(2,1)S(1)} %get-tuple-element.146), channel_id=1, source_target_pairs={{0,6},{1,7},{2,4},{3,5},{4,2},{5,3},{6,0},{7,1},{8,14},{9,15},{10,... | collective-permute-start | bytes 589832 | tf_op jit(solution)/shard_map/ppermute | solution.py:83
  107.6 10.2 %all-to-all-start.1 = ((bf16[8,48,128]{2,1,0:T(8,128)(2,1)}), bf16[8,48,128]{2,1,0:T(8,128)(2,1)S(1)}, u32[]{:S(2)}, u32[]{:S(2)}) async-start(bf16[8,48,128]{2,1,0:T(8,128)(2,1)} %bitcast.13), calls=%async_computation.1 | async-start | bytes 196608 | tf_op jit(solution)/shard_map/all_to_all | solution.py:271
  110.9 6.9 %copy-start.6 = (bf16[384,128]{1,0:T(8,128)(2,1)S(1)}, bf16[384,128]{1,0:T(8,128)(2,1)}, u32[]{:S(2)}) copy-start(bf16[384,128]{1,0:T(8,128)(2,1)} %copy-done.5) | copy-start | bytes 294916

commit v7 on v6

--- a/solution.py
+++ b/solution.py
@@ -168,8 +168,12 @@
     for s in range(count):
         hot = block_masks(plane, capacity, ranks, refs[s][...], targets)
         picked = dot(hot.astype(bf16), refs[count + s][...], 1, 0).astype(bf16)
-        for i, out_ref in enumerate(refs[2 * count + 1 :]):
-            out_ref[s * capacity : (s + 1) * capacity, :] = picked[i * capacity : (i + 1) * capacity]
+        at = slice(s * capacity, (s + 1) * capacity)
+        for i, out_ref in enumerate(refs[2 * count + 1 : -HALVES]):
+            out_ref[at, :] = picked[i * capacity : (i + 1) * capacity]
+        width = refs[-1].shape[1]
+        for h, out_ref in enumerate(refs[-HALVES:]):
+            out_ref[at, :] = picked[-capacity:, h * width : (h + 1) * width]
 
 
 def pick_own_kernel(hot_ref, raw_ref, out_ref):
@@ -202,7 +206,8 @@
     flops = 2 * tokens * width * capacity * len(plan[1]) * len(plan[2])
     if pad is not None:
         kernel = functools.partial(own_select_kernel, plane, capacity, plan)
-        return call(kernel, [pad] + outs, *meta, *raws, pad_out=True)
+        parts = [shaped((outs[0].shape[0], width // HALVES), bf16)] * HALVES
+        return call(kernel, [pad] + outs[:-1] + parts, *meta, *raws, pad_out=True)
     if hot is None:
         return call(functools.partial(select_kernel, plane, capacity, plan), outs, meta, *raws, flops=flops)
     (own,) = call(pick_own_kernel, [shaped((hot.shape[1], width), bf16)], hot, raws[0], flops=LONG)
@@ -570,8 +575,10 @@
         metas = [own_meta, plane.send(own_meta, (0, 0, 1))]
         x1 = inputs[0, 1]
         pad, *x1 = pick(ranks[1], 2, x1, metas, pad=pad)
-        x1_near, _ = sent_rows(plane, 2, x1[:-1])
-        x1_groups, x1_rest = [(0, sent_layout(plane, 2))], x1[-1:]
+        x1_near, _ = sent_rows(plane, 2, x1[:-HALVES])
+        *near_layout, rest_layout = sent_layout(plane, 2)
+        x1_groups = [(0, near_layout)] + [(h * half, [rest_layout]) for h in range(HALVES)]
+        x1_rest = x1[-HALVES:]
         select_meta = behind(meta, x1)
         x0, x0_layout = sent_rows(plane, 1, pick(ranks[0], 1, x0, select_meta))
         *g0_first, g0_last = pick(ranks[0], 0, g0, select_meta)
@@ -606,8 +613,9 @@
     pad = stash(pad, (X0, G0, HID0, GP0, COLS), x0, g0_in, hid0, gp0, cols)
     leaving, after = [], []
     if stepped:
-        x1_rest = [plane.send(p, t) for p, t in zip(behind(x1_rest, [hid0, *arrived]), plane.across(2)[-1:])]
-        after = [pad, *x1_rest]
+        far = plane.across(2)[-1]
+        x1_rest[0] = plane.send(behind(x1_rest[0], [hid0, *arrived]), far)
+        after = [pad, x1_rest[0]]
     for h, axis in enumerate(AXES):
         if stepped:
             count = len(plane.across(axis))
@@ -622,6 +630,7 @@
         after = [out]
 
     if stepped:
+        x1_rest[1:] = [plane.send(p, far) for p in behind(x1_rest[1:], leaving)]
         x1 = x1_near + x1_rest
     else:
         x1, x1_groups = [exchange(spread(hot1, inputs[0, 1]), experts)], [(0, None)]

time: 119 us -> 118 us (level)
  waiting for transfers between devices: 37.6 us -> 34.7 us
    ppermute x29 -> x30, waiting for transfers between devices: 34.2 us -> 32.5 us  [send(): return lax.ppermute(value, 'expert', route)]
    ppermute x2, waiting for transfers between devices: 3.42 us -> 2.13 us  [body(): lax.ppermute(leaving[h], 'segment', [(i, i - 1) for i in range(1, segment...]
    ppermute x29 -> x30, starting transfers between devices: 27.8 us -> 28.5 us  [send(): return lax.ppermute(value, 'expert', route)]
  transfers between devices with their start and end apart: 33 -> 34, of which waited for: 17 -> 15; matrix products, arithmetic and copies ran while one was open for 2% -> 2% of each run, Pallas kernels for 28% -> 28%
where the time goes in v7:
time: 118 us; the launch traced here: 117 us
  starting transfers between devices  38 us (32%)
  Pallas kernels  36.2 us (31%)
  waiting for transfers between devices  34.7 us (29%)
  local copies, waits for them, and re-layouts  5.99 us (5%)
  other arithmetic  1.37 us (1%)
    ppermute x30, waiting for transfers between devices, send(): return lax.ppermute(value, 'expert', route)  32.5 us
    ppermute x30, starting transfers between devices, send(): return lax.ppermute(value, 'expert', route)  28.5 us
    pallas_call x20, Pallas kernels, call(): pl.pallas_call(kernel, out_shape=outs, in_specs=specs, out_specs=[in_hbm(...  22.8 us
    pallas_call x1, Pallas kernels, late(): pl.pallas_call(functools.partial(late_kernel, width, part, units), out_sh...  6.85 us
    pallas_call x1, Pallas kernels, early(): pl.pallas_call(functools.partial(early_kernel, plane, capacity, groups),...  4.44 us
    all_to_all x1, starting transfers between devices, exchange(): lax.all_to_all(pieces, 'expert', split_axis=0, concat_axis=0, tiled=True)  3.37 us
    all_to_all x1, starting transfers between devices, body(): lax.all_to_all(meta, 'expert', split_axis=0, concat_axis=0, tiled=True)  3.33 us
    unnamed x18, local copies, waits for them, and re-layouts  3.13 us
  transfers between devices with their start and end apart: 34, of which 15 were waited for; matrix products, arithmetic and copies ran while one was open for 2% of the time, Pallas kernels for 28%

profile of v7, /device:TPU:0, one launch (start us, length us, event | category | flops | bytes accessed | tf_op | source)
XLA Modules:
  0.0 117.2 jit_solution(14333164502681543573)
XLA Ops:
  0.6 2.2 %slice_bitcast_fusion = (bf16[128,2048]{1,0:T(8,128)(2,1)}, bf16[128,2048]{1,0:T(8,128)(2,1)S(1)}) fusion(bf16[1,2,128,2048]{3,2,1,0:T(8,128)(2,1)} %param.6), kind=kLoop, calls=%fused_computation | loop fusion | bytes 2097152 | tf_op jit(solution)/shard_map/squeeze | solution.py:576
  3.3 2.5 %collective-permute-start.2 = (bf16[128,2048]{1,0:T(8,128)(2,1)S(1)}, bf16[128,2048]{1,0:T(8,128)(2,1)}, u32[]{:S(2)}, u32[]{:S(2)}) collective-permute-start(bf16[128,2048]{1,0:T(8,128)(2,1)S(1)} %get-tuple-element.174.refs_0_), channel_id=1, source_target_pairs={{0,2},{1,3},{2,0},{3,1},{4,6},{5,7},{6,4},{7,5},{8,10},{9,11},{10,... | collective-permute-start | bytes 1572872 | tf_op jit(solution)/shard_map/ppermute | solution.py:83
  5.8 1.5 %collective-permute-start.8 = (bf16[128,2048]{1,0:T(8,128)(2,1)}, bf16[128,2048]{1,0:T(8,128)(2,1)}, u32[]{:S(2)}, u32[]{:S(2)}) collective-permute-start(bf16[128,2048]{1,0:T(8,128)(2,1)} %bitcast.33), channel_id=1, source_target_pairs={{0,4},{1,5},{2,6},{3,7},{4,0},{5,1},{6,2},{7,3},{8,12},{9,13},{10,... | collective-permute-start | bytes 1572872 | tf_op jit(solution)/shard_map/ppermute | solution.py:83
  9.3 3.3 %all-to-all-start = ((f32[8,8,128]{2,1,0:T(8,128)}), f32[8,8,128]{2,1,0:T(8,128)S(1)}, u32[]{:S(2)}, u32[]{:S(2)}) async-start(f32[8,8,128]{2,1,0:T(8,128)} %broadcast_in_dim.15), calls=%async_computation | async-start | bytes 65536 | tf_op jit(solution)/shard_map/all_to_all | solution.py:562
  13.9 3.2 %shard_map.85 = (bf16[44,384,2048]{2,1,0:T(8,128)(2,1)}, bf16[96,2048]{1,0:T(8,128)(2,1)S(1)}, bf16[96,2048]{1,0:T(8,128)(2,1)}, bf16[96,2048]{1,0:T(8,128)(2,1)...) custom-call(f32[8,128]{1,0:T(8,128)S(1)} %pad_maximum_fusion.refs_0_, ...), custom_call_target="tpu_custom_call" | custom-call | bytes 4597481472 | tf_op jit(solution)/shard_map/pallas_call | solution.py:44
  18.5 1.9 %collective-permute-start.6 = (bf16[96,2048]{1,0:T(8,128)(2,1)}, bf16[96,2048]{1,0:T(8,128)(2,1)}, u32[]{:S(2)}, u32[]{:S(2)}) collective-permute-start(bf16[96,2048]{1,0:T(8,128)(2,1)} %get-tuple-element.91), channel_id=1, source_target_pairs={{0,2},{1,3},{2,0},{3,1},{4,6},{5,7},{6,4},{7,5},{8,10},{9,11},{10,... | collective-permute-start | bytes 1179656 | tf_op jit(solution)/shard_map/ppermute | solution.py:83
  20.4 1.5 %collective-permute-start.7 = (bf16[96,2048]{1,0:T(8,128)(2,1)}, bf16[96,2048]{1,0:T(8,128)(2,1)}, u32[]{:S(2)}, u32[]{:S(2)}) collective-permute-start(bf16[96,2048]{1,0:T(8,128)(2,1)} %get-tuple-element.92), channel_id=1, source_target_pairs={{0,4},{1,5},{2,6},{3,7},{4,0},{5,1},{6,2},{7,3},{8,12},{9,13},{10,... | collective-permute-start | bytes 1179656 | tf_op jit(solution)/shard_map/ppermute | solution.py:83
  21.9 2.1 %shard_map.86 = (bf16[96,2048]{1,0:T(8,128)(2,1)S(1)}, bf16[96,2048]{1,0:T(8,128)(2,1)S(1)}, bf16[96,2048]{1,0:T(8,128)(2,1)S(1)}, bf16[96,2048]{1,0:T(8,128)(2,1)S(1)}) custom-call(f32[8,8,128]{2,1,0:T(8,128)S(1)} %all-to-all-done.meta_ref, bf16[128,2048]{1,0:T(8,128)(2,1)S(1)} %get-tuple-element.174.refs_0_, bf16[128,2048]{1,0:T(8,128)(2,1)} %collective-permute-done.2.refs_1_), custom_call_target="tpu_custom_call" | custom-call | bytes 169869312 | tf_op jit(solution)/shard_map/pallas_call | solution.py:44
  25.9 1.3 %collective-permute-start.5 = (bf16[96,2048]{1,0:T(8,128)(2,1)S(1)}, bf16[96,2048]{1,0:T(8,128)(2,1)S(1)}, u32[]{:S(2)}, u32[]{:S(2)}) collective-permute-start(bf16[96,2048]{1,0:T(8,128)(2,1)S(1)} %get-tuple-element.99), channel_id=1, source_target_pairs={{0,5},{1,4},{2,7},{3,6},{4,1},{5,0},{6,3},{7,2},{8,13},{9,12},{10,... | collective-permute-start | bytes 1179656 | tf_op jit(solution)/shard_map/ppermute | solution.py:83
  27.2 1.0 copy-done.2
  28.3 2.1 %shard_map.89 = (bf16[96,2048]{1,0:T(8,128)(2,1)S(1)}, bf16[96,2048]{1,0:T(8,128)(2,1)S(1)}, bf16[96,2048]{1,0:T(8,128)(2,1)S(1)}, bf16[96,2048]{1,0:T(8,128)(2,1)S(1)}) custom-call(f32[8,8,128]{2,1,0:T(8,128)S(1)} %all-to-all-done.meta_ref, bf16[128,2048]{1,0:T(8,128)(2,1)S(1)} %bitcast.34, bf16[128,2048]{1,0:T(8,128)(2,1)} %collective-permute-done.8.refs_1_), custom_call_target="tpu_custom_call" | custom-call | bytes 169869312 | tf_op jit(solution)/shard_map/pallas_call | solution.py:44
  30.3 1.5 %collective-permute-start.10 = (bf16[96,2048]{1,0:T(8,128)(2,1)S(1)}, bf16[96,2048]{1,0:T(8,128)(2,1)S(1)}, u32[]{:S(2)}, u32[]{:S(2)}) collective-permute-start(bf16[96,2048]{1,0:T(8,128)(2,1)S(1)} %get-tuple-element.110), channel_id=1, source_target_pairs={{0,2},{1,3},{2,0},{3,1},{4,6},{5,7},{6,4},{7,5},{8,10},{9,11},{10,... | collective-permute-start | bytes 1179656 | tf_op jit(solution)/shard_map/ppermute | solution.py:83
  32.9 8.1 %collective-permute-done.4.refs_2_ = bf16[96,2048]{1,0:T(8,128)(2,1)S(1)} collective-permute-done((bf16[96,2048]{1,0:T(8,128)(2,1)S(1)}, bf16[96,2048]{1,0:T(8,128)(2,1)S(1)}, u32[]{:S(2)}, u32[]{:S(2)}) %collective-permute-start.4) | collective-permute-done | bytes 393248 | tf_op jit(solution)/shard_map/ppermute | solution.py:83
  41.0 6.3 %collective-permute-done.5.refs_3_ = bf16[96,2048]{1,0:T(8,128)(2,1)S(1)} collective-permute-done((bf16[96,2048]{1,0:T(8,128)(2,1)S(1)}, bf16[96,2048]{1,0:T(8,128)(2,1)S(1)}, u32[]{:S(2)}, u32[]{:S(2)}) %collective-permute-start.5) | collective-permute-done | bytes 393248 | tf_op jit(solution)/shard_map/ppermute | solution.py:83
  47.3 1.8 %shard_map.87 = (bf16[384,2048]{1,0:T(8,128)(2,1)S(1)}, bf16[384,768]{1,0:T(8,128)(2,1)S(1)}, f32[384,704]{1,0:T(8,128)S(1)}) custom-call(bf16[704,2048]{1,0:T(8,128)(2,1)S(1)} %bitcast.27, bf16[96,2048]{1,0:T(8,128)(2,1)S(1)} %get-tuple-element.100.refs_0_, bf16[96,2048]{1,0:T(8,128)(2,1)S(1)} %collective-permute-done.3.refs_1_, ...), custom_call_target="tpu_custom_call" | custom-call | bytes 492830720 | tf_op jit(solution)/shard_map/pallas_call | solution.py:44
  49.5 1.1 collective-permute-start.12
  50.6 3.2 %shard_map.90 = (bf16[384,2048]{1,0:T(8,128)(2,1)S(1)}, bf16[384,768]{1,0:T(8,128)(2,1)S(1)}, bf16[384,256]{1,0:T(8,128)(2,1)S(1)}, bf16[96,1024]{1,0:T(8,128)(2...) custom-call(bf16[704,2048]{1,0:T(8,128)(2,1)S(1)} %bitcast.28, ...), custom_call_target="tpu_custom_call" | custom-call | bytes 834666496 | tf_op jit(solution)/shard_map/pallas_call | solution.py:44
  53.9 1.5 %collective-permute-start.13 = (bf16[96,1024]{1,0:T(8,128)(2,1)S(1)}, bf16[96,1024]{1,0:T(8,128)(2,1)S(1)}, u32[]{:S(2)}, u32[]{:S(2)}) collective-permute-start(bf16[96,1024]{1,0:T(8,128)(2,1)S(1)} %get-tuple-element.120), channel_id=1, source_target_pairs={{0,2},{1,3},{2,0},{3,1},{4,6},{5,7},{6,4},{7,5},{8,10},{9,11},{10,... | collective-permute-start | bytes 589832 | tf_op jit(solution)/shard_map/ppermute | solution.py:83
  55.4 1.0 collective-permute-start.14
  56.4 1.1 collective-permute-start.15
  57.4 0.9 shard_map.92
  58.3 1.5 %collective-permute-start.17 = (bf16[96,1024]{1,0:T(8,128)(2,1)S(1)}, bf16[96,1024]{1,0:T(8,128)(2,1)S(1)}, u32[]{:S(2)}, u32[]{:S(2)}) collective-permute-start(bf16[96,1024]{1,0:T(8,128)(2,1)S(1)} %get-tuple-element.131), channel_id=1, source_target_pairs={{0,2},{1,3},{2,0},{3,1},{4,6},{5,7},{6,4},{7,5},{8,10},{9,11},{10,... | collective-permute-start | bytes 589832 | tf_op jit(solution)/shard_map/ppermute | solution.py:83
  59.9 2.1 %shard_map.91._ = bf16[44,384,2048]{2,1,0:T(8,128)(2,1)} custom-call(bf16[384,2048]{1,0:T(8,128)(2,1)S(1)} %get-tuple-element.104.refs_0_, bf16[384,2048]{1,0:T(8,128)(2,1)S(1)} %get-tuple-element.113.refs_1_, bf16[384,768]{1,0:T(8,128)(2,1)S(1)} %get-tuple-element.105.hid_ref.refs_2_, ...), custom_call_target="tpu_custom_call", output_to_operand_aliasing={{}: (5, {})} | custom-call | tf_op jit(solution)/shard_map/pallas_call | solution.py:397
  62.0 1.0 collective-permute-start.18
  63.0 1.1 collective-permute-start.19
  64.1 2.9 %collective-permute-done.14.refs_2_ = bf16[96,1024]{1,0:T(8,128)(2,1)S(1)} collective-permute-done((bf16[96,1024]{1,0:T(8,128)(2,1)S(1)}, bf16[96,1024]{1,0:T(8,128)(2,1)S(1)}, u32[]{:S(2)}, u32[]{:S(2)}) %collective-permute-start.14) | collective-permute-done | bytes 196640 | tf_op jit(solution)/shard_map/ppermute | solution.py:83
  67.4 1.5 %collective-permute-done.16.refs_0_ = bf16[128,1024]{1,0:T(8,128)(2,1)S(1)} collective-permute-done((bf16[128,1024]{1,0:T(8,128)(2,1)S(1)}, bf16[128,1024]{1,0:T(8,128)(2,1)S(1)}, u32[]{:S(2)}, u32[]{:S(2)}) %collective-permute-start.16) | collective-permute-done | bytes 262176 | tf_op jit(solution)/shard_map/ppermute | solution.py:83
  68.9 1.3 %collective-permute-start.23 = (bf16[128,1024]{1,0:T(8,128)(2,1)S(1)}, bf16[128,1024]{1,0:T(8,128)(2,1)S(1)}, u32[]{:S(2)}, u32[]{:S(2)}) collective-permute-start(bf16[128,1024]{1,0:T(8,128)(2,1)S(1)} %shard_map.95), channel_id=1, source_target_pairs={{8,0},{16,8},{24,16},{9,1},{17,9},{25,17},{10,2},{18,10},{26,18},{... | collective-permute-start | bytes 786440 | tf_op jit(solution)/shard_map/ppermute | solution.py:639
  70.5 4.7 %collective-permute-done.18.refs_2_ = bf16[96,1024]{1,0:T(8,128)(2,1)S(1)} collective-permute-done((bf16[96,1024]{1,0:T(8,128)(2,1)S(1)}, bf16[96,1024]{1,0:T(8,128)(2,1)S(1)}, u32[]{:S(2)}, u32[]{:S(2)}) %collective-permute-start.18) | collective-permute-done | bytes 196640 | tf_op jit(solution)/shard_map/ppermute | solution.py:83
  75.7 1.5 %collective-permute-done.20.refs_0_ = bf16[128,1024]{1,0:T(8,128)(2,1)S(1)} collective-permute-done((bf16[128,1024]{1,0:T(8,128)(2,1)S(1)}, bf16[128,1024]{1,0:T(8,128)(2,1)S(1)}, u32[]{:S(2)}, u32[]{:S(2)}) %collective-permute-start.20) | collective-permute-done | bytes 262176 | tf_op jit(solution)/shard_map/ppermute | solution.py:83
  77.2 1.5 %collective-permute-start.22 = (bf16[128,1024]{1,0:T(8,128)(2,1)S(1)}, bf16[128,1024]{1,0:T(8,128)(2,1)S(1)}, u32[]{:S(2)}, u32[]{:S(2)}) collective-permute-start(bf16[128,1024]{1,0:T(8,128)(2,1)S(1)} %shard_map.98), channel_id=1, source_target_pairs={{8,0},{16,8},{24,16},{9,1},{17,9},{25,17},{10,2},{18,10},{26,18},{... | collective-permute-start | bytes 786440 | tf_op jit(solution)/shard_map/ppermute | solution.py:639
  78.7 1.3 %collective-permute-start.21 = (bf16[96,1024]{1,0:T(8,128)(2,1)}, bf16[96,1024]{1,0:T(8,128)(2,1)}, u32[]{:S(2)}, u32[]{:S(2)}) collective-permute-start(bf16[96,1024]{1,0:T(8,128)(2,1)} %get-tuple-element.140), channel_id=1, source_target_pairs={{0,6},{1,7},{2,4},{3,5},{4,2},{5,3},{6,0},{7,1},{8,14},{9,15},{10,... | collective-permute-start | bytes 589832 | tf_op jit(solution)/shard_map/ppermute | solution.py:83
  80.2 1.3 %collective-permute-done.24.refs_0_ = bf16[128,1024]{1,0:T(8,128)(2,1)S(1)} collective-permute-done((bf16[128,1024]{1,0:T(8,128)(2,1)S(1)}, bf16[128,1024]{1,0:T(8,128)(2,1)S(1)}, u32[]{:S(2)}, u32[]{:S(2)}) %collective-permute-start.24) | collective-permute-done | bytes 262176 | tf_op jit(solution)/shard_map/ppermute | solution.py:83
  81.8 1.2 %collective-permute-start.26 = (bf16[96,1024]{1,0:T(8,128)(2,1)S(1)}, bf16[96,1024]{1,0:T(8,128)(2,1)S(1)}, u32[]{:S(2)}, u32[]{:S(2)}) collective-permute-start(bf16[96,1024]{1,0:T(8,128)(2,1)S(1)} %get-tuple-element.144), channel_id=1, source_target_pairs={{0,2},{1,3},{2,0},{3,1},{4,6},{5,7},{6,4},{7,5},{8,10},{9,11},{10,... | collective-permute-start | bytes 589832 | tf_op jit(solution)/shard_map/ppermute | solution.py:83
  83.0 1.1 collective-permute-start.27
  84.1 1.2 %collective-permute-start.28 = (bf16[96,1024]{1,0:T(8,128)(2,1)S(1)}, bf16[96,1024]{1,0:T(8,128)(2,1)S(1)}, u32[]{:S(2)}, u32[]{:S(2)}) collective-permute-start(bf16[96,1024]{1,0:T(8,128)(2,1)S(1)} %get-tuple-element.146), channel_id=1, source_target_pairs={{0,6},{1,7},{2,4},{3,5},{4,2},{5,3},{6,0},{7,1},{8,14},{9,15},{10,... | collective-permute-start | bytes 589832 | tf_op jit(solution)/shard_map/ppermute | solution.py:83
  85.3 2.1 %collective-permute-done.22.raw_ref = bf16[128,1024]{1,0:T(8,128)(2,1)S(1)} collective-permute-done((bf16[128,1024]{1,0:T(8,128)(2,1)S(1)}, bf16[128,1024]{1,0:T(8,128)(2,1)S(1)}, u32[]{:S(2)}, u32[]{:S(2)}) %collective-permute-start.22) | collective-permute-done | bytes 262176 | tf_op jit(solution)/shard_map/ppermute | solution.py:639
  87.7 1.3 %collective-permute-done.25.refs_0_ = bf16[128,1024]{1,0:T(8,128)(2,1)S(1)} collective-permute-done((bf16[128,1024]{1,0:T(8,128)(2,1)S(1)}, bf16[128,1024]{1,0:T(8,128)(2,1)S(1)}, u32[]{:S(2)}, u32[]{:S(2)}) %collective-permute-start.25) | collective-permute-done | bytes 262176 | tf_op jit(solution)/shard_map/ppermute | solution.py:83
  89.2 0.9 collective-permute-start.29
  90.1 0.9 collective-permute-start.30
  91.3 1.5 %collective-permute-start.31 = (bf16[96,1024]{1,0:T(8,128)(2,1)S(1)}, bf16[96,1024]{1,0:T(8,128)(2,1)S(1)}, u32[]{:S(2)}, u32[]{:S(2)}) collective-permute-start(bf16[96,1024]{1,0:T(8,128)(2,1)S(1)} %get-tuple-element.151), channel_id=1, source_target_pairs={{0,6},{1,7},{2,4},{3,5},{4,2},{5,3},{6,0},{7,1},{8,14},{9,15},{10,... | collective-permute-start | bytes 589832 | tf_op jit(solution)/shard_map/ppermute | solution.py:83
  92.8 3.9 %shard_map.103 = (bf16[44,384,2048]{2,1,0:T(8,128)(2,1)}, bf16[384,704]{1,0:T(8,128)(2,1)S(1)}, f32[384,704]{1,0:T(8,128)S(1)}) custom-call(bf16[704,2048]{1,0:T(8,128)(2,1)S(1)} %bitcast.29, bf16[44,384,2048]{2,1,0:T(8,128)(2,1)} %shard_map.91._, bf16[96,2048]{1,0:T(8,128)(2,1)S(1)} %copy-done.4, ...), custom_call_target="tpu_custom_call", output_to_operand_aliasing={{0}: (1, {})} | custom-call | bytes 9247391744 | tf_op jit(solution)/shard_map/pallas_call | solution.py:44
  96.7 4.4 %shard_map.104 = (f32[384,704]{1,0:T(8,128)S(1)}, bf16[704,2048]{1,0:T(8,128)(2,1)}) custom-call(bf16[704,2048]{1,0:T(8,128)(2,1)S(1)} %bitcast.31, bf16[384,704]{1,0:T(8,128)(2,1)S(1)} %get-tuple-element.157.hid1_ref.hid_ref, bf16[44,384,2048]{2,1,0:T(8,128)(2,1)} %get-tuple-element.158.pad_ref, bf16[96,1024]{1,0:T(8,128)(2,1)S(1)} %get-tuple-element.143.refs_0_, ...), custom_call_target="tpu_custom_call" | custom-call | bytes 523239424 | tf_op jit(solution)/shard_map/pallas_call | solution.py:435
  101.2 2.5 %collective-permute-done.31.refs_3_ = bf16[96,1024]{1,0:T(8,128)(2,1)S(1)} collective-permute-done((bf16[96,1024]{1,0:T(8,128)(2,1)S(1)}, bf16[96,1024]{1,0:T(8,128)(2,1)S(1)}, u32[]{:S(2)}, u32[]{:S(2)}) %collective-permute-start.31) | collective-permute-done | bytes 196640 | tf_op jit(solution)/shard_map/ppermute | solution.py:83
  103.7 2.4 %shard_map.105 = (bf16[384,1024]{1,0:T(8,128)(2,1)S(1)}, bf16[384,768]{1,0:T(8,128)(2,1)S(1)}, bf16[384,128]{1,0:T(8,128)(2,1)}) custom-call(bf16[704,2048]{1,0:T(8,128)(2,1)S(1)} %bitcast.32, bf16[384,704]{1,0:T(8,128)(2,1)S(1)} %get-tuple-element.157.hid1_ref.hid_ref, f32[384,704]{1,0:T(8,128)S(1)} %get-tuple-element.160.slope_ref, ...), custom_call_target="tpu_custom_call" | custom-call | bytes 4931452928 | tf_op jit(solution)/shard_map/pallas_call | solution.py:44
  106.1 3.4 %all-to-all-start.1 = ((bf16[8,48,128]{2,1,0:T(8,128)(2,1)}), bf16[8,48,128]{2,1,0:T(8,128)(2,1)S(1)}, u32[]{:S(2)}, u32[]{:S(2)}) async-start(bf16[8,48,128]{2,1,0:T(8,128)(2,1)} %bitcast.13), calls=%async_computation.1 | async-start | bytes 196608 | tf_op jit(solution)/shard_map/all_to_all | solution.py:276
  109.5 6.8 %shard_map.106 = (bf16[704,2048]{1,0:T(8,128)(2,1)}, bf16[704,2048]{1,0:T(8,128)(2,1)}) custom-call(bf16[704,2048]{1,0:T(8,128)(2,1)} %get-tuple-element.159._, bf16[44,384,2048]{2,1,0:T(8,128)(2,1)} %get-tuple-element.158.pad_ref, bf16[384,1024]{1,0:T(8,128)(2,1)S(1)} %get-tuple-element.166.g1_ref, ...), custom_call_target="tpu_custom_call", output_to_operand_aliasing={{1}: (0, {})} | custom-call | bytes 369098752 | tf_op jit(solution)/shard_map/pallas_call | solution.py:511
  116.4 0.9 shard_map.107
  (66 shorter events, 10.9 us)
Async XLA Ops:
  0.6 46.7 %copy-start = (bf16[1,1,704,2048]{3,2,1,0:T(8,128)(2,1)S(1)}, bf16[1,1,704,2048]{3,2,1,0:T(8,128)(2,1)}, u32[]{:S(2)}) copy-start(bf16[1,1,704,2048]{3,2,1,0:T(8,128)(2,1)} %param.8) | copy-start | bytes 8650756
  2.9 11.0 %collective-permute-start.1 = (bf16[128,2048]{1,0:T(8,128)(2,1)}, bf16[128,2048]{1,0:T(8,128)(2,1)}, u32[]{:S(2)}, u32[]{:S(2)}) collective-permute-start(bf16[128,2048]{1,0:T(8,128)(2,1)} %get-tuple-element.173.refs_2_), channel_id=1, source_target_pairs={{0,1},{1,0},{2,3},{3,2},{4,5},{5,4},{6,7},{7,6},{8,9},{9,8},{10,11... | collective-permute-start | bytes 1572872 | tf_op jit(solution)/shard_map/ppermute | solution.py:83
  3.3 18.5 %collective-permute-start.2 = (bf16[128,2048]{1,0:T(8,128)(2,1)S(1)}, bf16[128,2048]{1,0:T(8,128)(2,1)}, u32[]{:S(2)}, u32[]{:S(2)}) collective-permute-start(bf16[128,2048]{1,0:T(8,128)(2,1)S(1)} %get-tuple-element.174.refs_0_), channel_id=1, source_target_pairs={{0,2},{1,3},{2,0},{3,1},{4,6},{5,7},{6,4},{7,5},{8,10},{9,11},{10,... | collective-permute-start | bytes 1572872 | tf_op jit(solution)/shard_map/ppermute | solution.py:83
  5.8 20.1 %collective-permute-start.8 = (bf16[128,2048]{1,0:T(8,128)(2,1)}, bf16[128,2048]{1,0:T(8,128)(2,1)}, u32[]{:S(2)}, u32[]{:S(2)}) collective-permute-start(bf16[128,2048]{1,0:T(8,128)(2,1)} %bitcast.33), channel_id=1, source_target_pairs={{0,4},{1,5},{2,6},{3,7},{4,0},{5,1},{6,2},{7,3},{8,12},{9,13},{10,... | collective-permute-start | bytes 1572872 | tf_op jit(solution)/shard_map/ppermute | solution.py:83
  9.3 12.5 %all-to-all-start = ((f32[8,8,128]{2,1,0:T(8,128)}), f32[8,8,128]{2,1,0:T(8,128)S(1)}, u32[]{:S(2)}, u32[]{:S(2)}) async-start(f32[8,8,128]{2,1,0:T(8,128)} %broadcast_in_dim.15), calls=%async_computation | async-start | bytes 65536 | tf_op jit(solution)/shard_map/all_to_all | solution.py:562
  12.7 1.2 %collective-permute-start = (f32[8,128]{1,0:T(8,128)S(1)}, f32[8,128]{1,0:T(8,128)S(1)}, u32[]{:S(2)}, u32[]{:S(2)}) collective-permute-start(f32[8,128]{1,0:T(8,128)S(1)} %pad_maximum_fusion.refs_0_), channel_id=1, source_target_pairs={{0,1},{1,0},{2,3},{3,2},{4,5},{5,4},{6,7},{7,6},{8,9},{9,8},{10,11... | collective-permute-start | bytes 12296 | tf_op jit(solution)/shard_map/ppermute | solution.py:83
  17.1 0.7 copy-start.3
  17.8 0.7 copy-start.7
  18.5 11.8 %collective-permute-start.6 = (bf16[96,2048]{1,0:T(8,128)(2,1)}, bf16[96,2048]{1,0:T(8,128)(2,1)}, u32[]{:S(2)}, u32[]{:S(2)}) collective-permute-start(bf16[96,2048]{1,0:T(8,128)(2,1)} %get-tuple-element.91), channel_id=1, source_target_pairs={{0,2},{1,3},{2,0},{3,1},{4,6},{5,7},{6,4},{7,5},{8,10},{9,11},{10,... | collective-permute-start | bytes 1179656 | tf_op jit(solution)/shard_map/ppermute | solution.py:83
  20.4 12.3 %collective-permute-start.7 = (bf16[96,2048]{1,0:T(8,128)(2,1)}, bf16[96,2048]{1,0:T(8,128)(2,1)}, u32[]{:S(2)}, u32[]{:S(2)}) collective-permute-start(bf16[96,2048]{1,0:T(8,128)(2,1)} %get-tuple-element.92), channel_id=1, source_target_pairs={{0,4},{1,5},{2,6},{3,7},{4,0},{5,1},{6,2},{7,3},{8,12},{9,13},{10,... | collective-permute-start | bytes 1179656 | tf_op jit(solution)/shard_map/ppermute | solution.py:83
  21.9 27.7 %copy-start.8 = (bf16[96,1024]{1,0:T(8,128)(2,1)S(1)}, bf16[96,1024]{1,0:T(8,128)(2,1)}, u32[]{:S(2)}) copy-start(bf16[96,1024]{1,0:T(8,128)(2,1)} %copy-done.7) | copy-start | bytes 589828
  24.0 26.6 %copy-start.1 = (bf16[1,1,704,2048]{3,2,1,0:T(8,128)(2,1)S(1)}, bf16[1,1,704,2048]{3,2,1,0:T(8,128)(2,1)}, u32[]{:S(2)}) copy-start(bf16[1,1,704,2048]{3,2,1,0:T(8,128)(2,1)} %param.9) | copy-start | bytes 8650756
  24.0 8.7 %collective-permute-start.3 = (bf16[96,2048]{1,0:T(8,128)(2,1)S(1)}, bf16[96,2048]{1,0:T(8,128)(2,1)S(1)}, u32[]{:S(2)}, u32[]{:S(2)}) collective-permute-start(bf16[96,2048]{1,0:T(8,128)(2,1)S(1)} %get-tuple-element.97), channel_id=1, source_target_pairs={{0,1},{1,0},{2,3},{3,2},{4,5},{5,4},{6,7},{7,6},{8,9},{9,8},{10,11... | collective-permute-start | bytes 1179656 | tf_op jit(solution)/shard_map/ppermute | solution.py:83
  24.7 0.6 copy-start.5
  25.4 15.6 %collective-permute-start.4 = (bf16[96,2048]{1,0:T(8,128)(2,1)S(1)}, bf16[96,2048]{1,0:T(8,128)(2,1)S(1)}, u32[]{:S(2)}, u32[]{:S(2)}) collective-permute-start(bf16[96,2048]{1,0:T(8,128)(2,1)S(1)} %get-tuple-element.98), channel_id=1, source_target_pairs={{0,4},{1,5},{2,6},{3,7},{4,0},{5,1},{6,2},{7,3},{8,12},{9,13},{10,... | collective-permute-start | bytes 1179656 | tf_op jit(solution)/shard_map/ppermute | solution.py:83
  25.9 21.4 %collective-permute-start.5 = (bf16[96,2048]{1,0:T(8,128)(2,1)S(1)}, bf16[96,2048]{1,0:T(8,128)(2,1)S(1)}, u32[]{:S(2)}, u32[]{:S(2)}) collective-permute-start(bf16[96,2048]{1,0:T(8,128)(2,1)S(1)} %get-tuple-element.99), channel_id=1, source_target_pairs={{0,5},{1,4},{2,7},{3,6},{4,1},{5,0},{6,3},{7,2},{8,13},{9,12},{10,... | collective-permute-start | bytes 1179656 | tf_op jit(solution)/shard_map/ppermute | solution.py:83
  27.2 1.0 copy-start.2
  30.3 18.8 %collective-permute-start.10 = (bf16[96,2048]{1,0:T(8,128)(2,1)S(1)}, bf16[96,2048]{1,0:T(8,128)(2,1)S(1)}, u32[]{:S(2)}, u32[]{:S(2)}) collective-permute-start(bf16[96,2048]{1,0:T(8,128)(2,1)S(1)} %get-tuple-element.110), channel_id=1, source_target_pairs={{0,2},{1,3},{2,0},{3,1},{4,6},{5,7},{6,4},{7,5},{8,10},{9,11},{10,... | collective-permute-start | bytes 1179656 | tf_op jit(solution)/shard_map/ppermute | solution.py:83
  32.7 16.5 %collective-permute-start.9 = (bf16[96,2048]{1,0:T(8,128)(2,1)S(1)}, bf16[96,2048]{1,0:T(8,128)(2,1)S(1)}, u32[]{:S(2)}, u32[]{:S(2)}) collective-permute-start(bf16[96,2048]{1,0:T(8,128)(2,1)S(1)} %get-tuple-element.109), channel_id=1, source_target_pairs={{0,1},{1,0},{2,3},{3,2},{4,5},{5,4},{6,7},{7,6},{8,9},{9,8},{10,11... | collective-permute-start | bytes 1179656 | tf_op jit(solution)/shard_map/ppermute | solution.py:83
  32.7 16.9 %collective-permute-start.11 = (bf16[96,2048]{1,0:T(8,128)(2,1)S(1)}, bf16[96,2048]{1,0:T(8,128)(2,1)S(1)}, u32[]{:S(2)}, u32[]{:S(2)}) collective-permute-start(bf16[96,2048]{1,0:T(8,128)(2,1)S(1)} %get-tuple-element.112), channel_id=1, source_target_pairs={{0,3},{1,2},{2,1},{3,0},{4,7},{5,6},{6,5},{7,4},{8,11},{9,10},{10,... | collective-permute-start | bytes 1179656 | tf_op jit(solution)/shard_map/ppermute | solution.py:83
  49.5 12.4 %collective-permute-start.12 = (bf16[96,1024]{1,0:T(8,128)(2,1)S(1)}, bf16[96,1024]{1,0:T(8,128)(2,1)S(1)}, u32[]{:S(2)}, u32[]{:S(2)}) collective-permute-start(bf16[96,1024]{1,0:T(8,128)(2,1)S(1)} %copy-done.8), channel_id=1, source_target_pairs={{0,6},{1,7},{2,4},{3,5},{4,2},{5,3},{6,0},{7,1},{8,14},{9,15},{10,... | collective-permute-start | bytes 589832 | tf_op jit(solution)/shard_map/ppermute | solution.py:83
  53.9 9.1 %collective-permute-start.13 = (bf16[96,1024]{1,0:T(8,128)(2,1)S(1)}, bf16[96,1024]{1,0:T(8,128)(2,1)S(1)}, u32[]{:S(2)}, u32[]{:S(2)}) collective-permute-start(bf16[96,1024]{1,0:T(8,128)(2,1)S(1)} %get-tuple-element.120), channel_id=1, source_target_pairs={{0,2},{1,3},{2,0},{3,1},{4,6},{5,7},{6,4},{7,5},{8,10},{9,11},{10,... | collective-permute-start | bytes 589832 | tf_op jit(solution)/shard_map/ppermute | solution.py:83
  55.4 11.5 %collective-permute-start.14 = (bf16[96,1024]{1,0:T(8,128)(2,1)S(1)}, bf16[96,1024]{1,0:T(8,128)(2,1)S(1)}, u32[]{:S(2)}, u32[]{:S(2)}) collective-permute-start(bf16[96,1024]{1,0:T(8,128)(2,1)S(1)} %get-tuple-element.121), channel_id=1, source_target_pairs={{0,4},{1,5},{2,6},{3,7},{4,0},{5,1},{6,2},{7,3},{8,12},{9,13},{10,... | collective-permute-start | bytes 589832 | tf_op jit(solution)/shard_map/ppermute | solution.py:83
  56.4 10.6 %collective-permute-start.15 = (bf16[96,1024]{1,0:T(8,128)(2,1)S(1)}, bf16[96,1024]{1,0:T(8,128)(2,1)S(1)}, u32[]{:S(2)}, u32[]{:S(2)}) collective-permute-start(bf16[96,1024]{1,0:T(8,128)(2,1)S(1)} %get-tuple-element.122), channel_id=1, source_target_pairs={{0,6},{1,7},{2,4},{3,5},{4,2},{5,3},{6,0},{7,1},{8,14},{9,15},{10,... | collective-permute-start | bytes 589832 | tf_op jit(solution)/shard_map/ppermute | solution.py:83
  58.3 12.2 %collective-permute-start.17 = (bf16[96,1024]{1,0:T(8,128)(2,1)S(1)}, bf16[96,1024]{1,0:T(8,128)(2,1)S(1)}, u32[]{:S(2)}, u32[]{:S(2)}) collective-permute-start(bf16[96,1024]{1,0:T(8,128)(2,1)S(1)} %get-tuple-element.131), channel_id=1, source_target_pairs={{0,2},{1,3},{2,0},{3,1},{4,6},{5,7},{6,4},{7,5},{8,10},{9,11},{10,... | collective-permute-start | bytes 589832 | tf_op jit(solution)/shard_map/ppermute | solution.py:83
  62.0 13.2 %collective-permute-start.18 = (bf16[96,1024]{1,0:T(8,128)(2,1)S(1)}, bf16[96,1024]{1,0:T(8,128)(2,1)S(1)}, u32[]{:S(2)}, u32[]{:S(2)}) collective-permute-start(bf16[96,1024]{1,0:T(8,128)(2,1)S(1)} %get-tuple-element.132), channel_id=1, source_target_pairs={{0,4},{1,5},{2,6},{3,7},{4,0},{5,1},{6,2},{7,3},{8,12},{9,13},{10,... | collective-permute-start | bytes 589832 | tf_op jit(solution)/shard_map/ppermute | solution.py:83
  63.0 12.2 %collective-permute-start.19 = (bf16[96,1024]{1,0:T(8,128)(2,1)S(1)}, bf16[96,1024]{1,0:T(8,128)(2,1)S(1)}, u32[]{:S(2)}, u32[]{:S(2)}) collective-permute-start(bf16[96,1024]{1,0:T(8,128)(2,1)S(1)} %get-tuple-element.133), channel_id=1, source_target_pairs={{0,6},{1,7},{2,4},{3,5},{4,2},{5,3},{6,0},{7,1},{8,14},{9,15},{10,... | collective-permute-start | bytes 589832 | tf_op jit(solution)/shard_map/ppermute | solution.py:83
  67.3 1.6 %collective-permute-start.16 = (bf16[128,1024]{1,0:T(8,128)(2,1)S(1)}, bf16[128,1024]{1,0:T(8,128)(2,1)S(1)}, u32[]{:S(2)}, u32[]{:S(2)}) collective-permute-start(bf16[128,1024]{1,0:T(8,128)(2,1)S(1)} %get-tuple-element.128), channel_id=1, source_target_pairs={{0,1},{1,0},{2,3},{3,2},{4,5},{5,4},{6,7},{7,6},{8,9},{9,8},{10,11... | collective-permute-start | bytes 786440 | tf_op jit(solution)/shard_map/ppermute | solution.py:83
  68.9 11.0 %collective-permute-start.23 = (bf16[128,1024]{1,0:T(8,128)(2,1)S(1)}, bf16[128,1024]{1,0:T(8,128)(2,1)S(1)}, u32[]{:S(2)}, u32[]{:S(2)}) collective-permute-start(bf16[128,1024]{1,0:T(8,128)(2,1)S(1)} %shard_map.95), channel_id=1, source_target_pairs={{8,0},{16,8},{24,16},{9,1},{17,9},{25,17},{10,2},{18,10},{26,18},{... | collective-permute-start | bytes 786440 | tf_op jit(solution)/shard_map/ppermute | solution.py:639
  75.5 1.6 %collective-permute-start.20 = (bf16[128,1024]{1,0:T(8,128)(2,1)S(1)}, bf16[128,1024]{1,0:T(8,128)(2,1)S(1)}, u32[]{:S(2)}, u32[]{:S(2)}) collective-permute-start(bf16[128,1024]{1,0:T(8,128)(2,1)S(1)} %get-tuple-element.139), channel_id=1, source_target_pairs={{0,1},{1,0},{2,3},{3,2},{4,5},{5,4},{6,7},{7,6},{8,9},{9,8},{10,11... | collective-permute-start | bytes 786440 | tf_op jit(solution)/shard_map/ppermute | solution.py:83
  77.2 10.2 %collective-permute-start.22 = (bf16[128,1024]{1,0:T(8,128)(2,1)S(1)}, bf16[128,1024]{1,0:T(8,128)(2,1)S(1)}, u32[]{:S(2)}, u32[]{:S(2)}) collective-permute-start(bf16[128,1024]{1,0:T(8,128)(2,1)S(1)} %shard_map.98), channel_id=1, source_target_pairs={{8,0},{16,8},{24,16},{9,1},{17,9},{25,17},{10,2},{18,10},{26,18},{... | collective-permute-start | bytes 786440 | tf_op jit(solution)/shard_map/ppermute | solution.py:639
  78.7 11.5 %collective-permute-start.21 = (bf16[96,1024]{1,0:T(8,128)(2,1)}, bf16[96,1024]{1,0:T(8,128)(2,1)}, u32[]{:S(2)}, u32[]{:S(2)}) collective-permute-start(bf16[96,1024]{1,0:T(8,128)(2,1)} %get-tuple-element.140), channel_id=1, source_target_pairs={{0,6},{1,7},{2,4},{3,5},{4,2},{5,3},{6,0},{7,1},{8,14},{9,15},{10,... | collective-permute-start | bytes 589832 | tf_op jit(solution)/shard_map/ppermute | solution.py:83
  80.0 1.5 %collective-permute-start.24 = (bf16[128,1024]{1,0:T(8,128)(2,1)S(1)}, bf16[128,1024]{1,0:T(8,128)(2,1)S(1)}, u32[]{:S(2)}, u32[]{:S(2)}) collective-permute-start(bf16[128,1024]{1,0:T(8,128)(2,1)S(1)} %collective-permute-done.23.raw_ref), channel_id=1, source_target_pairs={{0,1},{1,0},{2,3},{3,2},{4,5},{5,4},{6,7},{7,6},{8,9},{9,8},{10,11... | collective-permute-start | bytes 786440 | tf_op jit(solution)/shard_map/ppermute | solution.py:83
  81.8 9.5 %collective-permute-start.26 = (bf16[96,1024]{1,0:T(8,128)(2,1)S(1)}, bf16[96,1024]{1,0:T(8,128)(2,1)S(1)}, u32[]{:S(2)}, u32[]{:S(2)}) collective-permute-start(bf16[96,1024]{1,0:T(8,128)(2,1)S(1)} %get-tuple-element.144), channel_id=1, source_target_pairs={{0,2},{1,3},{2,0},{3,1},{4,6},{5,7},{6,4},{7,5},{8,10},{9,11},{10,... | collective-permute-start | bytes 589832 | tf_op jit(solution)/shard_map/ppermute | solution.py:83
  83.0 13.7 %collective-permute-start.27 = (bf16[96,1024]{1,0:T(8,128)(2,1)S(1)}, bf16[96,1024]{1,0:T(8,128)(2,1)S(1)}, u32[]{:S(2)}, u32[]{:S(2)}) collective-permute-start(bf16[96,1024]{1,0:T(8,128)(2,1)S(1)} %get-tuple-element.145), channel_id=1, source_target_pairs={{0,4},{1,5},{2,6},{3,7},{4,0},{5,1},{6,2},{7,3},{8,12},{9,13},{10,... | collective-permute-start | bytes 589832 | tf_op jit(solution)/shard_map/ppermute | solution.py:83
  84.1 12.6 %collective-permute-start.28 = (bf16[96,1024]{1,0:T(8,128)(2,1)S(1)}, bf16[96,1024]{1,0:T(8,128)(2,1)S(1)}, u32[]{:S(2)}, u32[]{:S(2)}) collective-permute-start(bf16[96,1024]{1,0:T(8,128)(2,1)S(1)} %get-tuple-element.146), channel_id=1, source_target_pairs={{0,6},{1,7},{2,4},{3,5},{4,2},{5,3},{6,0},{7,1},{8,14},{9,15},{10,... | collective-permute-start | bytes 589832 | tf_op jit(solution)/shard_map/ppermute | solution.py:83
  87.4 1.5 %collective-permute-start.25 = (bf16[128,1024]{1,0:T(8,128)(2,1)S(1)}, bf16[128,1024]{1,0:T(8,128)(2,1)S(1)}, u32[]{:S(2)}, u32[]{:S(2)}) collective-permute-start(bf16[128,1024]{1,0:T(8,128)(2,1)S(1)} %collective-permute-done.22.raw_ref), channel_id=1, source_target_pairs={{0,1},{1,0},{2,3},{3,2},{4,5},{5,4},{6,7},{7,6},{8,9},{9,8},{10,11... | collective-permute-start | bytes 786440 | tf_op jit(solution)/shard_map/ppermute | solution.py:83
  87.4 5.4 %copy-start.4 = (bf16[96,2048]{1,0:T(8,128)(2,1)S(1)}, bf16[96,2048]{1,0:T(8,128)(2,1)}, u32[]{:S(2)}) copy-start(bf16[96,2048]{1,0:T(8,128)(2,1)} %copy-done.3) | copy-start | bytes 1179652
  89.2 11.9 %collective-permute-start.29 = (bf16[96,1024]{1,0:T(8,128)(2,1)S(1)}, bf16[96,1024]{1,0:T(8,128)(2,1)S(1)}, u32[]{:S(2)}, u32[]{:S(2)}) collective-permute-start(bf16[96,1024]{1,0:T(8,128)(2,1)S(1)} %get-tuple-element.149), channel_id=1, source_target_pairs={{0,2},{1,3},{2,0},{3,1},{4,6},{5,7},{6,4},{7,5},{8,10},{9,11},{10,... | collective-permute-start | bytes 589832 | tf_op jit(solution)/shard_map/ppermute | solution.py:83
  90.1 11.0 %collective-permute-start.30 = (bf16[96,1024]{1,0:T(8,128)(2,1)S(1)}, bf16[96,1024]{1,0:T(8,128)(2,1)S(1)}, u32[]{:S(2)}, u32[]{:S(2)}) collective-permute-start(bf16[96,1024]{1,0:T(8,128)(2,1)S(1)} %get-tuple-element.150), channel_id=1, source_target_pairs={{0,4},{1,5},{2,6},{3,7},{4,0},{5,1},{6,2},{7,3},{8,12},{9,13},{10,... | collective-permute-start | bytes 589832 | tf_op jit(solution)/shard_map/ppermute | solution.py:83
  91.3 12.4 %collective-permute-start.31 = (bf16[96,1024]{1,0:T(8,128)(2,1)S(1)}, bf16[96,1024]{1,0:T(8,128)(2,1)S(1)}, u32[]{:S(2)}, u32[]{:S(2)}) collective-permute-start(bf16[96,1024]{1,0:T(8,128)(2,1)S(1)} %get-tuple-element.151), channel_id=1, source_target_pairs={{0,6},{1,7},{2,4},{3,5},{4,2},{5,3},{6,0},{7,1},{8,14},{9,15},{10,... | collective-permute-start | bytes 589832 | tf_op jit(solution)/shard_map/ppermute | solution.py:83
  106.1 10.2 %all-to-all-start.1 = ((bf16[8,48,128]{2,1,0:T(8,128)(2,1)}), bf16[8,48,128]{2,1,0:T(8,128)(2,1)S(1)}, u32[]{:S(2)}, u32[]{:S(2)}) async-start(bf16[8,48,128]{2,1,0:T(8,128)(2,1)} %bitcast.13), calls=%async_computation.1 | async-start | bytes 196608 | tf_op jit(solution)/shard_map/all_to_all | solution.py:276
  109.5 6.9 %copy-start.6 = (bf16[384,128]{1,0:T(8,128)(2,1)S(1)}, bf16[384,128]{1,0:T(8,128)(2,1)}, u32[]{:S(2)}) copy-start(bf16[384,128]{1,0:T(8,128)(2,1)} %copy-done.5) | copy-start | bytes 294916

commit v8 on v7

--- a/solution.py
+++ b/solution.py
@@ -14,6 +14,7 @@
 HALVES = len(AXES)
 TILES = 2
 LONG = 10**11
+OWN_LIMIT = 60 * 1024 * 1024
 LATE_LIMIT = 32 * 1024 * 1024
 X0, G0, X1, G1, HID0, HID1, GP0, GP1, COLS = range(9)
 PAD_BYTES = 66 * 1024 * 1024
@@ -162,18 +163,38 @@
             out_ref[s * capacity : (s + 1) * capacity, :] = picked[i * capacity : (i + 1) * capacity]
 
 
-def own_select_kernel(plane, capacity, plan, *refs):
+def own_select_kernel(plane, capacity, plan, tick, *refs):
     ranks, sources, targets = plan
+    refs, (raw, sem) = refs[:-2], refs[-2:]
     count = len(sources)
+    copies = [pltpu.make_async_copy(refs[count + s].at[tick], raw.at[s], sem.at[s]) for s in range(count)]
+    for copy in copies:
+        copy.start()
+    hots = [block_masks(plane, capacity, ranks, refs[s][...], targets).astype(bf16) for s in range(count)]
+    width = refs[-1].shape[1]
     for s in range(count):
-        hot = block_masks(plane, capacity, ranks, refs[s][...], targets)
-        picked = dot(hot.astype(bf16), refs[count + s][...], 1, 0).astype(bf16)
+        copies[s].wait()
+        picked = dot(hots[s], raw[s], 1, 0).astype(bf16)
         at = slice(s * capacity, (s + 1) * capacity)
         for i, out_ref in enumerate(refs[2 * count + 1 : -HALVES]):
             out_ref[at, :] = picked[i * capacity : (i + 1) * capacity]
-        width = refs[-1].shape[1]
         for h, out_ref in enumerate(refs[-HALVES:]):
             out_ref[at, :] = picked[-capacity:, h * width : (h + 1) * width]
+
+
+def own_picked(plane, capacity, plan, tick, metas, raws, pad):
+    _, tokens, width = raws[0].shape
+    count, rows = len(raws), len(plan[1]) * capacity
+    outs = [shaped((rows, width), bf16)] * (len(plan[2]) - 1) + [shaped((rows, width // HALVES), bf16)] * HALVES
+    return pl.pallas_call(
+        functools.partial(own_select_kernel, plane, capacity, plan, tick),
+        out_shape=[pad] + outs,
+        in_specs=[pl.BlockSpec()] * count + [in_hbm(r) for r in raws],
+        out_specs=[in_hbm(pad)] + [pl.BlockSpec()] * len(outs),
+        scratch_shapes=[pltpu.VMEM((count, tokens, width), bf16), pltpu.SemaphoreType.DMA((count,))],
+        compiler_params=pltpu.CompilerParams(vmem_limit_bytes=OWN_LIMIT),
+        cost_estimate=cost([*metas, *raws], outs, 0),
+    )(*metas, *raws)
 
 
 def pick_own_kernel(hot_ref, raw_ref, out_ref):
@@ -198,16 +219,12 @@
     return ranks, plane.along(axis), [plane.back(t) for t in plane.across(axis)]
 
 
-def picked_rows(plane, capacity, ranks, axis, value, meta, hot=None, pad=None):
+def picked_rows(plane, capacity, ranks, axis, value, meta, hot=None):
     tokens, width = value.shape
     plan = gather_plan(plane, ranks, axis)
     raws = [plane.send(value, u) for u in plane.along(axis)]
     outs = [shaped((len(plan[1]) * capacity, width), bf16)] * len(plan[2])
     flops = 2 * tokens * width * capacity * len(plan[1]) * len(plan[2])
-    if pad is not None:
-        kernel = functools.partial(own_select_kernel, plane, capacity, plan)
-        parts = [shaped((outs[0].shape[0], width // HALVES), bf16)] * HALVES
-        return call(kernel, [pad] + outs[:-1] + parts, *meta, *raws, pad_out=True)
     if hot is None:
         return call(functools.partial(select_kernel, plane, capacity, plan), outs, meta, *raws, flops=flops)
     (own,) = call(pick_own_kernel, [shaped((hot.shape[1], width), bf16)], hot, raws[0], flops=LONG)
@@ -573,8 +590,8 @@
     pick = functools.partial(picked_rows, plane, capacity)
     if stepped:
         metas = [own_meta, plane.send(own_meta, (0, 0, 1))]
-        x1 = inputs[0, 1]
-        pad, *x1 = pick(ranks[1], 2, x1, metas, pad=pad)
+        x1 = [inputs[0], plane.send(inputs[0], (0, 0, 1))]
+        pad, *x1 = own_picked(plane, capacity, gather_plan(plane, ranks[1], 2), 1, metas, x1, pad)
         x1_near, _ = sent_rows(plane, 2, x1[:-HALVES])
         *near_layout, rest_layout = sent_layout(plane, 2)
         x1_groups = [(0, near_layout)] + [(h * half, [rest_layout]) for h in range(HALVES)]

time: 118 us -> 117 us (level)
  local copies, waits for them, and re-layouts: 5.99 us -> 4.22 us
    pallas_call x0 -> x1, Pallas kernels: none -> 3.51 us  [own_picked(): pl.pallas_call(functools.partial(own_select_kernel, plane, capacity, plan...]
    pallas_call x20 -> x19, Pallas kernels: 22.8 us -> 19.6 us  [call(): pl.pallas_call(kernel, out_shape=outs, in_specs=specs, out_specs=[in_hbm(...]
  transfers between devices with their start and end apart: 34 -> 34, of which waited for: 15 -> 15; matrix products, arithmetic and copies ran while one was open for 2% -> 3% of each run, Pallas kernels for 28% -> 29%
where the time goes in v8:
time: 117 us; the launch traced here: 116 us
  starting transfers between devices  38.1 us (33%)
  Pallas kernels  36.5 us (31%)
  waiting for transfers between devices  34.7 us (30%)
  local copies, waits for them, and re-layouts  4.22 us (4%)
  other arithmetic  1.37 us (1%)
    ppermute x30, waiting for transfers between devices, send(): return lax.ppermute(value, 'expert', route)  32.6 us
    ppermute x30, starting transfers between devices, send(): return lax.ppermute(value, 'expert', route)  28.6 us
    pallas_call x19, Pallas kernels, call(): pl.pallas_call(kernel, out_shape=outs, in_specs=specs, out_specs=[in_hbm(...  19.6 us
    pallas_call x1, Pallas kernels, late(): pl.pallas_call(functools.partial(late_kernel, width, part, units), out_sh...  6.84 us
    pallas_call x1, Pallas kernels, early(): pl.pallas_call(functools.partial(early_kernel, plane, capacity, groups),...  4.44 us
    pallas_call x1, Pallas kernels, own_picked(): pl.pallas_call(functools.partial(own_select_kernel, plane, capacity, plan...  3.51 us
    all_to_all x1, starting transfers between devices, exchange(): lax.all_to_all(pieces, 'expert', split_axis=0, concat_axis=0, tiled=True)  3.37 us
    all_to_all x1, starting transfers between devices, body(): lax.all_to_all(meta, 'expert', split_axis=0, concat_axis=0, tiled=True)  3.33 us
  transfers between devices with their start and end apart: 34, of which 15 were waited for; matrix products, arithmetic and copies ran while one was open for 3% of the time, Pallas kernels for 29%

profile of v8, /device:TPU:0, one launch (start us, length us, event | category | flops | bytes accessed | tf_op | source)
XLA Modules:
  0.0 116.0 jit_solution(10969547515295036223)
XLA Ops:
  1.2 1.3 %slice_bitcast_fusion.refs_0_ = bf16[128,2048]{1,0:T(8,128)(2,1)S(1)} fusion(bf16[1,2,128,2048]{3,2,1,0:T(8,128)(2,1)} %param.6), kind=kLoop, calls=%fused_computation | loop fusion | bytes 1048576 | tf_op jit(solution)/shard_map/squeeze | solution.py:572
  2.5 2.5 %collective-permute-start.2 = (bf16[128,2048]{1,0:T(8,128)(2,1)S(1)}, bf16[128,2048]{1,0:T(8,128)(2,1)}, u32[]{:S(2)}, u32[]{:S(2)}) collective-permute-start(bf16[128,2048]{1,0:T(8,128)(2,1)S(1)} %slice_bitcast_fusion.refs_0_), channel_id=1, source_target_pairs={{0,2},{1,3},{2,0},{3,1},{4,6},{5,7},{6,4},{7,5},{8,10},{9,11},{10,... | collective-permute-start | bytes 1572872 | tf_op jit(solution)/shard_map/ppermute | solution.py:84
  5.0 1.5 %collective-permute-start.8 = (bf16[128,2048]{1,0:T(8,128)(2,1)}, bf16[128,2048]{1,0:T(8,128)(2,1)}, u32[]{:S(2)}, u32[]{:S(2)}) collective-permute-start(bf16[128,2048]{1,0:T(8,128)(2,1)} %bitcast.32), channel_id=1, source_target_pairs={{0,4},{1,5},{2,6},{3,7},{4,0},{5,1},{6,2},{7,3},{8,12},{9,13},{10,... | collective-permute-start | bytes 1572872 | tf_op jit(solution)/shard_map/ppermute | solution.py:84
  8.5 3.3 %all-to-all-start = ((f32[8,8,128]{2,1,0:T(8,128)}), f32[8,8,128]{2,1,0:T(8,128)S(1)}, u32[]{:S(2)}, u32[]{:S(2)}) async-start(f32[8,8,128]{2,1,0:T(8,128)} %broadcast_in_dim.15), calls=%async_computation | async-start | bytes 65536 | tf_op jit(solution)/shard_map/all_to_all | solution.py:579
  13.6 3.5 %shard_map.85 = (bf16[44,384,2048]{2,1,0:T(8,128)(2,1)}, bf16[96,2048]{1,0:T(8,128)(2,1)}, bf16[96,2048]{1,0:T(8,128)(2,1)}, bf16[96,2048]{1,0:T(8,128)(2,1)}, b...) custom-call(f32[8,128]{1,0:T(8,128)} %copy-done.6, f32[8,128]{1,0:T(8,128)} %copy-done.7, ...), custom_call_target="tpu_custom_call" | custom-call | bytes 235405312 | tf_op jit(solution)/shard_map/pallas_call | solution.py:189
  17.1 1.9 %collective-permute-start.6 = (bf16[96,2048]{1,0:T(8,128)(2,1)}, bf16[96,2048]{1,0:T(8,128)(2,1)}, u32[]{:S(2)}, u32[]{:S(2)}) collective-permute-start(bf16[96,2048]{1,0:T(8,128)(2,1)} %get-tuple-element.91), channel_id=1, source_target_pairs={{0,2},{1,3},{2,0},{3,1},{4,6},{5,7},{6,4},{7,5},{8,10},{9,11},{10,... | collective-permute-start | bytes 1179656 | tf_op jit(solution)/shard_map/ppermute | solution.py:84
  19.1 1.5 %collective-permute-start.7 = (bf16[96,2048]{1,0:T(8,128)(2,1)}, bf16[96,2048]{1,0:T(8,128)(2,1)}, u32[]{:S(2)}, u32[]{:S(2)}) collective-permute-start(bf16[96,2048]{1,0:T(8,128)(2,1)} %get-tuple-element.92), channel_id=1, source_target_pairs={{0,4},{1,5},{2,6},{3,7},{4,0},{5,1},{6,2},{7,3},{8,12},{9,13},{10,... | collective-permute-start | bytes 1179656 | tf_op jit(solution)/shard_map/ppermute | solution.py:84
  20.6 2.1 %shard_map.86 = (bf16[96,2048]{1,0:T(8,128)(2,1)S(1)}, bf16[96,2048]{1,0:T(8,128)(2,1)S(1)}, bf16[96,2048]{1,0:T(8,128)(2,1)S(1)}, bf16[96,2048]{1,0:T(8,128)(2,1)S(1)}) custom-call(f32[8,8,128]{2,1,0:T(8,128)S(1)} %all-to-all-done.meta_ref, bf16[128,2048]{1,0:T(8,128)(2,1)S(1)} %slice_bitcast_fusion.refs_0_, bf16[128,2048]{1,0:T(8,128)(2,1)} %collective-permute-done.2.refs_1_), custom_call_target="tpu_custom_call" | custom-call | bytes 169869312 | tf_op jit(solution)/shard_map/pallas_call | solution.py:45
  24.7 1.3 %collective-permute-start.5 = (bf16[96,2048]{1,0:T(8,128)(2,1)S(1)}, bf16[96,2048]{1,0:T(8,128)(2,1)S(1)}, u32[]{:S(2)}, u32[]{:S(2)}) collective-permute-start(bf16[96,2048]{1,0:T(8,128)(2,1)S(1)} %get-tuple-element.99), channel_id=1, source_target_pairs={{0,5},{1,4},{2,7},{3,6},{4,1},{5,0},{6,3},{7,2},{8,13},{9,12},{10,... | collective-permute-start | bytes 1179656 | tf_op jit(solution)/shard_map/ppermute | solution.py:84
  25.9 1.0 copy-done.2
  27.0 2.1 %shard_map.89 = (bf16[96,2048]{1,0:T(8,128)(2,1)S(1)}, bf16[96,2048]{1,0:T(8,128)(2,1)S(1)}, bf16[96,2048]{1,0:T(8,128)(2,1)S(1)}, bf16[96,2048]{1,0:T(8,128)(2,1)S(1)}) custom-call(f32[8,8,128]{2,1,0:T(8,128)S(1)} %all-to-all-done.meta_ref, bf16[128,2048]{1,0:T(8,128)(2,1)S(1)} %bitcast.33, bf16[128,2048]{1,0:T(8,128)(2,1)} %collective-permute-done.8.refs_1_), custom_call_target="tpu_custom_call" | custom-call | bytes 169869312 | tf_op jit(solution)/shard_map/pallas_call | solution.py:45
  29.1 1.5 %collective-permute-start.10 = (bf16[96,2048]{1,0:T(8,128)(2,1)S(1)}, bf16[96,2048]{1,0:T(8,128)(2,1)S(1)}, u32[]{:S(2)}, u32[]{:S(2)}) collective-permute-start(bf16[96,2048]{1,0:T(8,128)(2,1)S(1)} %get-tuple-element.110), channel_id=1, source_target_pairs={{0,2},{1,3},{2,0},{3,1},{4,6},{5,7},{6,4},{7,5},{8,10},{9,11},{10,... | collective-permute-start | bytes 1179656 | tf_op jit(solution)/shard_map/ppermute | solution.py:84
  31.6 8.1 %collective-permute-done.4.refs_2_ = bf16[96,2048]{1,0:T(8,128)(2,1)S(1)} collective-permute-done((bf16[96,2048]{1,0:T(8,128)(2,1)S(1)}, bf16[96,2048]{1,0:T(8,128)(2,1)S(1)}, u32[]{:S(2)}, u32[]{:S(2)}) %collective-permute-start.4) | collective-permute-done | bytes 393248 | tf_op jit(solution)/shard_map/ppermute | solution.py:84
  39.7 6.3 %collective-permute-done.5.refs_3_ = bf16[96,2048]{1,0:T(8,128)(2,1)S(1)} collective-permute-done((bf16[96,2048]{1,0:T(8,128)(2,1)S(1)}, bf16[96,2048]{1,0:T(8,128)(2,1)S(1)}, u32[]{:S(2)}, u32[]{:S(2)}) %collective-permute-start.5) | collective-permute-done | bytes 393248 | tf_op jit(solution)/shard_map/ppermute | solution.py:84
  46.1 1.8 %shard_map.87 = (bf16[384,2048]{1,0:T(8,128)(2,1)S(1)}, bf16[384,768]{1,0:T(8,128)(2,1)S(1)}, f32[384,704]{1,0:T(8,128)S(1)}) custom-call(bf16[704,2048]{1,0:T(8,128)(2,1)S(1)} %bitcast.26, bf16[96,2048]{1,0:T(8,128)(2,1)S(1)} %get-tuple-element.100.refs_0_, bf16[96,2048]{1,0:T(8,128)(2,1)S(1)} %collective-permute-done.3.refs_1_, ...), custom_call_target="tpu_custom_call" | custom-call | bytes 492830720 | tf_op jit(solution)/shard_map/pallas_call | solution.py:45
  48.2 1.1 collective-permute-start.12
  49.3 3.2 %shard_map.90 = (bf16[384,2048]{1,0:T(8,128)(2,1)S(1)}, bf16[384,768]{1,0:T(8,128)(2,1)S(1)}, bf16[384,256]{1,0:T(8,128)(2,1)S(1)}, bf16[96,1024]{1,0:T(8,128)(2...) custom-call(bf16[704,2048]{1,0:T(8,128)(2,1)S(1)} %bitcast.27, ...), custom_call_target="tpu_custom_call" | custom-call | bytes 834666496 | tf_op jit(solution)/shard_map/pallas_call | solution.py:45
  52.6 1.5 %collective-permute-start.13 = (bf16[96,1024]{1,0:T(8,128)(2,1)S(1)}, bf16[96,1024]{1,0:T(8,128)(2,1)S(1)}, u32[]{:S(2)}, u32[]{:S(2)}) collective-permute-start(bf16[96,1024]{1,0:T(8,128)(2,1)S(1)} %get-tuple-element.120), channel_id=1, source_target_pairs={{0,2},{1,3},{2,0},{3,1},{4,6},{5,7},{6,4},{7,5},{8,10},{9,11},{10,... | collective-permute-start | bytes 589832 | tf_op jit(solution)/shard_map/ppermute | solution.py:84
  54.1 0.9 collective-permute-start.14
  55.0 1.1 collective-permute-start.15
  56.2 0.9 shard_map.92
  57.0 1.5 %collective-permute-start.17 = (bf16[96,1024]{1,0:T(8,128)(2,1)S(1)}, bf16[96,1024]{1,0:T(8,128)(2,1)S(1)}, u32[]{:S(2)}, u32[]{:S(2)}) collective-permute-start(bf16[96,1024]{1,0:T(8,128)(2,1)S(1)} %get-tuple-element.131), channel_id=1, source_target_pairs={{0,2},{1,3},{2,0},{3,1},{4,6},{5,7},{6,4},{7,5},{8,10},{9,11},{10,... | collective-permute-start | bytes 589832 | tf_op jit(solution)/shard_map/ppermute | solution.py:84
  58.6 2.1 %shard_map.91._ = bf16[44,384,2048]{2,1,0:T(8,128)(2,1)} custom-call(bf16[384,2048]{1,0:T(8,128)(2,1)S(1)} %get-tuple-element.104.refs_0_, bf16[384,2048]{1,0:T(8,128)(2,1)S(1)} %get-tuple-element.113.refs_1_, bf16[384,768]{1,0:T(8,128)(2,1)S(1)} %get-tuple-element.105.hid_ref.refs_2_, ...), custom_call_target="tpu_custom_call", output_to_operand_aliasing={{}: (5, {})} | custom-call | tf_op jit(solution)/shard_map/pallas_call | solution.py:414
  60.7 1.0 collective-permute-start.18
  61.7 1.1 collective-permute-start.19
  62.8 2.9 %collective-permute-done.14.refs_2_ = bf16[96,1024]{1,0:T(8,128)(2,1)S(1)} collective-permute-done((bf16[96,1024]{1,0:T(8,128)(2,1)S(1)}, bf16[96,1024]{1,0:T(8,128)(2,1)S(1)}, u32[]{:S(2)}, u32[]{:S(2)}) %collective-permute-start.14) | collective-permute-done | bytes 196640 | tf_op jit(solution)/shard_map/ppermute | solution.py:84
  66.1 1.5 %collective-permute-done.16.refs_0_ = bf16[128,1024]{1,0:T(8,128)(2,1)S(1)} collective-permute-done((bf16[128,1024]{1,0:T(8,128)(2,1)S(1)}, bf16[128,1024]{1,0:T(8,128)(2,1)S(1)}, u32[]{:S(2)}, u32[]{:S(2)}) %collective-permute-start.16) | collective-permute-done | bytes 262176 | tf_op jit(solution)/shard_map/ppermute | solution.py:84
  67.6 1.3 %collective-permute-start.23 = (bf16[128,1024]{1,0:T(8,128)(2,1)S(1)}, bf16[128,1024]{1,0:T(8,128)(2,1)S(1)}, u32[]{:S(2)}, u32[]{:S(2)}) collective-permute-start(bf16[128,1024]{1,0:T(8,128)(2,1)S(1)} %shard_map.95), channel_id=1, source_target_pairs={{8,0},{16,8},{24,16},{9,1},{17,9},{25,17},{10,2},{18,10},{26,18},{... | collective-permute-start | bytes 786440 | tf_op jit(solution)/shard_map/ppermute | solution.py:656
  69.2 4.7 %collective-permute-done.18.refs_2_ = bf16[96,1024]{1,0:T(8,128)(2,1)S(1)} collective-permute-done((bf16[96,1024]{1,0:T(8,128)(2,1)S(1)}, bf16[96,1024]{1,0:T(8,128)(2,1)S(1)}, u32[]{:S(2)}, u32[]{:S(2)}) %collective-permute-start.18) | collective-permute-done | bytes 196640 | tf_op jit(solution)/shard_map/ppermute | solution.py:84
  74.4 1.5 %collective-permute-done.20.refs_0_ = bf16[128,1024]{1,0:T(8,128)(2,1)S(1)} collective-permute-done((bf16[128,1024]{1,0:T(8,128)(2,1)S(1)}, bf16[128,1024]{1,0:T(8,128)(2,1)S(1)}, u32[]{:S(2)}, u32[]{:S(2)}) %collective-permute-start.20) | collective-permute-done | bytes 262176 | tf_op jit(solution)/shard_map/ppermute | solution.py:84
  75.9 1.5 %collective-permute-start.22 = (bf16[128,1024]{1,0:T(8,128)(2,1)S(1)}, bf16[128,1024]{1,0:T(8,128)(2,1)S(1)}, u32[]{:S(2)}, u32[]{:S(2)}) collective-permute-start(bf16[128,1024]{1,0:T(8,128)(2,1)S(1)} %shard_map.98), channel_id=1, source_target_pairs={{8,0},{16,8},{24,16},{9,1},{17,9},{25,17},{10,2},{18,10},{26,18},{... | collective-permute-start | bytes 786440 | tf_op jit(solution)/shard_map/ppermute | solution.py:656
  77.4 1.3 %collective-permute-start.21 = (bf16[96,1024]{1,0:T(8,128)(2,1)}, bf16[96,1024]{1,0:T(8,128)(2,1)}, u32[]{:S(2)}, u32[]{:S(2)}) collective-permute-start(bf16[96,1024]{1,0:T(8,128)(2,1)} %get-tuple-element.140), channel_id=1, source_target_pairs={{0,6},{1,7},{2,4},{3,5},{4,2},{5,3},{6,0},{7,1},{8,14},{9,15},{10,... | collective-permute-start | bytes 589832 | tf_op jit(solution)/shard_map/ppermute | solution.py:84
  78.9 1.3 %collective-permute-done.24.refs_0_ = bf16[128,1024]{1,0:T(8,128)(2,1)S(1)} collective-permute-done((bf16[128,1024]{1,0:T(8,128)(2,1)S(1)}, bf16[128,1024]{1,0:T(8,128)(2,1)S(1)}, u32[]{:S(2)}, u32[]{:S(2)}) %collective-permute-start.24) | collective-permute-done | bytes 262176 | tf_op jit(solution)/shard_map/ppermute | solution.py:84
  80.5 1.2 %collective-permute-start.26 = (bf16[96,1024]{1,0:T(8,128)(2,1)S(1)}, bf16[96,1024]{1,0:T(8,128)(2,1)S(1)}, u32[]{:S(2)}, u32[]{:S(2)}) collective-permute-start(bf16[96,1024]{1,0:T(8,128)(2,1)S(1)} %get-tuple-element.144), channel_id=1, source_target_pairs={{0,2},{1,3},{2,0},{3,1},{4,6},{5,7},{6,4},{7,5},{8,10},{9,11},{10,... | collective-permute-start | bytes 589832 | tf_op jit(solution)/shard_map/ppermute | solution.py:84
  81.7 1.1 collective-permute-start.27
  82.8 1.2 %collective-permute-start.28 = (bf16[96,1024]{1,0:T(8,128)(2,1)S(1)}, bf16[96,1024]{1,0:T(8,128)(2,1)S(1)}, u32[]{:S(2)}, u32[]{:S(2)}) collective-permute-start(bf16[96,1024]{1,0:T(8,128)(2,1)S(1)} %get-tuple-element.146), channel_id=1, source_target_pairs={{0,6},{1,7},{2,4},{3,5},{4,2},{5,3},{6,0},{7,1},{8,14},{9,15},{10,... | collective-permute-start | bytes 589832 | tf_op jit(solution)/shard_map/ppermute | solution.py:84
  84.0 2.1 %collective-permute-done.22.raw_ref = bf16[128,1024]{1,0:T(8,128)(2,1)S(1)} collective-permute-done((bf16[128,1024]{1,0:T(8,128)(2,1)S(1)}, bf16[128,1024]{1,0:T(8,128)(2,1)S(1)}, u32[]{:S(2)}, u32[]{:S(2)}) %collective-permute-start.22) | collective-permute-done | bytes 262176 | tf_op jit(solution)/shard_map/ppermute | solution.py:656
  86.4 1.3 %collective-permute-done.25.refs_0_ = bf16[128,1024]{1,0:T(8,128)(2,1)S(1)} collective-permute-done((bf16[128,1024]{1,0:T(8,128)(2,1)S(1)}, bf16[128,1024]{1,0:T(8,128)(2,1)S(1)}, u32[]{:S(2)}, u32[]{:S(2)}) %collective-permute-start.25) | collective-permute-done | bytes 262176 | tf_op jit(solution)/shard_map/ppermute | solution.py:84
  87.9 0.9 collective-permute-start.29
  88.9 0.9 collective-permute-start.30
  90.0 1.5 %collective-permute-start.31 = (bf16[96,1024]{1,0:T(8,128)(2,1)S(1)}, bf16[96,1024]{1,0:T(8,128)(2,1)S(1)}, u32[]{:S(2)}, u32[]{:S(2)}) collective-permute-start(bf16[96,1024]{1,0:T(8,128)(2,1)S(1)} %get-tuple-element.151), channel_id=1, source_target_pairs={{0,6},{1,7},{2,4},{3,5},{4,2},{5,3},{6,0},{7,1},{8,14},{9,15},{10,... | collective-permute-start | bytes 589832 | tf_op jit(solution)/shard_map/ppermute | solution.py:84
  91.5 3.8 %shard_map.103 = (bf16[44,384,2048]{2,1,0:T(8,128)(2,1)}, bf16[384,704]{1,0:T(8,128)(2,1)S(1)}, f32[384,704]{1,0:T(8,128)S(1)}) custom-call(bf16[704,2048]{1,0:T(8,128)(2,1)S(1)} %bitcast.28, bf16[44,384,2048]{2,1,0:T(8,128)(2,1)} %shard_map.91._, bf16[96,2048]{1,0:T(8,128)(2,1)S(1)} %copy-done.3, ...), custom_call_target="tpu_custom_call", output_to_operand_aliasing={{0}: (1, {})} | custom-call | bytes 9247391744 | tf_op jit(solution)/shard_map/pallas_call | solution.py:45
  95.4 4.4 %shard_map.104 = (f32[384,704]{1,0:T(8,128)S(1)}, bf16[704,2048]{1,0:T(8,128)(2,1)}) custom-call(bf16[704,2048]{1,0:T(8,128)(2,1)S(1)} %bitcast.30, bf16[384,704]{1,0:T(8,128)(2,1)S(1)} %get-tuple-element.157.hid1_ref.hid_ref, bf16[44,384,2048]{2,1,0:T(8,128)(2,1)} %get-tuple-element.158.pad_ref, bf16[96,1024]{1,0:T(8,128)(2,1)S(1)} %get-tuple-element.143.refs_0_, ...), custom_call_target="tpu_custom_call" | custom-call | bytes 523239424 | tf_op jit(solution)/shard_map/pallas_call | solution.py:452
  99.8 2.6 %collective-permute-done.31.refs_3_ = bf16[96,1024]{1,0:T(8,128)(2,1)S(1)} collective-permute-done((bf16[96,1024]{1,0:T(8,128)(2,1)S(1)}, bf16[96,1024]{1,0:T(8,128)(2,1)S(1)}, u32[]{:S(2)}, u32[]{:S(2)}) %collective-permute-start.31) | collective-permute-done | bytes 196640 | tf_op jit(solution)/shard_map/ppermute | solution.py:84
  102.4 2.4 %shard_map.105 = (bf16[384,1024]{1,0:T(8,128)(2,1)S(1)}, bf16[384,768]{1,0:T(8,128)(2,1)S(1)}, bf16[384,128]{1,0:T(8,128)(2,1)}) custom-call(bf16[704,2048]{1,0:T(8,128)(2,1)S(1)} %bitcast.31, bf16[384,704]{1,0:T(8,128)(2,1)S(1)} %get-tuple-element.157.hid1_ref.hid_ref, f32[384,704]{1,0:T(8,128)S(1)} %get-tuple-element.160.slope_ref, ...), custom_call_target="tpu_custom_call" | custom-call | bytes 4931452928 | tf_op jit(solution)/shard_map/pallas_call | solution.py:45
  104.8 3.4 %all-to-all-start.1 = ((bf16[8,48,128]{2,1,0:T(8,128)(2,1)}), bf16[8,48,128]{2,1,0:T(8,128)(2,1)S(1)}, u32[]{:S(2)}, u32[]{:S(2)}) async-start(bf16[8,48,128]{2,1,0:T(8,128)(2,1)} %bitcast.13), calls=%async_computation.1 | async-start | bytes 196608 | tf_op jit(solution)/shard_map/all_to_all | solution.py:293
  108.2 6.8 %shard_map.106 = (bf16[704,2048]{1,0:T(8,128)(2,1)}, bf16[704,2048]{1,0:T(8,128)(2,1)}) custom-call(bf16[704,2048]{1,0:T(8,128)(2,1)} %get-tuple-element.159._, bf16[44,384,2048]{2,1,0:T(8,128)(2,1)} %get-tuple-element.158.pad_ref, bf16[384,1024]{1,0:T(8,128)(2,1)S(1)} %get-tuple-element.166.g1_ref, ...), custom_call_target="tpu_custom_call", output_to_operand_aliasing={{1}: (0, {})} | custom-call | bytes 369098752 | tf_op jit(solution)/shard_map/pallas_call | solution.py:528
  115.1 0.9 shard_map.107
  (66 shorter events, 10.2 us)
Async XLA Ops:
  0.6 45.4 %copy-start = (bf16[1,1,704,2048]{3,2,1,0:T(8,128)(2,1)S(1)}, bf16[1,1,704,2048]{3,2,1,0:T(8,128)(2,1)}, u32[]{:S(2)}) copy-start(bf16[1,1,704,2048]{3,2,1,0:T(8,128)(2,1)} %param.8) | copy-start | bytes 8650756
  0.6 12.4 %collective-permute-start.1 = (bf16[2,128,2048]{2,1,0:T(8,128)(2,1)}, bf16[2,128,2048]{2,1,0:T(8,128)(2,1)}, u32[]{:S(2)}, u32[]{:S(2)}) collective-permute-start(bf16[2,128,2048]{2,1,0:T(8,128)(2,1)} %bitcast.38), channel_id=1, source_target_pairs={{0,1},{1,0},{2,3},{3,2},{4,5},{5,4},{6,7},{7,6},{8,9},{9,8},{10,11... | collective-permute-start | bytes 3145736 | tf_op jit(solution)/shard_map/ppermute | solution.py:84
  2.5 18.1 %collective-permute-start.2 = (bf16[128,2048]{1,0:T(8,128)(2,1)S(1)}, bf16[128,2048]{1,0:T(8,128)(2,1)}, u32[]{:S(2)}, u32[]{:S(2)}) collective-permute-start(bf16[128,2048]{1,0:T(8,128)(2,1)S(1)} %slice_bitcast_fusion.refs_0_), channel_id=1, source_target_pairs={{0,2},{1,3},{2,0},{3,1},{4,6},{5,7},{6,4},{7,5},{8,10},{9,11},{10,... | collective-permute-start | bytes 1572872 | tf_op jit(solution)/shard_map/ppermute | solution.py:84
  5.0 19.7 %collective-permute-start.8 = (bf16[128,2048]{1,0:T(8,128)(2,1)}, bf16[128,2048]{1,0:T(8,128)(2,1)}, u32[]{:S(2)}, u32[]{:S(2)}) collective-permute-start(bf16[128,2048]{1,0:T(8,128)(2,1)} %bitcast.32), channel_id=1, source_target_pairs={{0,4},{1,5},{2,6},{3,7},{4,0},{5,1},{6,2},{7,3},{8,12},{9,13},{10,... | collective-permute-start | bytes 1572872 | tf_op jit(solution)/shard_map/ppermute | solution.py:84
  7.9 5.2 %copy-start.6 = (f32[8,128]{1,0:T(8,128)}, f32[8,128]{1,0:T(8,128)S(1)}, u32[]{:S(2)}) copy-start(f32[8,128]{1,0:T(8,128)S(1)} %pad_maximum_fusion.refs_0_) | copy-start | bytes 12292
  8.5 12.1 %all-to-all-start = ((f32[8,8,128]{2,1,0:T(8,128)}), f32[8,8,128]{2,1,0:T(8,128)S(1)}, u32[]{:S(2)}, u32[]{:S(2)}) async-start(f32[8,8,128]{2,1,0:T(8,128)} %broadcast_in_dim.15), calls=%async_computation | async-start | bytes 65536 | tf_op jit(solution)/shard_map/all_to_all | solution.py:579
  11.8 1.2 %collective-permute-start = (f32[8,128]{1,0:T(8,128)S(1)}, f32[8,128]{1,0:T(8,128)S(1)}, u32[]{:S(2)}, u32[]{:S(2)}) collective-permute-start(f32[8,128]{1,0:T(8,128)S(1)} %pad_maximum_fusion.refs_0_), channel_id=1, source_target_pairs={{0,1},{1,0},{2,3},{3,2},{4,5},{5,4},{6,7},{7,6},{8,9},{9,8},{10,11... | collective-permute-start | bytes 12296 | tf_op jit(solution)/shard_map/ppermute | solution.py:84
  13.0 0.6 copy-start.7
  17.1 11.9 %collective-permute-start.6 = (bf16[96,2048]{1,0:T(8,128)(2,1)}, bf16[96,2048]{1,0:T(8,128)(2,1)}, u32[]{:S(2)}, u32[]{:S(2)}) collective-permute-start(bf16[96,2048]{1,0:T(8,128)(2,1)} %get-tuple-element.91), channel_id=1, source_target_pairs={{0,2},{1,3},{2,0},{3,1},{4,6},{5,7},{6,4},{7,5},{8,10},{9,11},{10,... | collective-permute-start | bytes 1179656 | tf_op jit(solution)/shard_map/ppermute | solution.py:84
  19.1 12.3 %collective-permute-start.7 = (bf16[96,2048]{1,0:T(8,128)(2,1)}, bf16[96,2048]{1,0:T(8,128)(2,1)}, u32[]{:S(2)}, u32[]{:S(2)}) collective-permute-start(bf16[96,2048]{1,0:T(8,128)(2,1)} %get-tuple-element.92), channel_id=1, source_target_pairs={{0,4},{1,5},{2,6},{3,7},{4,0},{5,1},{6,2},{7,3},{8,12},{9,13},{10,... | collective-permute-start | bytes 1179656 | tf_op jit(solution)/shard_map/ppermute | solution.py:84
  20.6 27.7 %copy-start.8 = (bf16[96,1024]{1,0:T(8,128)(2,1)S(1)}, bf16[96,1024]{1,0:T(8,128)(2,1)}, u32[]{:S(2)}) copy-start(bf16[96,1024]{1,0:T(8,128)(2,1)} %get-tuple-element.117) | copy-start | bytes 589828
  22.7 26.6 %copy-start.1 = (bf16[1,1,704,2048]{3,2,1,0:T(8,128)(2,1)S(1)}, bf16[1,1,704,2048]{3,2,1,0:T(8,128)(2,1)}, u32[]{:S(2)}) copy-start(bf16[1,1,704,2048]{3,2,1,0:T(8,128)(2,1)} %param.9) | copy-start | bytes 8650756
  22.7 8.7 %collective-permute-start.3 = (bf16[96,2048]{1,0:T(8,128)(2,1)S(1)}, bf16[96,2048]{1,0:T(8,128)(2,1)S(1)}, u32[]{:S(2)}, u32[]{:S(2)}) collective-permute-start(bf16[96,2048]{1,0:T(8,128)(2,1)S(1)} %get-tuple-element.97), channel_id=1, source_target_pairs={{0,1},{1,0},{2,3},{3,2},{4,5},{5,4},{6,7},{7,6},{8,9},{9,8},{10,11... | collective-permute-start | bytes 1179656 | tf_op jit(solution)/shard_map/ppermute | solution.py:84
  23.4 0.6 copy-start.4
  24.1 15.7 %collective-permute-start.4 = (bf16[96,2048]{1,0:T(8,128)(2,1)S(1)}, bf16[96,2048]{1,0:T(8,128)(2,1)S(1)}, u32[]{:S(2)}, u32[]{:S(2)}) collective-permute-start(bf16[96,2048]{1,0:T(8,128)(2,1)S(1)} %get-tuple-element.98), channel_id=1, source_target_pairs={{0,4},{1,5},{2,6},{3,7},{4,0},{5,1},{6,2},{7,3},{8,12},{9,13},{10,... | collective-permute-start | bytes 1179656 | tf_op jit(solution)/shard_map/ppermute | solution.py:84
  24.7 21.4 %collective-permute-start.5 = (bf16[96,2048]{1,0:T(8,128)(2,1)S(1)}, bf16[96,2048]{1,0:T(8,128)(2,1)S(1)}, u32[]{:S(2)}, u32[]{:S(2)}) collective-permute-start(bf16[96,2048]{1,0:T(8,128)(2,1)S(1)} %get-tuple-element.99), channel_id=1, source_target_pairs={{0,5},{1,4},{2,7},{3,6},{4,1},{5,0},{6,3},{7,2},{8,13},{9,12},{10,... | collective-permute-start | bytes 1179656 | tf_op jit(solution)/shard_map/ppermute | solution.py:84
  25.9 1.0 copy-start.2
  29.1 18.8 %collective-permute-start.10 = (bf16[96,2048]{1,0:T(8,128)(2,1)S(1)}, bf16[96,2048]{1,0:T(8,128)(2,1)S(1)}, u32[]{:S(2)}, u32[]{:S(2)}) collective-permute-start(bf16[96,2048]{1,0:T(8,128)(2,1)S(1)} %get-tuple-element.110), channel_id=1, source_target_pairs={{0,2},{1,3},{2,0},{3,1},{4,6},{5,7},{6,4},{7,5},{8,10},{9,11},{10,... | collective-permute-start | bytes 1179656 | tf_op jit(solution)/shard_map/ppermute | solution.py:84
  31.4 16.5 %collective-permute-start.9 = (bf16[96,2048]{1,0:T(8,128)(2,1)S(1)}, bf16[96,2048]{1,0:T(8,128)(2,1)S(1)}, u32[]{:S(2)}, u32[]{:S(2)}) collective-permute-start(bf16[96,2048]{1,0:T(8,128)(2,1)S(1)} %get-tuple-element.109), channel_id=1, source_target_pairs={{0,1},{1,0},{2,3},{3,2},{4,5},{5,4},{6,7},{7,6},{8,9},{9,8},{10,11... | collective-permute-start | bytes 1179656 | tf_op jit(solution)/shard_map/ppermute | solution.py:84
  31.4 16.8 %collective-permute-start.11 = (bf16[96,2048]{1,0:T(8,128)(2,1)S(1)}, bf16[96,2048]{1,0:T(8,128)(2,1)S(1)}, u32[]{:S(2)}, u32[]{:S(2)}) collective-permute-start(bf16[96,2048]{1,0:T(8,128)(2,1)S(1)} %get-tuple-element.112), channel_id=1, source_target_pairs={{0,3},{1,2},{2,1},{3,0},{4,7},{5,6},{6,5},{7,4},{8,11},{9,10},{10,... | collective-permute-start | bytes 1179656 | tf_op jit(solution)/shard_map/ppermute | solution.py:84
  48.2 12.5 %collective-permute-start.12 = (bf16[96,1024]{1,0:T(8,128)(2,1)S(1)}, bf16[96,1024]{1,0:T(8,128)(2,1)S(1)}, u32[]{:S(2)}, u32[]{:S(2)}) collective-permute-start(bf16[96,1024]{1,0:T(8,128)(2,1)S(1)} %copy-done.8), channel_id=1, source_target_pairs={{0,6},{1,7},{2,4},{3,5},{4,2},{5,3},{6,0},{7,1},{8,14},{9,15},{10,... | collective-permute-start | bytes 589832 | tf_op jit(solution)/shard_map/ppermute | solution.py:84
  52.6 9.1 %collective-permute-start.13 = (bf16[96,1024]{1,0:T(8,128)(2,1)S(1)}, bf16[96,1024]{1,0:T(8,128)(2,1)S(1)}, u32[]{:S(2)}, u32[]{:S(2)}) collective-permute-start(bf16[96,1024]{1,0:T(8,128)(2,1)S(1)} %get-tuple-element.120), channel_id=1, source_target_pairs={{0,2},{1,3},{2,0},{3,1},{4,6},{5,7},{6,4},{7,5},{8,10},{9,11},{10,... | collective-permute-start | bytes 589832 | tf_op jit(solution)/shard_map/ppermute | solution.py:84
  54.1 11.5 %collective-permute-start.14 = (bf16[96,1024]{1,0:T(8,128)(2,1)S(1)}, bf16[96,1024]{1,0:T(8,128)(2,1)S(1)}, u32[]{:S(2)}, u32[]{:S(2)}) collective-permute-start(bf16[96,1024]{1,0:T(8,128)(2,1)S(1)} %get-tuple-element.121), channel_id=1, source_target_pairs={{0,4},{1,5},{2,6},{3,7},{4,0},{5,1},{6,2},{7,3},{8,12},{9,13},{10,... | collective-permute-start | bytes 589832 | tf_op jit(solution)/shard_map/ppermute | solution.py:84
  55.0 10.6 %collective-permute-start.15 = (bf16[96,1024]{1,0:T(8,128)(2,1)S(1)}, bf16[96,1024]{1,0:T(8,128)(2,1)S(1)}, u32[]{:S(2)}, u32[]{:S(2)}) collective-permute-start(bf16[96,1024]{1,0:T(8,128)(2,1)S(1)} %get-tuple-element.122), channel_id=1, source_target_pairs={{0,6},{1,7},{2,4},{3,5},{4,2},{5,3},{6,0},{7,1},{8,14},{9,15},{10,... | collective-permute-start | bytes 589832 | tf_op jit(solution)/shard_map/ppermute | solution.py:84
  57.0 12.2 %collective-permute-start.17 = (bf16[96,1024]{1,0:T(8,128)(2,1)S(1)}, bf16[96,1024]{1,0:T(8,128)(2,1)S(1)}, u32[]{:S(2)}, u32[]{:S(2)}) collective-permute-start(bf16[96,1024]{1,0:T(8,128)(2,1)S(1)} %get-tuple-element.131), channel_id=1, source_target_pairs={{0,2},{1,3},{2,0},{3,1},{4,6},{5,7},{6,4},{7,5},{8,10},{9,11},{10,... | collective-permute-start | bytes 589832 | tf_op jit(solution)/shard_map/ppermute | solution.py:84
  60.7 13.2 %collective-permute-start.18 = (bf16[96,1024]{1,0:T(8,128)(2,1)S(1)}, bf16[96,1024]{1,0:T(8,128)(2,1)S(1)}, u32[]{:S(2)}, u32[]{:S(2)}) collective-permute-start(bf16[96,1024]{1,0:T(8,128)(2,1)S(1)} %get-tuple-element.132), channel_id=1, source_target_pairs={{0,4},{1,5},{2,6},{3,7},{4,0},{5,1},{6,2},{7,3},{8,12},{9,13},{10,... | collective-permute-start | bytes 589832 | tf_op jit(solution)/shard_map/ppermute | solution.py:84
  61.7 12.3 %collective-permute-start.19 = (bf16[96,1024]{1,0:T(8,128)(2,1)S(1)}, bf16[96,1024]{1,0:T(8,128)(2,1)S(1)}, u32[]{:S(2)}, u32[]{:S(2)}) collective-permute-start(bf16[96,1024]{1,0:T(8,128)(2,1)S(1)} %get-tuple-element.133), channel_id=1, source_target_pairs={{0,6},{1,7},{2,4},{3,5},{4,2},{5,3},{6,0},{7,1},{8,14},{9,15},{10,... | collective-permute-start | bytes 589832 | tf_op jit(solution)/shard_map/ppermute | solution.py:84
  66.0 1.6 %collective-permute-start.16 = (bf16[128,1024]{1,0:T(8,128)(2,1)S(1)}, bf16[128,1024]{1,0:T(8,128)(2,1)S(1)}, u32[]{:S(2)}, u32[]{:S(2)}) collective-permute-start(bf16[128,1024]{1,0:T(8,128)(2,1)S(1)} %get-tuple-element.128), channel_id=1, source_target_pairs={{0,1},{1,0},{2,3},{3,2},{4,5},{5,4},{6,7},{7,6},{8,9},{9,8},{10,11... | collective-permute-start | bytes 786440 | tf_op jit(solution)/shard_map/ppermute | solution.py:84
  67.6 11.1 %collective-permute-start.23 = (bf16[128,1024]{1,0:T(8,128)(2,1)S(1)}, bf16[128,1024]{1,0:T(8,128)(2,1)S(1)}, u32[]{:S(2)}, u32[]{:S(2)}) collective-permute-start(bf16[128,1024]{1,0:T(8,128)(2,1)S(1)} %shard_map.95), channel_id=1, source_target_pairs={{8,0},{16,8},{24,16},{9,1},{17,9},{25,17},{10,2},{18,10},{26,18},{... | collective-permute-start | bytes 786440 | tf_op jit(solution)/shard_map/ppermute | solution.py:656
  74.3 1.6 %collective-permute-start.20 = (bf16[128,1024]{1,0:T(8,128)(2,1)S(1)}, bf16[128,1024]{1,0:T(8,128)(2,1)S(1)}, u32[]{:S(2)}, u32[]{:S(2)}) collective-permute-start(bf16[128,1024]{1,0:T(8,128)(2,1)S(1)} %get-tuple-element.139), channel_id=1, source_target_pairs={{0,1},{1,0},{2,3},{3,2},{4,5},{5,4},{6,7},{7,6},{8,9},{9,8},{10,11... | collective-permute-start | bytes 786440 | tf_op jit(solution)/shard_map/ppermute | solution.py:84
  75.9 10.2 %collective-permute-start.22 = (bf16[128,1024]{1,0:T(8,128)(2,1)S(1)}, bf16[128,1024]{1,0:T(8,128)(2,1)S(1)}, u32[]{:S(2)}, u32[]{:S(2)}) collective-permute-start(bf16[128,1024]{1,0:T(8,128)(2,1)S(1)} %shard_map.98), channel_id=1, source_target_pairs={{8,0},{16,8},{24,16},{9,1},{17,9},{25,17},{10,2},{18,10},{26,18},{... | collective-permute-start | bytes 786440 | tf_op jit(solution)/shard_map/ppermute | solution.py:656
  77.4 11.5 %collective-permute-start.21 = (bf16[96,1024]{1,0:T(8,128)(2,1)}, bf16[96,1024]{1,0:T(8,128)(2,1)}, u32[]{:S(2)}, u32[]{:S(2)}) collective-permute-start(bf16[96,1024]{1,0:T(8,128)(2,1)} %get-tuple-element.140), channel_id=1, source_target_pairs={{0,6},{1,7},{2,4},{3,5},{4,2},{5,3},{6,0},{7,1},{8,14},{9,15},{10,... | collective-permute-start | bytes 589832 | tf_op jit(solution)/shard_map/ppermute | solution.py:84
  78.7 1.5 %collective-permute-start.24 = (bf16[128,1024]{1,0:T(8,128)(2,1)S(1)}, bf16[128,1024]{1,0:T(8,128)(2,1)S(1)}, u32[]{:S(2)}, u32[]{:S(2)}) collective-permute-start(bf16[128,1024]{1,0:T(8,128)(2,1)S(1)} %collective-permute-done.23.raw_ref), channel_id=1, source_target_pairs={{0,1},{1,0},{2,3},{3,2},{4,5},{5,4},{6,7},{7,6},{8,9},{9,8},{10,11... | collective-permute-start | bytes 786440 | tf_op jit(solution)/shard_map/ppermute | solution.py:84
  80.5 9.5 %collective-permute-start.26 = (bf16[96,1024]{1,0:T(8,128)(2,1)S(1)}, bf16[96,1024]{1,0:T(8,128)(2,1)S(1)}, u32[]{:S(2)}, u32[]{:S(2)}) collective-permute-start(bf16[96,1024]{1,0:T(8,128)(2,1)S(1)} %get-tuple-element.144), channel_id=1, source_target_pairs={{0,2},{1,3},{2,0},{3,1},{4,6},{5,7},{6,4},{7,5},{8,10},{9,11},{10,... | collective-permute-start | bytes 589832 | tf_op jit(solution)/shard_map/ppermute | solution.py:84
  81.7 13.6 %collective-permute-start.27 = (bf16[96,1024]{1,0:T(8,128)(2,1)S(1)}, bf16[96,1024]{1,0:T(8,128)(2,1)S(1)}, u32[]{:S(2)}, u32[]{:S(2)}) collective-permute-start(bf16[96,1024]{1,0:T(8,128)(2,1)S(1)} %get-tuple-element.145), channel_id=1, source_target_pairs={{0,4},{1,5},{2,6},{3,7},{4,0},{5,1},{6,2},{7,3},{8,12},{9,13},{10,... | collective-permute-start | bytes 589832 | tf_op jit(solution)/shard_map/ppermute | solution.py:84
  82.8 12.5 %collective-permute-start.28 = (bf16[96,1024]{1,0:T(8,128)(2,1)S(1)}, bf16[96,1024]{1,0:T(8,128)(2,1)S(1)}, u32[]{:S(2)}, u32[]{:S(2)}) collective-permute-start(bf16[96,1024]{1,0:T(8,128)(2,1)S(1)} %get-tuple-element.146), channel_id=1, source_target_pairs={{0,6},{1,7},{2,4},{3,5},{4,2},{5,3},{6,0},{7,1},{8,14},{9,15},{10,... | collective-permute-start | bytes 589832 | tf_op jit(solution)/shard_map/ppermute | solution.py:84
  86.2 1.5 %collective-permute-start.25 = (bf16[128,1024]{1,0:T(8,128)(2,1)S(1)}, bf16[128,1024]{1,0:T(8,128)(2,1)S(1)}, u32[]{:S(2)}, u32[]{:S(2)}) collective-permute-start(bf16[128,1024]{1,0:T(8,128)(2,1)S(1)} %collective-permute-done.22.raw_ref), channel_id=1, source_target_pairs={{0,1},{1,0},{2,3},{3,2},{4,5},{5,4},{6,7},{7,6},{8,9},{9,8},{10,11... | collective-permute-start | bytes 786440 | tf_op jit(solution)/shard_map/ppermute | solution.py:84
  86.2 5.4 %copy-start.3 = (bf16[96,2048]{1,0:T(8,128)(2,1)S(1)}, bf16[96,2048]{1,0:T(8,128)(2,1)}, u32[]{:S(2)}) copy-start(bf16[96,2048]{1,0:T(8,128)(2,1)} %get-tuple-element.152.refs_0_) | copy-start | bytes 1179652
  87.9 11.9 %collective-permute-start.29 = (bf16[96,1024]{1,0:T(8,128)(2,1)S(1)}, bf16[96,1024]{1,0:T(8,128)(2,1)S(1)}, u32[]{:S(2)}, u32[]{:S(2)}) collective-permute-start(bf16[96,1024]{1,0:T(8,128)(2,1)S(1)} %get-tuple-element.149), channel_id=1, source_target_pairs={{0,2},{1,3},{2,0},{3,1},{4,6},{5,7},{6,4},{7,5},{8,10},{9,11},{10,... | collective-permute-start | bytes 589832 | tf_op jit(solution)/shard_map/ppermute | solution.py:84
  88.9 10.9 %collective-permute-start.30 = (bf16[96,1024]{1,0:T(8,128)(2,1)S(1)}, bf16[96,1024]{1,0:T(8,128)(2,1)S(1)}, u32[]{:S(2)}, u32[]{:S(2)}) collective-permute-start(bf16[96,1024]{1,0:T(8,128)(2,1)S(1)} %get-tuple-element.150), channel_id=1, source_target_pairs={{0,4},{1,5},{2,6},{3,7},{4,0},{5,1},{6,2},{7,3},{8,12},{9,13},{10,... | collective-permute-start | bytes 589832 | tf_op jit(solution)/shard_map/ppermute | solution.py:84
  90.0 12.4 %collective-permute-start.31 = (bf16[96,1024]{1,0:T(8,128)(2,1)S(1)}, bf16[96,1024]{1,0:T(8,128)(2,1)S(1)}, u32[]{:S(2)}, u32[]{:S(2)}) collective-permute-start(bf16[96,1024]{1,0:T(8,128)(2,1)S(1)} %get-tuple-element.151), channel_id=1, source_target_pairs={{0,6},{1,7},{2,4},{3,5},{4,2},{5,3},{6,0},{7,1},{8,14},{9,15},{10,... | collective-permute-start | bytes 589832 | tf_op jit(solution)/shard_map/ppermute | solution.py:84
  104.8 10.2 %all-to-all-start.1 = ((bf16[8,48,128]{2,1,0:T(8,128)(2,1)}), bf16[8,48,128]{2,1,0:T(8,128)(2,1)S(1)}, u32[]{:S(2)}, u32[]{:S(2)}) async-start(bf16[8,48,128]{2,1,0:T(8,128)(2,1)} %bitcast.13), calls=%async_computation.1 | async-start | bytes 196608 | tf_op jit(solution)/shard_map/all_to_all | solution.py:293
  108.2 6.9 %copy-start.5 = (bf16[384,128]{1,0:T(8,128)(2,1)S(1)}, bf16[384,128]{1,0:T(8,128)(2,1)}, u32[]{:S(2)}) copy-start(bf16[384,128]{1,0:T(8,128)(2,1)} %copy-done.4) | copy-start | bytes 294916

commit v9 on v8

--- a/solution.py
+++ b/solution.py
@@ -647,7 +647,7 @@
         after = [out]
 
     if stepped:
-        x1_rest[1:] = [plane.send(p, far) for p in behind(x1_rest[1:], leaving)]
+        x1_rest[1:] = [plane.send(p, far) for p in behind(x1_rest[1:], leaving[:1])]
         x1 = x1_near + x1_rest
     else:
         x1, x1_groups = [exchange(spread(hot1, inputs[0, 1]), experts)], [(0, None)]

time: 117 us -> 114 us (0.974)
  waiting for transfers between devices: 34.7 us -> 32.1 us
    ppermute x30, waiting for transfers between devices: 32.6 us -> 28.7 us  [send(): return lax.ppermute(value, 'expert', route)]
    ppermute x2, waiting for transfers between devices: 2.13 us -> 3.41 us  [body(): lax.ppermute(leaving[h], 'segment', [(i, i - 1) for i in range(1, segment...]
where the time goes in v9:
time: 114 us
  starting transfers between devices  38.3 us (34%)
  Pallas kernels  36.6 us (32%)
  waiting for transfers between devices  32.1 us (28%)
  local copies, waits for them, and re-layouts  4.22 us (4%)
  other arithmetic  1.37 us (1%)
    ppermute x30, starting transfers between devices, send(): return lax.ppermute(value, 'expert', route)  28.8 us
    ppermute x30, waiting for transfers between devices, send(): return lax.ppermute(value, 'expert', route)  28.7 us
    pallas_call x19, Pallas kernels, call(): pl.pallas_call(kernel, out_shape=outs, in_specs=specs, out_specs=[in_hbm(...  19.7 us
    pallas_call x1, Pallas kernels, late(): pl.pallas_call(functools.partial(late_kernel, width, part, units), out_sh...  6.84 us
    pallas_call x1, Pallas kernels, early(): pl.pallas_call(functools.partial(early_kernel, plane, capacity, groups),...  4.44 us
    pallas_call x1, Pallas kernels, own_picked(): pl.pallas_call(functools.partial(own_select_kernel, plane, capacity, plan...  3.51 us
    ppermute x2, waiting for transfers between devices, body(): lax.ppermute(leaving[h], 'segment', [(i, i - 1) for i in range(1, segment...  3.41 us
    all_to_all x1, starting transfers between devices, exchange(): lax.all_to_all(pieces, 'expert', split_axis=0, concat_axis=0, tiled=True)  3.37 us
  transfers between devices with their start and end apart: 34, of which 15 were waited for; matrix products, arithmetic and copies ran while one was open for 3% of the time, Pallas kernels for 29%

profile of v9, /device:TPU:0, one launch (start us, length us, event | category | flops | bytes accessed | tf_op | source)
XLA Modules:
  0.0 113.5 jit_solution(14815611434767036771)
XLA Ops:
  1.2 1.3 %slice_bitcast_fusion.refs_0_ = bf16[128,2048]{1,0:T(8,128)(2,1)S(1)} fusion(bf16[1,2,128,2048]{3,2,1,0:T(8,128)(2,1)} %param.6), kind=kLoop, calls=%fused_computation | loop fusion | bytes 1048576 | tf_op jit(solution)/shard_map/squeeze | solution.py:572
  2.5 2.5 %collective-permute-start.2 = (bf16[128,2048]{1,0:T(8,128)(2,1)S(1)}, bf16[128,2048]{1,0:T(8,128)(2,1)}, u32[]{:S(2)}, u32[]{:S(2)}) collective-permute-start(bf16[128,2048]{1,0:T(8,128)(2,1)S(1)} %slice_bitcast_fusion.refs_0_), channel_id=1, source_target_pairs={{0,2},{1,3},{2,0},{3,1},{4,6},{5,7},{6,4},{7,5},{8,10},{9,11},{10,... | collective-permute-start | bytes 1572872 | tf_op jit(solution)/shard_map/ppermute | solution.py:84
  5.0 1.5 %collective-permute-start.8 = (bf16[128,2048]{1,0:T(8,128)(2,1)}, bf16[128,2048]{1,0:T(8,128)(2,1)}, u32[]{:S(2)}, u32[]{:S(2)}) collective-permute-start(bf16[128,2048]{1,0:T(8,128)(2,1)} %bitcast.32), channel_id=1, source_target_pairs={{0,4},{1,5},{2,6},{3,7},{4,0},{5,1},{6,2},{7,3},{8,12},{9,13},{10,... | collective-permute-start | bytes 1572872 | tf_op jit(solution)/shard_map/ppermute | solution.py:84
  8.5 3.3 %all-to-all-start = ((f32[8,8,128]{2,1,0:T(8,128)}), f32[8,8,128]{2,1,0:T(8,128)S(1)}, u32[]{:S(2)}, u32[]{:S(2)}) async-start(f32[8,8,128]{2,1,0:T(8,128)} %broadcast_in_dim.15), calls=%async_computation | async-start | bytes 65536 | tf_op jit(solution)/shard_map/all_to_all | solution.py:579
  12.2 0.8 collective-permute-done.refs_1_
  13.6 3.5 %shard_map.85 = (bf16[44,384,2048]{2,1,0:T(8,128)(2,1)}, bf16[96,2048]{1,0:T(8,128)(2,1)}, bf16[96,2048]{1,0:T(8,128)(2,1)}, bf16[96,2048]{1,0:T(8,128)(2,1)}, b...) custom-call(f32[8,128]{1,0:T(8,128)} %copy-done.6, f32[8,128]{1,0:T(8,128)} %copy-done.7, ...), custom_call_target="tpu_custom_call" | custom-call | bytes 235405312 | tf_op jit(solution)/shard_map/pallas_call | solution.py:189
  17.1 1.9 %collective-permute-start.6 = (bf16[96,2048]{1,0:T(8,128)(2,1)}, bf16[96,2048]{1,0:T(8,128)(2,1)}, u32[]{:S(2)}, u32[]{:S(2)}) collective-permute-start(bf16[96,2048]{1,0:T(8,128)(2,1)} %get-tuple-element.91), channel_id=1, source_target_pairs={{0,2},{1,3},{2,0},{3,1},{4,6},{5,7},{6,4},{7,5},{8,10},{9,11},{10,... | collective-permute-start | bytes 1179656 | tf_op jit(solution)/shard_map/ppermute | solution.py:84
  19.1 1.5 %collective-permute-start.7 = (bf16[96,2048]{1,0:T(8,128)(2,1)}, bf16[96,2048]{1,0:T(8,128)(2,1)}, u32[]{:S(2)}, u32[]{:S(2)}) collective-permute-start(bf16[96,2048]{1,0:T(8,128)(2,1)} %get-tuple-element.92), channel_id=1, source_target_pairs={{0,4},{1,5},{2,6},{3,7},{4,0},{5,1},{6,2},{7,3},{8,12},{9,13},{10,... | collective-permute-start | bytes 1179656 | tf_op jit(solution)/shard_map/ppermute | solution.py:84
  20.6 2.1 %shard_map.86 = (bf16[96,2048]{1,0:T(8,128)(2,1)S(1)}, bf16[96,2048]{1,0:T(8,128)(2,1)S(1)}, bf16[96,2048]{1,0:T(8,128)(2,1)S(1)}, bf16[96,2048]{1,0:T(8,128)(2,1)S(1)}) custom-call(f32[8,8,128]{2,1,0:T(8,128)S(1)} %all-to-all-done.meta_ref, bf16[128,2048]{1,0:T(8,128)(2,1)S(1)} %slice_bitcast_fusion.refs_0_, bf16[128,2048]{1,0:T(8,128)(2,1)} %collective-permute-done.2.refs_1_), custom_call_target="tpu_custom_call" | custom-call | bytes 169869312 | tf_op jit(solution)/shard_map/pallas_call | solution.py:45
  24.7 1.3 %collective-permute-start.5 = (bf16[96,2048]{1,0:T(8,128)(2,1)S(1)}, bf16[96,2048]{1,0:T(8,128)(2,1)S(1)}, u32[]{:S(2)}, u32[]{:S(2)}) collective-permute-start(bf16[96,2048]{1,0:T(8,128)(2,1)S(1)} %get-tuple-element.99), channel_id=1, source_target_pairs={{0,5},{1,4},{2,7},{3,6},{4,1},{5,0},{6,3},{7,2},{8,13},{9,12},{10,... | collective-permute-start | bytes 1179656 | tf_op jit(solution)/shard_map/ppermute | solution.py:84
  25.9 1.0 copy-done.2
  27.0 2.1 %shard_map.89 = (bf16[96,2048]{1,0:T(8,128)(2,1)S(1)}, bf16[96,2048]{1,0:T(8,128)(2,1)S(1)}, bf16[96,2048]{1,0:T(8,128)(2,1)S(1)}, bf16[96,2048]{1,0:T(8,128)(2,1)S(1)}) custom-call(f32[8,8,128]{2,1,0:T(8,128)S(1)} %all-to-all-done.meta_ref, bf16[128,2048]{1,0:T(8,128)(2,1)S(1)} %bitcast.33, bf16[128,2048]{1,0:T(8,128)(2,1)} %collective-permute-done.8.refs_1_), custom_call_target="tpu_custom_call" | custom-call | bytes 169869312 | tf_op jit(solution)/shard_map/pallas_call | solution.py:45
  29.1 1.5 %collective-permute-start.10 = (bf16[96,2048]{1,0:T(8,128)(2,1)S(1)}, bf16[96,2048]{1,0:T(8,128)(2,1)S(1)}, u32[]{:S(2)}, u32[]{:S(2)}) collective-permute-start(bf16[96,2048]{1,0:T(8,128)(2,1)S(1)} %get-tuple-element.110), channel_id=1, source_target_pairs={{0,2},{1,3},{2,0},{3,1},{4,6},{5,7},{6,4},{7,5},{8,10},{9,11},{10,... | collective-permute-start | bytes 1179656 | tf_op jit(solution)/shard_map/ppermute | solution.py:84
  30.6 0.8 collective-permute-done.7.refs_2_
  31.6 8.1 %collective-permute-done.4.refs_2_ = bf16[96,2048]{1,0:T(8,128)(2,1)S(1)} collective-permute-done((bf16[96,2048]{1,0:T(8,128)(2,1)S(1)}, bf16[96,2048]{1,0:T(8,128)(2,1)S(1)}, u32[]{:S(2)}, u32[]{:S(2)}) %collective-permute-start.4) | collective-permute-done | bytes 393248 | tf_op jit(solution)/shard_map/ppermute | solution.py:84
  39.7 6.3 %collective-permute-done.5.refs_3_ = bf16[96,2048]{1,0:T(8,128)(2,1)S(1)} collective-permute-done((bf16[96,2048]{1,0:T(8,128)(2,1)S(1)}, bf16[96,2048]{1,0:T(8,128)(2,1)S(1)}, u32[]{:S(2)}, u32[]{:S(2)}) %collective-permute-start.5) | collective-permute-done | bytes 393248 | tf_op jit(solution)/shard_map/ppermute | solution.py:84
  46.1 1.8 %shard_map.87 = (bf16[384,2048]{1,0:T(8,128)(2,1)S(1)}, bf16[384,768]{1,0:T(8,128)(2,1)S(1)}, f32[384,704]{1,0:T(8,128)S(1)}) custom-call(bf16[704,2048]{1,0:T(8,128)(2,1)S(1)} %bitcast.26, bf16[96,2048]{1,0:T(8,128)(2,1)S(1)} %get-tuple-element.100.refs_0_, bf16[96,2048]{1,0:T(8,128)(2,1)S(1)} %collective-permute-done.3.refs_1_, ...), custom_call_target="tpu_custom_call" | custom-call | bytes 492830720 | tf_op jit(solution)/shard_map/pallas_call | solution.py:45
  48.2 1.1 collective-permute-start.12
  49.3 3.2 %shard_map.90 = (bf16[384,2048]{1,0:T(8,128)(2,1)S(1)}, bf16[384,768]{1,0:T(8,128)(2,1)S(1)}, bf16[384,256]{1,0:T(8,128)(2,1)S(1)}, bf16[96,1024]{1,0:T(8,128)(2...) custom-call(bf16[704,2048]{1,0:T(8,128)(2,1)S(1)} %bitcast.27, ...), custom_call_target="tpu_custom_call" | custom-call | bytes 834666496 | tf_op jit(solution)/shard_map/pallas_call | solution.py:45
  52.6 1.5 %collective-permute-start.13 = (bf16[96,1024]{1,0:T(8,128)(2,1)S(1)}, bf16[96,1024]{1,0:T(8,128)(2,1)S(1)}, u32[]{:S(2)}, u32[]{:S(2)}) collective-permute-start(bf16[96,1024]{1,0:T(8,128)(2,1)S(1)} %get-tuple-element.120), channel_id=1, source_target_pairs={{0,2},{1,3},{2,0},{3,1},{4,6},{5,7},{6,4},{7,5},{8,10},{9,11},{10,... | collective-permute-start | bytes 589832 | tf_op jit(solution)/shard_map/ppermute | solution.py:84
  54.1 0.9 collective-permute-start.14
  55.0 1.1 collective-permute-start.15
  56.2 0.9 shard_map.92
  57.0 1.5 %collective-permute-start.18 = (bf16[96,1024]{1,0:T(8,128)(2,1)S(1)}, bf16[96,1024]{1,0:T(8,128)(2,1)S(1)}, u32[]{:S(2)}, u32[]{:S(2)}) collective-permute-start(bf16[96,1024]{1,0:T(8,128)(2,1)S(1)} %get-tuple-element.133), channel_id=1, source_target_pairs={{0,2},{1,3},{2,0},{3,1},{4,6},{5,7},{6,4},{7,5},{8,10},{9,11},{10,... | collective-permute-start | bytes 589832 | tf_op jit(solution)/shard_map/ppermute | solution.py:84
  58.6 2.1 %shard_map.91._ = bf16[44,384,2048]{2,1,0:T(8,128)(2,1)} custom-call(bf16[384,2048]{1,0:T(8,128)(2,1)S(1)} %get-tuple-element.104.refs_0_, bf16[384,2048]{1,0:T(8,128)(2,1)S(1)} %get-tuple-element.113.refs_1_, bf16[384,768]{1,0:T(8,128)(2,1)S(1)} %get-tuple-element.105.hid_ref.refs_2_, ...), custom_call_target="tpu_custom_call", output_to_operand_aliasing={{}: (5, {})} | custom-call | tf_op jit(solution)/shard_map/pallas_call | solution.py:414
  60.7 1.0 collective-permute-start.19
  61.7 1.1 collective-permute-start.20
  62.8 2.9 %collective-permute-done.14.refs_2_ = bf16[96,1024]{1,0:T(8,128)(2,1)S(1)} collective-permute-done((bf16[96,1024]{1,0:T(8,128)(2,1)S(1)}, bf16[96,1024]{1,0:T(8,128)(2,1)S(1)}, u32[]{:S(2)}, u32[]{:S(2)}) %collective-permute-start.14) | collective-permute-done | bytes 196640 | tf_op jit(solution)/shard_map/ppermute | solution.py:84
  66.1 1.5 %collective-permute-done.16.refs_0_ = bf16[128,1024]{1,0:T(8,128)(2,1)S(1)} collective-permute-done((bf16[128,1024]{1,0:T(8,128)(2,1)S(1)}, bf16[128,1024]{1,0:T(8,128)(2,1)S(1)}, u32[]{:S(2)}, u32[]{:S(2)}) %collective-permute-start.16) | collective-permute-done | bytes 262176 | tf_op jit(solution)/shard_map/ppermute | solution.py:84
  67.6 1.3 %collective-permute-start.23 = (bf16[128,1024]{1,0:T(8,128)(2,1)S(1)}, bf16[128,1024]{1,0:T(8,128)(2,1)S(1)}, u32[]{:S(2)}, u32[]{:S(2)}) collective-permute-start(bf16[128,1024]{1,0:T(8,128)(2,1)S(1)} %shard_map.95), channel_id=1, source_target_pairs={{8,0},{16,8},{24,16},{9,1},{17,9},{25,17},{10,2},{18,10},{26,18},{... | collective-permute-start | bytes 786440 | tf_op jit(solution)/shard_map/ppermute | solution.py:656
  69.2 4.7 %collective-permute-done.19.refs_2_ = bf16[96,1024]{1,0:T(8,128)(2,1)S(1)} collective-permute-done((bf16[96,1024]{1,0:T(8,128)(2,1)S(1)}, bf16[96,1024]{1,0:T(8,128)(2,1)S(1)}, u32[]{:S(2)}, u32[]{:S(2)}) %collective-permute-start.19) | collective-permute-done | bytes 196640 | tf_op jit(solution)/shard_map/ppermute | solution.py:84
  74.4 1.3 %collective-permute-start.17 = (bf16[96,1024]{1,0:T(8,128)(2,1)}, bf16[96,1024]{1,0:T(8,128)(2,1)}, u32[]{:S(2)}, u32[]{:S(2)}) collective-permute-start(bf16[96,1024]{1,0:T(8,128)(2,1)} %get-tuple-element.129), channel_id=1, source_target_pairs={{0,6},{1,7},{2,4},{3,5},{4,2},{5,3},{6,0},{7,1},{8,14},{9,15},{10,... | collective-permute-start | bytes 589832 | tf_op jit(solution)/shard_map/ppermute | solution.py:84
  75.9 1.5 %collective-permute-start.22 = (bf16[128,1024]{1,0:T(8,128)(2,1)S(1)}, bf16[128,1024]{1,0:T(8,128)(2,1)S(1)}, u32[]{:S(2)}, u32[]{:S(2)}) collective-permute-start(bf16[128,1024]{1,0:T(8,128)(2,1)S(1)} %shard_map.98), channel_id=1, source_target_pairs={{8,0},{16,8},{24,16},{9,1},{17,9},{25,17},{10,2},{18,10},{26,18},{... | collective-permute-start | bytes 786440 | tf_op jit(solution)/shard_map/ppermute | solution.py:656
  78.1 1.3 %collective-permute-done.24.refs_0_ = bf16[128,1024]{1,0:T(8,128)(2,1)S(1)} collective-permute-done((bf16[128,1024]{1,0:T(8,128)(2,1)S(1)}, bf16[128,1024]{1,0:T(8,128)(2,1)S(1)}, u32[]{:S(2)}, u32[]{:S(2)}) %collective-permute-start.24) | collective-permute-done | bytes 262176 | tf_op jit(solution)/shard_map/ppermute | solution.py:84
  79.7 0.9 collective-permute-start.26
  80.6 1.1 %collective-permute-start.27 = (bf16[96,1024]{1,0:T(8,128)(2,1)S(1)}, bf16[96,1024]{1,0:T(8,128)(2,1)S(1)}, u32[]{:S(2)}, u32[]{:S(2)}) collective-permute-start(bf16[96,1024]{1,0:T(8,128)(2,1)S(1)} %get-tuple-element.145), channel_id=1, source_target_pairs={{0,4},{1,5},{2,6},{3,7},{4,0},{5,1},{6,2},{7,3},{8,12},{9,13},{10,... | collective-permute-start | bytes 589832 | tf_op jit(solution)/shard_map/ppermute | solution.py:84
  81.7 1.5 %collective-permute-start.28 = (bf16[96,1024]{1,0:T(8,128)(2,1)S(1)}, bf16[96,1024]{1,0:T(8,128)(2,1)S(1)}, u32[]{:S(2)}, u32[]{:S(2)}) collective-permute-start(bf16[96,1024]{1,0:T(8,128)(2,1)S(1)} %get-tuple-element.146), channel_id=1, source_target_pairs={{0,6},{1,7},{2,4},{3,5},{4,2},{5,3},{6,0},{7,1},{8,14},{9,15},{10,... | collective-permute-start | bytes 589832 | tf_op jit(solution)/shard_map/ppermute | solution.py:84
  83.2 2.9 %collective-permute-done.22.raw_ref = bf16[128,1024]{1,0:T(8,128)(2,1)S(1)} collective-permute-done((bf16[128,1024]{1,0:T(8,128)(2,1)S(1)}, bf16[128,1024]{1,0:T(8,128)(2,1)S(1)}, u32[]{:S(2)}, u32[]{:S(2)}) %collective-permute-start.22) | collective-permute-done | bytes 262176 | tf_op jit(solution)/shard_map/ppermute | solution.py:656
  86.4 1.3 %collective-permute-done.25.refs_0_ = bf16[128,1024]{1,0:T(8,128)(2,1)S(1)} collective-permute-done((bf16[128,1024]{1,0:T(8,128)(2,1)S(1)}, bf16[128,1024]{1,0:T(8,128)(2,1)S(1)}, u32[]{:S(2)}, u32[]{:S(2)}) %collective-permute-start.25) | collective-permute-done | bytes 262176 | tf_op jit(solution)/shard_map/ppermute | solution.py:84
  87.9 1.1 collective-permute-start.29
  89.1 1.1 collective-permute-start.30
  90.2 1.3 %collective-permute-start.31 = (bf16[96,1024]{1,0:T(8,128)(2,1)S(1)}, bf16[96,1024]{1,0:T(8,128)(2,1)S(1)}, u32[]{:S(2)}, u32[]{:S(2)}) collective-permute-start(bf16[96,1024]{1,0:T(8,128)(2,1)S(1)} %get-tuple-element.151), channel_id=1, source_target_pairs={{0,6},{1,7},{2,4},{3,5},{4,2},{5,3},{6,0},{7,1},{8,14},{9,15},{10,... | collective-permute-start | bytes 589832 | tf_op jit(solution)/shard_map/ppermute | solution.py:84
  91.5 3.8 %shard_map.103 = (bf16[44,384,2048]{2,1,0:T(8,128)(2,1)}, bf16[384,704]{1,0:T(8,128)(2,1)S(1)}, f32[384,704]{1,0:T(8,128)S(1)}) custom-call(bf16[704,2048]{1,0:T(8,128)(2,1)S(1)} %bitcast.28, bf16[44,384,2048]{2,1,0:T(8,128)(2,1)} %shard_map.91._, bf16[96,2048]{1,0:T(8,128)(2,1)S(1)} %copy-done.3, ...), custom_call_target="tpu_custom_call", output_to_operand_aliasing={{0}: (1, {})} | custom-call | bytes 9247391744 | tf_op jit(solution)/shard_map/pallas_call | solution.py:45
  95.4 4.4 %shard_map.104 = (f32[384,704]{1,0:T(8,128)S(1)}, bf16[704,2048]{1,0:T(8,128)(2,1)}) custom-call(bf16[704,2048]{1,0:T(8,128)(2,1)S(1)} %bitcast.30, bf16[384,704]{1,0:T(8,128)(2,1)S(1)} %get-tuple-element.157.hid1_ref.hid_ref, bf16[44,384,2048]{2,1,0:T(8,128)(2,1)} %get-tuple-element.158.pad_ref, bf16[96,1024]{1,0:T(8,128)(2,1)S(1)} %get-tuple-element.143.refs_0_, ...), custom_call_target="tpu_custom_call" | custom-call | bytes 523239424 | tf_op jit(solution)/shard_map/pallas_call | solution.py:452
  100.0 2.4 %shard_map.105 = (bf16[384,1024]{1,0:T(8,128)(2,1)S(1)}, bf16[384,768]{1,0:T(8,128)(2,1)S(1)}, bf16[384,128]{1,0:T(8,128)(2,1)}) custom-call(bf16[704,2048]{1,0:T(8,128)(2,1)S(1)} %bitcast.31, bf16[384,704]{1,0:T(8,128)(2,1)S(1)} %get-tuple-element.157.hid1_ref.hid_ref, f32[384,704]{1,0:T(8,128)S(1)} %get-tuple-element.160.slope_ref, ...), custom_call_target="tpu_custom_call" | custom-call | bytes 4931452928 | tf_op jit(solution)/shard_map/pallas_call | solution.py:45
  102.4 3.4 %all-to-all-start.1 = ((bf16[8,48,128]{2,1,0:T(8,128)(2,1)}), bf16[8,48,128]{2,1,0:T(8,128)(2,1)S(1)}, u32[]{:S(2)}, u32[]{:S(2)}) async-start(bf16[8,48,128]{2,1,0:T(8,128)(2,1)} %bitcast.13), calls=%async_computation.1 | async-start | bytes 196608 | tf_op jit(solution)/shard_map/all_to_all | solution.py:293
  105.8 6.8 %shard_map.106 = (bf16[704,2048]{1,0:T(8,128)(2,1)}, bf16[704,2048]{1,0:T(8,128)(2,1)}) custom-call(bf16[704,2048]{1,0:T(8,128)(2,1)} %get-tuple-element.159._, bf16[44,384,2048]{2,1,0:T(8,128)(2,1)} %get-tuple-element.158.pad_ref, bf16[384,1024]{1,0:T(8,128)(2,1)S(1)} %get-tuple-element.166.g1_ref, ...), custom_call_target="tpu_custom_call", output_to_operand_aliasing={{1}: (0, {})} | custom-call | bytes 369098752 | tf_op jit(solution)/shard_map/pallas_call | solution.py:528
  112.7 0.9 shard_map.107
  (66 shorter events, 9.1 us)
Async XLA Ops:
  0.6 45.4 %copy-start = (bf16[1,1,704,2048]{3,2,1,0:T(8,128)(2,1)S(1)}, bf16[1,1,704,2048]{3,2,1,0:T(8,128)(2,1)}, u32[]{:S(2)}) copy-start(bf16[1,1,704,2048]{3,2,1,0:T(8,128)(2,1)} %param.8) | copy-start | bytes 8650756
  0.6 12.4 %collective-permute-start.1 = (bf16[2,128,2048]{2,1,0:T(8,128)(2,1)}, bf16[2,128,2048]{2,1,0:T(8,128)(2,1)}, u32[]{:S(2)}, u32[]{:S(2)}) collective-permute-start(bf16[2,128,2048]{2,1,0:T(8,128)(2,1)} %bitcast.38), channel_id=1, source_target_pairs={{0,1},{1,0},{2,3},{3,2},{4,5},{5,4},{6,7},{7,6},{8,9},{9,8},{10,11... | collective-permute-start | bytes 3145736 | tf_op jit(solution)/shard_map/ppermute | solution.py:84
  2.5 18.1 %collective-permute-start.2 = (bf16[128,2048]{1,0:T(8,128)(2,1)S(1)}, bf16[128,2048]{1,0:T(8,128)(2,1)}, u32[]{:S(2)}, u32[]{:S(2)}) collective-permute-start(bf16[128,2048]{1,0:T(8,128)(2,1)S(1)} %slice_bitcast_fusion.refs_0_), channel_id=1, source_target_pairs={{0,2},{1,3},{2,0},{3,1},{4,6},{5,7},{6,4},{7,5},{8,10},{9,11},{10,... | collective-permute-start | bytes 1572872 | tf_op jit(solution)/shard_map/ppermute | solution.py:84
  5.0 19.7 %collective-permute-start.8 = (bf16[128,2048]{1,0:T(8,128)(2,1)}, bf16[128,2048]{1,0:T(8,128)(2,1)}, u32[]{:S(2)}, u32[]{:S(2)}) collective-permute-start(bf16[128,2048]{1,0:T(8,128)(2,1)} %bitcast.32), channel_id=1, source_target_pairs={{0,4},{1,5},{2,6},{3,7},{4,0},{5,1},{6,2},{7,3},{8,12},{9,13},{10,... | collective-permute-start | bytes 1572872 | tf_op jit(solution)/shard_map/ppermute | solution.py:84
  7.9 5.2 %copy-start.6 = (f32[8,128]{1,0:T(8,128)}, f32[8,128]{1,0:T(8,128)S(1)}, u32[]{:S(2)}) copy-start(f32[8,128]{1,0:T(8,128)S(1)} %pad_maximum_fusion.refs_0_) | copy-start | bytes 12292
  8.5 12.1 %all-to-all-start = ((f32[8,8,128]{2,1,0:T(8,128)}), f32[8,8,128]{2,1,0:T(8,128)S(1)}, u32[]{:S(2)}, u32[]{:S(2)}) async-start(f32[8,8,128]{2,1,0:T(8,128)} %broadcast_in_dim.15), calls=%async_computation | async-start | bytes 65536 | tf_op jit(solution)/shard_map/all_to_all | solution.py:579
  11.8 1.2 %collective-permute-start = (f32[8,128]{1,0:T(8,128)S(1)}, f32[8,128]{1,0:T(8,128)S(1)}, u32[]{:S(2)}, u32[]{:S(2)}) collective-permute-start(f32[8,128]{1,0:T(8,128)S(1)} %pad_maximum_fusion.refs_0_), channel_id=1, source_target_pairs={{0,1},{1,0},{2,3},{3,2},{4,5},{5,4},{6,7},{7,6},{8,9},{9,8},{10,11... | collective-permute-start | bytes 12296 | tf_op jit(solution)/shard_map/ppermute | solution.py:84
  13.0 0.6 copy-start.7
  17.1 11.9 %collective-permute-start.6 = (bf16[96,2048]{1,0:T(8,128)(2,1)}, bf16[96,2048]{1,0:T(8,128)(2,1)}, u32[]{:S(2)}, u32[]{:S(2)}) collective-permute-start(bf16[96,2048]{1,0:T(8,128)(2,1)} %get-tuple-element.91), channel_id=1, source_target_pairs={{0,2},{1,3},{2,0},{3,1},{4,6},{5,7},{6,4},{7,5},{8,10},{9,11},{10,... | collective-permute-start | bytes 1179656 | tf_op jit(solution)/shard_map/ppermute | solution.py:84
  19.1 12.3 %collective-permute-start.7 = (bf16[96,2048]{1,0:T(8,128)(2,1)}, bf16[96,2048]{1,0:T(8,128)(2,1)}, u32[]{:S(2)}, u32[]{:S(2)}) collective-permute-start(bf16[96,2048]{1,0:T(8,128)(2,1)} %get-tuple-element.92), channel_id=1, source_target_pairs={{0,4},{1,5},{2,6},{3,7},{4,0},{5,1},{6,2},{7,3},{8,12},{9,13},{10,... | collective-permute-start | bytes 1179656 | tf_op jit(solution)/shard_map/ppermute | solution.py:84
  20.6 27.7 %copy-start.8 = (bf16[96,1024]{1,0:T(8,128)(2,1)S(1)}, bf16[96,1024]{1,0:T(8,128)(2,1)}, u32[]{:S(2)}) copy-start(bf16[96,1024]{1,0:T(8,128)(2,1)} %get-tuple-element.117) | copy-start | bytes 589828
  22.7 26.6 %copy-start.1 = (bf16[1,1,704,2048]{3,2,1,0:T(8,128)(2,1)S(1)}, bf16[1,1,704,2048]{3,2,1,0:T(8,128)(2,1)}, u32[]{:S(2)}) copy-start(bf16[1,1,704,2048]{3,2,1,0:T(8,128)(2,1)} %param.9) | copy-start | bytes 8650756
  22.7 8.7 %collective-permute-start.3 = (bf16[96,2048]{1,0:T(8,128)(2,1)S(1)}, bf16[96,2048]{1,0:T(8,128)(2,1)S(1)}, u32[]{:S(2)}, u32[]{:S(2)}) collective-permute-start(bf16[96,2048]{1,0:T(8,128)(2,1)S(1)} %get-tuple-element.97), channel_id=1, source_target_pairs={{0,1},{1,0},{2,3},{3,2},{4,5},{5,4},{6,7},{7,6},{8,9},{9,8},{10,11... | collective-permute-start | bytes 1179656 | tf_op jit(solution)/shard_map/ppermute | solution.py:84
  23.4 0.6 copy-start.4
  24.1 15.7 %collective-permute-start.4 = (bf16[96,2048]{1,0:T(8,128)(2,1)S(1)}, bf16[96,2048]{1,0:T(8,128)(2,1)S(1)}, u32[]{:S(2)}, u32[]{:S(2)}) collective-permute-start(bf16[96,2048]{1,0:T(8,128)(2,1)S(1)} %get-tuple-element.98), channel_id=1, source_target_pairs={{0,4},{1,5},{2,6},{3,7},{4,0},{5,1},{6,2},{7,3},{8,12},{9,13},{10,... | collective-permute-start | bytes 1179656 | tf_op jit(solution)/shard_map/ppermute | solution.py:84
  24.7 21.4 %collective-permute-start.5 = (bf16[96,2048]{1,0:T(8,128)(2,1)S(1)}, bf16[96,2048]{1,0:T(8,128)(2,1)S(1)}, u32[]{:S(2)}, u32[]{:S(2)}) collective-permute-start(bf16[96,2048]{1,0:T(8,128)(2,1)S(1)} %get-tuple-element.99), channel_id=1, source_target_pairs={{0,5},{1,4},{2,7},{3,6},{4,1},{5,0},{6,3},{7,2},{8,13},{9,12},{10,... | collective-permute-start | bytes 1179656 | tf_op jit(solution)/shard_map/ppermute | solution.py:84
  25.9 1.0 copy-start.2
  29.1 18.8 %collective-permute-start.10 = (bf16[96,2048]{1,0:T(8,128)(2,1)S(1)}, bf16[96,2048]{1,0:T(8,128)(2,1)S(1)}, u32[]{:S(2)}, u32[]{:S(2)}) collective-permute-start(bf16[96,2048]{1,0:T(8,128)(2,1)S(1)} %get-tuple-element.110), channel_id=1, source_target_pairs={{0,2},{1,3},{2,0},{3,1},{4,6},{5,7},{6,4},{7,5},{8,10},{9,11},{10,... | collective-permute-start | bytes 1179656 | tf_op jit(solution)/shard_map/ppermute | solution.py:84
  31.4 16.5 %collective-permute-start.9 = (bf16[96,2048]{1,0:T(8,128)(2,1)S(1)}, bf16[96,2048]{1,0:T(8,128)(2,1)S(1)}, u32[]{:S(2)}, u32[]{:S(2)}) collective-permute-start(bf16[96,2048]{1,0:T(8,128)(2,1)S(1)} %get-tuple-element.109), channel_id=1, source_target_pairs={{0,1},{1,0},{2,3},{3,2},{4,5},{5,4},{6,7},{7,6},{8,9},{9,8},{10,11... | collective-permute-start | bytes 1179656 | tf_op jit(solution)/shard_map/ppermute | solution.py:84
  31.4 16.8 %collective-permute-start.11 = (bf16[96,2048]{1,0:T(8,128)(2,1)S(1)}, bf16[96,2048]{1,0:T(8,128)(2,1)S(1)}, u32[]{:S(2)}, u32[]{:S(2)}) collective-permute-start(bf16[96,2048]{1,0:T(8,128)(2,1)S(1)} %get-tuple-element.112), channel_id=1, source_target_pairs={{0,3},{1,2},{2,1},{3,0},{4,7},{5,6},{6,5},{7,4},{8,11},{9,10},{10,... | collective-permute-start | bytes 1179656 | tf_op jit(solution)/shard_map/ppermute | solution.py:84
  48.2 12.5 %collective-permute-start.12 = (bf16[96,1024]{1,0:T(8,128)(2,1)S(1)}, bf16[96,1024]{1,0:T(8,128)(2,1)S(1)}, u32[]{:S(2)}, u32[]{:S(2)}) collective-permute-start(bf16[96,1024]{1,0:T(8,128)(2,1)S(1)} %copy-done.8), channel_id=1, source_target_pairs={{0,6},{1,7},{2,4},{3,5},{4,2},{5,3},{6,0},{7,1},{8,14},{9,15},{10,... | collective-permute-start | bytes 589832 | tf_op jit(solution)/shard_map/ppermute | solution.py:84
  52.6 9.1 %collective-permute-start.13 = (bf16[96,1024]{1,0:T(8,128)(2,1)S(1)}, bf16[96,1024]{1,0:T(8,128)(2,1)S(1)}, u32[]{:S(2)}, u32[]{:S(2)}) collective-permute-start(bf16[96,1024]{1,0:T(8,128)(2,1)S(1)} %get-tuple-element.120), channel_id=1, source_target_pairs={{0,2},{1,3},{2,0},{3,1},{4,6},{5,7},{6,4},{7,5},{8,10},{9,11},{10,... | collective-permute-start | bytes 589832 | tf_op jit(solution)/shard_map/ppermute | solution.py:84
  54.1 11.5 %collective-permute-start.14 = (bf16[96,1024]{1,0:T(8,128)(2,1)S(1)}, bf16[96,1024]{1,0:T(8,128)(2,1)S(1)}, u32[]{:S(2)}, u32[]{:S(2)}) collective-permute-start(bf16[96,1024]{1,0:T(8,128)(2,1)S(1)} %get-tuple-element.121), channel_id=1, source_target_pairs={{0,4},{1,5},{2,6},{3,7},{4,0},{5,1},{6,2},{7,3},{8,12},{9,13},{10,... | collective-permute-start | bytes 589832 | tf_op jit(solution)/shard_map/ppermute | solution.py:84
  55.0 10.6 %collective-permute-start.15 = (bf16[96,1024]{1,0:T(8,128)(2,1)S(1)}, bf16[96,1024]{1,0:T(8,128)(2,1)S(1)}, u32[]{:S(2)}, u32[]{:S(2)}) collective-permute-start(bf16[96,1024]{1,0:T(8,128)(2,1)S(1)} %get-tuple-element.122), channel_id=1, source_target_pairs={{0,6},{1,7},{2,4},{3,5},{4,2},{5,3},{6,0},{7,1},{8,14},{9,15},{10,... | collective-permute-start | bytes 589832 | tf_op jit(solution)/shard_map/ppermute | solution.py:84
  57.0 12.2 %collective-permute-start.18 = (bf16[96,1024]{1,0:T(8,128)(2,1)S(1)}, bf16[96,1024]{1,0:T(8,128)(2,1)S(1)}, u32[]{:S(2)}, u32[]{:S(2)}) collective-permute-start(bf16[96,1024]{1,0:T(8,128)(2,1)S(1)} %get-tuple-element.133), channel_id=1, source_target_pairs={{0,2},{1,3},{2,0},{3,1},{4,6},{5,7},{6,4},{7,5},{8,10},{9,11},{10,... | collective-permute-start | bytes 589832 | tf_op jit(solution)/shard_map/ppermute | solution.py:84
  60.7 13.2 %collective-permute-start.19 = (bf16[96,1024]{1,0:T(8,128)(2,1)S(1)}, bf16[96,1024]{1,0:T(8,128)(2,1)S(1)}, u32[]{:S(2)}, u32[]{:S(2)}) collective-permute-start(bf16[96,1024]{1,0:T(8,128)(2,1)S(1)} %get-tuple-element.134), channel_id=1, source_target_pairs={{0,4},{1,5},{2,6},{3,7},{4,0},{5,1},{6,2},{7,3},{8,12},{9,13},{10,... | collective-permute-start | bytes 589832 | tf_op jit(solution)/shard_map/ppermute | solution.py:84
  61.7 12.3 %collective-permute-start.20 = (bf16[96,1024]{1,0:T(8,128)(2,1)S(1)}, bf16[96,1024]{1,0:T(8,128)(2,1)S(1)}, u32[]{:S(2)}, u32[]{:S(2)}) collective-permute-start(bf16[96,1024]{1,0:T(8,128)(2,1)S(1)} %get-tuple-element.135), channel_id=1, source_target_pairs={{0,6},{1,7},{2,4},{3,5},{4,2},{5,3},{6,0},{7,1},{8,14},{9,15},{10,... | collective-permute-start | bytes 589832 | tf_op jit(solution)/shard_map/ppermute | solution.py:84
  66.0 1.6 %collective-permute-start.16 = (bf16[128,1024]{1,0:T(8,128)(2,1)S(1)}, bf16[128,1024]{1,0:T(8,128)(2,1)S(1)}, u32[]{:S(2)}, u32[]{:S(2)}) collective-permute-start(bf16[128,1024]{1,0:T(8,128)(2,1)S(1)} %get-tuple-element.128), channel_id=1, source_target_pairs={{0,1},{1,0},{2,3},{3,2},{4,5},{5,4},{6,7},{7,6},{8,9},{9,8},{10,11... | collective-permute-start | bytes 786440 | tf_op jit(solution)/shard_map/ppermute | solution.py:84
  67.6 10.2 %collective-permute-start.23 = (bf16[128,1024]{1,0:T(8,128)(2,1)S(1)}, bf16[128,1024]{1,0:T(8,128)(2,1)S(1)}, u32[]{:S(2)}, u32[]{:S(2)}) collective-permute-start(bf16[128,1024]{1,0:T(8,128)(2,1)S(1)} %shard_map.95), channel_id=1, source_target_pairs={{8,0},{16,8},{24,16},{9,1},{17,9},{25,17},{10,2},{18,10},{26,18},{... | collective-permute-start | bytes 786440 | tf_op jit(solution)/shard_map/ppermute | solution.py:656
  74.3 1.6 %collective-permute-start.21 = (bf16[128,1024]{1,0:T(8,128)(2,1)S(1)}, bf16[128,1024]{1,0:T(8,128)(2,1)S(1)}, u32[]{:S(2)}, u32[]{:S(2)}) collective-permute-start(bf16[128,1024]{1,0:T(8,128)(2,1)S(1)} %get-tuple-element.141), channel_id=1, source_target_pairs={{0,1},{1,0},{2,3},{3,2},{4,5},{5,4},{6,7},{7,6},{8,9},{9,8},{10,11... | collective-permute-start | bytes 786440 | tf_op jit(solution)/shard_map/ppermute | solution.py:84
  74.4 14.7 %collective-permute-start.17 = (bf16[96,1024]{1,0:T(8,128)(2,1)}, bf16[96,1024]{1,0:T(8,128)(2,1)}, u32[]{:S(2)}, u32[]{:S(2)}) collective-permute-start(bf16[96,1024]{1,0:T(8,128)(2,1)} %get-tuple-element.129), channel_id=1, source_target_pairs={{0,6},{1,7},{2,4},{3,5},{4,2},{5,3},{6,0},{7,1},{8,14},{9,15},{10,... | collective-permute-start | bytes 589832 | tf_op jit(solution)/shard_map/ppermute | solution.py:84
  75.9 10.2 %collective-permute-start.22 = (bf16[128,1024]{1,0:T(8,128)(2,1)S(1)}, bf16[128,1024]{1,0:T(8,128)(2,1)S(1)}, u32[]{:S(2)}, u32[]{:S(2)}) collective-permute-start(bf16[128,1024]{1,0:T(8,128)(2,1)S(1)} %shard_map.98), channel_id=1, source_target_pairs={{8,0},{16,8},{24,16},{9,1},{17,9},{25,17},{10,2},{18,10},{26,18},{... | collective-permute-start | bytes 786440 | tf_op jit(solution)/shard_map/ppermute | solution.py:656
  77.9 1.5 %collective-permute-start.24 = (bf16[128,1024]{1,0:T(8,128)(2,1)S(1)}, bf16[128,1024]{1,0:T(8,128)(2,1)S(1)}, u32[]{:S(2)}, u32[]{:S(2)}) collective-permute-start(bf16[128,1024]{1,0:T(8,128)(2,1)S(1)} %collective-permute-done.23.raw_ref), channel_id=1, source_target_pairs={{0,1},{1,0},{2,3},{3,2},{4,5},{5,4},{6,7},{7,6},{8,9},{9,8},{10,11... | collective-permute-start | bytes 786440 | tf_op jit(solution)/shard_map/ppermute | solution.py:84
  79.7 10.5 %collective-permute-start.26 = (bf16[96,1024]{1,0:T(8,128)(2,1)S(1)}, bf16[96,1024]{1,0:T(8,128)(2,1)S(1)}, u32[]{:S(2)}, u32[]{:S(2)}) collective-permute-start(bf16[96,1024]{1,0:T(8,128)(2,1)S(1)} %get-tuple-element.144), channel_id=1, source_target_pairs={{0,2},{1,3},{2,0},{3,1},{4,6},{5,7},{6,4},{7,5},{8,10},{9,11},{10,... | collective-permute-start | bytes 589832 | tf_op jit(solution)/shard_map/ppermute | solution.py:84
  80.6 14.8 %collective-permute-start.27 = (bf16[96,1024]{1,0:T(8,128)(2,1)S(1)}, bf16[96,1024]{1,0:T(8,128)(2,1)S(1)}, u32[]{:S(2)}, u32[]{:S(2)}) collective-permute-start(bf16[96,1024]{1,0:T(8,128)(2,1)S(1)} %get-tuple-element.145), channel_id=1, source_target_pairs={{0,4},{1,5},{2,6},{3,7},{4,0},{5,1},{6,2},{7,3},{8,12},{9,13},{10,... | collective-permute-start | bytes 589832 | tf_op jit(solution)/shard_map/ppermute | solution.py:84
  81.7 13.6 %collective-permute-start.28 = (bf16[96,1024]{1,0:T(8,128)(2,1)S(1)}, bf16[96,1024]{1,0:T(8,128)(2,1)S(1)}, u32[]{:S(2)}, u32[]{:S(2)}) collective-permute-start(bf16[96,1024]{1,0:T(8,128)(2,1)S(1)} %get-tuple-element.146), channel_id=1, source_target_pairs={{0,6},{1,7},{2,4},{3,5},{4,2},{5,3},{6,0},{7,1},{8,14},{9,15},{10,... | collective-permute-start | bytes 589832 | tf_op jit(solution)/shard_map/ppermute | solution.py:84
  86.2 1.5 %collective-permute-start.25 = (bf16[128,1024]{1,0:T(8,128)(2,1)S(1)}, bf16[128,1024]{1,0:T(8,128)(2,1)S(1)}, u32[]{:S(2)}, u32[]{:S(2)}) collective-permute-start(bf16[128,1024]{1,0:T(8,128)(2,1)S(1)} %collective-permute-done.22.raw_ref), channel_id=1, source_target_pairs={{0,1},{1,0},{2,3},{3,2},{4,5},{5,4},{6,7},{7,6},{8,9},{9,8},{10,11... | collective-permute-start | bytes 786440 | tf_op jit(solution)/shard_map/ppermute | solution.py:84
  86.2 5.4 %copy-start.3 = (bf16[96,2048]{1,0:T(8,128)(2,1)S(1)}, bf16[96,2048]{1,0:T(8,128)(2,1)}, u32[]{:S(2)}) copy-start(bf16[96,2048]{1,0:T(8,128)(2,1)} %get-tuple-element.152.refs_0_) | copy-start | bytes 1179652
  87.9 11.9 %collective-permute-start.29 = (bf16[96,1024]{1,0:T(8,128)(2,1)S(1)}, bf16[96,1024]{1,0:T(8,128)(2,1)S(1)}, u32[]{:S(2)}, u32[]{:S(2)}) collective-permute-start(bf16[96,1024]{1,0:T(8,128)(2,1)S(1)} %get-tuple-element.149), channel_id=1, source_target_pairs={{0,2},{1,3},{2,0},{3,1},{4,6},{5,7},{6,4},{7,5},{8,10},{9,11},{10,... | collective-permute-start | bytes 589832 | tf_op jit(solution)/shard_map/ppermute | solution.py:84
  89.1 10.9 %collective-permute-start.30 = (bf16[96,1024]{1,0:T(8,128)(2,1)S(1)}, bf16[96,1024]{1,0:T(8,128)(2,1)S(1)}, u32[]{:S(2)}, u32[]{:S(2)}) collective-permute-start(bf16[96,1024]{1,0:T(8,128)(2,1)S(1)} %get-tuple-element.150), channel_id=1, source_target_pairs={{0,4},{1,5},{2,6},{3,7},{4,0},{5,1},{6,2},{7,3},{8,12},{9,13},{10,... | collective-permute-start | bytes 589832 | tf_op jit(solution)/shard_map/ppermute | solution.py:84
  90.2 9.8 %collective-permute-start.31 = (bf16[96,1024]{1,0:T(8,128)(2,1)S(1)}, bf16[96,1024]{1,0:T(8,128)(2,1)S(1)}, u32[]{:S(2)}, u32[]{:S(2)}) collective-permute-start(bf16[96,1024]{1,0:T(8,128)(2,1)S(1)} %get-tuple-element.151), channel_id=1, source_target_pairs={{0,6},{1,7},{2,4},{3,5},{4,2},{5,3},{6,0},{7,1},{8,14},{9,15},{10,... | collective-permute-start | bytes 589832 | tf_op jit(solution)/shard_map/ppermute | solution.py:84
  102.4 10.2 %all-to-all-start.1 = ((bf16[8,48,128]{2,1,0:T(8,128)(2,1)}), bf16[8,48,128]{2,1,0:T(8,128)(2,1)S(1)}, u32[]{:S(2)}, u32[]{:S(2)}) async-start(bf16[8,48,128]{2,1,0:T(8,128)(2,1)} %bitcast.13), calls=%async_computation.1 | async-start | bytes 196608 | tf_op jit(solution)/shard_map/all_to_all | solution.py:293
  105.8 6.9 %copy-start.5 = (bf16[384,128]{1,0:T(8,128)(2,1)S(1)}, bf16[384,128]{1,0:T(8,128)(2,1)}, u32[]{:S(2)}) copy-start(bf16[384,128]{1,0:T(8,128)(2,1)} %copy-done.4) | copy-start | bytes 294916

commit v10 on v9

--- a/solution.py
+++ b/solution.py
@@ -428,14 +428,15 @@
 
 
 def early_kernel(plane, capacity, groups, wout_ref, hid1_ref, pad_ref, *refs):
-    pulled_ref, gout_ref, g, g0, hid0, cols, sem = refs[-7:]
+    pulled_ref, gout_ref, cols_ref, g, g0, hid0, cols, sem = refs[-8:]
     units, copies = wout_ref.shape[0], Copies(sem)
     copies.start(plate(pad_ref, G0, g0.shape[1]), g0)
     copies.start(plate(pad_ref, HID0, hid0.shape[1]), hid0)
     copies.start(plate(pad_ref, COLS, cols.shape[1]), cols)
-    arrange(plane, capacity, groups, refs[:-7], g)
+    arrange(plane, capacity, groups, refs[:-8], g)
     pulled_ref[...] = dot(g[...], wout_ref[...], 1, 1)
     copies.wait()
+    cols_ref[...] = cols[...]
     y = jnp.concatenate([weighted(cols, 0, g0[...]), weighted(cols, 1, g[...])], axis=0)
     hid = jnp.concatenate([hid0[:, :units], hid1_ref[...]], axis=0)
     gout_ref[...] = dot(hid, y, 0, 0).astype(bf16)
@@ -446,7 +447,7 @@
     features = w_out.shape[1]
     width = features // HALVES
     args = (w_out, hid1, *pieces)
-    outs = [shaped((rows, units), f32), shaped((units, features), bf16)]
+    outs = [shaped((rows, units), f32), shaped((units, features), bf16), shaped((rows, 2 * LANES), bf16)]
     whole = lambda a: pl.BlockSpec(a.shape, lambda i: (0, 0))
     first = lambda a: pl.BlockSpec((a.shape[0], width), lambda i: (0, 0))
     return pl.pallas_call(
@@ -454,7 +455,7 @@
         grid=(1,),
         out_shape=outs,
         in_specs=[first(w_out), whole(hid1), in_hbm(pad)] + [whole(p) for p in pieces],
-        out_specs=[whole(outs[0]), first(outs[1])],
+        out_specs=[whole(outs[0]), first(outs[1]), whole(outs[2])],
         scratch_shapes=[pltpu.VMEM((rows, n), bf16) for n in (width, width, lanes_of(units), 2 * LANES)]
         + [pltpu.SemaphoreType.DMA((3,))],
         compiler_params=pltpu.CompilerParams(vmem_limit_bytes=VMEM_LIMIT),
@@ -462,13 +463,11 @@
     )(w_out, hid1, pad, *pieces)
 
 
-def second_kernel(plane, capacity, groups, first, wout_ref, hid_ref, slope_ref, pulled_ref, pad_ref, *refs):
-    g_ref, gp_ref, score_ref, cols, sem = refs[-5:]
-    units, copies = wout_ref.shape[0], Copies(sem)
-    copies.start(plate(pad_ref, COLS, cols.shape[1]), cols)
-    arrange(plane, capacity, groups, refs[:-5], g_ref)
+def second_kernel(plane, capacity, groups, first, wout_ref, hid_ref, slope_ref, pulled_ref, cols, *refs):
+    g_ref, gp_ref, score_ref = refs[-3:]
+    units = wout_ref.shape[0]
+    arrange(plane, capacity, groups, refs[:-3], g_ref)
     pulled = pulled_ref[...] + dot(g_ref[...], wout_ref[:, first:], 1, 1)
-    copies.wait()
     gp_ref[:, :units] = (cols[:, 1:2].astype(f32) * pulled * slope_ref[...]).astype(bf16)
     score = jnp.sum(hid_ref[...].astype(f32) * pulled, axis=1, keepdims=True)
     lane = lax.broadcasted_iota(jnp.int32, score_ref.shape, 1)
@@ -664,13 +663,12 @@
         parts.append((pieces, [(0, layout)]))
     x1 = behind(x1, after)
     pad, hid1, slope1 = preact(plane, capacity, x1_groups, (X1, HID1), w_in, pad, *x1)
-    pulled, gout = early(plane, capacity, parts[0][1], w_out, hid1, pad, *parts[0][0])
+    pulled, gout, cols = early(plane, capacity, parts[0][1], w_out, hid1, pad, *parts[0][0])
     pieces = behind(parts[1][0], [pulled])
     g1, gp1, scores = call(
         functools.partial(second_kernel, plane, capacity, parts[1][1], half),
         [shaped((rows, half), bf16), shaped((rows, wide), bf16), shaped((rows, LANES), bf16)],
-        w_out, hid1, slope1, pulled, pad, *pieces, flops=matmul // 2, pad=4,
-        scratch=[vmem(2 * LANES), pltpu.SemaphoreType.DMA((1,))],
+        w_out, hid1, slope1, pulled, cols, *pieces, flops=matmul // 2,
     )
     scores = exchange(scores, experts)
     grad_in, grad_out = late(features // TILES, gout, pad, g1, gp1)

time: 114 us -> 113 us (level)
  transfers between devices with their start and end apart: 34 -> 34, of which waited for: 15 -> 14; matrix products, arithmetic and copies ran while one was open for 3% -> 3% of each run, Pallas kernels for 29% -> 30%
where the time goes in v10:
time: 113 us
  starting transfers between devices  38.3 us (34%)
  Pallas kernels  35.9 us (32%)
  waiting for transfers between devices  31.9 us (28%)
  local copies, waits for them, and re-layouts  4.22 us (4%)
  other arithmetic  1.37 us (1%)
    ppermute x30, starting transfers between devices, send(): return lax.ppermute(value, 'expert', route)  28.8 us
    ppermute x30, waiting for transfers between devices, send(): return lax.ppermute(value, 'expert', route)  28.5 us
    pallas_call x19, Pallas kernels, call(): pl.pallas_call(kernel, out_shape=outs, in_specs=specs, out_specs=[in_hbm(...  18.9 us
    pallas_call x1, Pallas kernels, late(): pl.pallas_call(functools.partial(late_kernel, width, part, units), out_sh...  6.84 us
    pallas_call x1, Pallas kernels, early(): pl.pallas_call(functools.partial(early_kernel, plane, capacity, groups),...  4.59 us
    pallas_call x1, Pallas kernels, own_picked(): pl.pallas_call(functools.partial(own_select_kernel, plane, capacity, plan...  3.51 us
    ppermute x2, waiting for transfers between devices, body(): lax.ppermute(leaving[h], 'segment', [(i, i - 1) for i in range(1, segment...  3.41 us
    all_to_all x1, starting transfers between devices, exchange(): lax.all_to_all(pieces, 'expert', split_axis=0, concat_axis=0, tiled=True)  3.36 us
  transfers between devices with their start and end apart: 34, of which 14 were waited for; matrix products, arithmetic and copies ran while one was open for 3% of the time, Pallas kernels for 30%

profile of v10, /device:TPU:0, one launch (start us, length us, event | category | flops | bytes accessed | tf_op | source)
XLA Modules:
  0.0 112.7 jit_solution(11606538712962787064)
XLA Ops:
  1.2 1.3 %slice_bitcast_fusion.refs_0_ = bf16[128,2048]{1,0:T(8,128)(2,1)S(1)} fusion(bf16[1,2,128,2048]{3,2,1,0:T(8,128)(2,1)} %param.6), kind=kLoop, calls=%fused_computation | loop fusion | bytes 1048576 | tf_op jit(solution)/shard_map/squeeze | solution.py:571
  2.5 2.5 %collective-permute-start.2 = (bf16[128,2048]{1,0:T(8,128)(2,1)S(1)}, bf16[128,2048]{1,0:T(8,128)(2,1)}, u32[]{:S(2)}, u32[]{:S(2)}) collective-permute-start(bf16[128,2048]{1,0:T(8,128)(2,1)S(1)} %slice_bitcast_fusion.refs_0_), channel_id=1, source_target_pairs={{0,2},{1,3},{2,0},{3,1},{4,6},{5,7},{6,4},{7,5},{8,10},{9,11},{10,... | collective-permute-start | bytes 1572872 | tf_op jit(solution)/shard_map/ppermute | solution.py:84
  5.0 1.5 %collective-permute-start.8 = (bf16[128,2048]{1,0:T(8,128)(2,1)}, bf16[128,2048]{1,0:T(8,128)(2,1)}, u32[]{:S(2)}, u32[]{:S(2)}) collective-permute-start(bf16[128,2048]{1,0:T(8,128)(2,1)} %bitcast.32), channel_id=1, source_target_pairs={{0,4},{1,5},{2,6},{3,7},{4,0},{5,1},{6,2},{7,3},{8,12},{9,13},{10,... | collective-permute-start | bytes 1572872 | tf_op jit(solution)/shard_map/ppermute | solution.py:84
  8.5 3.3 %all-to-all-start = ((f32[8,8,128]{2,1,0:T(8,128)}), f32[8,8,128]{2,1,0:T(8,128)S(1)}, u32[]{:S(2)}, u32[]{:S(2)}) async-start(f32[8,8,128]{2,1,0:T(8,128)} %broadcast_in_dim.15), calls=%async_computation | async-start | bytes 65536 | tf_op jit(solution)/shard_map/all_to_all | solution.py:578
  12.2 0.8 collective-permute-done.refs_1_
  13.6 3.5 %shard_map.85 = (bf16[44,384,2048]{2,1,0:T(8,128)(2,1)}, bf16[96,2048]{1,0:T(8,128)(2,1)}, bf16[96,2048]{1,0:T(8,128)(2,1)}, bf16[96,2048]{1,0:T(8,128)(2,1)}, b...) custom-call(f32[8,128]{1,0:T(8,128)} %copy-done.6, f32[8,128]{1,0:T(8,128)} %copy-done.7, ...), custom_call_target="tpu_custom_call" | custom-call | bytes 235405312 | tf_op jit(solution)/shard_map/pallas_call | solution.py:189
  17.1 1.9 %collective-permute-start.6 = (bf16[96,2048]{1,0:T(8,128)(2,1)}, bf16[96,2048]{1,0:T(8,128)(2,1)}, u32[]{:S(2)}, u32[]{:S(2)}) collective-permute-start(bf16[96,2048]{1,0:T(8,128)(2,1)} %get-tuple-element.92), channel_id=1, source_target_pairs={{0,2},{1,3},{2,0},{3,1},{4,6},{5,7},{6,4},{7,5},{8,10},{9,11},{10,... | collective-permute-start | bytes 1179656 | tf_op jit(solution)/shard_map/ppermute | solution.py:84
  19.1 1.5 %collective-permute-start.7 = (bf16[96,2048]{1,0:T(8,128)(2,1)}, bf16[96,2048]{1,0:T(8,128)(2,1)}, u32[]{:S(2)}, u32[]{:S(2)}) collective-permute-start(bf16[96,2048]{1,0:T(8,128)(2,1)} %get-tuple-element.93), channel_id=1, source_target_pairs={{0,4},{1,5},{2,6},{3,7},{4,0},{5,1},{6,2},{7,3},{8,12},{9,13},{10,... | collective-permute-start | bytes 1179656 | tf_op jit(solution)/shard_map/ppermute | solution.py:84
  20.6 2.1 %shard_map.86 = (bf16[96,2048]{1,0:T(8,128)(2,1)S(1)}, bf16[96,2048]{1,0:T(8,128)(2,1)S(1)}, bf16[96,2048]{1,0:T(8,128)(2,1)S(1)}, bf16[96,2048]{1,0:T(8,128)(2,1)S(1)}) custom-call(f32[8,8,128]{2,1,0:T(8,128)S(1)} %all-to-all-done.meta_ref, bf16[128,2048]{1,0:T(8,128)(2,1)S(1)} %slice_bitcast_fusion.refs_0_, bf16[128,2048]{1,0:T(8,128)(2,1)} %collective-permute-done.2.refs_1_), custom_call_target="tpu_custom_call" | custom-call | bytes 169869312 | tf_op jit(solution)/shard_map/pallas_call | solution.py:45
  24.7 1.3 %collective-permute-start.5 = (bf16[96,2048]{1,0:T(8,128)(2,1)S(1)}, bf16[96,2048]{1,0:T(8,128)(2,1)S(1)}, u32[]{:S(2)}, u32[]{:S(2)}) collective-permute-start(bf16[96,2048]{1,0:T(8,128)(2,1)S(1)} %get-tuple-element.100), channel_id=1, source_target_pairs={{0,5},{1,4},{2,7},{3,6},{4,1},{5,0},{6,3},{7,2},{8,13},{9,12},{10,... | collective-permute-start | bytes 1179656 | tf_op jit(solution)/shard_map/ppermute | solution.py:84
  25.9 1.0 copy-done.2
  27.0 2.1 %shard_map.89 = (bf16[96,2048]{1,0:T(8,128)(2,1)S(1)}, bf16[96,2048]{1,0:T(8,128)(2,1)S(1)}, bf16[96,2048]{1,0:T(8,128)(2,1)S(1)}, bf16[96,2048]{1,0:T(8,128)(2,1)S(1)}) custom-call(f32[8,8,128]{2,1,0:T(8,128)S(1)} %all-to-all-done.meta_ref, bf16[128,2048]{1,0:T(8,128)(2,1)S(1)} %bitcast.33, bf16[128,2048]{1,0:T(8,128)(2,1)} %collective-permute-done.8.refs_1_), custom_call_target="tpu_custom_call" | custom-call | bytes 169869312 | tf_op jit(solution)/shard_map/pallas_call | solution.py:45
  29.1 1.5 %collective-permute-start.10 = (bf16[96,2048]{1,0:T(8,128)(2,1)S(1)}, bf16[96,2048]{1,0:T(8,128)(2,1)S(1)}, u32[]{:S(2)}, u32[]{:S(2)}) collective-permute-start(bf16[96,2048]{1,0:T(8,128)(2,1)S(1)} %get-tuple-element.111), channel_id=1, source_target_pairs={{0,2},{1,3},{2,0},{3,1},{4,6},{5,7},{6,4},{7,5},{8,10},{9,11},{10,... | collective-permute-start | bytes 1179656 | tf_op jit(solution)/shard_map/ppermute | solution.py:84
  30.6 0.8 collective-permute-done.7.refs_2_
  31.6 8.1 %collective-permute-done.4.refs_2_ = bf16[96,2048]{1,0:T(8,128)(2,1)S(1)} collective-permute-done((bf16[96,2048]{1,0:T(8,128)(2,1)S(1)}, bf16[96,2048]{1,0:T(8,128)(2,1)S(1)}, u32[]{:S(2)}, u32[]{:S(2)}) %collective-permute-start.4) | collective-permute-done | bytes 393248 | tf_op jit(solution)/shard_map/ppermute | solution.py:84
  39.7 6.3 %collective-permute-done.5.refs_3_ = bf16[96,2048]{1,0:T(8,128)(2,1)S(1)} collective-permute-done((bf16[96,2048]{1,0:T(8,128)(2,1)S(1)}, bf16[96,2048]{1,0:T(8,128)(2,1)S(1)}, u32[]{:S(2)}, u32[]{:S(2)}) %collective-permute-start.5) | collective-permute-done | bytes 393248 | tf_op jit(solution)/shard_map/ppermute | solution.py:84
  46.1 1.8 %shard_map.87 = (bf16[384,2048]{1,0:T(8,128)(2,1)S(1)}, bf16[384,768]{1,0:T(8,128)(2,1)S(1)}, f32[384,704]{1,0:T(8,128)S(1)}) custom-call(bf16[704,2048]{1,0:T(8,128)(2,1)S(1)} %bitcast.26, bf16[96,2048]{1,0:T(8,128)(2,1)S(1)} %get-tuple-element.101.refs_0_, bf16[96,2048]{1,0:T(8,128)(2,1)S(1)} %collective-permute-done.3.refs_1_, ...), custom_call_target="tpu_custom_call" | custom-call | bytes 492830720 | tf_op jit(solution)/shard_map/pallas_call | solution.py:45
  48.2 1.1 collective-permute-start.12
  49.3 3.2 %shard_map.90 = (bf16[384,2048]{1,0:T(8,128)(2,1)S(1)}, bf16[384,768]{1,0:T(8,128)(2,1)S(1)}, bf16[384,256]{1,0:T(8,128)(2,1)S(1)}, bf16[96,1024]{1,0:T(8,128)(2...) custom-call(bf16[704,2048]{1,0:T(8,128)(2,1)S(1)} %bitcast.27, ...), custom_call_target="tpu_custom_call" | custom-call | bytes 834666496 | tf_op jit(solution)/shard_map/pallas_call | solution.py:45
  52.6 1.5 %collective-permute-start.13 = (bf16[96,1024]{1,0:T(8,128)(2,1)S(1)}, bf16[96,1024]{1,0:T(8,128)(2,1)S(1)}, u32[]{:S(2)}, u32[]{:S(2)}) collective-permute-start(bf16[96,1024]{1,0:T(8,128)(2,1)S(1)} %get-tuple-element.121), channel_id=1, source_target_pairs={{0,2},{1,3},{2,0},{3,1},{4,6},{5,7},{6,4},{7,5},{8,10},{9,11},{10,... | collective-permute-start | bytes 589832 | tf_op jit(solution)/shard_map/ppermute | solution.py:84
  54.1 0.9 collective-permute-start.14
  55.0 1.1 collective-permute-start.15
  56.2 0.9 shard_map.92
  57.0 1.5 %collective-permute-start.18 = (bf16[96,1024]{1,0:T(8,128)(2,1)S(1)}, bf16[96,1024]{1,0:T(8,128)(2,1)S(1)}, u32[]{:S(2)}, u32[]{:S(2)}) collective-permute-start(bf16[96,1024]{1,0:T(8,128)(2,1)S(1)} %get-tuple-element.134), channel_id=1, source_target_pairs={{0,2},{1,3},{2,0},{3,1},{4,6},{5,7},{6,4},{7,5},{8,10},{9,11},{10,... | collective-permute-start | bytes 589832 | tf_op jit(solution)/shard_map/ppermute | solution.py:84
  58.6 2.1 %shard_map.91._ = bf16[44,384,2048]{2,1,0:T(8,128)(2,1)} custom-call(bf16[384,2048]{1,0:T(8,128)(2,1)S(1)} %get-tuple-element.105.refs_0_, bf16[384,2048]{1,0:T(8,128)(2,1)S(1)} %get-tuple-element.114.refs_1_, bf16[384,768]{1,0:T(8,128)(2,1)S(1)} %get-tuple-element.106.hid_ref.refs_2_, ...), custom_call_target="tpu_custom_call", output_to_operand_aliasing={{}: (5, {})} | custom-call | tf_op jit(solution)/shard_map/pallas_call | solution.py:414
  60.7 1.0 collective-permute-start.19
  61.7 1.1 collective-permute-start.20
  62.8 2.9 %collective-permute-done.14.refs_2_ = bf16[96,1024]{1,0:T(8,128)(2,1)S(1)} collective-permute-done((bf16[96,1024]{1,0:T(8,128)(2,1)S(1)}, bf16[96,1024]{1,0:T(8,128)(2,1)S(1)}, u32[]{:S(2)}, u32[]{:S(2)}) %collective-permute-start.14) | collective-permute-done | bytes 196640 | tf_op jit(solution)/shard_map/ppermute | solution.py:84
  66.1 1.5 %collective-permute-done.16.refs_0_ = bf16[128,1024]{1,0:T(8,128)(2,1)S(1)} collective-permute-done((bf16[128,1024]{1,0:T(8,128)(2,1)S(1)}, bf16[128,1024]{1,0:T(8,128)(2,1)S(1)}, u32[]{:S(2)}, u32[]{:S(2)}) %collective-permute-start.16) | collective-permute-done | bytes 262176 | tf_op jit(solution)/shard_map/ppermute | solution.py:84
  67.6 1.3 %collective-permute-start.23 = (bf16[128,1024]{1,0:T(8,128)(2,1)S(1)}, bf16[128,1024]{1,0:T(8,128)(2,1)S(1)}, u32[]{:S(2)}, u32[]{:S(2)}) collective-permute-start(bf16[128,1024]{1,0:T(8,128)(2,1)S(1)} %shard_map.95), channel_id=1, source_target_pairs={{8,0},{16,8},{24,16},{9,1},{17,9},{25,17},{10,2},{18,10},{26,18},{... | collective-permute-start | bytes 786440 | tf_op jit(solution)/shard_map/ppermute | solution.py:655
  69.2 4.7 %collective-permute-done.19.refs_2_ = bf16[96,1024]{1,0:T(8,128)(2,1)S(1)} collective-permute-done((bf16[96,1024]{1,0:T(8,128)(2,1)S(1)}, bf16[96,1024]{1,0:T(8,128)(2,1)S(1)}, u32[]{:S(2)}, u32[]{:S(2)}) %collective-permute-start.19) | collective-permute-done | bytes 196640 | tf_op jit(solution)/shard_map/ppermute | solution.py:84
  74.4 1.3 %collective-permute-start.17 = (bf16[96,1024]{1,0:T(8,128)(2,1)}, bf16[96,1024]{1,0:T(8,128)(2,1)}, u32[]{:S(2)}, u32[]{:S(2)}) collective-permute-start(bf16[96,1024]{1,0:T(8,128)(2,1)} %get-tuple-element.130), channel_id=1, source_target_pairs={{0,6},{1,7},{2,4},{3,5},{4,2},{5,3},{6,0},{7,1},{8,14},{9,15},{10,... | collective-permute-start | bytes 589832 | tf_op jit(solution)/shard_map/ppermute | solution.py:84
  75.9 1.5 %collective-permute-start.22 = (bf16[128,1024]{1,0:T(8,128)(2,1)S(1)}, bf16[128,1024]{1,0:T(8,128)(2,1)S(1)}, u32[]{:S(2)}, u32[]{:S(2)}) collective-permute-start(bf16[128,1024]{1,0:T(8,128)(2,1)S(1)} %shard_map.98), channel_id=1, source_target_pairs={{8,0},{16,8},{24,16},{9,1},{17,9},{25,17},{10,2},{18,10},{26,18},{... | collective-permute-start | bytes 786440 | tf_op jit(solution)/shard_map/ppermute | solution.py:655
  78.1 1.3 %collective-permute-done.24.refs_0_ = bf16[128,1024]{1,0:T(8,128)(2,1)S(1)} collective-permute-done((bf16[128,1024]{1,0:T(8,128)(2,1)S(1)}, bf16[128,1024]{1,0:T(8,128)(2,1)S(1)}, u32[]{:S(2)}, u32[]{:S(2)}) %collective-permute-start.24) | collective-permute-done | bytes 262176 | tf_op jit(solution)/shard_map/ppermute | solution.py:84
  79.7 0.9 collective-permute-start.26
  80.6 1.1 %collective-permute-start.27 = (bf16[96,1024]{1,0:T(8,128)(2,1)S(1)}, bf16[96,1024]{1,0:T(8,128)(2,1)S(1)}, u32[]{:S(2)}, u32[]{:S(2)}) collective-permute-start(bf16[96,1024]{1,0:T(8,128)(2,1)S(1)} %get-tuple-element.146), channel_id=1, source_target_pairs={{0,4},{1,5},{2,6},{3,7},{4,0},{5,1},{6,2},{7,3},{8,12},{9,13},{10,... | collective-permute-start | bytes 589832 | tf_op jit(solution)/shard_map/ppermute | solution.py:84
  81.7 1.5 %collective-permute-start.28 = (bf16[96,1024]{1,0:T(8,128)(2,1)S(1)}, bf16[96,1024]{1,0:T(8,128)(2,1)S(1)}, u32[]{:S(2)}, u32[]{:S(2)}) collective-permute-start(bf16[96,1024]{1,0:T(8,128)(2,1)S(1)} %get-tuple-element.147), channel_id=1, source_target_pairs={{0,6},{1,7},{2,4},{3,5},{4,2},{5,3},{6,0},{7,1},{8,14},{9,15},{10,... | collective-permute-start | bytes 589832 | tf_op jit(solution)/shard_map/ppermute | solution.py:84
  83.2 2.9 %collective-permute-done.22.raw_ref = bf16[128,1024]{1,0:T(8,128)(2,1)S(1)} collective-permute-done((bf16[128,1024]{1,0:T(8,128)(2,1)S(1)}, bf16[128,1024]{1,0:T(8,128)(2,1)S(1)}, u32[]{:S(2)}, u32[]{:S(2)}) %collective-permute-start.22) | collective-permute-done | bytes 262176 | tf_op jit(solution)/shard_map/ppermute | solution.py:655
  86.4 1.3 %collective-permute-done.25.refs_0_ = bf16[128,1024]{1,0:T(8,128)(2,1)S(1)} collective-permute-done((bf16[128,1024]{1,0:T(8,128)(2,1)S(1)}, bf16[128,1024]{1,0:T(8,128)(2,1)S(1)}, u32[]{:S(2)}, u32[]{:S(2)}) %collective-permute-start.25) | collective-permute-done | bytes 262176 | tf_op jit(solution)/shard_map/ppermute | solution.py:84
  87.9 1.1 %collective-permute-start.29 = (bf16[96,1024]{1,0:T(8,128)(2,1)S(1)}, bf16[96,1024]{1,0:T(8,128)(2,1)S(1)}, u32[]{:S(2)}, u32[]{:S(2)}) collective-permute-start(bf16[96,1024]{1,0:T(8,128)(2,1)S(1)} %get-tuple-element.150), channel_id=1, source_target_pairs={{0,2},{1,3},{2,0},{3,1},{4,6},{5,7},{6,4},{7,5},{8,10},{9,11},{10,... | collective-permute-start | bytes 589832 | tf_op jit(solution)/shard_map/ppermute | solution.py:84
  89.1 1.1 collective-permute-start.30
  90.2 1.3 %collective-permute-start.31 = (bf16[96,1024]{1,0:T(8,128)(2,1)S(1)}, bf16[96,1024]{1,0:T(8,128)(2,1)S(1)}, u32[]{:S(2)}, u32[]{:S(2)}) collective-permute-start(bf16[96,1024]{1,0:T(8,128)(2,1)S(1)} %get-tuple-element.152), channel_id=1, source_target_pairs={{0,6},{1,7},{2,4},{3,5},{4,2},{5,3},{6,0},{7,1},{8,14},{9,15},{10,... | collective-permute-start | bytes 589832 | tf_op jit(solution)/shard_map/ppermute | solution.py:84
  91.5 3.8 %shard_map.103 = (bf16[44,384,2048]{2,1,0:T(8,128)(2,1)}, bf16[384,704]{1,0:T(8,128)(2,1)S(1)}, f32[384,704]{1,0:T(8,128)S(1)}) custom-call(bf16[704,2048]{1,0:T(8,128)(2,1)S(1)} %bitcast.28, bf16[44,384,2048]{2,1,0:T(8,128)(2,1)} %shard_map.91._, bf16[96,2048]{1,0:T(8,128)(2,1)S(1)} %copy-done.3, ...), custom_call_target="tpu_custom_call", output_to_operand_aliasing={{0}: (1, {})} | custom-call | bytes 9247391744 | tf_op jit(solution)/shard_map/pallas_call | solution.py:45
  95.4 4.6 %shard_map.104 = (f32[384,704]{1,0:T(8,128)S(1)}, bf16[704,2048]{1,0:T(8,128)(2,1)}, bf16[384,256]{1,0:T(8,128)(2,1)S(1)}) custom-call(bf16[704,2048]{1,0:T(8,128)(2,1)S(1)} %bitcast.30, bf16[384,704]{1,0:T(8,128)(2,1)S(1)} %get-tuple-element.158.hid1_ref.hid_ref, bf16[44,384,2048]{2,1,0:T(8,128)(2,1)} %get-tuple-element.159.pad_ref, ...), custom_call_target="tpu_custom_call" | custom-call | bytes 535822336 | tf_op jit(solution)/shard_map/pallas_call | solution.py:453
  100.0 1.6 %shard_map.105 = (bf16[384,1024]{1,0:T(8,128)(2,1)S(1)}, bf16[384,768]{1,0:T(8,128)(2,1)S(1)}, bf16[384,128]{1,0:T(8,128)(2,1)}) custom-call(bf16[704,2048]{1,0:T(8,128)(2,1)S(1)} %bitcast.31, bf16[384,704]{1,0:T(8,128)(2,1)S(1)} %get-tuple-element.158.hid1_ref.hid_ref, f32[384,704]{1,0:T(8,128)S(1)} %get-tuple-element.161.slope_ref, ...), custom_call_target="tpu_custom_call" | custom-call | bytes 514850816 | tf_op jit(solution)/shard_map/pallas_call | solution.py:45
  101.6 3.4 %all-to-all-start.1 = ((bf16[8,48,128]{2,1,0:T(8,128)(2,1)}), bf16[8,48,128]{2,1,0:T(8,128)(2,1)S(1)}, u32[]{:S(2)}, u32[]{:S(2)}) async-start(bf16[8,48,128]{2,1,0:T(8,128)(2,1)} %bitcast.13), calls=%async_computation.1 | async-start | bytes 196608 | tf_op jit(solution)/shard_map/all_to_all | solution.py:293
  105.0 6.8 %shard_map.106 = (bf16[704,2048]{1,0:T(8,128)(2,1)}, bf16[704,2048]{1,0:T(8,128)(2,1)}) custom-call(bf16[704,2048]{1,0:T(8,128)(2,1)} %get-tuple-element.160._, bf16[44,384,2048]{2,1,0:T(8,128)(2,1)} %get-tuple-element.159.pad_ref, bf16[384,1024]{1,0:T(8,128)(2,1)S(1)} %get-tuple-element.168.g1_ref, ...), custom_call_target="tpu_custom_call", output_to_operand_aliasing={{1}: (0, {})} | custom-call | bytes 369098752 | tf_op jit(solution)/shard_map/pallas_call | solution.py:527
  111.9 0.9 shard_map.107
  (66 shorter events, 9.0 us)
Async XLA Ops:
  0.6 45.4 %copy-start = (bf16[1,1,704,2048]{3,2,1,0:T(8,128)(2,1)S(1)}, bf16[1,1,704,2048]{3,2,1,0:T(8,128)(2,1)}, u32[]{:S(2)}) copy-start(bf16[1,1,704,2048]{3,2,1,0:T(8,128)(2,1)} %param.8) | copy-start | bytes 8650756
  0.6 12.4 %collective-permute-start.1 = (bf16[2,128,2048]{2,1,0:T(8,128)(2,1)}, bf16[2,128,2048]{2,1,0:T(8,128)(2,1)}, u32[]{:S(2)}, u32[]{:S(2)}) collective-permute-start(bf16[2,128,2048]{2,1,0:T(8,128)(2,1)} %bitcast.38), channel_id=1, source_target_pairs={{0,1},{1,0},{2,3},{3,2},{4,5},{5,4},{6,7},{7,6},{8,9},{9,8},{10,11... | collective-permute-start | bytes 3145736 | tf_op jit(solution)/shard_map/ppermute | solution.py:84
  2.5 18.1 %collective-permute-start.2 = (bf16[128,2048]{1,0:T(8,128)(2,1)S(1)}, bf16[128,2048]{1,0:T(8,128)(2,1)}, u32[]{:S(2)}, u32[]{:S(2)}) collective-permute-start(bf16[128,2048]{1,0:T(8,128)(2,1)S(1)} %slice_bitcast_fusion.refs_0_), channel_id=1, source_target_pairs={{0,2},{1,3},{2,0},{3,1},{4,6},{5,7},{6,4},{7,5},{8,10},{9,11},{10,... | collective-permute-start | bytes 1572872 | tf_op jit(solution)/shard_map/ppermute | solution.py:84
  5.0 19.7 %collective-permute-start.8 = (bf16[128,2048]{1,0:T(8,128)(2,1)}, bf16[128,2048]{1,0:T(8,128)(2,1)}, u32[]{:S(2)}, u32[]{:S(2)}) collective-permute-start(bf16[128,2048]{1,0:T(8,128)(2,1)} %bitcast.32), channel_id=1, source_target_pairs={{0,4},{1,5},{2,6},{3,7},{4,0},{5,1},{6,2},{7,3},{8,12},{9,13},{10,... | collective-permute-start | bytes 1572872 | tf_op jit(solution)/shard_map/ppermute | solution.py:84
  7.9 5.2 %copy-start.6 = (f32[8,128]{1,0:T(8,128)}, f32[8,128]{1,0:T(8,128)S(1)}, u32[]{:S(2)}) copy-start(f32[8,128]{1,0:T(8,128)S(1)} %pad_maximum_fusion.refs_0_) | copy-start | bytes 12292
  8.5 12.1 %all-to-all-start = ((f32[8,8,128]{2,1,0:T(8,128)}), f32[8,8,128]{2,1,0:T(8,128)S(1)}, u32[]{:S(2)}, u32[]{:S(2)}) async-start(f32[8,8,128]{2,1,0:T(8,128)} %broadcast_in_dim.15), calls=%async_computation | async-start | bytes 65536 | tf_op jit(solution)/shard_map/all_to_all | solution.py:578
  11.8 1.2 %collective-permute-start = (f32[8,128]{1,0:T(8,128)S(1)}, f32[8,128]{1,0:T(8,128)S(1)}, u32[]{:S(2)}, u32[]{:S(2)}) collective-permute-start(f32[8,128]{1,0:T(8,128)S(1)} %pad_maximum_fusion.refs_0_), channel_id=1, source_target_pairs={{0,1},{1,0},{2,3},{3,2},{4,5},{5,4},{6,7},{7,6},{8,9},{9,8},{10,11... | collective-permute-start | bytes 12296 | tf_op jit(solution)/shard_map/ppermute | solution.py:84
  13.0 0.6 copy-start.7
  17.1 11.9 %collective-permute-start.6 = (bf16[96,2048]{1,0:T(8,128)(2,1)}, bf16[96,2048]{1,0:T(8,128)(2,1)}, u32[]{:S(2)}, u32[]{:S(2)}) collective-permute-start(bf16[96,2048]{1,0:T(8,128)(2,1)} %get-tuple-element.92), channel_id=1, source_target_pairs={{0,2},{1,3},{2,0},{3,1},{4,6},{5,7},{6,4},{7,5},{8,10},{9,11},{10,... | collective-permute-start | bytes 1179656 | tf_op jit(solution)/shard_map/ppermute | solution.py:84
  19.1 12.3 %collective-permute-start.7 = (bf16[96,2048]{1,0:T(8,128)(2,1)}, bf16[96,2048]{1,0:T(8,128)(2,1)}, u32[]{:S(2)}, u32[]{:S(2)}) collective-permute-start(bf16[96,2048]{1,0:T(8,128)(2,1)} %get-tuple-element.93), channel_id=1, source_target_pairs={{0,4},{1,5},{2,6},{3,7},{4,0},{5,1},{6,2},{7,3},{8,12},{9,13},{10,... | collective-permute-start | bytes 1179656 | tf_op jit(solution)/shard_map/ppermute | solution.py:84
  20.6 27.7 %copy-start.8 = (bf16[96,1024]{1,0:T(8,128)(2,1)S(1)}, bf16[96,1024]{1,0:T(8,128)(2,1)}, u32[]{:S(2)}) copy-start(bf16[96,1024]{1,0:T(8,128)(2,1)} %get-tuple-element.118) | copy-start | bytes 589828
  22.7 26.6 %copy-start.1 = (bf16[1,1,704,2048]{3,2,1,0:T(8,128)(2,1)S(1)}, bf16[1,1,704,2048]{3,2,1,0:T(8,128)(2,1)}, u32[]{:S(2)}) copy-start(bf16[1,1,704,2048]{3,2,1,0:T(8,128)(2,1)} %param.9) | copy-start | bytes 8650756
  22.7 8.7 %collective-permute-start.3 = (bf16[96,2048]{1,0:T(8,128)(2,1)S(1)}, bf16[96,2048]{1,0:T(8,128)(2,1)S(1)}, u32[]{:S(2)}, u32[]{:S(2)}) collective-permute-start(bf16[96,2048]{1,0:T(8,128)(2,1)S(1)} %get-tuple-element.98), channel_id=1, source_target_pairs={{0,1},{1,0},{2,3},{3,2},{4,5},{5,4},{6,7},{7,6},{8,9},{9,8},{10,11... | collective-permute-start | bytes 1179656 | tf_op jit(solution)/shard_map/ppermute | solution.py:84
  23.4 0.6 copy-start.4
  24.1 15.7 %collective-permute-start.4 = (bf16[96,2048]{1,0:T(8,128)(2,1)S(1)}, bf16[96,2048]{1,0:T(8,128)(2,1)S(1)}, u32[]{:S(2)}, u32[]{:S(2)}) collective-permute-start(bf16[96,2048]{1,0:T(8,128)(2,1)S(1)} %get-tuple-element.99), channel_id=1, source_target_pairs={{0,4},{1,5},{2,6},{3,7},{4,0},{5,1},{6,2},{7,3},{8,12},{9,13},{10,... | collective-permute-start | bytes 1179656 | tf_op jit(solution)/shard_map/ppermute | solution.py:84
  24.7 21.4 %collective-permute-start.5 = (bf16[96,2048]{1,0:T(8,128)(2,1)S(1)}, bf16[96,2048]{1,0:T(8,128)(2,1)S(1)}, u32[]{:S(2)}, u32[]{:S(2)}) collective-permute-start(bf16[96,2048]{1,0:T(8,128)(2,1)S(1)} %get-tuple-element.100), channel_id=1, source_target_pairs={{0,5},{1,4},{2,7},{3,6},{4,1},{5,0},{6,3},{7,2},{8,13},{9,12},{10,... | collective-permute-start | bytes 1179656 | tf_op jit(solution)/shard_map/ppermute | solution.py:84
  25.9 1.0 copy-start.2
  29.1 18.8 %collective-permute-start.10 = (bf16[96,2048]{1,0:T(8,128)(2,1)S(1)}, bf16[96,2048]{1,0:T(8,128)(2,1)S(1)}, u32[]{:S(2)}, u32[]{:S(2)}) collective-permute-start(bf16[96,2048]{1,0:T(8,128)(2,1)S(1)} %get-tuple-element.111), channel_id=1, source_target_pairs={{0,2},{1,3},{2,0},{3,1},{4,6},{5,7},{6,4},{7,5},{8,10},{9,11},{10,... | collective-permute-start | bytes 1179656 | tf_op jit(solution)/shard_map/ppermute | solution.py:84
  31.4 16.5 %collective-permute-start.9 = (bf16[96,2048]{1,0:T(8,128)(2,1)S(1)}, bf16[96,2048]{1,0:T(8,128)(2,1)S(1)}, u32[]{:S(2)}, u32[]{:S(2)}) collective-permute-start(bf16[96,2048]{1,0:T(8,128)(2,1)S(1)} %get-tuple-element.110), channel_id=1, source_target_pairs={{0,1},{1,0},{2,3},{3,2},{4,5},{5,4},{6,7},{7,6},{8,9},{9,8},{10,11... | collective-permute-start | bytes 1179656 | tf_op jit(solution)/shard_map/ppermute | solution.py:84
  31.4 16.8 %collective-permute-start.11 = (bf16[96,2048]{1,0:T(8,128)(2,1)S(1)}, bf16[96,2048]{1,0:T(8,128)(2,1)S(1)}, u32[]{:S(2)}, u32[]{:S(2)}) collective-permute-start(bf16[96,2048]{1,0:T(8,128)(2,1)S(1)} %get-tuple-element.113), channel_id=1, source_target_pairs={{0,3},{1,2},{2,1},{3,0},{4,7},{5,6},{6,5},{7,4},{8,11},{9,10},{10,... | collective-permute-start | bytes 1179656 | tf_op jit(solution)/shard_map/ppermute | solution.py:84
  48.2 12.5 %collective-permute-start.12 = (bf16[96,1024]{1,0:T(8,128)(2,1)S(1)}, bf16[96,1024]{1,0:T(8,128)(2,1)S(1)}, u32[]{:S(2)}, u32[]{:S(2)}) collective-permute-start(bf16[96,1024]{1,0:T(8,128)(2,1)S(1)} %copy-done.8), channel_id=1, source_target_pairs={{0,6},{1,7},{2,4},{3,5},{4,2},{5,3},{6,0},{7,1},{8,14},{9,15},{10,... | collective-permute-start | bytes 589832 | tf_op jit(solution)/shard_map/ppermute | solution.py:84
  52.6 9.1 %collective-permute-start.13 = (bf16[96,1024]{1,0:T(8,128)(2,1)S(1)}, bf16[96,1024]{1,0:T(8,128)(2,1)S(1)}, u32[]{:S(2)}, u32[]{:S(2)}) collective-permute-start(bf16[96,1024]{1,0:T(8,128)(2,1)S(1)} %get-tuple-element.121), channel_id=1, source_target_pairs={{0,2},{1,3},{2,0},{3,1},{4,6},{5,7},{6,4},{7,5},{8,10},{9,11},{10,... | collective-permute-start | bytes 589832 | tf_op jit(solution)/shard_map/ppermute | solution.py:84
  54.1 11.5 %collective-permute-start.14 = (bf16[96,1024]{1,0:T(8,128)(2,1)S(1)}, bf16[96,1024]{1,0:T(8,128)(2,1)S(1)}, u32[]{:S(2)}, u32[]{:S(2)}) collective-permute-start(bf16[96,1024]{1,0:T(8,128)(2,1)S(1)} %get-tuple-element.122), channel_id=1, source_target_pairs={{0,4},{1,5},{2,6},{3,7},{4,0},{5,1},{6,2},{7,3},{8,12},{9,13},{10,... | collective-permute-start | bytes 589832 | tf_op jit(solution)/shard_map/ppermute | solution.py:84
  55.0 10.6 %collective-permute-start.15 = (bf16[96,1024]{1,0:T(8,128)(2,1)S(1)}, bf16[96,1024]{1,0:T(8,128)(2,1)S(1)}, u32[]{:S(2)}, u32[]{:S(2)}) collective-permute-start(bf16[96,1024]{1,0:T(8,128)(2,1)S(1)} %get-tuple-element.123), channel_id=1, source_target_pairs={{0,6},{1,7},{2,4},{3,5},{4,2},{5,3},{6,0},{7,1},{8,14},{9,15},{10,... | collective-permute-start | bytes 589832 | tf_op jit(solution)/shard_map/ppermute | solution.py:84
  57.0 12.2 %collective-permute-start.18 = (bf16[96,1024]{1,0:T(8,128)(2,1)S(1)}, bf16[96,1024]{1,0:T(8,128)(2,1)S(1)}, u32[]{:S(2)}, u32[]{:S(2)}) collective-permute-start(bf16[96,1024]{1,0:T(8,128)(2,1)S(1)} %get-tuple-element.134), channel_id=1, source_target_pairs={{0,2},{1,3},{2,0},{3,1},{4,6},{5,7},{6,4},{7,5},{8,10},{9,11},{10,... | collective-permute-start | bytes 589832 | tf_op jit(solution)/shard_map/ppermute | solution.py:84
  60.7 13.2 %collective-permute-start.19 = (bf16[96,1024]{1,0:T(8,128)(2,1)S(1)}, bf16[96,1024]{1,0:T(8,128)(2,1)S(1)}, u32[]{:S(2)}, u32[]{:S(2)}) collective-permute-start(bf16[96,1024]{1,0:T(8,128)(2,1)S(1)} %get-tuple-element.135), channel_id=1, source_target_pairs={{0,4},{1,5},{2,6},{3,7},{4,0},{5,1},{6,2},{7,3},{8,12},{9,13},{10,... | collective-permute-start | bytes 589832 | tf_op jit(solution)/shard_map/ppermute | solution.py:84
  61.7 12.3 %collective-permute-start.20 = (bf16[96,1024]{1,0:T(8,128)(2,1)S(1)}, bf16[96,1024]{1,0:T(8,128)(2,1)S(1)}, u32[]{:S(2)}, u32[]{:S(2)}) collective-permute-start(bf16[96,1024]{1,0:T(8,128)(2,1)S(1)} %get-tuple-element.136), channel_id=1, source_target_pairs={{0,6},{1,7},{2,4},{3,5},{4,2},{5,3},{6,0},{7,1},{8,14},{9,15},{10,... | collective-permute-start | bytes 589832 | tf_op jit(solution)/shard_map/ppermute | solution.py:84
  66.0 1.6 %collective-permute-start.16 = (bf16[128,1024]{1,0:T(8,128)(2,1)S(1)}, bf16[128,1024]{1,0:T(8,128)(2,1)S(1)}, u32[]{:S(2)}, u32[]{:S(2)}) collective-permute-start(bf16[128,1024]{1,0:T(8,128)(2,1)S(1)} %get-tuple-element.129), channel_id=1, source_target_pairs={{0,1},{1,0},{2,3},{3,2},{4,5},{5,4},{6,7},{7,6},{8,9},{9,8},{10,11... | collective-permute-start | bytes 786440 | tf_op jit(solution)/shard_map/ppermute | solution.py:84
  67.6 10.2 %collective-permute-start.23 = (bf16[128,1024]{1,0:T(8,128)(2,1)S(1)}, bf16[128,1024]{1,0:T(8,128)(2,1)S(1)}, u32[]{:S(2)}, u32[]{:S(2)}) collective-permute-start(bf16[128,1024]{1,0:T(8,128)(2,1)S(1)} %shard_map.95), channel_id=1, source_target_pairs={{8,0},{16,8},{24,16},{9,1},{17,9},{25,17},{10,2},{18,10},{26,18},{... | collective-permute-start | bytes 786440 | tf_op jit(solution)/shard_map/ppermute | solution.py:655
  74.3 1.6 %collective-permute-start.21 = (bf16[128,1024]{1,0:T(8,128)(2,1)S(1)}, bf16[128,1024]{1,0:T(8,128)(2,1)S(1)}, u32[]{:S(2)}, u32[]{:S(2)}) collective-permute-start(bf16[128,1024]{1,0:T(8,128)(2,1)S(1)} %get-tuple-element.142), channel_id=1, source_target_pairs={{0,1},{1,0},{2,3},{3,2},{4,5},{5,4},{6,7},{7,6},{8,9},{9,8},{10,11... | collective-permute-start | bytes 786440 | tf_op jit(solution)/shard_map/ppermute | solution.py:84
  74.4 14.7 %collective-permute-start.17 = (bf16[96,1024]{1,0:T(8,128)(2,1)}, bf16[96,1024]{1,0:T(8,128)(2,1)}, u32[]{:S(2)}, u32[]{:S(2)}) collective-permute-start(bf16[96,1024]{1,0:T(8,128)(2,1)} %get-tuple-element.130), channel_id=1, source_target_pairs={{0,6},{1,7},{2,4},{3,5},{4,2},{5,3},{6,0},{7,1},{8,14},{9,15},{10,... | collective-permute-start | bytes 589832 | tf_op jit(solution)/shard_map/ppermute | solution.py:84
  75.9 10.2 %collective-permute-start.22 = (bf16[128,1024]{1,0:T(8,128)(2,1)S(1)}, bf16[128,1024]{1,0:T(8,128)(2,1)S(1)}, u32[]{:S(2)}, u32[]{:S(2)}) collective-permute-start(bf16[128,1024]{1,0:T(8,128)(2,1)S(1)} %shard_map.98), channel_id=1, source_target_pairs={{8,0},{16,8},{24,16},{9,1},{17,9},{25,17},{10,2},{18,10},{26,18},{... | collective-permute-start | bytes 786440 | tf_op jit(solution)/shard_map/ppermute | solution.py:655
  77.9 1.5 %collective-permute-start.24 = (bf16[128,1024]{1,0:T(8,128)(2,1)S(1)}, bf16[128,1024]{1,0:T(8,128)(2,1)S(1)}, u32[]{:S(2)}, u32[]{:S(2)}) collective-permute-start(bf16[128,1024]{1,0:T(8,128)(2,1)S(1)} %collective-permute-done.23.raw_ref), channel_id=1, source_target_pairs={{0,1},{1,0},{2,3},{3,2},{4,5},{5,4},{6,7},{7,6},{8,9},{9,8},{10,11... | collective-permute-start | bytes 786440 | tf_op jit(solution)/shard_map/ppermute | solution.py:84
  79.7 10.5 %collective-permute-start.26 = (bf16[96,1024]{1,0:T(8,128)(2,1)S(1)}, bf16[96,1024]{1,0:T(8,128)(2,1)S(1)}, u32[]{:S(2)}, u32[]{:S(2)}) collective-permute-start(bf16[96,1024]{1,0:T(8,128)(2,1)S(1)} %get-tuple-element.145), channel_id=1, source_target_pairs={{0,2},{1,3},{2,0},{3,1},{4,6},{5,7},{6,4},{7,5},{8,10},{9,11},{10,... | collective-permute-start | bytes 589832 | tf_op jit(solution)/shard_map/ppermute | solution.py:84
  80.6 14.8 %collective-permute-start.27 = (bf16[96,1024]{1,0:T(8,128)(2,1)S(1)}, bf16[96,1024]{1,0:T(8,128)(2,1)S(1)}, u32[]{:S(2)}, u32[]{:S(2)}) collective-permute-start(bf16[96,1024]{1,0:T(8,128)(2,1)S(1)} %get-tuple-element.146), channel_id=1, source_target_pairs={{0,4},{1,5},{2,6},{3,7},{4,0},{5,1},{6,2},{7,3},{8,12},{9,13},{10,... | collective-permute-start | bytes 589832 | tf_op jit(solution)/shard_map/ppermute | solution.py:84
  81.7 13.6 %collective-permute-start.28 = (bf16[96,1024]{1,0:T(8,128)(2,1)S(1)}, bf16[96,1024]{1,0:T(8,128)(2,1)S(1)}, u32[]{:S(2)}, u32[]{:S(2)}) collective-permute-start(bf16[96,1024]{1,0:T(8,128)(2,1)S(1)} %get-tuple-element.147), channel_id=1, source_target_pairs={{0,6},{1,7},{2,4},{3,5},{4,2},{5,3},{6,0},{7,1},{8,14},{9,15},{10,... | collective-permute-start | bytes 589832 | tf_op jit(solution)/shard_map/ppermute | solution.py:84
  86.2 1.5 %collective-permute-start.25 = (bf16[128,1024]{1,0:T(8,128)(2,1)S(1)}, bf16[128,1024]{1,0:T(8,128)(2,1)S(1)}, u32[]{:S(2)}, u32[]{:S(2)}) collective-permute-start(bf16[128,1024]{1,0:T(8,128)(2,1)S(1)} %collective-permute-done.22.raw_ref), channel_id=1, source_target_pairs={{0,1},{1,0},{2,3},{3,2},{4,5},{5,4},{6,7},{7,6},{8,9},{9,8},{10,11... | collective-permute-start | bytes 786440 | tf_op jit(solution)/shard_map/ppermute | solution.py:84
  86.2 5.4 %copy-start.3 = (bf16[96,2048]{1,0:T(8,128)(2,1)S(1)}, bf16[96,2048]{1,0:T(8,128)(2,1)}, u32[]{:S(2)}) copy-start(bf16[96,2048]{1,0:T(8,128)(2,1)} %get-tuple-element.153.refs_0_) | copy-start | bytes 1179652
  87.9 12.0 %collective-permute-start.29 = (bf16[96,1024]{1,0:T(8,128)(2,1)S(1)}, bf16[96,1024]{1,0:T(8,128)(2,1)S(1)}, u32[]{:S(2)}, u32[]{:S(2)}) collective-permute-start(bf16[96,1024]{1,0:T(8,128)(2,1)S(1)} %get-tuple-element.150), channel_id=1, source_target_pairs={{0,2},{1,3},{2,0},{3,1},{4,6},{5,7},{6,4},{7,5},{8,10},{9,11},{10,... | collective-permute-start | bytes 589832 | tf_op jit(solution)/shard_map/ppermute | solution.py:84
  89.1 10.9 %collective-permute-start.30 = (bf16[96,1024]{1,0:T(8,128)(2,1)S(1)}, bf16[96,1024]{1,0:T(8,128)(2,1)S(1)}, u32[]{:S(2)}, u32[]{:S(2)}) collective-permute-start(bf16[96,1024]{1,0:T(8,128)(2,1)S(1)} %get-tuple-element.151), channel_id=1, source_target_pairs={{0,4},{1,5},{2,6},{3,7},{4,0},{5,1},{6,2},{7,3},{8,12},{9,13},{10,... | collective-permute-start | bytes 589832 | tf_op jit(solution)/shard_map/ppermute | solution.py:84
  90.2 9.8 %collective-permute-start.31 = (bf16[96,1024]{1,0:T(8,128)(2,1)S(1)}, bf16[96,1024]{1,0:T(8,128)(2,1)S(1)}, u32[]{:S(2)}, u32[]{:S(2)}) collective-permute-start(bf16[96,1024]{1,0:T(8,128)(2,1)S(1)} %get-tuple-element.152), channel_id=1, source_target_pairs={{0,6},{1,7},{2,4},{3,5},{4,2},{5,3},{6,0},{7,1},{8,14},{9,15},{10,... | collective-permute-start | bytes 589832 | tf_op jit(solution)/shard_map/ppermute | solution.py:84
  101.6 10.2 %all-to-all-start.1 = ((bf16[8,48,128]{2,1,0:T(8,128)(2,1)}), bf16[8,48,128]{2,1,0:T(8,128)(2,1)S(1)}, u32[]{:S(2)}, u32[]{:S(2)}) async-start(bf16[8,48,128]{2,1,0:T(8,128)(2,1)} %bitcast.13), calls=%async_computation.1 | async-start | bytes 196608 | tf_op jit(solution)/shard_map/all_to_all | solution.py:293
  105.0 6.9 %copy-start.5 = (bf16[384,128]{1,0:T(8,128)(2,1)S(1)}, bf16[384,128]{1,0:T(8,128)(2,1)}, u32[]{:S(2)}) copy-start(bf16[384,128]{1,0:T(8,128)(2,1)} %copy-done.4) | copy-start | bytes 294916
